TPU v7x, 32 devices: a whole 2x2x4 slice. The times are simulated.
32 devices in a mesh: dp: 2 (over core), expert: 16 (over z, y, x).
Axes of the slice: x: 2, y: 2, z: 4, core: 2. Of those that a mesh axis runs over, the one named last changes fastest.
Arguments:
- tokens: bfloat16 [16, 256, 768], P('expert', 'dp'), may hold values from -6 to 6
- gain_one: bfloat16 [768], P(('dp', 'expert')), may hold values from 0.5 to 1.5
- w_query: bfloat16 [768, 768], P(('dp', 'expert')), may hold values from -0.21875 to 0.21875
- w_key: bfloat16 [768, 768], P(('dp', 'expert')), may hold values from -0.21875 to 0.21875
- w_value: bfloat16 [768, 768], P(('dp', 'expert')), may hold values from -0.21875 to 0.21875
- w_out: bfloat16 [768, 768], P(('dp', 'expert')), may hold values from -0.875 to 0.875
- bias_table: float32 [32, 12], replicated, may hold values from -6 to 6
- gain_two: bfloat16 [768], P(('dp', 'expert')), may hold values from 0.5 to 1.5
- w_router: bfloat16 [768, 16], P(('dp', 'expert')), may hold values from -0.15625 to 0.15625
- w_inner: bfloat16 [16, 768, 3072], P('expert', None, 'dp'), may hold values from -0.21875 to 0.21875
- w_outer: bfloat16 [16, 3072, 768], P('expert', 'dp'), may hold values from -2.5 to 2.5
- segment_ids: int32 [16, 256], P('expert'), may hold values from 0 to 3, never falling along the last dimension, each value on 1 to 128 neighbouring positions
- routes: int32 [16, 256, 1], P('expert', 'dp'), may hold values from 0 to 15
- out_grad: bfloat16 [16, 256, 768], P('expert', 'dp'), may hold values from -6 to 6
Outputs:
- layer_output: bfloat16 [16, 256, 768], P('expert', 'dp')
- input_grad: bfloat16 [16, 256, 768], P('expert', 'dp')
- gain_one_grad: float32 [768], P(('dp', 'expert'))
- query_grad: float32 [768, 768], P(('dp', 'expert'))
- key_grad: float32 [768, 768], P(('dp', 'expert'))
- value_grad: float32 [768, 768], P(('dp', 'expert'))
- out_proj_grad: float32 [768, 768], P(('dp', 'expert'))
- table_grad: float32 [32, 12], replicated
- gain_two_grad: float32 [768], P(('dp', 'expert'))
- router_grad: float32 [768, 16], P(('dp', 'expert'))
- inner_grad: float32 [16, 768, 3072], P('expert', None, 'dp')
- outer_grad: float32 [16, 3072, 768], P('expert', 'dp')
Inputs may be any that keep to these rules, and one draw needn't show every extreme that they name: `segment_ids`: in each row the ids never fall; every document holds 1 to 128 tokens, one exactly 128.
All inputs are finite; a program needn't handle non-finite values.
Results may differ from a plain program's by a relative error of at most 0.015.
Values may be sent and summed in bfloat16 or wider, within the bound.
No kernel may reach another device: no remote copies, remote signals or barrier semaphores. Data moves between devices by JAX's collectives and lax.ppermute only.
A program may use at most 128 MiB of HBM per device.

v0:
```python
import functools

import jax
import jax.numpy as jnp
from jax import lax
from jax.experimental import pallas as pl
from jax.experimental.pallas import tpu as pltpu
from jax.sharding import PartitionSpec as P

EPSILON = 1e-06
MASKED = -1000000000.0
BUCKET_EDGES = (1, 2, 3, 4, 5, 6, 7, 8, 12, 16, 23, 32, 46, 64, 91)
F32 = jnp.float32
BF16 = jnp.bfloat16
PAIR_BIT = 2
PAIR = 1 << PAIR_BIT
VMEM_BYTES = 48 * 1024 * 1024


def dot(left, right, dims=((1,), (0,))):
    return lax.dot_general(left, right, (dims, ((), ())), preferred_element_type=F32)


def rms_inverse(values):
    return lax.rsqrt(jnp.mean(values * values, axis=-1, keepdims=True) + EPSILON)


def norm_backward(grad_normed, unit_values, inverse, gain_values):
    grad_unit = grad_normed * gain_values
    projected = jnp.mean(grad_unit * unit_values, axis=-1, keepdims=True)
    return inverse * (grad_unit - unit_values * projected)


def swap_core(value):
    return lax.ppermute(value, "dp", [(0, 1), (1, 0)])


def swap_pair(value):
    n = lax.axis_size("expert")
    return lax.ppermute(value, "expert", [(i, i ^ PAIR) for i in range(n)])


def exchange(value):
    return lax.all_to_all(value, "expert", split_axis=0, concat_axis=0, tiled=True)


def bucket_of(offset, total):
    distance = jnp.abs(offset)
    bucket = jnp.zeros(offset.shape, jnp.int32)
    for border in BUCKET_EDGES:
        bucket = bucket + (distance >= border).astype(jnp.int32)
    return bucket + total // 2 * (offset > 0).astype(jnp.int32)


def iota(shape, axis):
    return lax.broadcasted_iota(jnp.int32, shape, axis)


def kernel_call(body, outs, *args, scalars=0, flops=1_000_000, nbytes=1_000_000):
    specs = [pl.BlockSpec(memory_space=pltpu.SMEM)] * scalars
    specs += [pl.BlockSpec(memory_space=pltpu.VMEM)] * (len(args) - scalars)
    return pl.pallas_call(
        body,
        out_shape=[jax.ShapeDtypeStruct(shape, dtype) for shape, dtype in outs],
        in_specs=specs,
        out_specs=[pl.BlockSpec(memory_space=pltpu.VMEM)] * len(outs),
        compiler_params=pltpu.CompilerParams(vmem_limit_bytes=VMEM_BYTES),
        cost_estimate=pl.CostEstimate(flops=flops, bytes_accessed=nbytes, transcendentals=0),
    )(*args)


def pack_weights(q_ref, k_ref, v_ref, router_ref, gains_ref, out_ref):
    rows, width = q_ref.shape
    experts = router_ref.shape[1]
    out_ref[:, :width] = q_ref[...]
    out_ref[:, width : 2 * width] = k_ref[...]
    out_ref[:, 2 * width : 3 * width] = v_ref[...]
    eye = iota((rows, rows), 0) == iota((rows, rows), 1)
    columns = [
        jnp.sum(jnp.where(eye, gains_ref[i : i + 1, :].astype(F32), 0.0), axis=1, keepdims=True)
        for i in range(2)
    ]
    pad = out_ref.shape[1] - 3 * width - experts - 2
    small = jnp.concatenate(
        [router_ref[...].astype(F32)] + columns + [jnp.zeros((rows, pad), F32)], axis=1
    )
    out_ref[:, 3 * width :] = small.astype(BF16)


def spread_weights(cols, core_ref, own_ref, other_ref, out_ref):
    sources, _, wide = out_ref.shape
    width = 4 * cols
    half = 2 * cols
    first = core_ref[0] == 0
    own = own_ref[...]
    other = other_ref[...]
    both = jnp.concatenate(
        [jnp.where(first, own, other), jnp.where(first, other, own)], axis=0
    )
    for variant in range(2):
        at = variant * cols
        parts = []
        for k in range(3):
            low = k * width + at
            high = low + half
            parts.append(jnp.where(first, both[:, low : low + cols], both[:, high : high + cols]))
        parts.append(both[:, 3 * width : 3 * width + wide - 3 * cols])
        value = jnp.concatenate(parts, axis=1)
        for dest in range(sources):
            if (dest >> PAIR_BIT) & 1 == variant:
                out_ref[dest] = value


def prepare(capacity, pad, core_ref, group_ref, table_ref, docs_ref, routes_ref, bias_ref,
            spread_ref, gather_ref, send_ref):
    buckets = table_ref.shape[0]
    own_heads = bias_ref.shape[1]
    length = docs_ref.shape[1]
    toks = length // 2
    group = group_ref[0]
    spot = iota((1, length), 1)
    offset = jnp.where(spot >= toks, spot - length, spot)
    bucket = bucket_of(offset, buckets)
    vectors = []
    for h in range(own_heads):
        vector = jnp.zeros((1, length), F32)
        for b in range(buckets):
            vector = jnp.where(bucket == b, table_ref[b, group * own_heads + h], vector)
        full = jnp.broadcast_to(vector, (length, length))
        vectors.append(pltpu.roll(full, 0, 1, stride=1, stride_axis=0))
    for r in range(2):
        across = jnp.broadcast_to(docs_ref[r : r + 1, :].astype(F32), (length, length))
        same = across == jnp.transpose(across)
        for h in range(own_heads):
            bias_ref[r, h] = jnp.where(same, vectors[h], MASKED)
    experts = spread_ref.shape[1] // pad
    route = routes_ref[...]
    chosen = route == iota((toks, experts), 1)
    lower = (iota((toks, toks), 0) > iota((toks, toks), 1)).astype(BF16)
    counts = dot(lower, chosen.astype(BF16))
    slot = jnp.sum(jnp.where(chosen, counts, 0.0), axis=1, keepdims=True).astype(jnp.int32)
    kept = slot < capacity
    place = jnp.where(kept, route * pad + slot, -1)
    spread = (place == iota((toks, experts * pad), 1)).astype(F32)
    spread_ref[...] = spread.astype(BF16)
    wide = send_ref.shape[0] // experts
    place = jnp.where(kept, route * wide + slot, -1)
    later = jnp.where(kept, route * wide + capacity + slot, -1)
    across = iota((toks, experts * wide), 1)
    send_ref[:, :toks] = jnp.transpose((place == across).astype(F32)).astype(BF16)
    send_ref[:, toks:] = jnp.transpose((later == across).astype(F32)).astype(BF16)
    gather_ref[...] = chosen.astype(F32)


def attend(scale, head_dim, experts, w_ref, own_ref, across_ref, bias_ref, wout_ref, qkv_ref,
           normed_ref, probs_ref, att_ref, keep_ref, send_ref, gains_ref):
    own_heads = bias_ref.shape[1]
    cols = own_heads * head_dim
    toks = own_ref.shape[1]
    small = w_ref[:, 3 * cols :]
    pick = (iota((8, small.shape[1]), 1) == iota((8, small.shape[1]), 0) + experts).astype(BF16)
    gains = dot(pick, small, ((1,), (1,)))
    gains_ref[...] = gains
    for r in range(2):
        x = jnp.concatenate([own_ref[r], across_ref[r]], axis=0).astype(F32)
        normed = (x * rms_inverse(x) * gains[0:1]).astype(BF16)
        normed_ref[r] = normed
        qkv = dot(normed, w_ref[:, : 3 * cols]).astype(BF16)
        qkv_ref[r] = qkv
        parts = []
        for h in range(own_heads):
            at = h * head_dim
            q = qkv[:, at : at + head_dim]
            k = qkv[:, cols + at : cols + at + head_dim]
            v = qkv[:, 2 * cols + at : 2 * cols + at + head_dim]
            scores = dot(q, k, ((1,), (1,))) * scale + bias_ref[r, h]
            top = jnp.max(scores, axis=1, keepdims=True)
            raised = jnp.exp(scores - top)
            probs = raised * (1.0 / jnp.sum(raised, axis=1, keepdims=True))
            probs_ref[r, h] = probs
            parts.append(dot(probs.astype(BF16), v))
        attended = jnp.concatenate(parts, axis=1).astype(BF16)
        att_ref[r] = attended
        partial = dot(attended, wout_ref[...])
        keep_ref[r] = partial[:toks]
        send_ref[r] = partial[toks:].astype(BF16)


def route_tokens(experts, x_ref, keep_ref, came_ref, gains_ref, w_ref, chosen_ref, send_ref,
                 g_ref, middle_ref, gate_ref, out_ref):
    middle = x_ref[...].astype(F32) + (keep_ref[...] + came_ref[...].astype(F32))
    middle_ref[...] = middle
    normed = (middle * rms_inverse(middle) * gains_ref[1:2]).astype(BF16)
    both = jnp.concatenate([normed, g_ref[...]], axis=0)
    out_ref[...] = dot(send_ref[...], both).astype(BF16)
    probs = jax.nn.softmax(dot(normed, w_ref[...]), axis=-1)
    gate_ref[...] = jnp.sum(probs * chosen_ref[...], axis=1, keepdims=True)


def run_expert(capacity, place_ref, own_ref, other_ref, router_ref, inner_ref, outer_ref,
               buf_ref, dslot_ref, g_ref, probs_ref, gate_ref, hidden_ref, dpre_ref, keep_ref,
               send_ref, acc_ref):
    step = pl.program_id(0)
    slots = buf_ref.shape[0] // 2
    experts = router_ref.shape[1]
    pad = own_ref.shape[0] // (slots // capacity)

    @pl.when(step == 0)
    def _():
        shape = (slots, own_ref.shape[0])
        row = iota(shape, 0)
        source = row // capacity
        wanted = source * pad + (row - source * capacity)
        first = (iota(shape, 1) == wanted).astype(BF16)
        second = (iota(shape, 1) == wanted + capacity).astype(BF16)
        mine = (iota((1, experts), 1) == place_ref[0]).astype(F32)
        for side, ref in enumerate((own_ref, other_ref)):
            at = side * slots
            rows = ref[...]
            buffers = dot(first, rows).astype(BF16)
            buf_ref[at : at + slots] = buffers
            g = dot(second, rows)
            probs = jax.nn.softmax(dot(buffers, router_ref[...]), axis=-1)
            gate = jnp.sum(probs * mine, axis=1, keepdims=True)
            dslot_ref[at : at + slots] = (gate * g).astype(BF16)
            if side == 0:
                g_ref[...] = g.astype(BF16)
                probs_ref[...] = probs
                gate_ref[...] = gate
        acc_ref[...] = jnp.zeros_like(acc_ref)

    inner = inner_ref[...]
    outer = outer_ref[...]
    pre = dot(buf_ref[...], inner)
    cdf = 0.5 * (1.0 + lax.erf(pre * (0.5**0.5)))
    hidden = (pre * cdf).astype(BF16)
    hidden_ref[...] = hidden
    slope = cdf + pre * jnp.exp(-0.5 * pre * pre) * 0.3989422804014327
    dpre = (dot(dslot_ref[...], outer, ((1,), (1,))) * slope).astype(BF16)
    dpre_ref[...] = dpre
    acc_ref[0] += dot(hidden, outer)
    acc_ref[1] += dot(dpre, inner, ((1,), (1,)))

    @pl.when(step == pl.num_programs(0) - 1)
    def _():
        keep_ref[...] = acc_ref[:, :slots]
        send_ref[...] = acc_ref[:, slots:].astype(BF16)


def finish_expert(capacity, place_ref, keep_ref, came_ref, buf_ref, g_ref, probs_ref, gate_ref,
                  router_ref, result_ref, back_ref, grad_ref):
    slots = g_ref.shape[0]
    experts = router_ref.shape[1]
    pad = result_ref.shape[0] // (slots // capacity)
    total = (keep_ref[...] + came_ref[...].astype(F32)).astype(BF16)
    result = total[0]
    mine = (iota((1, experts), 1) == place_ref[0]).astype(F32)
    grad_gate = jnp.sum(g_ref[...].astype(F32) * result.astype(F32), axis=1, keepdims=True)
    grad_logits = (grad_gate * gate_ref[...] * (mine - probs_ref[...])).astype(BF16)
    grad_ref[...] = dot(buf_ref[...], grad_logits, ((0,), (0,))).astype(BF16)
    back = total[1].astype(F32) + dot(grad_logits, router_ref[...], ((1,), (1,)))
    shape = (result_ref.shape[0], slots)
    row = iota(shape, 0)
    source = row // pad
    inside = row - source * pad
    wanted = jnp.where(inside < capacity, source * capacity + inside, -1)
    expand = (iota(shape, 1) == wanted).astype(BF16)
    back_ref[...] = dot(expand, back.astype(BF16)).astype(BF16)
    result_ref[...] = dot(expand, result).astype(BF16)


def norm_two_backward(back_ref, spread_ref, middle_ref, gains_ref, g_ref, dmiddle_ref, da_ref,
                      gain_ref):
    middle = middle_ref[...]
    inverse = rms_inverse(middle)
    unit = middle * inverse
    grad_normed = dot(spread_ref[...], back_ref[...])
    gain_ref[...] = jnp.sum(grad_normed * unit, axis=0, keepdims=True)
    dmiddle = g_ref[...].astype(F32) + norm_backward(grad_normed, unit, inverse, gains_ref[1:2])
    dmiddle_ref[...] = dmiddle
    da_ref[...] = dmiddle.astype(BF16)


def finish_layer(result_ref, spread_ref, middle_ref, gate_ref, out_ref):
    combined = dot(spread_ref[...], result_ref[...])
    out_ref[...] = (middle_ref[...] + gate_ref[...] * combined).astype(BF16)


def attend_backward(scale, head_dim, buckets, own_ref, across_ref, wout_ref, att_ref, qkv_ref,
                    probs_ref, normed_ref, w_ref, x_own_ref, x_across_ref, gout_ref, gw_ref,
                    keep_ref, send_ref, gain_ref, table_ref):
    own_heads = probs_ref.shape[1]
    cols = own_heads * head_dim
    toks = own_ref.shape[1]
    length = 2 * toks
    width = own_ref.shape[2]
    flip = (iota((length, length), 0) + iota((length, length), 1) == length - 1).astype(BF16)
    wout = wout_ref[...]
    grads = []
    diagonals = [jnp.zeros((length, length), F32)] * own_heads
    for r in range(2):
        da = jnp.concatenate([own_ref[r], across_ref[r]], axis=0)
        grads.append(da)
        grad_att = dot(da, wout, ((1,), (1,))).astype(BF16)
        qkv = qkv_ref[r]
        parts = [[], [], []]
        for h in range(own_heads):
            at = h * head_dim
            q = qkv[:, at : at + head_dim]
            k = qkv[:, cols + at : cols + at + head_dim]
            v = qkv[:, 2 * cols + at : 2 * cols + at + head_dim]
            gh = grad_att[:, at : at + head_dim]
            probs = probs_ref[r, h]
            grad_probs = dot(gh, v, ((1,), (1,)))
            row_dot = jnp.sum(probs * grad_probs, axis=1, keepdims=True)
            ds = (probs * (grad_probs - row_dot)).astype(BF16)
            diagonals[h] = diagonals[h] + dot(flip, ds)
            parts[0].append(dot(ds, k) * scale)
            parts[1].append(dot(ds, q, ((0,), (0,))) * scale)
            parts[2].append(dot(probs.astype(BF16), gh, ((0,), (0,))))
        grad_qkv = jnp.concatenate(parts[0] + parts[1] + parts[2], axis=1).astype(BF16)
        weights = dot(normed_ref[r], grad_qkv, ((0,), (0,)))
        outs = dot(att_ref[r], da, ((0,), (0,)))
        grad_normed = dot(grad_qkv, w_ref[:, : 3 * cols], ((1,), (1,)))
        x = jnp.concatenate([x_own_ref[r], x_across_ref[r]], axis=0).astype(F32)
        gain = jnp.sum(grad_normed * (x * rms_inverse(x)), axis=0, keepdims=True)
        keep_ref[r] = grad_normed[:toks]
        send_ref[r] = grad_normed[toks:].astype(BF16)
        if r == 0:
            total, total_out, total_gain = weights, outs, gain
        else:
            total, total_out, total_gain = total + weights, total_out + outs, total_gain + gain
    gw_ref[...] = total.astype(BF16)
    gout_ref[...] = total_out.astype(BF16)
    gain_ref[...] = total_gain
    spot = iota((1, length), 1)
    offset = jnp.where(spot >= toks, spot - length, spot)
    bucket = bucket_of(offset, buckets)
    belongs = iota((buckets, length), 0) == bucket
    sums = []
    for h in range(own_heads):
        turned = pltpu.roll(diagonals[h], 1, 1, stride=1, stride_axis=0)
        by_offset = jnp.sum(turned, axis=0, keepdims=True)
        sums.append(jnp.sum(jnp.where(belongs, by_offset, 0.0), axis=1, keepdims=True))
    table_ref[...] = jnp.concatenate(sums, axis=1)


def gather_rows(w_out, place, sources):
    top = sources.bit_length() - 2
    if top != PAIR_BIT:
        w_out = lax.ppermute(w_out, "expert", swap_bits(sources))
    for level in range(top):
        bit = top if level == PAIR_BIT else level
        came = lax.ppermute(w_out, "expert", [(i, i ^ (1 << bit)) for i in range(sources)])
        low = (place >> bit) & 1 == 0
        w_out = jnp.where(
            low, jnp.concatenate([w_out, came], axis=0), jnp.concatenate([came, w_out], axis=0)
        )
    return w_out


def scatter_rows(grad, place, sources):
    top = sources.bit_length() - 2
    for level in reversed(range(top)):
        bit = top if level == PAIR_BIT else level
        middle = grad.shape[0] // 2
        low = (place >> bit) & 1 == 0
        away = jnp.where(low, grad[middle:], grad[:middle])
        came = lax.ppermute(
            away.astype(BF16), "expert", [(i, i ^ (1 << bit)) for i in range(sources)]
        )
        grad = jnp.where(low, grad[:middle], grad[middle:]).astype(F32) + came.astype(F32)
    if top != PAIR_BIT:
        grad = lax.ppermute(grad.astype(BF16), "expert", swap_bits(sources))
    return grad.astype(F32)


def swap_bits(sources):
    top = sources.bit_length() - 2
    pairs = []
    for i in range(sources):
        high, low = (i >> top) & 1, (i >> PAIR_BIT) & 1
        rest = i & ~((1 << top) | (1 << PAIR_BIT))
        pairs.append((i, rest | (low << top) | (high << PAIR_BIT)))
    return pairs


def local(
    tokens,
    gain_one,
    w_query,
    w_key,
    w_value,
    w_out,
    bias_table,
    gain_two,
    w_router,
    w_inner,
    w_outer,
    segment_ids,
    routes,
    out_grad,
):
    toks = tokens.shape[1]
    width = tokens.shape[2]
    heads = bias_table.shape[1]
    buckets = bias_table.shape[0]
    head_dim = width // heads
    own_heads = heads // 4
    cols = own_heads * head_dim
    length = 2 * toks
    scale = head_dim ** (-0.5)
    sources = lax.axis_size("expert")
    experts = sources
    capacity = (5 * toks + 4 * experts - 1) // (4 * experts)
    slots = experts * capacity
    pad = -(-capacity // 8) * 8
    pad_two = -(-2 * capacity // 8) * 8
    rows = w_query.shape[0]
    core = lax.axis_index("dp")
    place = lax.axis_index("expert")
    member = (place >> PAIR_BIT) & 1
    first_core = core == 0
    core_at = core.reshape(1).astype(jnp.int32)
    place_at = place.reshape(1).astype(jnp.int32)
    group_at = (2 * core + member).reshape(1).astype(jnp.int32)
    wide = -(-(3 * cols + experts + 2) // 128) * 128
    small = -(-(experts + 2) // 128) * 128

    gains = jnp.stack([gain_one, gain_two])
    (packed,) = kernel_call(
        pack_weights, [((rows, 3 * width + small), BF16)], w_query, w_key, w_value, w_router, gains
    )
    (message,) = kernel_call(
        functools.partial(spread_weights, cols),
        [((sources, 2 * rows, wide), BF16)],
        core_at, packed, swap_core(packed), scalars=1,
    )
    weights = exchange(message)
    weights = (
        weights.reshape(sources, 2, rows, wide).transpose(1, 0, 2, 3).reshape(width, wide)
    )
    router_w = weights[:, 3 * cols : 3 * cols + experts]
    out_w = gather_rows(w_out, place, sources)

    own_tokens = tokens.reshape(toks, width)
    x_own = jnp.stack([own_tokens, swap_pair(own_tokens)])
    x_across = swap_core(x_own)
    docs_two = jnp.concatenate([segment_ids, swap_pair(segment_ids)], axis=0)
    docs = jnp.where(first_core, docs_two, jnp.roll(docs_two, toks, axis=1))
    bias, spread, chosen, send = kernel_call(
        functools.partial(prepare, capacity, pad),
        [
            ((2, own_heads, length, length), F32),
            ((toks, experts * pad), BF16),
            ((toks, experts), F32),
            ((experts * pad_two, 2 * toks), BF16),
        ],
        core_at, group_at, bias_table, docs, routes.reshape(toks, 1), scalars=3,
    )
    g_low = out_grad.reshape(toks, width)

    qkv, normed, probs, attended, keep, away, gain_rows = kernel_call(
        functools.partial(attend, scale, head_dim, experts),
        [
            ((2, length, 3 * cols), BF16),
            ((2, length, width), BF16),
            ((2, own_heads, length, length), F32),
            ((2, length, cols), BF16),
            ((2, toks, width), F32),
            ((2, toks, width), BF16),
            ((8, width), F32),
        ],
        weights, x_own, x_across, bias, out_w,
    )
    keep = keep + swap_core(away).astype(F32)
    middle, gate, outgoing = kernel_call(
        functools.partial(route_tokens, experts),
        [((toks, width), F32), ((toks, 1), F32), ((experts * pad_two, width), BF16)],
        own_tokens, keep[0], swap_pair(keep[1].astype(BF16)), gain_rows, router_w, chosen, send,
        g_low,
    )
    incoming = exchange(outgoing.reshape(experts, pad_two, width)).reshape(-1, width)

    inner, outer = w_inner[0], w_outer[0]
    units = inner.shape[1]
    chunk = units // 3
    fixed = lambda shape: pl.BlockSpec(shape, lambda i: (0,) * len(shape))
    outs = [
        ((2 * slots, width), BF16, None),
        ((2 * slots, width), BF16, None),
        ((slots, width), BF16, None),
        ((slots, experts), F32, None),
        ((slots, 1), F32, None),
        ((2 * slots, units), BF16, pl.BlockSpec((2 * slots, chunk), lambda i: (0, i))),
        ((2 * slots, units), BF16, pl.BlockSpec((2 * slots, chunk), lambda i: (0, i))),
        ((2, slots, width), F32, None),
        ((2, slots, width), BF16, None),
    ]
    buffers, dslot, slot_g, slot_probs, slot_gate, hidden, dpre, keep, away = pl.pallas_call(
        functools.partial(run_expert, capacity),
        grid=(units // chunk,),
        out_shape=[jax.ShapeDtypeStruct(shape, dtype) for shape, dtype, _ in outs],
        in_specs=[
            pl.BlockSpec(memory_space=pltpu.SMEM),
            fixed((experts * pad_two, width)),
            fixed((experts * pad_two, width)),
            fixed((width, experts)),
            pl.BlockSpec((width, chunk), lambda i: (0, i)),
            pl.BlockSpec((chunk, width), lambda i: (i, 0)),
        ],
        out_specs=[spec or fixed(shape) for shape, _, spec in outs],
        scratch_shapes=[pltpu.VMEM((2, 2 * slots, width), F32)],
        compiler_params=pltpu.CompilerParams(vmem_limit_bytes=VMEM_BYTES),
    )(place_at, incoming, swap_core(incoming), router_w, inner, outer)
    grad_outer = dot(hidden, dslot, ((0,), (0,)))
    grad_inner = dot(buffers, dpre, ((0,), (0,)))
    result, back, grad_router = kernel_call(
        functools.partial(finish_expert, capacity),
        [
            ((sources * pad, width), BF16),
            ((sources * pad, width), BF16),
            ((width, experts), BF16),
        ],
        place_at, keep, swap_core(away), buffers[:slots], slot_g, slot_probs, slot_gate, router_w,
        scalars=1,
    )
    back = exchange(back.reshape(sources, pad, width)).reshape(-1, width)
    result = exchange(result.reshape(sources, pad, width)).reshape(-1, width)

    grad_middle, grad_attn, grad_gain_two = kernel_call(
        norm_two_backward,
        [((toks, width), F32), ((toks, width), BF16), ((1, width), F32)],
        back, spread, middle, gain_rows, g_low,
    )
    g_own = jnp.stack([grad_attn, swap_pair(grad_attn)])
    grad_out, grad_weights, keep, away, grad_gain_one, grad_table = kernel_call(
        functools.partial(attend_backward, scale, head_dim, buckets),
        [
            ((cols, width), BF16),
            ((width, 3 * cols), BF16),
            ((2, toks, width), F32),
            ((2, toks, width), BF16),
            ((1, width), F32),
            ((buckets, own_heads), F32),
        ],
        g_own, swap_core(g_own), out_w, attended, qkv, probs, normed, weights, x_own, x_across,
    )
    (final,) = kernel_call(
        finish_layer, [((toks, width), BF16)], result, spread, middle, gate
    )
    grad_out = scatter_rows(grad_out, place, sources)

    table_cols = max(1, own_heads * buckets // (2 * rows))
    table_rows = own_heads * buckets // table_cols
    table_part = jnp.zeros((2 * rows, table_cols), F32)
    table_part = table_part.at[:table_rows].set(grad_table.reshape(table_rows, table_cols))
    narrow = jnp.concatenate([grad_gain_one, grad_gain_two], axis=0).T.astype(BF16)
    narrow = jnp.concatenate([grad_weights, grad_router, narrow], axis=1)
    spread_cols = narrow.shape[1]
    narrow = narrow.reshape(2, sources, rows, spread_cols).transpose(1, 0, 2, 3)
    narrow = narrow.reshape(sources, 2 * rows, spread_cols)
    table_part = jnp.broadcast_to(
        table_part[None].astype(BF16), (sources, 2 * rows, table_cols)
    )
    message = jnp.concatenate([narrow, table_part], axis=2)
    arrived = exchange(message).astype(F32)
    by_parity = arrived.reshape(sources >> (PAIR_BIT + 1), 2, PAIR, 2 * rows, -1)
    summed = jnp.sum(by_parity, axis=(0, 2))
    by_member = summed[:, :, : 3 * cols].reshape(2, 2, rows, 3, cols)
    smalls = jnp.sum(summed[:, :, 3 * cols : spread_cols], axis=0)
    smalls = smalls.reshape(2, rows, spread_cols - 3 * cols)
    tables = summed[:, :table_rows, spread_cols:].reshape(2, buckets, own_heads)
    tables = tables.transpose(1, 0, 2).reshape(buckets, 2 * own_heads)
    mine_w = jnp.where(first_core, by_member[:, 0], by_member[:, 1])
    away_w = jnp.where(first_core, by_member[:, 1], by_member[:, 0])
    mine_s = jnp.where(first_core, smalls[0], smalls[1])
    away_s = jnp.where(first_core, smalls[1], smalls[0])
    came_w = swap_core(away_w.astype(BF16)).astype(F32)
    came_s = swap_core(away_s)
    came_t = swap_core(tables)
    full = jnp.where(first_core, jnp.stack([mine_w, came_w]), jnp.stack([came_w, mine_w]))
    full = full.transpose(3, 2, 0, 1, 4).reshape(3, rows, width)
    smalls = mine_s + came_s
    table_sum = jnp.where(
        first_core,
        jnp.concatenate([tables, came_t], axis=1),
        jnp.concatenate([came_t, tables], axis=1),
    )

    keep = keep + swap_core(away).astype(F32)
    grad_normed_one = keep[0] + swap_pair(keep[1].astype(BF16)).astype(F32)
    x = own_tokens.astype(F32)
    inverse_one = rms_inverse(x)
    grad_input = grad_middle + norm_backward(
        grad_normed_one, x * inverse_one, inverse_one, gain_rows[0:1]
    )
    return (
        final.reshape(tokens.shape),
        grad_input.astype(BF16).reshape(tokens.shape),
        smalls[:, experts],
        full[0],
        full[1],
        full[2],
        grad_out,
        table_sum,
        smalls[:, experts + 1],
        smalls[:, :experts],
        grad_inner[None],
        grad_outer[None],
    )


def solution(mesh):
    both = ("dp", "expert")
    return jax.shard_map(
        local,
        mesh=mesh,
        in_specs=(
            P("expert", "dp", None),
            P(both),
            P(both, None),
            P(both, None),
            P(both, None),
            P(both, None),
            P(),
            P(both),
            P(both, None),
            P("expert", None, "dp"),
            P("expert", "dp", None),
            P("expert", None),
            P("expert", "dp", None),
            P("expert", "dp", None),
        ),
        out_specs=(
            P("expert", "dp", None),
            P("expert", "dp", None),
            P(both),
            P(both, None),
            P(both, None),
            P(both, None),
            P(both, None),
            P(),
            P(both),
            P(both, None),
            P("expert", None, "dp"),
            P("expert", "dp", None),
        ),
        check_vma=False,
    )
```

profile of v0, /device:TPU:3, one launch (start us, length us, event | category | flops | bytes accessed | tf_op | source)
XLA Modules:
  0.0 196.7 jit_solution(12639536967028351439)
XLA Ops:
  5.2 1.0 collective-permute-done.other_ref
  6.2 1.1 shard_map.235
  7.3 6.7 %all-to-all-start = ((bf16[16,48,640]{2,1,0:T(8,128)(2,1)}), bf16[16,48,640]{2,1,0:T(8,128)(2,1)}, u32[]{:S(2)}, u32[]{:S(2)}) async-start(bf16[16,48,640]{2,1,0:T(8,128)(2,1)} %shard_map.235), calls=%async_computation | async-start | bytes 1966080 | tf_op jit(solution)/shard_map/all_to_all | solution.py:44
  14.0 1.2 collective-permute-start.1
  16.3 22.8 %collective-permute-start.3 = (s32[1,256]{1,0:T(1,128)S(1)}, s32[1,256]{1,0:T(1,128)S(1)}, u32[]{:S(2)}, u32[]{:S(2)}) collective-permute-start(s32[1,256]{1,0:T(1,128)S(1)} %copy-done.31), channel_id=1, source_target_pairs={{0,4},{1,5},{2,6},{3,7},{4,0},{5,1},{6,2},{7,3},{8,12},{9,13},{10,... | collective-permute-start | bytes 3080 | tf_op jit(solution)/shard_map/ppermute | solution.py:40
  39.4 1.0 collective-permute-start.6
  40.4 2.5 %collective-permute-start.2 = (bf16[2,128,768]{2,1,0:T(8,128)(2,1)S(1)}, bf16[2,128,768]{2,1,0:T(8,128)(2,1)S(1)}, u32[]{:S(2)}, u32[]{:S(2)}) collective-permute-start(bf16[2,128,768]{2,1,0:T(8,128)(2,1)S(1)} %pad_maximum_fusion.2.own_ref.x_own_ref), channel_id=1, source_target_pairs={{0,16},{16,0},{1,17},{17,1},{2,18},{18,2},{3,19},{19,3},{4,20},{20... | collective-permute-start | bytes 1179656 | tf_op jit(solution)/shard_map/ppermute | solution.py:35
  42.9 2.9 %collective-permute-start.7 = (bf16[96,768]{1,0:T(8,128)(2,1)S(1)}, bf16[96,768]{1,0:T(8,128)(2,1)S(1)}, u32[]{:S(2)}, u32[]{:S(2)}) collective-permute-start(bf16[96,768]{1,0:T(8,128)(2,1)S(1)} %maximum_select_fusion.2), channel_id=1, source_target_pairs={{0,8},{1,9},{2,10},{3,11},{4,12},{5,13},{6,14},{7,15},{8,0},{9,1},... | collective-permute-start | bytes 442376 | tf_op jit(solution)/shard_map/ppermute | solution.py:354
  45.9 1.6 shard_map.236
  47.5 1.1 copy-done.2
  48.7 1.3 copy.72
  50.0 5.4 %shard_map.237 = (bf16[2,256,576]{2,1,0:T(8,128)(2,1)S(1)}, bf16[2,256,768]{2,1,0:T(8,128)(2,1)S(1)}, f32[2,3,256,256]{3,2,1,0:T(8,128)}, bf16[2,256,192]{2,1,0:...) custom-call(bf16[768,640]{1,0:T(8,128)(2,1)S(1)} %bitcast.89, ...), custom_call_target="tpu_custom_call" | custom-call | flops 1000000 | bytes 1000000 | tf_op jit(solution)/shard_map/pallas_call | solution.py:62
  55.4 4.2 %collective-permute-start.8 = (bf16[2,128,768]{2,1,0:T(8,128)(2,1)S(1)}, bf16[2,128,768]{2,1,0:T(8,128)(2,1)S(1)}, u32[]{:S(2)}, u32[]{:S(2)}) collective-permute-start(bf16[2,128,768]{2,1,0:T(8,128)(2,1)S(1)} %get-tuple-element.69), channel_id=1, source_target_pairs={{0,16},{16,0},{1,17},{17,1},{2,18},{18,2},{3,19},{19,3},{4,20},{20... | collective-permute-start | bytes 1179656 | tf_op jit(solution)/shard_map/ppermute | solution.py:35
  59.8 1.2 collective-permute-done.8
  61.1 2.0 %collective-permute-start.9 = (bf16[128,768]{1,0:T(8,128)(2,1)S(1)}, bf16[128,768]{1,0:T(8,128)(2,1)S(1)}, u32[]{:S(2)}, u32[]{:S(2)}) collective-permute-start(bf16[128,768]{1,0:T(8,128)(2,1)S(1)} %fusion.11), channel_id=1, source_target_pairs={{0,4},{1,5},{2,6},{3,7},{4,0},{5,1},{6,2},{7,3},{8,12},{9,13},{10,... | collective-permute-start | bytes 589832 | tf_op jit(solution)/shard_map/ppermute | solution.py:40
  63.1 4.9 %collective-permute-done.9.came_ref = bf16[128,768]{1,0:T(8,128)(2,1)S(1)} collective-permute-done((bf16[128,768]{1,0:T(8,128)(2,1)S(1)}, bf16[128,768]{1,0:T(8,128)(2,1)S(1)}, u32[]{:S(2)}, u32[]{:S(2)}) %collective-permute-start.9) | collective-permute-done | bytes 196640 | tf_op jit(solution)/shard_map/ppermute | solution.py:40
  68.9 20.8 %all_to_all.25 = bf16[16,24,768]{2,1,0:T(8,128)(2,1)S(1)} all-to-all(bf16[16,24,768]{2,1,0:T(8,128)(2,1)S(1)} %bitcast.100), channel_id=1, replica_groups=mesh['dp'=2,'expert'=16] {'expert'}, dimensions={0} | all-to-all | bytes 1179648 | tf_op jit(solution)/shard_map/all_to_all | solution.py:44
  89.7 1.9 collective-permute-start.10
  91.6 1.6 collective-permute-done.10.other_ref
  93.2 6.6 %shard_map.239 = (bf16[320,768]{1,0:T(8,128)(2,1)S(1)}, bf16[320,768]{1,0:T(8,128)(2,1)S(1)}, bf16[160,768]{1,0:T(8,128)(2,1)S(1)}, f32[160,16]{1,0:T(8,128)S(1)...) custom-call(s32[1]{0:T(128)} %bitcast.place_ref, ...), custom_call_target="tpu_custom_call" | custom-call | tf_op jit(solution)/shard_map/pallas_call | solution.py:500
  100.3 1.5 collective-permute-done.11.came_ref
  102.7 14.1 %all_to_all.26 = bf16[16,16,768]{2,1,0:T(8,128)(2,1)S(1)} all-to-all(bf16[16,16,768]{2,1,0:T(8,128)(2,1)S(1)} %bitcast.102), channel_id=1, replica_groups=mesh['dp'=2,'expert'=16] {'expert'}, dimensions={0} | all-to-all | bytes 786432 | tf_op jit(solution)/shard_map/all_to_all | solution.py:44
  118.6 3.9 %collective-permute-done.12 = bf16[128,768]{1,0:T(8,128)(2,1)S(1)} collective-permute-done((bf16[128,768]{1,0:T(8,128)(2,1)S(1)}, bf16[128,768]{1,0:T(8,128)(2,1)S(1)}, u32[]{:S(2)}, u32[]{:S(2)}) %collective-permute-start.12) | collective-permute-done | bytes 196640 | tf_op jit(solution)/shard_map/ppermute | solution.py:40
  122.5 3.3 %collective-permute-start.13 = (bf16[2,128,768]{2,1,0:T(8,128)(2,1)S(1)}, bf16[2,128,768]{2,1,0:T(8,128)(2,1)S(1)}, u32[]{:S(2)}, u32[]{:S(2)}) collective-permute-start(bf16[2,128,768]{2,1,0:T(8,128)(2,1)S(1)} %pad_maximum_fusion.3.own_ref), channel_id=1, source_target_pairs={{0,16},{16,0},{1,17},{17,1},{2,18},{18,2},{3,19},{19,3},{4,20},{20... | collective-permute-start | bytes 1179656 | tf_op jit(solution)/shard_map/ppermute | solution.py:35
  125.9 4.8 %all-to-all-start.2 = ((bf16[16,16,768]{2,1,0:T(8,128)(2,1)}), bf16[16,16,768]{2,1,0:T(8,128)(2,1)S(1)}, u32[]{:S(2)}, u32[]{:S(2)}) async-start(bf16[16,16,768]{2,1,0:T(8,128)(2,1)} %bitcast.101), calls=%async_computation.2 | async-start | bytes 786432 | tf_op jit(solution)/shard_map/all_to_all | solution.py:44
  131.5 1.1 copy-done.7
  132.6 1.1 copy-done.12
  133.7 1.0 copy-done.14
  134.7 0.9 copy-done.19
  135.6 6.5 %shard_map.243 = (bf16[192,768]{1,0:T(8,128)(2,1)S(1)}, bf16[768,576]{1,0:T(8,128)(2,1)S(1)}, f32[2,128,768]{2,1,0:T(8,128)S(1)}, bf16[2,128,768]{2,1,0:T(8,128)...) custom-call(bf16[2,128,768]{2,1,0:T(8,128)(2,1)S(1)} %pad_maximum_fusion.3.own_ref, ...), custom_call_target="tpu_custom_call" | custom-call | flops 1000000 | bytes 1000000 | tf_op jit(solution)/shard_map/pallas_call | solution.py:62
  142.2 0.9 copy-done.5
  143.1 0.9 copy-done.8
  144.1 2.2 %collective-permute-start.18 = (bf16[96,768]{1,0:T(8,128)(2,1)S(1)}, bf16[96,768]{1,0:T(8,128)(2,1)}, u32[]{:S(2)}, u32[]{:S(2)}) collective-permute-start(bf16[96,768]{1,0:T(8,128)(2,1)S(1)} %broadcast_select_fusion), channel_id=1, source_target_pairs={{0,8},{1,9},{2,10},{3,11},{4,12},{5,13},{6,14},{7,15},{8,0},{9,1},... | collective-permute-start | bytes 442376 | tf_op jit(solution)/shard_map/ppermute | solution.py:369
  146.5 1.5 pad_maximum_fusion
  148.1 0.9 collective-permute-start.14
  149.1 4.1 %collective-permute-done.18 = bf16[96,768]{1,0:T(8,128)(2,1)} collective-permute-done((bf16[96,768]{1,0:T(8,128)(2,1)S(1)}, bf16[96,768]{1,0:T(8,128)(2,1)}, u32[]{:S(2)}, u32[]{:S(2)}) %collective-permute-start.18) | collective-permute-done | bytes 147488 | tf_op jit(solution)/shard_map/ppermute | solution.py:369
  153.1 1.0 convert_add_fusion.2
  154.1 1.3 collective-permute-start.19
  155.4 1.1 pad_maximum_fusion.1
  158.1 6.9 %all-to-all-start.4 = ((bf16[16,48,596]{2,1,0:T(8,128)(2,1)}), bf16[16,48,596]{2,1,0:T(8,128)(2,1)}, u32[]{:S(2)}, u32[]{:S(2)}) async-start(bf16[16,48,596]{2,1,0:T(8,128)(2,1)} %pad_maximum_fusion.1), calls=%async_computation.4 | async-start | bytes 1966080 | tf_op jit(solution)/shard_map/all_to_all | solution.py:44
  165.1 3.6 %convolution_bitcast_fusion.1 = f32[1,768,1536]{2,1,0:T(8,128)} fusion(bf16[320,768]{1,0:T(8,128)(2,1)S(1)} %get-tuple-element.76, bf16[320,1536]{1,0:T(8,128)(2,1)S(1)} %copy-done.4), kind=kOutput, calls=%fused_computation.1 | convolution fusion | flops 754974720 | bytes 6193152 | tf_op jit(solution)/shard_map/dot_general | solution.py:21
  169.5 1.1 convert_add_fusion
  170.6 3.7 %collective-permute-start.15 = (bf16[128,768]{1,0:T(8,128)(2,1)S(1)}, bf16[128,768]{1,0:T(8,128)(2,1)S(1)}, u32[]{:S(2)}, u32[]{:S(2)}) collective-permute-start(bf16[128,768]{1,0:T(8,128)(2,1)S(1)} %fusion.12), channel_id=1, source_target_pairs={{0,4},{1,5},{2,6},{3,7},{4,0},{5,1},{6,2},{7,3},{8,12},{9,13},{10,... | collective-permute-start | bytes 589832 | tf_op jit(solution)/shard_map/ppermute | solution.py:40
  174.3 3.6 %convolution_bitcast_fusion = f32[1,1536,768]{2,1,0:T(8,128)} fusion(bf16[320,1536]{1,0:T(8,128)(2,1)S(1)} %copy-done.27, bf16[320,768]{1,0:T(8,128)(2,1)S(1)} %copy-done.29), kind=kOutput, calls=%fused_computation | convolution fusion | flops 754974720 | bytes 6193152 | tf_op jit(solution)/shard_map/dot_general | solution.py:21
  177.9 0.9 shard_map.241
  179.5 5.4 %collective-permute-done.15 = bf16[128,768]{1,0:T(8,128)(2,1)S(1)} collective-permute-done((bf16[128,768]{1,0:T(8,128)(2,1)S(1)}, bf16[128,768]{1,0:T(8,128)(2,1)S(1)}, u32[]{:S(2)}, u32[]{:S(2)}) %collective-permute-start.15) | collective-permute-done | bytes 196640 | tf_op jit(solution)/shard_map/ppermute | solution.py:40
  186.0 1.4 convert_reduce_fusion
  188.0 3.1 %collective-permute-start.22 = (f32[32,6]{0,1:T(8,128)S(1)}, f32[32,6]{0,1:T(8,128)S(1)}, u32[]{:S(2)}, u32[]{:S(2)}) collective-permute-start(f32[32,6]{0,1:T(8,128)S(1)} %reshape.193), channel_id=1, source_target_pairs={{0,16},{16,0},{1,17},{17,1},{2,18},{18,2},{3,19},{19,3},{4,20},{20... | collective-permute-start | bytes 2312 | tf_op jit(solution)/shard_map/ppermute | solution.py:35
  (151 shorter events, 21.9 us)
Async XLA Ops:
  0.6 13.4 %copy-start.1 = (bf16[1,128,768]{2,1,0:T(8,128)(2,1)S(1)}, bf16[1,128,768]{2,1,0:T(8,128)(2,1)}, u32[]{:S(2)}) copy-start(bf16[1,128,768]{2,1,0:T(8,128)(2,1)} %param.18) | copy-start | bytes 589828
  4.4 10.9 %copy-start.33 = (bf16[24,768]{1,0:T(8,128)(2,1)S(1)}, bf16[24,768]{1,0:T(8,128)(2,1)}, u32[]{:S(2)}) copy-start(bf16[24,768]{1,0:T(8,128)(2,1)} %param.23) | copy-start | bytes 110596
  4.4 11.9 %copy-start.31 = (s32[1,256]{1,0:T(1,128)S(1)}, s32[1,256]{1,0:T(1,128)}, u32[]{:S(2)}) copy-start(s32[1,256]{1,0:T(1,128)} %param.29) | copy-start | bytes 3076
  4.5 34.7 %copy-start.30 = (f32[32,12]{0,1:T(8,128)S(1)}, f32[32,12]{0,1:T(8,128)}, u32[]{:S(2)}) copy-start(f32[32,12]{0,1:T(8,128)} %param.24) | copy-start | bytes 4612
  4.5 34.8 %copy-start.32 = (s32[1,128,1]{1,2,0:T(1,128)S(1)}, s32[1,128,1]{1,2,0:T(1,128)}, u32[]{:S(2)}) copy-start(s32[1,128,1]{1,2,0:T(1,128)} %param.30) | copy-start | bytes 1540
  4.5 1.6 collective-permute-start
  7.3 41.4 %all-to-all-start = ((bf16[16,48,640]{2,1,0:T(8,128)(2,1)}), bf16[16,48,640]{2,1,0:T(8,128)(2,1)}, u32[]{:S(2)}, u32[]{:S(2)}) async-start(bf16[16,48,640]{2,1,0:T(8,128)(2,1)} %shard_map.235), calls=%async_computation | async-start | bytes 1966080 | tf_op jit(solution)/shard_map/all_to_all | solution.py:44
  14.0 26.3 %collective-permute-start.1 = (bf16[128,768]{1,0:T(8,128)(2,1)S(1)}, bf16[128,768]{1,0:T(8,128)(2,1)S(1)}, u32[]{:S(2)}, u32[]{:S(2)}) collective-permute-start(bf16[128,768]{1,0:T(8,128)(2,1)S(1)} %bitcast.92), channel_id=1, source_target_pairs={{0,4},{1,5},{2,6},{3,7},{4,0},{5,1},{6,2},{7,3},{8,12},{9,13},{10,... | collective-permute-start | bytes 589832 | tf_op jit(solution)/shard_map/ppermute | solution.py:40
  15.3 0.7 collective-permute-start.4
  16.0 23.4 %collective-permute-start.5 = (bf16[24,768]{1,0:T(8,128)(2,1)S(1)}, bf16[24,768]{1,0:T(8,128)(2,1)S(1)}, u32[]{:S(2)}, u32[]{:S(2)}) collective-permute-start(bf16[24,768]{1,0:T(8,128)(2,1)S(1)} %collective-permute-done.4), channel_id=1, source_target_pairs={{0,1},{1,0},{2,3},{3,2},{4,5},{5,4},{6,7},{7,6},{8,9},{9,8},{10,11... | collective-permute-start | bytes 110600 | tf_op jit(solution)/shard_map/ppermute | solution.py:354
  16.3 29.6 %collective-permute-start.3 = (s32[1,256]{1,0:T(1,128)S(1)}, s32[1,256]{1,0:T(1,128)S(1)}, u32[]{:S(2)}, u32[]{:S(2)}) collective-permute-start(s32[1,256]{1,0:T(1,128)S(1)} %copy-done.31), channel_id=1, source_target_pairs={{0,4},{1,5},{2,6},{3,7},{4,0},{5,1},{6,2},{7,3},{8,12},{9,13},{10,... | collective-permute-start | bytes 3080 | tf_op jit(solution)/shard_map/ppermute | solution.py:40
  39.4 3.5 %collective-permute-start.6 = (bf16[48,768]{1,0:T(8,128)(2,1)S(1)}, bf16[48,768]{1,0:T(8,128)(2,1)S(1)}, u32[]{:S(2)}, u32[]{:S(2)}) collective-permute-start(bf16[48,768]{1,0:T(8,128)(2,1)S(1)} %maximum_select_fusion.3), channel_id=1, source_target_pairs={{0,2},{1,3},{2,0},{3,1},{4,6},{5,7},{6,4},{7,5},{8,10},{9,11},{10,... | collective-permute-start | bytes 221192 | tf_op jit(solution)/shard_map/ppermute | solution.py:354
  40.4 9.6 %collective-permute-start.2 = (bf16[2,128,768]{2,1,0:T(8,128)(2,1)S(1)}, bf16[2,128,768]{2,1,0:T(8,128)(2,1)S(1)}, u32[]{:S(2)}, u32[]{:S(2)}) collective-permute-start(bf16[2,128,768]{2,1,0:T(8,128)(2,1)S(1)} %pad_maximum_fusion.2.own_ref.x_own_ref), channel_id=1, source_target_pairs={{0,16},{16,0},{1,17},{17,1},{2,18},{18,2},{3,19},{19,3},{4,20},{20... | collective-permute-start | bytes 1179656 | tf_op jit(solution)/shard_map/ppermute | solution.py:35
  42.9 5.7 %collective-permute-start.7 = (bf16[96,768]{1,0:T(8,128)(2,1)S(1)}, bf16[96,768]{1,0:T(8,128)(2,1)S(1)}, u32[]{:S(2)}, u32[]{:S(2)}) collective-permute-start(bf16[96,768]{1,0:T(8,128)(2,1)S(1)} %maximum_select_fusion.2), channel_id=1, source_target_pairs={{0,8},{1,9},{2,10},{3,11},{4,12},{5,13},{6,14},{7,15},{8,0},{9,1},... | collective-permute-start | bytes 442376 | tf_op jit(solution)/shard_map/ppermute | solution.py:354
  50.0 9.8 %copy-start = (bf16[16,2,24,640]{3,2,0,1:T(8,128)(2,1)}, bf16[16,2,24,640]{3,2,0,1:T(8,128)(2,1)S(1)}, u32[]{:S(2)}) copy-start(bf16[16,2,24,640]{3,2,0,1:T(8,128)(2,1)S(1)} %copy.72) | copy-start | bytes 2949124
  55.4 12.7 %copy-start.11 = (bf16[2,256,576]{2,1,0:T(8,128)(2,1)}, bf16[2,256,576]{2,1,0:T(8,128)(2,1)S(1)}, u32[]{:S(2)}) copy-start(bf16[2,256,576]{2,1,0:T(8,128)(2,1)S(1)} %get-tuple-element.88.qkv_ref) | copy-start | bytes 1769476
  55.4 13.4 %copy-start.6 = (bf16[2,256,768]{2,1,0:T(8,128)(2,1)}, bf16[2,256,768]{2,1,0:T(8,128)(2,1)S(1)}, u32[]{:S(2)}) copy-start(bf16[2,256,768]{2,1,0:T(8,128)(2,1)S(1)} %get-tuple-element.90.normed_ref) | copy-start | bytes 2359300
  55.4 13.4 %copy-start.18 = (bf16[2,256,192]{2,1,0:T(8,128)(2,1)}, bf16[2,256,192]{2,1,0:T(8,128)(2,1)S(1)}, u32[]{:S(2)}) copy-start(bf16[2,256,192]{2,1,0:T(8,128)(2,1)S(1)} %get-tuple-element.87.att_ref) | copy-start | bytes 589828
  55.4 12.7 %copy-start.10 = (bf16[1,128,768]{2,1,0:T(8,128)(2,1)S(1)}, bf16[1,128,768]{2,1,0:T(8,128)(2,1)}, u32[]{:S(2)}) copy-start(bf16[1,128,768]{2,1,0:T(8,128)(2,1)} %param.31) | copy-start | bytes 589828
  55.4 5.5 %collective-permute-start.8 = (bf16[2,128,768]{2,1,0:T(8,128)(2,1)S(1)}, bf16[2,128,768]{2,1,0:T(8,128)(2,1)S(1)}, u32[]{:S(2)}, u32[]{:S(2)}) collective-permute-start(bf16[2,128,768]{2,1,0:T(8,128)(2,1)S(1)} %get-tuple-element.69), channel_id=1, source_target_pairs={{0,16},{16,0},{1,17},{17,1},{2,18},{18,2},{3,19},{19,3},{4,20},{20... | collective-permute-start | bytes 1179656 | tf_op jit(solution)/shard_map/ppermute | solution.py:35
  61.1 7.0 %collective-permute-start.9 = (bf16[128,768]{1,0:T(8,128)(2,1)S(1)}, bf16[128,768]{1,0:T(8,128)(2,1)S(1)}, u32[]{:S(2)}, u32[]{:S(2)}) collective-permute-start(bf16[128,768]{1,0:T(8,128)(2,1)S(1)} %fusion.11), channel_id=1, source_target_pairs={{0,4},{1,5},{2,6},{3,7},{4,0},{5,1},{6,2},{7,3},{8,12},{9,13},{10,... | collective-permute-start | bytes 589832 | tf_op jit(solution)/shard_map/ppermute | solution.py:40
  68.9 24.3 %copy-start.21 = (f32[128,1]{1,0:T(8,128)}, f32[128,1]{1,0:T(8,128)S(1)}, u32[]{:S(2)}) copy-start(f32[128,1]{1,0:T(8,128)S(1)} %get-tuple-element.83.gate_ref) | copy-start | bytes 1540
  89.7 3.5 %collective-permute-start.10 = (bf16[384,768]{1,0:T(8,128)(2,1)S(1)}, bf16[384,768]{1,0:T(8,128)(2,1)S(1)}, u32[]{:S(2)}, u32[]{:S(2)}) collective-permute-start(bf16[384,768]{1,0:T(8,128)(2,1)S(1)} %bitcast.94), channel_id=1, source_target_pairs={{0,16},{16,0},{1,17},{17,1},{2,18},{18,2},{3,19},{19,3},{4,20},{20... | collective-permute-start | bytes 1769480 | tf_op jit(solution)/shard_map/ppermute | solution.py:35
  99.8 17.3 %copy-start.3 = (bf16[320,1536]{1,0:T(8,128)(2,1)}, bf16[320,1536]{1,0:T(8,128)(2,1)S(1)}, u32[]{:S(2)}) copy-start(bf16[320,1536]{1,0:T(8,128)(2,1)S(1)} %get-tuple-element.99) | copy-start | bytes 2949124
  99.8 17.3 %copy-start.26 = (bf16[320,1536]{1,0:T(8,128)(2,1)}, bf16[320,1536]{1,0:T(8,128)(2,1)S(1)}, u32[]{:S(2)}) copy-start(bf16[320,1536]{1,0:T(8,128)(2,1)S(1)} %get-tuple-element.100) | copy-start | bytes 2949124
  99.9 17.3 %copy-start.28 = (bf16[320,768]{1,0:T(8,128)(2,1)}, bf16[320,768]{1,0:T(8,128)(2,1)S(1)}, u32[]{:S(2)}) copy-start(bf16[320,768]{1,0:T(8,128)(2,1)S(1)} %get-tuple-element.101) | copy-start | bytes 1474564
  99.9 1.9 collective-permute-start.11
  102.7 14.1 %copy-start.20 = (bf16[768,16]{1,0:T(8,128)(2,1)}, bf16[768,16]{1,0:T(8,128)(2,1)S(1)}, u32[]{:S(2)}) copy-start(bf16[768,16]{1,0:T(8,128)(2,1)S(1)} %get-tuple-element.94) | copy-start | bytes 73732
  102.7 23.2 %copy-start.15 = (bf16[256,768]{1,0:T(8,128)(2,1)}, bf16[256,768]{1,0:T(8,128)(2,1)S(1)}, u32[]{:S(2)}) copy-start(bf16[256,768]{1,0:T(8,128)(2,1)S(1)} %get-tuple-element.80) | copy-start | bytes 1179652
  117.9 4.5 %collective-permute-start.12 = (bf16[128,768]{1,0:T(8,128)(2,1)S(1)}, bf16[128,768]{1,0:T(8,128)(2,1)S(1)}, u32[]{:S(2)}, u32[]{:S(2)}) collective-permute-start(bf16[128,768]{1,0:T(8,128)(2,1)S(1)} %get-tuple-element.86), channel_id=1, source_target_pairs={{0,4},{1,5},{2,6},{3,7},{4,0},{5,1},{6,2},{7,3},{8,12},{9,13},{10,... | collective-permute-start | bytes 589832 | tf_op jit(solution)/shard_map/ppermute | solution.py:40
  122.5 8.2 %collective-permute-start.13 = (bf16[2,128,768]{2,1,0:T(8,128)(2,1)S(1)}, bf16[2,128,768]{2,1,0:T(8,128)(2,1)S(1)}, u32[]{:S(2)}, u32[]{:S(2)}) collective-permute-start(bf16[2,128,768]{2,1,0:T(8,128)(2,1)S(1)} %pad_maximum_fusion.3.own_ref), channel_id=1, source_target_pairs={{0,16},{16,0},{1,17},{17,1},{2,18},{18,2},{3,19},{19,3},{4,20},{20... | collective-permute-start | bytes 1179656 | tf_op jit(solution)/shard_map/ppermute | solution.py:35
  125.9 32.2 %all-to-all-start.2 = ((bf16[16,16,768]{2,1,0:T(8,128)(2,1)}), bf16[16,16,768]{2,1,0:T(8,128)(2,1)S(1)}, u32[]{:S(2)}, u32[]{:S(2)}) async-start(bf16[16,16,768]{2,1,0:T(8,128)(2,1)} %bitcast.101), calls=%async_computation.2 | async-start | bytes 786432 | tf_op jit(solution)/shard_map/all_to_all | solution.py:44
  144.1 9.1 %collective-permute-start.18 = (bf16[96,768]{1,0:T(8,128)(2,1)S(1)}, bf16[96,768]{1,0:T(8,128)(2,1)}, u32[]{:S(2)}, u32[]{:S(2)}) collective-permute-start(bf16[96,768]{1,0:T(8,128)(2,1)S(1)} %broadcast_select_fusion), channel_id=1, source_target_pairs={{0,8},{1,9},{2,10},{3,11},{4,12},{5,13},{6,14},{7,15},{8,0},{9,1},... | collective-permute-start | bytes 442376 | tf_op jit(solution)/shard_map/ppermute | solution.py:369
  148.1 21.4 %collective-permute-start.14 = (bf16[2,128,768]{2,1,0:T(8,128)(2,1)}, bf16[2,128,768]{2,1,0:T(8,128)(2,1)}, u32[]{:S(2)}, u32[]{:S(2)}) collective-permute-start(bf16[2,128,768]{2,1,0:T(8,128)(2,1)} %get-tuple-element.92), channel_id=1, source_target_pairs={{0,16},{16,0},{1,17},{17,1},{2,18},{18,2},{3,19},{19,3},{4,20},{20... | collective-permute-start | bytes 1179656 | tf_op jit(solution)/shard_map/ppermute | solution.py:35
  154.1 3.3 %collective-permute-start.19 = (bf16[48,768]{1,0:T(8,128)(2,1)S(1)}, bf16[48,768]{1,0:T(8,128)(2,1)S(1)}, u32[]{:S(2)}, u32[]{:S(2)}) collective-permute-start(bf16[48,768]{1,0:T(8,128)(2,1)S(1)} %select_convert_fusion.1), channel_id=1, source_target_pairs={{0,2},{1,3},{2,0},{3,1},{4,6},{5,7},{6,4},{7,5},{8,10},{9,11},{10,... | collective-permute-start | bytes 221192 | tf_op jit(solution)/shard_map/ppermute | solution.py:369
  155.4 9.6 %copy-start.4 = (bf16[320,1536]{1,0:T(8,128)(2,1)S(1)}, bf16[320,1536]{1,0:T(8,128)(2,1)}, u32[]{:S(2)}) copy-start(bf16[320,1536]{1,0:T(8,128)(2,1)} %copy-done.3) | copy-start | bytes 2949124
  157.4 11.2 %collective-permute-start.20 = (bf16[24,768]{1,0:T(8,128)(2,1)S(1)}, bf16[24,768]{1,0:T(8,128)(2,1)S(1)}, u32[]{:S(2)}, u32[]{:S(2)}) collective-permute-start(bf16[24,768]{1,0:T(8,128)(2,1)S(1)} %select_convert_fusion.2), channel_id=1, source_target_pairs={{0,1},{1,0},{2,3},{3,2},{4,5},{5,4},{6,7},{7,6},{8,9},{9,8},{10,11... | collective-permute-start | bytes 110600 | tf_op jit(solution)/shard_map/ppermute | solution.py:369
  158.1 27.8 %all-to-all-start.4 = ((bf16[16,48,596]{2,1,0:T(8,128)(2,1)}), bf16[16,48,596]{2,1,0:T(8,128)(2,1)}, u32[]{:S(2)}, u32[]{:S(2)}) async-start(bf16[16,48,596]{2,1,0:T(8,128)(2,1)} %pad_maximum_fusion.1), calls=%async_computation.4 | async-start | bytes 1966080 | tf_op jit(solution)/shard_map/all_to_all | solution.py:44
  165.1 4.5 %copy-start.9 = (f32[2,128,768]{2,1,0:T(8,128)S(1)}, f32[2,128,768]{2,1,0:T(8,128)}, u32[]{:S(2)}) copy-start(f32[2,128,768]{2,1,0:T(8,128)} %copy-done.8) | copy-start | bytes 2359300
  168.7 5.6 %copy-start.27 = (bf16[320,1536]{1,0:T(8,128)(2,1)S(1)}, bf16[320,1536]{1,0:T(8,128)(2,1)}, u32[]{:S(2)}) copy-start(bf16[320,1536]{1,0:T(8,128)(2,1)} %copy-done.26) | copy-start | bytes 2949124
  168.7 5.6 %copy-start.29 = (bf16[320,768]{1,0:T(8,128)(2,1)S(1)}, bf16[320,768]{1,0:T(8,128)(2,1)}, u32[]{:S(2)}) copy-start(bf16[320,768]{1,0:T(8,128)(2,1)} %copy-done.28) | copy-start | bytes 1474564
  168.7 10.1 %collective-permute-start.21 = (bf16[24,768]{1,0:T(8,128)(2,1)S(1)}, bf16[24,768]{1,0:T(8,128)(2,1)S(1)}, u32[]{:S(2)}, u32[]{:S(2)}) collective-permute-start(bf16[24,768]{1,0:T(8,128)(2,1)S(1)} %add_convert_fusion), channel_id=1, source_target_pairs={{0,0},{1,1},{2,2},{3,3},{4,8},{5,9},{6,10},{7,11},{8,4},{9,5},{10,... | collective-permute-start | bytes 110600 | tf_op jit(solution)/shard_map/ppermute | solution.py:374
  170.6 14.2 %collective-permute-start.15 = (bf16[128,768]{1,0:T(8,128)(2,1)S(1)}, bf16[128,768]{1,0:T(8,128)(2,1)S(1)}, u32[]{:S(2)}, u32[]{:S(2)}) collective-permute-start(bf16[128,768]{1,0:T(8,128)(2,1)S(1)} %fusion.12), channel_id=1, source_target_pairs={{0,4},{1,5},{2,6},{3,7},{4,0},{5,1},{6,2},{7,3},{8,12},{9,13},{10,... | collective-permute-start | bytes 589832 | tf_op jit(solution)/shard_map/ppermute | solution.py:40
  174.3 3.6 %copy-start.22 = (f32[128,1]{1,0:T(8,128)S(1)}, f32[128,1]{1,0:T(8,128)}, u32[]{:S(2)}) copy-start(f32[128,1]{1,0:T(8,128)} %copy-done.21) | copy-start | bytes 1540
  177.9 7.1 %copy-start.17 = (f32[128,768]{1,0:T(8,128)S(1)}, f32[128,768]{1,0:T(8,128)}, u32[]{:S(2)}) copy-start(f32[128,768]{1,0:T(8,128)} %copy-done.16) | copy-start | bytes 1179652
  188.0 3.9 %collective-permute-start.22 = (f32[32,6]{0,1:T(8,128)S(1)}, f32[32,6]{0,1:T(8,128)S(1)}, u32[]{:S(2)}, u32[]{:S(2)}) collective-permute-start(f32[32,6]{0,1:T(8,128)S(1)} %reshape.193), channel_id=1, source_target_pairs={{0,16},{16,0},{1,17},{17,1},{2,18},{18,2},{3,19},{19,3},{4,20},{20... | collective-permute-start | bytes 2312 | tf_op jit(solution)/shard_map/ppermute | solution.py:35
  191.1 1.4 collective-permute-start.16
  191.2 2.7 %collective-permute-start.17 = (bf16[2,24,3,192]{3,2,1,0:T(4,128)(2,1)S(1)}, bf16[2,24,3,192]{3,2,1,0:T(4,128)(2,1)S(1)}, u32[]{:S(2)}, u32[]{:S(2)}) collective-permute-start(bf16[2,24,3,192]{3,2,1,0:T(4,128)(2,1)S(1)} %fusion.15), channel_id=1, source_target_pairs={{0,16},{16,0},{1,17},{17,1},{2,18},{18,2},{3,19},{19,3},{4,20},{20... | collective-permute-start | bytes 165896 | tf_op jit(solution)/shard_map/ppermute | solution.py:35
  (12 other events, 11.0 us)
where the time goes:
time: 200 us; the launch traced here: 197 us
  starting transfers between devices  76.1 us (38%)
  blocking collectives  34.8 us (17%)
  waiting for transfers between devices  24.8 us (12%)
  Pallas kernels  24.3 us (12%)
  local copies, waits for them, and re-layouts  18.4 us (9%)
  other arithmetic  9.86 us (5%)
  matrix products  7.21 us (4%)
    all_to_all x2, blocking collectives, exchange(): lax.all_to_all(value, 'expert', split_axis=0, concat_axis=0, tiled=True)  34.8 us
    ppermute x5, starting transfers between devices, swap_pair(): return lax.ppermute(value, 'expert', [(i, i ^ PAIR) for i in range(n)])  30.4 us
    all_to_all x3, starting transfers between devices, exchange(): lax.all_to_all(value, 'expert', split_axis=0, concat_axis=0, tiled=True)  18.5 us
    pallas_call x9, Pallas kernels, kernel_call(): pl.pallas_call(body, out_shape=[jax.ShapeDtypeStruct(shape, dtype) for sh...  17.6 us
    ppermute x10, starting transfers between devices, swap_core(): return lax.ppermute(value, 'dp', [(0, 1), (1, 0)])  17.5 us
    ppermute x5, waiting for transfers between devices, swap_pair(): return lax.ppermute(value, 'expert', [(i, i ^ PAIR) for i in range(n)])  14.2 us
    unnamed x71, local copies, waits for them, and re-layouts  12.6 us
    dot_general x2, matrix products, dot(): lax.dot_general(left, right, (dims, ((), ())), preferred_element_type=F32)  7.21 us
  transfers between devices with their start and end apart: 26, of which 10 were waited for; matrix products, arithmetic and copies ran while one was open for 9% of the time, Pallas kernels for 5%

commit v1 on v0

v1 whole, which is shorter than its diff:
```python
import functools

import jax
import jax.numpy as jnp
from jax import lax
from jax.experimental import pallas as pl
from jax.experimental.pallas import tpu as pltpu
from jax.sharding import PartitionSpec as P

EPSILON = 1e-06
MASKED = -1000000000.0
BUCKET_EDGES = (1, 2, 3, 4, 5, 6, 7, 8, 12, 16, 23, 32, 46, 64, 91)
F32 = jnp.float32
BF16 = jnp.bfloat16
VMEM_BYTES = 24 * 1024 * 1024


def dot(left, right, dims=((1,), (0,))):
    return lax.dot_general(left, right, (dims, ((), ())), preferred_element_type=F32)


def rms_inverse(values):
    return lax.rsqrt(jnp.mean(values * values, axis=-1, keepdims=True) + EPSILON)


def norm_backward(grad_normed, unit_values, inverse, gain_values):
    grad_unit = grad_normed * gain_values
    projected = jnp.mean(grad_unit * unit_values, axis=-1, keepdims=True)
    return inverse * (grad_unit - unit_values * projected)


def swap_core(value):
    return lax.ppermute(value, "dp", [(0, 1), (1, 0)])


def swap_pair(value):
    n = lax.axis_size("expert")
    other = 3 * n // 4
    return lax.ppermute(value, "expert", [(i, i ^ other) for i in range(n)])


def exchange(value):
    return lax.all_to_all(value, "expert", split_axis=0, concat_axis=0, tiled=True)


def exchange_half(value):
    half = lax.axis_size("expert") // 2
    groups = [[q * half + s for s in range(half)] for q in range(2)]
    return lax.all_to_all(
        value, "expert", split_axis=0, concat_axis=0, tiled=True, axis_index_groups=groups
    )


def bucket_of(offset, total):
    distance = jnp.abs(offset)
    bucket = jnp.zeros(offset.shape, jnp.int32)
    for border in BUCKET_EDGES:
        bucket = bucket + (distance >= border).astype(jnp.int32)
    return bucket + total // 2 * (offset > 0).astype(jnp.int32)


def iota(shape, axis):
    return lax.broadcasted_iota(jnp.int32, shape, axis)


def kernel_call(body, outs, *args, scalars=0, flops=1_000_000, nbytes=1_000_000):
    specs = [pl.BlockSpec(memory_space=pltpu.SMEM)] * scalars
    specs += [pl.BlockSpec(memory_space=pltpu.VMEM)] * (len(args) - scalars)
    return pl.pallas_call(
        body,
        out_shape=[jax.ShapeDtypeStruct(shape, dtype) for shape, dtype in outs],
        in_specs=specs,
        out_specs=[pl.BlockSpec(memory_space=pltpu.VMEM)] * len(outs),
        compiler_params=pltpu.CompilerParams(vmem_limit_bytes=VMEM_BYTES),
        cost_estimate=pl.CostEstimate(flops=flops, bytes_accessed=nbytes, transcendentals=0),
    )(*args)


def choose(index, values):
    picked = values[0]
    for i in range(1, len(values)):
        picked = jnp.where(index == i, values[i], picked)
    return picked


def pack_weights(group_ref, q_ref, k_ref, v_ref, router_ref, gains_ref, *out_refs):
    rows, width = q_ref.shape
    experts = router_ref.shape[1]
    cols = width // 4
    eye = iota((rows, rows), 0) == iota((rows, rows), 1)
    columns = [
        jnp.sum(jnp.where(eye, gains_ref[i : i + 1, :].astype(F32), 0.0), axis=1, keepdims=True)
        for i in range(2)
    ]
    pad = out_refs[0].shape[1] - 3 * cols - experts - 2
    small = jnp.concatenate(
        [router_ref[...].astype(F32)] + columns + [jnp.zeros((rows, pad), F32)], axis=1
    ).astype(BF16)
    pieces = [
        jnp.concatenate(
            [ref[:, j * cols : (j + 1) * cols] for ref in (q_ref, k_ref, v_ref)] + [small], axis=1
        )
        for j in range(4)
    ]
    for d, out_ref in enumerate(out_refs):
        out_ref[...] = choose(group_ref[0] ^ d, pieces)


def spread_weights(group_ref, p0_ref, p1_ref, p2_ref, p3_ref, wout_ref, out_ref):
    dests, _, wide = out_ref.shape
    rows, used = p0_ref.shape
    pieces = [ref[...] for ref in (p0_ref, p1_ref, p2_ref, p3_ref)]
    value = jnp.concatenate([choose(group_ref[0] ^ j, pieces) for j in range(4)], axis=0)
    if wide > used:
        value = jnp.concatenate([value, jnp.zeros((4 * rows, wide - used), BF16)], axis=1)
    last = wout_ref[...]
    if wide > last.shape[1]:
        last = jnp.concatenate([last, jnp.zeros((rows, wide - last.shape[1]), BF16)], axis=1)
    value = jnp.concatenate([value, last], axis=0)
    for dest in range(dests):
        out_ref[dest] = value


def prepare(capacity, pad_two, group_ref, table_ref, docs_ref, routes_ref, own_bias_ref,
            pair_bias_ref, spread_ref, later_ref, gather_ref, send_ref):
    buckets = table_ref.shape[0]
    own_heads = own_bias_ref.shape[0]
    length = docs_ref.shape[1]
    toks = length // 2
    group = group_ref[0]
    spot = iota((1, length), 1)
    offset = jnp.where(spot >= toks, spot - length, spot)
    bucket = bucket_of(offset, buckets)
    vectors = []
    for h in range(own_heads):
        vector = jnp.zeros((1, length), F32)
        for b in range(buckets):
            vector = jnp.where(bucket == b, table_ref[b, group * own_heads + h], vector)
        full = jnp.broadcast_to(vector, (length, length))
        vectors.append(pltpu.roll(full, 0, 1, stride=1, stride_axis=0))
    for r, bias_ref in enumerate((own_bias_ref, pair_bias_ref)):
        across = jnp.broadcast_to(docs_ref[r : r + 1, :].astype(F32), (length, length))
        same = across == jnp.transpose(across)
        for h in range(own_heads):
            bias_ref[h] = jnp.where(same, vectors[h], MASKED)
    experts = spread_ref.shape[1] // pad_two
    route = routes_ref[...]
    chosen = route == iota((toks, experts), 1)
    lower = (iota((toks, toks), 0) > iota((toks, toks), 1)).astype(BF16)
    counts = dot(lower, chosen.astype(BF16))
    slot = jnp.sum(jnp.where(chosen, counts, 0.0), axis=1, keepdims=True).astype(jnp.int32)
    kept = slot < capacity
    place = jnp.where(kept, route * pad_two + slot, -1)
    later = jnp.where(kept, route * pad_two + capacity + slot, -1)
    across = iota((toks, experts * pad_two), 1)
    first = (place == across).astype(F32)
    second = (later == across).astype(F32)
    spread_ref[...] = first.astype(BF16)
    later_ref[...] = second.astype(BF16)
    send_ref[:, :toks] = jnp.transpose(first).astype(BF16)
    send_ref[:, toks:] = jnp.transpose(second).astype(BF16)
    gather_ref[...] = chosen.astype(F32)


def place_weights(arrived_ref, w_ref, wout_ref):
    sources, total, _ = arrived_ref.shape
    rows = total // 5
    used = w_ref.shape[1]
    width = wout_ref.shape[1]
    block = sources * rows
    for s in range(sources):
        for j in range(4):
            w_ref[j * block + s * rows : j * block + (s + 1) * rows] = arrived_ref[
                s, j * rows : (j + 1) * rows, :used
            ]
        wout_ref[s * rows : (s + 1) * rows] = arrived_ref[s, 4 * rows :, :width]


def gain_rows(experts, cols, w_ref, gains_ref):
    small = w_ref[:, 3 * cols :]
    pick = (iota((8, small.shape[1]), 1) == iota((8, small.shape[1]), 0) + experts).astype(BF16)
    gains_ref[...] = dot(pick, small, ((1,), (1,)))


def attend(scale, head_dim, w_ref, wout_ref, gains_ref, own_ref, across_ref, bias_ref, qkv_ref,
           probs_ref, att_ref, keep_ref, send_ref):
    own_heads = bias_ref.shape[0]
    cols = own_heads * head_dim
    toks = own_ref.shape[0]
    x = jnp.concatenate([own_ref[...], across_ref[...]], axis=0).astype(F32)
    normed = (x * rms_inverse(x) * gains_ref[0:1]).astype(BF16)
    qkv = dot(normed, w_ref[:, : 3 * cols]).astype(BF16)
    qkv_ref[...] = qkv
    parts = []
    for h in range(own_heads):
        at = h * head_dim
        q = qkv[:, at : at + head_dim]
        k = qkv[:, cols + at : cols + at + head_dim]
        v = qkv[:, 2 * cols + at : 2 * cols + at + head_dim]
        scores = dot(q, k, ((1,), (1,))) * scale + bias_ref[h]
        top = jnp.max(scores, axis=1, keepdims=True)
        raised = jnp.exp(scores - top)
        probs = raised * (1.0 / jnp.sum(raised, axis=1, keepdims=True))
        probs_ref[h] = probs
        parts.append(dot(probs.astype(BF16), v))
    attended = jnp.concatenate(parts, axis=1).astype(BF16)
    att_ref[...] = attended
    partial = dot(attended, wout_ref[...])
    keep_ref[...] = partial[:toks]
    send_ref[...] = partial[toks:].astype(BF16)


def attend_first(scale, head_dim, experts, arrived_ref, own_ref, across_ref, bias_ref, w_ref,
                 wout_ref, gains_ref, *out_refs):
    place_weights(arrived_ref, w_ref, wout_ref)
    gain_rows(experts, bias_ref.shape[0] * head_dim, w_ref, gains_ref)
    attend(scale, head_dim, w_ref, wout_ref, gains_ref, own_ref, across_ref, bias_ref, *out_refs)


def attend_first_placed(scale, head_dim, experts, w_ref, wout_ref, own_ref, across_ref, bias_ref,
                        gains_ref, *out_refs):
    gain_rows(experts, bias_ref.shape[0] * head_dim, w_ref, gains_ref)
    attend(scale, head_dim, w_ref, wout_ref, gains_ref, own_ref, across_ref, bias_ref, *out_refs)


def route_tokens(x_ref, keep_ref, core_ref, came_ref, gains_ref, w_ref, chosen_ref, send_ref,
                 g_ref, middle_ref, gate_ref, out_ref):
    middle = x_ref[...].astype(F32) + (
        (keep_ref[...] + core_ref[...].astype(F32)) + came_ref[...].astype(F32)
    )
    middle_ref[...] = middle
    normed = (middle * rms_inverse(middle) * gains_ref[1:2]).astype(BF16)
    both = jnp.concatenate([normed, g_ref[...]], axis=0)
    out_ref[...] = dot(send_ref[...], both).astype(BF16)
    probs = jax.nn.softmax(dot(normed, w_ref[...]), axis=-1)
    gate_ref[...] = jnp.sum(probs * chosen_ref[...], axis=1, keepdims=True)


def run_expert(capacity, place_ref, own_ref, other_ref, router_ref, inner_ref, outer_ref,
               buf_ref, dslot_ref, g_ref, probs_ref, gate_ref, hidden_ref, dpre_ref, keep_ref,
               send_ref, acc_ref):
    step = pl.program_id(0)
    slots = buf_ref.shape[0] // 2
    experts = router_ref.shape[1]
    pad = own_ref.shape[0] // (slots // capacity)

    @pl.when(step == 0)
    def _():
        shape = (slots, own_ref.shape[0])
        row = iota(shape, 0)
        source = row // capacity
        wanted = source * pad + (row - source * capacity)
        first = (iota(shape, 1) == wanted).astype(BF16)
        second = (iota(shape, 1) == wanted + capacity).astype(BF16)
        mine = (iota((1, experts), 1) == place_ref[0]).astype(F32)
        for side, ref in enumerate((own_ref, other_ref)):
            at = side * slots
            rows = ref[...]
            buffers = dot(first, rows).astype(BF16)
            buf_ref[at : at + slots] = buffers
            g = dot(second, rows)
            probs = jax.nn.softmax(dot(buffers, router_ref[...]), axis=-1)
            gate = jnp.sum(probs * mine, axis=1, keepdims=True)
            dslot_ref[at : at + slots] = (gate * g).astype(BF16)
            if side == 0:
                g_ref[...] = g.astype(BF16)
                probs_ref[...] = probs
                gate_ref[...] = gate
        acc_ref[...] = jnp.zeros_like(acc_ref)

    inner = inner_ref[...]
    outer = outer_ref[...]
    pre = dot(buf_ref[...], inner)
    cdf = 0.5 * (1.0 + lax.erf(pre * (0.5**0.5)))
    hidden = (pre * cdf).astype(BF16)
    hidden_ref[...] = hidden
    slope = cdf + pre * jnp.exp(-0.5 * pre * pre) * 0.3989422804014327
    dpre = (dot(dslot_ref[...], outer, ((1,), (1,))) * slope).astype(BF16)
    dpre_ref[...] = dpre
    acc_ref[0] += dot(hidden, outer)
    acc_ref[1] += dot(dpre, inner, ((1,), (1,)))

    @pl.when(step == pl.num_programs(0) - 1)
    def _():
        keep_ref[...] = acc_ref[:, :slots]
        send_ref[...] = acc_ref[:, slots:].astype(BF16)


def finish_expert(capacity, place_ref, keep_ref, came_ref, buf_ref, g_ref, probs_ref, gate_ref,
                  router_ref, out_ref, grad_ref):
    slots = g_ref.shape[0]
    experts = router_ref.shape[1]
    pad = out_ref.shape[0] // (slots // capacity)
    total = (keep_ref[...] + came_ref[...].astype(F32)).astype(BF16)
    result = total[0]
    mine = (iota((1, experts), 1) == place_ref[0]).astype(F32)
    grad_gate = jnp.sum(g_ref[...].astype(F32) * result.astype(F32), axis=1, keepdims=True)
    grad_logits = (grad_gate * gate_ref[...] * (mine - probs_ref[...])).astype(BF16)
    grad_ref[...] = dot(buf_ref[...], grad_logits, ((0,), (0,))).astype(BF16)
    back = total[1].astype(F32) + dot(grad_logits, router_ref[...], ((1,), (1,)))
    shape = (out_ref.shape[0], 2 * slots)
    row = iota(shape, 0)
    source = row // pad
    inside = row - source * pad
    wanted = jnp.where(
        inside < capacity,
        source * capacity + inside,
        jnp.where(inside < 2 * capacity, slots + source * capacity + inside - capacity, -1),
    )
    expand = (iota(shape, 1) == wanted).astype(BF16)
    both = jnp.concatenate([back.astype(BF16), result], axis=0)
    out_ref[...] = dot(expand, both).astype(BF16)


def norm_two_backward(back_ref, spread_ref, middle_ref, gains_ref, g_ref, dmiddle_ref, da_ref,
                      gain_ref):
    middle = middle_ref[...]
    inverse = rms_inverse(middle)
    unit = middle * inverse
    grad_normed = dot(spread_ref[...], back_ref[...])
    gain_ref[...] = jnp.sum(grad_normed * unit, axis=0, keepdims=True)
    dmiddle = g_ref[...].astype(F32) + norm_backward(grad_normed, unit, inverse, gains_ref[1:2])
    dmiddle_ref[...] = dmiddle
    da_ref[...] = dmiddle.astype(BF16)


def finish_layer(result_ref, spread_ref, middle_ref, gate_ref, out_ref):
    combined = dot(spread_ref[...], result_ref[...])
    out_ref[...] = (middle_ref[...] + gate_ref[...] * combined).astype(BF16)


def attend_backward(scale, head_dim, own_ref, across_ref, wout_ref, att_ref, qkv_ref, probs_ref,
                    gains_ref, w_ref, x_own_ref, x_across_ref):
    own_heads = probs_ref.shape[0]
    cols = own_heads * head_dim
    length = 2 * own_ref.shape[0]
    flip = (iota((length, length), 0) + iota((length, length), 1) == length - 1).astype(BF16)
    da = jnp.concatenate([own_ref[...], across_ref[...]], axis=0)
    grad_att = dot(da, wout_ref[...], ((1,), (1,))).astype(BF16)
    qkv = qkv_ref[...]
    parts = [[], [], []]
    offsets = []
    for h in range(own_heads):
        at = h * head_dim
        q = qkv[:, at : at + head_dim]
        k = qkv[:, cols + at : cols + at + head_dim]
        v = qkv[:, 2 * cols + at : 2 * cols + at + head_dim]
        gh = grad_att[:, at : at + head_dim]
        probs = probs_ref[h]
        grad_probs = dot(gh, v, ((1,), (1,)))
        row_dot = jnp.sum(probs * grad_probs, axis=1, keepdims=True)
        ds = (probs * (grad_probs - row_dot)).astype(BF16)
        turned = pltpu.roll(dot(flip, ds), 1, 1, stride=1, stride_axis=0)
        offsets.append(jnp.sum(turned, axis=0, keepdims=True))
        parts[0].append(dot(ds, k) * scale)
        parts[1].append(dot(ds, q, ((0,), (0,))) * scale)
        parts[2].append(dot(probs.astype(BF16), gh, ((0,), (0,))))
    grad_qkv = jnp.concatenate(parts[0] + parts[1] + parts[2], axis=1).astype(BF16)
    x = jnp.concatenate([x_own_ref[...], x_across_ref[...]], axis=0).astype(F32)
    unit = x * rms_inverse(x)
    normed = (unit * gains_ref[0:1]).astype(BF16)
    weights = dot(normed, grad_qkv, ((0,), (0,)))
    outs = dot(att_ref[...], da, ((0,), (0,)))
    grad_normed = dot(grad_qkv, w_ref[:, : 3 * cols], ((1,), (1,)))
    gain = jnp.sum(grad_normed * unit, axis=0, keepdims=True)
    return weights, outs, grad_normed, gain, offsets


def backward_own(scale, head_dim, *refs):
    gw_ref, gout_ref, keep_ref, gain_ref, offsets_ref = refs[10:]
    weights, outs, grad_normed, gain, offsets = attend_backward(scale, head_dim, *refs[:10])
    gw_ref[...] = weights
    gout_ref[...] = outs
    keep_ref[...] = grad_normed
    gain_ref[...] = gain
    for h, value in enumerate(offsets):
        offsets_ref[h : h + 1] = value


def backward_pair(scale, head_dim, buckets, table_cols, *refs):
    gw_ref, gout_ref, gain_ref, offsets_ref, gain_two_ref, router_ref = refs[10:16]
    send_ref, full_ref, out_ref = refs[16:]
    weights, outs, grad_normed, gain, offsets = attend_backward(scale, head_dim, *refs[:10])
    own_heads = offsets_ref.shape[0]
    width, experts = router_ref.shape
    length = offsets_ref.shape[1]
    toks = length // 2
    send_ref[...] = grad_normed.astype(BF16)
    rows = own_heads * buckets // table_cols
    spot = iota((1, length), 1)
    offset = jnp.where(spot >= toks, spot - length, spot)
    bucket = bucket_of(offset, buckets)
    table = []
    for t in range(table_cols):
        column = jnp.zeros((rows, 1), F32)
        for h in range(own_heads):
            belongs = iota((rows, length), 0) * table_cols + t == bucket * own_heads + h
            value = offsets[h] + offsets_ref[h : h + 1]
            column = column + jnp.sum(jnp.where(belongs, value, 0.0), axis=1, keepdims=True)
        table.append(column)
    table = jnp.concatenate([jnp.concatenate(table, axis=1)] * (width // rows), axis=0)
    narrow = jnp.concatenate(
        [gain_ref[...] + gain, gain_two_ref[...], jnp.zeros((6, width), F32)], axis=0
    )
    narrow = jnp.transpose(narrow)[:, :2]
    weights = weights + gw_ref[...]
    pieces = [weights, router_ref[...].astype(F32), narrow, table]
    spare = full_ref.shape[-1] - sum(p.shape[1] for p in pieces)
    if len(full_ref.shape) == 2:
        full_ref[...] = jnp.concatenate(
            pieces + [jnp.zeros((width, spare), F32)], axis=1
        ).astype(BF16)
        out_ref[...] = (outs + gout_ref[...]).astype(BF16)


def backward_pair_message(scale, head_dim, buckets, table_cols, *refs):
    *rest, send_ref, message_ref, full_ref, out_ref = refs
    backward_pair(scale, head_dim, buckets, table_cols, *rest, send_ref, full_ref, out_ref)
    dests, total, wide = message_ref.shape
    rows = total // 5
    used = full_ref.shape[1]
    block = dests * rows
    for s in range(dests):
        for j in range(4):
            at = j * block + s * rows
            message_ref[s, j * rows : (j + 1) * rows, :used] = full_ref[at : at + rows]
            if wide > used:
                message_ref[s, j * rows : (j + 1) * rows, used:] = jnp.zeros(
                    (rows, wide - used), BF16
                )
        width = out_ref.shape[1]
        message_ref[s, 4 * rows :, :width] = out_ref[s * rows : (s + 1) * rows]
        if wide > width:
            message_ref[s, 4 * rows :, width:] = jnp.zeros((rows, wide - width), BF16)


def sum_arrived(group_ref, arrived_ref, out_ref, own_ref, *send_refs):
    rows, used = own_ref.shape
    total = arrived_ref[0].astype(F32)
    for s in range(1, arrived_ref.shape[0]):
        total = total + arrived_ref[s].astype(F32)
    out_ref[...] = total[4 * rows :, : out_ref.shape[1]]
    pieces = [total[j * rows : (j + 1) * rows, :used] for j in range(4)]
    own_ref[...] = choose(group_ref[0], pieces)
    for d, ref in enumerate(send_refs):
        ref[...] = choose(group_ref[0] ^ (d + 1), pieces).astype(BF16)


def finish_weights(own_heads, buckets, table_cols, group_ref, p0_ref, p1_ref, p2_ref, p3_ref,
                   q_ref, k_ref, v_ref, router_ref, gains_ref, table_ref):
    rows, width = q_ref.shape
    experts = router_ref.shape[1]
    cols = width // 4
    pieces = [ref[...].astype(F32) for ref in (p0_ref, p1_ref, p2_ref, p3_ref)]
    ordered = [choose(group_ref[0] ^ j, pieces) for j in range(4)]
    for n, ref in enumerate((q_ref, k_ref, v_ref)):
        ref[...] = jnp.concatenate([p[:, n * cols : (n + 1) * cols] for p in ordered], axis=1)
    at = 3 * cols
    small = sum(p[:, at : at + experts + 2] for p in pieces)
    router_ref[...] = small[:, :experts]
    eye = iota((rows, rows), 0) == iota((rows, rows), 1)
    for i in range(2):
        column = small[:, experts + i : experts + i + 1]
        gains_ref[i : i + 1] = jnp.sum(jnp.where(eye, column, 0.0), axis=0, keepdims=True)
    at += experts + 2
    lines = []
    lane = iota((rows, 128), 1)
    for p in ordered:
        for h in range(own_heads):
            line = jnp.zeros((1, 128), F32)
            for t in range(table_cols):
                belongs = iota((rows, 128), 0) * table_cols + t == lane * own_heads + h
                value = jnp.where(belongs & (lane < buckets), p[:, at + t : at + t + 1], 0.0)
                line = line + jnp.sum(value, axis=0, keepdims=True)
            lines.append(line)
    heads = len(lines)
    padded = jnp.concatenate(lines + [jnp.zeros((128 - heads, 128), F32)], axis=0)
    table_ref[...] = jnp.transpose(padded)[:buckets, :heads]


def local(
    tokens,
    gain_one,
    w_query,
    w_key,
    w_value,
    w_out,
    bias_table,
    gain_two,
    w_router,
    w_inner,
    w_outer,
    segment_ids,
    routes,
    out_grad,
):
    toks = tokens.shape[1]
    width = tokens.shape[2]
    heads = bias_table.shape[1]
    buckets = bias_table.shape[0]
    head_dim = width // heads
    own_heads = heads // 4
    cols = own_heads * head_dim
    length = 2 * toks
    scale = head_dim ** (-0.5)
    sources = lax.axis_size("expert")
    experts = sources
    capacity = (5 * toks + 4 * experts - 1) // (4 * experts)
    slots = experts * capacity
    pad_two = -(-2 * capacity // 8) * 8
    rows = w_query.shape[0]
    core = lax.axis_index("dp")
    place = lax.axis_index("expert")
    half = sources // 2
    member = place // half
    first_core = core == 0
    place_at = place.reshape(1).astype(jnp.int32)
    group_at = (2 * core + member).reshape(1).astype(jnp.int32)
    table_cols = max(1, own_heads * buckets // rows)
    used = -(-(3 * cols + experts + 2 + table_cols) // 128) * 128
    wide = max(used, width)
    aligned = rows % 8 == 0

    def across_group(pieces):
        return [
            lax.ppermute(
                piece,
                ("dp", "expert"),
                [
                    (c * sources + e, (c ^ (d >> 1)) * sources + (e ^ (half * (d & 1))))
                    for c in range(2)
                    for e in range(sources)
                ],
            )
            for d, piece in enumerate(pieces, 1)
        ]

    own_tokens = tokens.reshape(toks, width)
    pair_tokens = swap_pair(own_tokens)
    pair_docs = swap_pair(segment_ids)

    own_piece, *pieces = kernel_call(
        pack_weights, [((rows, used), BF16)] * 4,
        group_at, w_query, w_key, w_value, w_router, jnp.stack([gain_one, gain_two]), scalars=1,
    )
    pieces = across_group(pieces)
    pair_tokens, pair_docs, own_piece, *pieces = lax.optimization_barrier(
        (pair_tokens, pair_docs, own_piece, *pieces)
    )
    (message,) = kernel_call(
        spread_weights, [((half, 5 * rows, wide), BF16)],
        group_at, own_piece, *pieces, w_out, scalars=1,
    )
    arrived = exchange_half(message)

    own_across = swap_core(own_tokens)
    pair_across = swap_core(pair_tokens)
    docs_two = jnp.concatenate([segment_ids, pair_docs], axis=0)
    docs = jnp.where(first_core, docs_two, jnp.roll(docs_two, toks, axis=1))
    own_bias, pair_bias, spread, later, chosen, send = kernel_call(
        functools.partial(prepare, capacity, pad_two),
        [
            ((own_heads, length, length), F32),
            ((own_heads, length, length), F32),
            ((toks, experts * pad_two), BF16),
            ((toks, experts * pad_two), BF16),
            ((toks, experts), F32),
            ((experts * pad_two, 2 * toks), BF16),
        ],
        group_at, bias_table, docs, routes.reshape(toks, 1), scalars=2,
    )
    g_low = out_grad.reshape(toks, width)

    row_outs = [
        ((length, 3 * cols), BF16),
        ((own_heads, length, length), F32),
        ((length, cols), BF16),
        ((toks, width), F32),
        ((toks, width), BF16),
    ]
    placed = [((width, used), BF16), ((cols, width), BF16)]
    if aligned:
        weights, out_w, gains, *pair_kept = kernel_call(
            functools.partial(attend_first, scale, head_dim, experts),
            placed + [((8, width), F32)] + row_outs,
            arrived, pair_tokens, pair_across, pair_bias,
        )
    else:
        weights = arrived[:, : 4 * rows, :used].reshape(half, 2, 2, rows, used)
        weights = weights.transpose(1, 2, 0, 3, 4).reshape(width, used)
        out_w = arrived[:, 4 * rows :, :width].reshape(cols, width)
        gains, *pair_kept = kernel_call(
            functools.partial(attend_first_placed, scale, head_dim, experts),
            [((8, width), F32)] + row_outs,
            weights, out_w, pair_tokens, pair_across, pair_bias,
        )
    pair_qkv, pair_probs, pair_att, keep, away = pair_kept
    pair_sum = (keep + swap_core(away).astype(F32)).astype(BF16)
    pair_sum = swap_pair(pair_sum)
    own_qkv, own_probs, own_att, keep, away = kernel_call(
        functools.partial(attend, scale, head_dim), row_outs,
        weights, out_w, gains, own_tokens, own_across, own_bias,
    )
    router_w = weights[:, 3 * cols : 3 * cols + experts]
    middle, gate, outgoing = kernel_call(
        route_tokens,
        [((toks, width), F32), ((toks, 1), F32), ((experts * pad_two, width), BF16)],
        own_tokens, keep, swap_core(away), pair_sum, gains, router_w, chosen, send, g_low,
    )
    incoming = exchange(outgoing.reshape(experts, pad_two, width)).reshape(-1, width)

    inner, outer = w_inner[0], w_outer[0]
    units = inner.shape[1]
    chunk = units // 3
    fixed = lambda shape: pl.BlockSpec(shape, lambda i: (0,) * len(shape))
    outs = [
        ((2 * slots, width), BF16, None),
        ((2 * slots, width), BF16, None),
        ((slots, width), BF16, None),
        ((slots, experts), F32, None),
        ((slots, 1), F32, None),
        ((2 * slots, units), BF16, pl.BlockSpec((2 * slots, chunk), lambda i: (0, i))),
        ((2 * slots, units), BF16, pl.BlockSpec((2 * slots, chunk), lambda i: (0, i))),
        ((2, slots, width), F32, None),
        ((2, slots, width), BF16, None),
    ]
    buffers, dslot, slot_g, slot_probs, slot_gate, hidden, dpre, keep, away = pl.pallas_call(
        functools.partial(run_expert, capacity),
        grid=(units // chunk,),
        out_shape=[jax.ShapeDtypeStruct(shape, dtype) for shape, dtype, _ in outs],
        in_specs=[
            pl.BlockSpec(memory_space=pltpu.SMEM),
            fixed((experts * pad_two, width)),
            fixed((experts * pad_two, width)),
            fixed((width, experts)),
            pl.BlockSpec((width, chunk), lambda i: (0, i)),
            pl.BlockSpec((chunk, width), lambda i: (i, 0)),
        ],
        out_specs=[spec or fixed(shape) for shape, _, spec in outs],
        scratch_shapes=[pltpu.VMEM((2, 2 * slots, width), F32)],
        compiler_params=pltpu.CompilerParams(vmem_limit_bytes=VMEM_BYTES),
    )(place_at, incoming, swap_core(incoming), router_w, inner, outer)
    grad_outer = dot(hidden, dslot, ((0,), (0,)))
    grad_inner = dot(buffers, dpre, ((0,), (0,)))
    back, grad_router = kernel_call(
        functools.partial(finish_expert, capacity),
        [((sources * pad_two, width), BF16), ((width, experts), BF16)],
        place_at, keep, swap_core(away), buffers[:slots], slot_g, slot_probs, slot_gate, router_w,
        scalars=1,
    )
    back = exchange(back.reshape(sources, pad_two, width)).reshape(-1, width)

    grad_middle, grad_attn, grad_gain_two = kernel_call(
        norm_two_backward,
        [((toks, width), F32), ((toks, width), BF16), ((1, width), F32)],
        back, spread, middle, gains, g_low,
    )
    pair_grad = swap_pair(grad_attn)
    shared = (gains, weights)
    grad_w, grad_out, grad_normed, gain_part, offsets = kernel_call(
        functools.partial(backward_own, scale, head_dim),
        [
            ((width, 3 * cols), F32),
            ((cols, width), F32),
            ((length, width), F32),
            ((1, width), F32),
            ((own_heads, length), F32),
        ],
        grad_attn, swap_core(grad_attn), out_w, own_att, own_qkv, own_probs, *shared,
        own_tokens, own_across,
    )
    last = (
        pair_grad, swap_core(pair_grad), out_w, pair_att, pair_qkv, pair_probs, *shared,
        pair_tokens, pair_across, grad_w, grad_out, gain_part, offsets, grad_gain_two, grad_router,
    )
    outs = [((length, width), BF16), ((width, used), BF16), ((cols, width), BF16)]
    options = (scale, head_dim, buckets, table_cols)
    if aligned:
        away, message, _, _ = kernel_call(
            functools.partial(backward_pair_message, *options),
            [outs[0], ((half, 5 * rows, wide), BF16), *outs[1:]], *last,
        )
    else:
        away, full, grad_out = kernel_call(functools.partial(backward_pair, *options), outs, *last)
        full = full.reshape(2, 2, half, rows, used).transpose(2, 0, 1, 3, 4)
        full = full.reshape(half, 4 * rows, used)
        grad_out = grad_out.reshape(half, rows, width)
        message = jnp.concatenate(
            [
                jnp.pad(full, ((0, 0), (0, 0), (0, wide - used))),
                jnp.pad(grad_out, ((0, 0), (0, 0), (0, wide - width))),
            ],
            axis=1,
        )
    came = swap_pair(away)
    arrived = exchange_half(message)
    (final,) = kernel_call(finish_layer, [((toks, width), BF16)], back, later, middle, gate)

    out_grad_w, own_piece, *pieces = kernel_call(
        sum_arrived, [((rows, width), F32), ((rows, used), F32)] + [((rows, used), BF16)] * 3,
        group_at, arrived, scalars=1,
    )
    pieces = across_group(pieces)
    query_grad, key_grad, value_grad, router_grad, gain_grads, table_grad = kernel_call(
        functools.partial(finish_weights, own_heads, buckets, table_cols),
        [((rows, width), F32)] * 3
        + [((rows, experts), F32), ((2, rows), F32), ((buckets, heads), F32)],
        group_at, own_piece, *pieces, scalars=1,
    )

    grad_normed = grad_normed + came.astype(F32)
    across = swap_core(grad_normed[toks:].astype(BF16)).astype(F32)
    x = own_tokens.astype(F32)
    inverse_one = rms_inverse(x)
    grad_input = grad_middle + norm_backward(
        grad_normed[:toks] + across, x * inverse_one, inverse_one, gains[0:1]
    )
    return (
        final.reshape(tokens.shape),
        grad_input.astype(BF16).reshape(tokens.shape),
        gain_grads[0],
        query_grad,
        key_grad,
        value_grad,
        out_grad_w,
        table_grad,
        gain_grads[1],
        router_grad,
        grad_inner[None],
        grad_outer[None],
    )


def solution(mesh):
    both = ("dp", "expert")
    return jax.shard_map(
        local,
        mesh=mesh,
        in_specs=(
            P("expert", "dp", None),
            P(both),
            P(both, None),
            P(both, None),
            P(both, None),
            P(both, None),
            P(),
            P(both),
            P(both, None),
            P("expert", None, "dp"),
            P("expert", "dp", None),
            P("expert", None),
            P("expert", "dp", None),
            P("expert", "dp", None),
        ),
        out_specs=(
            P("expert", "dp", None),
            P("expert", "dp", None),
            P(both),
            P(both, None),
            P(both, None),
            P(both, None),
            P(both, None),
            P(),
            P(both),
            P(both, None),
            P("expert", None, "dp"),
            P("expert", "dp", None),
        ),
        check_vma=False,
    )
```

time: 200 us -> 181 us (0.905); the launches traced: 197 us -> 180 us
  starting transfers between devices: 76.1 us -> 37.7 us
  waiting for transfers between devices: 24.8 us -> 51 us
  blocking collectives: 34.8 us -> 43.1 us
  other arithmetic: 9.86 us -> 3.06 us
  local copies, waits for them, and re-layouts: 18.4 us -> 13.3 us
    ppermute x13 -> x11, starting transfers between devices: 40.2 us -> 17.8 us  [the longest x5 11.5 us: swap_pair(): return lax.ppermute(value, 'expert', [(i, i ^ other) for i in range(n)])]
    ppermute x13 -> x11, waiting for transfers between devices: 19.2 us -> 35 us  [the longest x5 34.4 us: swap_pair(): return lax.ppermute(value, 'expert', [(i, i ^ other) for i in range(n)])]
    all_to_all x3 -> x2, waiting for transfers between devices: 0.01 us -> 12.8 us  [exchange_half(): lax.all_to_all(value, 'expert', split_axis=0, concat_axis=0, tiled=True,...]
    all_to_all x3 -> x2, starting transfers between devices: 18.5 us -> 9.25 us  [exchange_half(): lax.all_to_all(value, 'expert', split_axis=0, concat_axis=0, tiled=True,...]
    all_to_all x2, blocking collectives: 34.8 us -> 43.1 us  [exchange(): lax.all_to_all(value, 'expert', split_axis=0, concat_axis=0, tiled=True)]
    ppermute x10 -> x9, starting transfers between devices: 17.5 us -> 10.6 us  [swap_core(): return lax.ppermute(value, 'dp', [(0, 1), (1, 0)])]
    concatenate x3 -> x1, other arithmetic: 2.62 us -> 0.01 us  [local(): docs_two = jnp.concatenate([segment_ids, pair_docs], axis=0)]
    ppermute x10 -> x9, waiting for transfers between devices: 5.61 us -> 3.12 us  [swap_core(): return lax.ppermute(value, 'dp', [(0, 1), (1, 0)])]
  transfers between devices with their start and end apart: 26 -> 22, of which waited for: 10 -> 8; matrix products, arithmetic and copies ran while one was open for 9% -> 7% of each run, Pallas kernels for 5% -> 5%
where the time goes in v1:
time: 181 us; the launch traced here: 180 us
  waiting for transfers between devices  51 us (28%)
  blocking collectives  43.1 us (24%)
  starting transfers between devices  37.7 us (21%)
  Pallas kernels  22.5 us (12%)
  local copies, waits for them, and re-layouts  13.3 us (7%)
  matrix products  8.49 us (5%)
  other arithmetic  3.06 us (2%)
    all_to_all x2, blocking collectives, exchange(): lax.all_to_all(value, 'expert', split_axis=0, concat_axis=0, tiled=True)  43.1 us
    ppermute x5, waiting for transfers between devices, swap_pair(): return lax.ppermute(value, 'expert', [(i, i ^ other) for i in range(n)])  34.4 us
    pallas_call x13, Pallas kernels, kernel_call(): pl.pallas_call(body, out_shape=[jax.ShapeDtypeStruct(shape, dtype) for sh...  17 us
    all_to_all x2, waiting for transfers between devices, exchange_half(): lax.all_to_all(value, 'expert', split_axis=0, concat_axis=0, tiled=True,...  12.8 us
    unnamed x82, local copies, waits for them, and re-layouts  11.7 us
    ppermute x5, starting transfers between devices, swap_pair(): return lax.ppermute(value, 'expert', [(i, i ^ other) for i in range(n)])  11.5 us
    ppermute x9, starting transfers between devices, swap_core(): return lax.ppermute(value, 'dp', [(0, 1), (1, 0)])  10.6 us
    all_to_all x2, starting transfers between devices, exchange_half(): lax.all_to_all(value, 'expert', split_axis=0, concat_axis=0, tiled=True,...  9.25 us
  transfers between devices with their start and end apart: 22, of which 8 were waited for; matrix products, arithmetic and copies ran while one was open for 7% of the time, Pallas kernels for 5%

profile of v1, /device:TPU:3, one launch (start us, length us, event | category | flops | bytes accessed | tf_op | source)
XLA Modules:
  0.0 180.2 jit_solution(16103874300272391286)
XLA Ops:
  0.6 3.4 %collective-permute-start = (bf16[128,768]{1,0:T(8,128)(2,1)}, bf16[128,768]{1,0:T(8,128)(2,1)S(1)}, u32[]{:S(2)}, u32[]{:S(2)}) collective-permute-start(bf16[128,768]{1,0:T(8,128)(2,1)} %bitcast.31), channel_id=1, source_target_pairs={{0,12},{1,13},{2,14},{3,15},{4,8},{5,9},{6,10},{7,11},{8,4},{9,5},... | collective-permute-start | bytes 589832 | tf_op jit(solution)/shard_map/ppermute | solution.py:39
  4.0 0.8 copy.26.router_ref
  5.6 0.8 copy-done.26
  6.3 0.8 copy-done.27
  7.1 0.8 copy-done.28
  8.1 1.0 collective-permute-start.3
  9.1 2.5 %collective-permute-start.4 = (bf16[24,640]{1,0:T(8,128)(2,1)S(1)}, bf16[24,640]{1,0:T(8,128)(2,1)S(1)}, u32[]{:S(2)}, u32[]{:S(2)}) collective-permute-start(bf16[24,640]{1,0:T(8,128)(2,1)S(1)} %get-tuple-element.79), channel_id=1, source_target_pairs={{0,24},{1,25},{2,26},{3,27},{4,28},{5,29},{6,30},{7,31},{8,16},{9,... | collective-permute-start | bytes 92168 | tf_op jit(solution)/shard_map/ppermute | solution.py:526
  11.6 4.4 %collective-permute-done.1 = s32[1,256]{1,0:T(1,128)S(1)} collective-permute-done((s32[1,256]{1,0:T(1,128)}, s32[1,256]{1,0:T(1,128)S(1)}, u32[]{:S(2)}, u32[]{:S(2)}) %collective-permute-start.1) | collective-permute-done | bytes 1056 | tf_op jit(solution)/shard_map/ppermute | solution.py:39
  16.1 0.8 copy-done.25
  16.8 1.2 shard_map.230
  18.0 3.7 %all-to-all-start = ((bf16[8,120,768]{2,1,0:T(8,128)(2,1)}), bf16[8,120,768]{2,1,0:T(8,128)(2,1)S(1)}, u32[]{:S(2)}, u32[]{:S(2)}) async-start(bf16[8,120,768]{2,1,0:T(8,128)(2,1)} %shard_map.230), calls=%async_computation | async-start | bytes 2949120 | tf_op jit(solution)/shard_map/all_to_all | solution.py:49
  21.8 2.2 %collective-permute-start.6 = (bf16[128,768]{1,0:T(8,128)(2,1)S(1)}, bf16[128,768]{1,0:T(8,128)(2,1)S(1)}, u32[]{:S(2)}, u32[]{:S(2)}) collective-permute-start(bf16[128,768]{1,0:T(8,128)(2,1)S(1)} %bitcast.32), channel_id=1, source_target_pairs={{0,16},{16,0},{1,17},{17,1},{2,18},{18,2},{3,19},{19,3},{4,20},{20... | collective-permute-start | bytes 589832 | tf_op jit(solution)/shard_map/ppermute | solution.py:33
  24.3 1.5 shard_map.231
  25.8 0.9 copy-done.10
  27.3 12.8 %all-to-all-done.arrived_ref = bf16[8,120,768]{2,1,0:T(8,128)(2,1)S(1)} async-done(((bf16[8,120,768]{2,1,0:T(8,128)(2,1)}), bf16[8,120,768]{2,1,0:T(8,128)(2,1)S(1)}, u32[]{:S(2)}, u32[]{:S(2)}) %all-to-all-start) | async-done | bytes 1474592 | tf_op jit(solution)/shard_map/all_to_all | solution.py:49
  40.1 1.1 copy-done.11
  41.2 1.6 shard_map.232
  43.6 1.4 shard_map.233
  45.2 3.1 %collective-permute-start.9 = (bf16[128,768]{1,0:T(8,128)(2,1)S(1)}, bf16[128,768]{1,0:T(8,128)(2,1)S(1)}, u32[]{:S(2)}, u32[]{:S(2)}) collective-permute-start(bf16[128,768]{1,0:T(8,128)(2,1)S(1)} %add_convert_fusion), channel_id=1, source_target_pairs={{0,12},{1,13},{2,14},{3,15},{4,8},{5,9},{6,10},{7,11},{8,4},{9,5},... | collective-permute-start | bytes 589832 | tf_op jit(solution)/shard_map/ppermute | solution.py:39
  48.4 4.7 %collective-permute-done.9.came_ref = bf16[128,768]{1,0:T(8,128)(2,1)S(1)} collective-permute-done((bf16[128,768]{1,0:T(8,128)(2,1)S(1)}, bf16[128,768]{1,0:T(8,128)(2,1)S(1)}, u32[]{:S(2)}, u32[]{:S(2)}) %collective-permute-start.9) | collective-permute-done | bytes 196640 | tf_op jit(solution)/shard_map/ppermute | solution.py:39
  53.1 0.9 copy-done.16
  54.1 0.8 shard_map.234
  54.9 24.0 %all_to_all.20 = bf16[16,24,768]{2,1,0:T(8,128)(2,1)S(1)} all-to-all(bf16[16,24,768]{2,1,0:T(8,128)(2,1)S(1)} %bitcast.45), channel_id=1, replica_groups=mesh['dp'=2,'expert'=16] {'expert'}, dimensions={0} | all-to-all | bytes 1179648 | tf_op jit(solution)/shard_map/all_to_all | solution.py:43
  78.9 1.9 %collective-permute-start.10 = (bf16[384,768]{1,0:T(8,128)(2,1)S(1)}, bf16[384,768]{1,0:T(8,128)(2,1)S(1)}, u32[]{:S(2)}, u32[]{:S(2)}) collective-permute-start(bf16[384,768]{1,0:T(8,128)(2,1)S(1)} %bitcast.38), channel_id=1, source_target_pairs={{0,16},{16,0},{1,17},{17,1},{2,18},{18,2},{3,19},{19,3},{4,20},{20... | collective-permute-start | bytes 1769480 | tf_op jit(solution)/shard_map/ppermute | solution.py:33
  80.8 1.6 collective-permute-done.10.other_ref
  82.4 5.5 %shard_map.235 = (bf16[320,768]{1,0:T(8,128)(2,1)S(1)}, bf16[320,768]{1,0:T(8,128)(2,1)S(1)}, bf16[160,768]{1,0:T(8,128)(2,1)S(1)}, f32[160,16]{1,0:T(8,128)S(1)...) custom-call(s32[1]{0:T(128)} %bitcast.place_ref, ...), custom_call_target="tpu_custom_call" | custom-call | tf_op jit(solution)/shard_map/pallas_call | solution.py:627
  88.4 1.5 collective-permute-done.11.came_ref
  89.9 0.9 shard_map.236
  90.9 19.1 %all_to_all.21 = bf16[16,24,768]{2,1,0:T(8,128)(2,1)S(1)} all-to-all(bf16[16,24,768]{2,1,0:T(8,128)(2,1)S(1)} %bitcast.44), channel_id=1, replica_groups=mesh['dp'=2,'expert'=16] {'expert'}, dimensions={0} | all-to-all | bytes 1179648 | tf_op jit(solution)/shard_map/all_to_all | solution.py:43
  110.4 1.9 %collective-permute-start.13 = (bf16[128,768]{1,0:T(8,128)(2,1)S(1)}, bf16[128,768]{1,0:T(8,128)(2,1)S(1)}, u32[]{:S(2)}, u32[]{:S(2)}) collective-permute-start(bf16[128,768]{1,0:T(8,128)(2,1)S(1)} %get-tuple-element.110.refs_0_), channel_id=1, source_target_pairs={{0,12},{1,13},{2,14},{3,15},{4,8},{5,9},{6,10},{7,11},{8,4},{9,5},... | collective-permute-start | bytes 589832 | tf_op jit(solution)/shard_map/ppermute | solution.py:39
  112.3 1.5 collective-permute-start.12
  113.8 3.1 %collective-permute-done.13.refs_0_ = bf16[128,768]{1,0:T(8,128)(2,1)S(1)} collective-permute-done((bf16[128,768]{1,0:T(8,128)(2,1)S(1)}, bf16[128,768]{1,0:T(8,128)(2,1)S(1)}, u32[]{:S(2)}, u32[]{:S(2)}) %collective-permute-start.13) | collective-permute-done | bytes 196640 | tf_op jit(solution)/shard_map/ppermute | solution.py:39
  116.9 2.9 %collective-permute-start.14 = (bf16[128,768]{1,0:T(8,128)(2,1)S(1)}, bf16[128,768]{1,0:T(8,128)(2,1)S(1)}, u32[]{:S(2)}, u32[]{:S(2)}) collective-permute-start(bf16[128,768]{1,0:T(8,128)(2,1)S(1)} %collective-permute-done.13.refs_0_), channel_id=1, source_target_pairs={{0,16},{16,0},{1,17},{17,1},{2,18},{18,2},{3,19},{19,3},{4,20},{20... | collective-permute-start | bytes 589832 | tf_op jit(solution)/shard_map/ppermute | solution.py:33
  119.9 2.7 %shard_map.239 = (f32[768,576]{1,0:T(8,128)S(1)}, f32[192,768]{1,0:T(8,128)S(1)}, f32[256,768]{1,0:T(8,128)S(1)}, f32[1,768]{1,0:T(1,128)S(1)}, f32[3,256]{1,0:T(4,128)S(1)}) custom-call(bf16[128,768]{1,0:T(8,128)(2,1)S(1)} %get-tuple-element.110.refs_0_, bf16[128,768]{1,0:T(8,128)(2,1)S(1)} %collective-permute-done.12.refs_1_, ...), custom_call_target="tpu_custom_call" | custom-call | flops 1000000 | bytes 1000000 | tf_op jit(solution)/shard_map/pallas_call | solution.py:69
  122.6 0.9 copy-done.8
  123.5 3.8 %shard_map.240 = (bf16[256,768]{1,0:T(8,128)(2,1)S(1)}, bf16[8,120,768]{2,1,0:T(8,128)(2,1)S(1)}, bf16[768,640]{1,0:T(8,128)(2,1)}, bf16[192,768]{1,0:T(8,128)(2,1)}) custom-call(bf16[128,768]{1,0:T(8,128)(2,1)S(1)} %collective-permute-done.13.refs_0_, bf16[128,768]{1,0:T(8,128)(2,1)S(1)} %collective-permute-done.14.refs_1_, ...), custom_call_target="tpu_custom_call" | custom-call | flops 1000000 | bytes 1000000 | tf_op jit(solution)/shard_map/pallas_call | solution.py:69
  127.3 1.2 copy-done.3
  129.2 5.5 %all-to-all-start.3 = ((bf16[8,120,768]{2,1,0:T(8,128)(2,1)}), bf16[8,120,768]{2,1,0:T(8,128)(2,1)S(1)}, u32[]{:S(2)}, u32[]{:S(2)}) async-start(bf16[8,120,768]{2,1,0:T(8,128)(2,1)} %copy-done.3), calls=%async_computation.3 | async-start | bytes 2949120 | tf_op jit(solution)/shard_map/all_to_all | solution.py:49
  134.8 3.2 %collective-permute-start.15 = (bf16[256,768]{1,0:T(8,128)(2,1)S(1)}, bf16[256,768]{1,0:T(8,128)(2,1)S(1)}, u32[]{:S(2)}, u32[]{:S(2)}) collective-permute-start(bf16[256,768]{1,0:T(8,128)(2,1)S(1)} %copy-done.34), channel_id=1, source_target_pairs={{0,12},{1,13},{2,14},{3,15},{4,8},{5,9},{6,10},{7,11},{8,4},{9,5},... | collective-permute-start | bytes 1179656 | tf_op jit(solution)/shard_map/ppermute | solution.py:39
  138.0 0.8 slice_reduce_fusion
  138.8 4.9 %convolution_bitcast_fusion.1 = f32[1,768,1536]{2,1,0:T(8,128)} fusion(bf16[320,768]{1,0:T(8,128)(2,1)S(1)} %get-tuple-element.100, bf16[320,1536]{1,0:T(8,128)(2,1)} %copy-done.4), kind=kOutput, calls=%fused_computation.1 | convolution fusion | flops 754974720 | bytes 6193152 | tf_op jit(solution)/shard_map/dot_general | solution.py:19
  143.7 22.1 %collective-permute-done.15 = bf16[256,768]{1,0:T(8,128)(2,1)S(1)} collective-permute-done((bf16[256,768]{1,0:T(8,128)(2,1)S(1)}, bf16[256,768]{1,0:T(8,128)(2,1)S(1)}, u32[]{:S(2)}, u32[]{:S(2)}) %collective-permute-start.15) | collective-permute-done | bytes 393248 | tf_op jit(solution)/shard_map/ppermute | solution.py:39
  165.9 0.9 collective-permute-start.16
  166.7 3.6 %convolution_bitcast_fusion = f32[1,1536,768]{2,1,0:T(8,128)} fusion(bf16[320,1536]{1,0:T(8,128)(2,1)S(1)} %copy-done.30, bf16[320,768]{1,0:T(8,128)(2,1)S(1)} %copy-done.32), kind=kOutput, calls=%fused_computation | convolution fusion | flops 754974720 | bytes 6193152 | tf_op jit(solution)/shard_map/dot_general | solution.py:19
  170.4 0.9 shard_map.237
  172.3 2.7 %collective-permute-start.19 = (bf16[24,640]{1,0:T(8,128)(2,1)S(1)}, bf16[24,640]{1,0:T(8,128)(2,1)S(1)}, u32[]{:S(2)}, u32[]{:S(2)}) collective-permute-start(bf16[24,640]{1,0:T(8,128)(2,1)S(1)} %get-tuple-element.129), channel_id=1, source_target_pairs={{0,24},{1,25},{2,26},{3,27},{4,28},{5,29},{6,30},{7,31},{8,16},{9,... | collective-permute-start | bytes 92168 | tf_op jit(solution)/shard_map/ppermute | solution.py:526
  175.0 1.9 %fusion.9 = bf16[1,128,768]{2,1,0:T(8,128)(2,1)} fusion(f32[128,768]{1,0:T(8,128)S(1)} %copy-done.14, bf16[128,768]{1,0:T(8,128)(2,1)S(1)} %collective-permute-done.16, f32[256,768]{1,0:T(8,128)} %copy-done.35, f32[128]{0:T(128)S(1)} %broadcast_multiply_fusion, f32[768]{0:T(1024)S(1)} %slice_reduce_fusion, f32[128]{0:T(128)S(1)} %add_rsqrt_fusion, ...), kind=kLoop, calls=%fused_computation.17 | loop fusion | flops 983040 | bytes 1380352 | tf_op jit(solution)/shard_map/reshape | solution.py:720
  177.5 0.8 shard_map.242
  (112 shorter events, 8.3 us)
Async XLA Ops:
  0.6 15.4 %collective-permute-start = (bf16[128,768]{1,0:T(8,128)(2,1)}, bf16[128,768]{1,0:T(8,128)(2,1)S(1)}, u32[]{:S(2)}, u32[]{:S(2)}) collective-permute-start(bf16[128,768]{1,0:T(8,128)(2,1)} %bitcast.31), channel_id=1, source_target_pairs={{0,12},{1,13},{2,14},{3,15},{4,8},{5,9},{6,10},{7,11},{8,4},{9,5},... | collective-permute-start | bytes 589832 | tf_op jit(solution)/shard_map/ppermute | solution.py:39
  4.8 19.1 %copy-start.36 = (f32[32,12]{0,1:T(8,128)S(1)}, f32[32,12]{0,1:T(8,128)}, u32[]{:S(2)}) copy-start(f32[32,12]{0,1:T(8,128)} %param.20) | copy-start | bytes 4612
  4.8 19.2 %copy-start.38 = (s32[1,128,1]{1,2,0:T(1,128)S(1)}, s32[1,128,1]{1,2,0:T(1,128)}, u32[]{:S(2)}) copy-start(s32[1,128,1]{1,2,0:T(1,128)} %param.26) | copy-start | bytes 1540
  4.8 19.4 %copy-start.37 = (s32[1,256]{1,0:T(1,128)S(1)}, s32[1,256]{1,0:T(1,128)}, u32[]{:S(2)}) copy-start(s32[1,256]{1,0:T(1,128)} %param.25) | copy-start | bytes 3076
  4.8 16.9 %copy-start = (bf16[1,128,768]{2,1,0:T(8,128)(2,1)S(1)}, bf16[1,128,768]{2,1,0:T(8,128)(2,1)}, u32[]{:S(2)}) copy-start(bf16[1,128,768]{2,1,0:T(8,128)(2,1)} %param.14) | copy-start | bytes 589828
  8.0 8.0 %collective-permute-start.2 = (bf16[24,640]{1,0:T(8,128)(2,1)S(1)}, bf16[24,640]{1,0:T(8,128)(2,1)S(1)}, u32[]{:S(2)}, u32[]{:S(2)}) collective-permute-start(bf16[24,640]{1,0:T(8,128)(2,1)S(1)} %get-tuple-element.77), channel_id=1, source_target_pairs={{0,8},{1,9},{2,10},{3,11},{4,12},{5,13},{6,14},{7,15},{8,0},{9,1},... | collective-permute-start | bytes 92168 | tf_op jit(solution)/shard_map/ppermute | solution.py:526
  8.1 7.9 %collective-permute-start.3 = (bf16[24,640]{1,0:T(8,128)(2,1)S(1)}, bf16[24,640]{1,0:T(8,128)(2,1)S(1)}, u32[]{:S(2)}, u32[]{:S(2)}) collective-permute-start(bf16[24,640]{1,0:T(8,128)(2,1)S(1)} %get-tuple-element.78), channel_id=1, source_target_pairs={{0,16},{1,17},{2,18},{3,19},{4,20},{5,21},{6,22},{7,23},{8,24},{9,... | collective-permute-start | bytes 92168 | tf_op jit(solution)/shard_map/ppermute | solution.py:526
  9.1 6.9 %collective-permute-start.4 = (bf16[24,640]{1,0:T(8,128)(2,1)S(1)}, bf16[24,640]{1,0:T(8,128)(2,1)S(1)}, u32[]{:S(2)}, u32[]{:S(2)}) collective-permute-start(bf16[24,640]{1,0:T(8,128)(2,1)S(1)} %get-tuple-element.79), channel_id=1, source_target_pairs={{0,24},{1,25},{2,26},{3,27},{4,28},{5,29},{6,30},{7,31},{8,16},{9,... | collective-permute-start | bytes 92168 | tf_op jit(solution)/shard_map/ppermute | solution.py:526
  11.6 4.4 %collective-permute-start.1 = (s32[1,256]{1,0:T(1,128)}, s32[1,256]{1,0:T(1,128)S(1)}, u32[]{:S(2)}, u32[]{:S(2)}) collective-permute-start(s32[1,256]{1,0:T(1,128)} %param.25), channel_id=1, source_target_pairs={{0,12},{1,13},{2,14},{3,15},{4,8},{5,9},{6,10},{7,11},{8,4},{9,5},... | collective-permute-start | bytes 3080 | tf_op jit(solution)/shard_map/ppermute | solution.py:39
  18.0 22.1 %all-to-all-start = ((bf16[8,120,768]{2,1,0:T(8,128)(2,1)}), bf16[8,120,768]{2,1,0:T(8,128)(2,1)S(1)}, u32[]{:S(2)}, u32[]{:S(2)}) async-start(bf16[8,120,768]{2,1,0:T(8,128)(2,1)} %shard_map.230), calls=%async_computation | async-start | bytes 2949120 | tf_op jit(solution)/shard_map/all_to_all | solution.py:49
  21.8 21.8 %collective-permute-start.6 = (bf16[128,768]{1,0:T(8,128)(2,1)S(1)}, bf16[128,768]{1,0:T(8,128)(2,1)S(1)}, u32[]{:S(2)}, u32[]{:S(2)}) collective-permute-start(bf16[128,768]{1,0:T(8,128)(2,1)S(1)} %bitcast.32), channel_id=1, source_target_pairs={{0,16},{16,0},{1,17},{17,1},{2,18},{18,2},{3,19},{19,3},{4,20},{20... | collective-permute-start | bytes 589832 | tf_op jit(solution)/shard_map/ppermute | solution.py:33
  24.1 3.1 %collective-permute-start.5 = (bf16[128,768]{1,0:T(8,128)(2,1)S(1)}, bf16[128,768]{1,0:T(8,128)(2,1)S(1)}, u32[]{:S(2)}, u32[]{:S(2)}) collective-permute-start(bf16[128,768]{1,0:T(8,128)(2,1)S(1)} %collective-permute-done.own_ref.refs_8_), channel_id=1, source_target_pairs={{0,16},{16,0},{1,17},{17,1},{2,18},{18,2},{3,19},{19,3},{4,20},{20... | collective-permute-start | bytes 589832 | tf_op jit(solution)/shard_map/ppermute | solution.py:33
  27.3 17.7 %copy-start.15 = (bf16[384,256]{1,0:T(8,128)(2,1)}, bf16[384,256]{1,0:T(8,128)(2,1)S(1)}, u32[]{:S(2)}) copy-start(bf16[384,256]{1,0:T(8,128)(2,1)S(1)} %get-tuple-element.96.send_ref) | copy-start | bytes 589828
  27.3 17.7 %copy-start.17 = (bf16[128,384]{1,0:T(8,128)(2,1)}, bf16[128,384]{1,0:T(8,128)(2,1)S(1)}, u32[]{:S(2)}) copy-start(bf16[128,384]{1,0:T(8,128)(2,1)S(1)} %get-tuple-element.108.spread_ref) | copy-start | bytes 294916
  27.3 17.8 %copy-start.19 = (bf16[128,384]{1,0:T(8,128)(2,1)}, bf16[128,384]{1,0:T(8,128)(2,1)S(1)}, u32[]{:S(2)}) copy-start(bf16[128,384]{1,0:T(8,128)(2,1)S(1)} %get-tuple-element.105.spread_ref) | copy-start | bytes 294916
  41.2 11.9 %copy-start.22 = (f32[128,16]{1,0:T(8,128)S(1)}, f32[128,16]{1,0:T(8,128)}, u32[]{:S(2)}) copy-start(f32[128,16]{1,0:T(8,128)} %copy-done.21) | copy-start | bytes 24580
  42.9 80.6 %copy-start.12 = (f32[8,768]{1,0:T(8,128)}, f32[8,768]{1,0:T(8,128)S(1)}, u32[]{:S(2)}) copy-start(f32[8,768]{1,0:T(8,128)S(1)} %get-tuple-element.89.gains_ref.refs_6_) | copy-start | bytes 73732
  42.9 10.2 %copy-start.5 = (bf16[1,128,768]{2,1,0:T(8,128)(2,1)S(1)}, bf16[1,128,768]{2,1,0:T(8,128)(2,1)}, u32[]{:S(2)}) copy-start(bf16[1,128,768]{2,1,0:T(8,128)(2,1)} %param.27) | copy-start | bytes 589828
  42.9 2.3 %collective-permute-start.8 = (bf16[128,768]{1,0:T(8,128)(2,1)S(1)}, bf16[128,768]{1,0:T(8,128)(2,1)S(1)}, u32[]{:S(2)}, u32[]{:S(2)}) collective-permute-start(bf16[128,768]{1,0:T(8,128)(2,1)S(1)} %get-tuple-element.94), channel_id=1, source_target_pairs={{0,16},{16,0},{1,17},{17,1},{2,18},{18,2},{3,19},{19,3},{4,20},{20... | collective-permute-start | bytes 589832 | tf_op jit(solution)/shard_map/ppermute | solution.py:33
  43.6 11.3 %copy-start.6 = (bf16[128,768]{1,0:T(8,128)(2,1)}, bf16[128,768]{1,0:T(8,128)(2,1)S(1)}, u32[]{:S(2)}) copy-start(bf16[128,768]{1,0:T(8,128)(2,1)S(1)} %collective-permute-done.6.across_ref.refs_9_) | copy-start | bytes 589828
  43.6 38.8 %copy-start.2 = (bf16[1,1536,768]{2,1,0:T(8,128)(2,1)S(1)}, bf16[1,1536,768]{2,1,0:T(8,128)(2,1)}, u32[]{:S(2)}) copy-start(bf16[1,1536,768]{2,1,0:T(8,128)(2,1)} %param.24) | copy-start | bytes 7077892
  45.0 37.4 %copy-start.1 = (bf16[1,768,1536]{2,1,0:T(8,128)(2,1)S(1)}, bf16[1,768,1536]{2,1,0:T(8,128)(2,1)}, u32[]{:S(2)}) copy-start(bf16[1,768,1536]{2,1,0:T(8,128)(2,1)} %param.23) | copy-start | bytes 7077892
  45.1 3.3 %collective-permute-start.7 = (bf16[128,768]{1,0:T(8,128)(2,1)S(1)}, bf16[128,768]{1,0:T(8,128)(2,1)S(1)}, u32[]{:S(2)}, u32[]{:S(2)}) collective-permute-start(bf16[128,768]{1,0:T(8,128)(2,1)S(1)} %get-tuple-element.92), channel_id=1, source_target_pairs={{0,16},{16,0},{1,17},{17,1},{2,18},{18,2},{3,19},{19,3},{4,20},{20... | collective-permute-start | bytes 589832 | tf_op jit(solution)/shard_map/ppermute | solution.py:33
  45.2 7.9 %collective-permute-start.9 = (bf16[128,768]{1,0:T(8,128)(2,1)S(1)}, bf16[128,768]{1,0:T(8,128)(2,1)S(1)}, u32[]{:S(2)}, u32[]{:S(2)}) collective-permute-start(bf16[128,768]{1,0:T(8,128)(2,1)S(1)} %add_convert_fusion), channel_id=1, source_target_pairs={{0,12},{1,13},{2,14},{3,15},{4,8},{5,9},{6,10},{7,11},{8,4},{9,5},... | collective-permute-start | bytes 589832 | tf_op jit(solution)/shard_map/ppermute | solution.py:39
  54.9 33.1 %copy-start.23 = (f32[128,1]{1,0:T(8,128)}, f32[128,1]{1,0:T(8,128)S(1)}, u32[]{:S(2)}) copy-start(f32[128,1]{1,0:T(8,128)S(1)} %get-tuple-element.107.gate_ref) | copy-start | bytes 1540
  78.9 3.5 %collective-permute-start.10 = (bf16[384,768]{1,0:T(8,128)(2,1)S(1)}, bf16[384,768]{1,0:T(8,128)(2,1)S(1)}, u32[]{:S(2)}, u32[]{:S(2)}) collective-permute-start(bf16[384,768]{1,0:T(8,128)(2,1)S(1)} %bitcast.38), channel_id=1, source_target_pairs={{0,16},{16,0},{1,17},{17,1},{2,18},{18,2},{3,19},{19,3},{4,20},{20... | collective-permute-start | bytes 1769480 | tf_op jit(solution)/shard_map/ppermute | solution.py:33
  87.9 22.5 %copy-start.29 = (bf16[320,1536]{1,0:T(8,128)(2,1)}, bf16[320,1536]{1,0:T(8,128)(2,1)S(1)}, u32[]{:S(2)}) copy-start(bf16[320,1536]{1,0:T(8,128)(2,1)S(1)} %get-tuple-element.138) | copy-start | bytes 2949124
  87.9 22.5 %copy-start.31 = (bf16[320,768]{1,0:T(8,128)(2,1)}, bf16[320,768]{1,0:T(8,128)(2,1)S(1)}, u32[]{:S(2)}) copy-start(bf16[320,768]{1,0:T(8,128)(2,1)S(1)} %get-tuple-element.139) | copy-start | bytes 1474564
  88.0 35.5 %copy-start.4 = (bf16[320,1536]{1,0:T(8,128)(2,1)}, bf16[320,1536]{1,0:T(8,128)(2,1)S(1)}, u32[]{:S(2)}) copy-start(bf16[320,1536]{1,0:T(8,128)(2,1)S(1)} %get-tuple-element.137) | copy-start | bytes 2949124
  88.0 22.0 %copy-start.18 = (bf16[128,384]{1,0:T(8,128)(2,1)S(1)}, bf16[128,384]{1,0:T(8,128)(2,1)}, u32[]{:S(2)}) copy-start(bf16[128,384]{1,0:T(8,128)(2,1)} %copy-done.17) | copy-start | bytes 294916
  88.0 1.9 %collective-permute-start.11 = (bf16[2,160,768]{2,1,0:T(8,128)(2,1)S(1)}, bf16[2,160,768]{2,1,0:T(8,128)(2,1)S(1)}, u32[]{:S(2)}, u32[]{:S(2)}) collective-permute-start(bf16[2,160,768]{2,1,0:T(8,128)(2,1)S(1)} %get-tuple-element.99), channel_id=1, source_target_pairs={{0,16},{16,0},{1,17},{17,1},{2,18},{18,2},{3,19},{19,3},{4,20},{20... | collective-permute-start | bytes 1474568 | tf_op jit(solution)/shard_map/ppermute | solution.py:33
  89.9 30.0 %copy-start.7 = (bf16[128,768]{1,0:T(8,128)(2,1)S(1)}, bf16[128,768]{1,0:T(8,128)(2,1)}, u32[]{:S(2)}) copy-start(bf16[128,768]{1,0:T(8,128)(2,1)} %copy-done.6) | copy-start | bytes 589828
  110.4 16.8 %copy-start.13 = (f32[128,768]{1,0:T(8,128)}, f32[128,768]{1,0:T(8,128)S(1)}, u32[]{:S(2)}) copy-start(f32[128,768]{1,0:T(8,128)S(1)} %get-tuple-element.109) | copy-start | bytes 1179652
  110.4 6.5 %collective-permute-start.13 = (bf16[128,768]{1,0:T(8,128)(2,1)S(1)}, bf16[128,768]{1,0:T(8,128)(2,1)S(1)}, u32[]{:S(2)}, u32[]{:S(2)}) collective-permute-start(bf16[128,768]{1,0:T(8,128)(2,1)S(1)} %get-tuple-element.110.refs_0_), channel_id=1, source_target_pairs={{0,12},{1,13},{2,14},{3,15},{4,8},{5,9},{6,10},{7,11},{8,4},{9,5},... | collective-permute-start | bytes 589832 | tf_op jit(solution)/shard_map/ppermute | solution.py:39
  112.3 7.5 %collective-permute-start.12 = (bf16[128,768]{1,0:T(8,128)(2,1)S(1)}, bf16[128,768]{1,0:T(8,128)(2,1)S(1)}, u32[]{:S(2)}, u32[]{:S(2)}) collective-permute-start(bf16[128,768]{1,0:T(8,128)(2,1)S(1)} %get-tuple-element.110.refs_0_), channel_id=1, source_target_pairs={{0,16},{16,0},{1,17},{17,1},{2,18},{18,2},{3,19},{19,3},{4,20},{20... | collective-permute-start | bytes 589832 | tf_op jit(solution)/shard_map/ppermute | solution.py:33
  116.9 6.5 %collective-permute-start.14 = (bf16[128,768]{1,0:T(8,128)(2,1)S(1)}, bf16[128,768]{1,0:T(8,128)(2,1)S(1)}, u32[]{:S(2)}, u32[]{:S(2)}) collective-permute-start(bf16[128,768]{1,0:T(8,128)(2,1)S(1)} %collective-permute-done.13.refs_0_), channel_id=1, source_target_pairs={{0,16},{16,0},{1,17},{17,1},{2,18},{18,2},{3,19},{19,3},{4,20},{20... | collective-permute-start | bytes 589832 | tf_op jit(solution)/shard_map/ppermute | solution.py:33
  129.2 5.6 %copy-start.34 = (bf16[256,768]{1,0:T(8,128)(2,1)S(1)}, bf16[256,768]{1,0:T(8,128)(2,1)}, u32[]{:S(2)}) copy-start(bf16[256,768]{1,0:T(8,128)(2,1)} %copy-done.33) | copy-start | bytes 1179652
  129.2 42.4 %all-to-all-start.3 = ((bf16[8,120,768]{2,1,0:T(8,128)(2,1)}), bf16[8,120,768]{2,1,0:T(8,128)(2,1)S(1)}, u32[]{:S(2)}, u32[]{:S(2)}) async-start(bf16[8,120,768]{2,1,0:T(8,128)(2,1)} %copy-done.3), calls=%async_computation.3 | async-start | bytes 2949120 | tf_op jit(solution)/shard_map/all_to_all | solution.py:49
  134.8 30.9 %collective-permute-start.15 = (bf16[256,768]{1,0:T(8,128)(2,1)S(1)}, bf16[256,768]{1,0:T(8,128)(2,1)S(1)}, u32[]{:S(2)}, u32[]{:S(2)}) collective-permute-start(bf16[256,768]{1,0:T(8,128)(2,1)S(1)} %copy-done.34), channel_id=1, source_target_pairs={{0,12},{1,13},{2,14},{3,15},{4,8},{5,9},{6,10},{7,11},{8,4},{9,5},... | collective-permute-start | bytes 1179656 | tf_op jit(solution)/shard_map/ppermute | solution.py:39
  138.8 27.0 %copy-start.9 = (f32[256,768]{1,0:T(8,128)S(1)}, f32[256,768]{1,0:T(8,128)}, u32[]{:S(2)}) copy-start(f32[256,768]{1,0:T(8,128)} %copy-done.8) | copy-start | bytes 2359300
  143.6 23.1 %copy-start.30 = (bf16[320,1536]{1,0:T(8,128)(2,1)S(1)}, bf16[320,1536]{1,0:T(8,128)(2,1)}, u32[]{:S(2)}) copy-start(bf16[320,1536]{1,0:T(8,128)(2,1)} %copy-done.29) | copy-start | bytes 2949124
  143.7 23.1 %copy-start.32 = (bf16[320,768]{1,0:T(8,128)(2,1)S(1)}, bf16[320,768]{1,0:T(8,128)(2,1)}, u32[]{:S(2)}) copy-start(bf16[320,768]{1,0:T(8,128)(2,1)} %copy-done.31) | copy-start | bytes 1474564
  165.8 5.7 %copy-start.35 = (f32[256,768]{1,0:T(8,128)}, f32[256,768]{1,0:T(8,128)S(1)}, u32[]{:S(2)}) copy-start(f32[256,768]{1,0:T(8,128)S(1)} %convert_add_fusion) | copy-start | bytes 2359300
  165.9 5.4 %collective-permute-start.16 = (bf16[128,768]{1,0:T(8,128)(2,1)S(1)}, bf16[128,768]{1,0:T(8,128)(2,1)S(1)}, u32[]{:S(2)}, u32[]{:S(2)}) collective-permute-start(bf16[128,768]{1,0:T(8,128)(2,1)S(1)} %slice.70), channel_id=1, source_target_pairs={{0,16},{16,0},{1,17},{17,1},{2,18},{18,2},{3,19},{19,3},{4,20},{20... | collective-permute-start | bytes 589832 | tf_op jit(solution)/shard_map/ppermute | solution.py:33
  170.3 4.6 %copy-start.14 = (f32[128,768]{1,0:T(8,128)S(1)}, f32[128,768]{1,0:T(8,128)}, u32[]{:S(2)}) copy-start(f32[128,768]{1,0:T(8,128)} %copy-done.13) | copy-start | bytes 1179652
  172.2 4.7 %collective-permute-start.17 = (bf16[24,640]{1,0:T(8,128)(2,1)S(1)}, bf16[24,640]{1,0:T(8,128)(2,1)S(1)}, u32[]{:S(2)}, u32[]{:S(2)}) collective-permute-start(bf16[24,640]{1,0:T(8,128)(2,1)S(1)} %get-tuple-element.127), channel_id=1, source_target_pairs={{0,8},{1,9},{2,10},{3,11},{4,12},{5,13},{6,14},{7,15},{8,0},{9,1},... | collective-permute-start | bytes 92168 | tf_op jit(solution)/shard_map/ppermute | solution.py:526
  172.2 4.7 %collective-permute-start.18 = (bf16[24,640]{1,0:T(8,128)(2,1)S(1)}, bf16[24,640]{1,0:T(8,128)(2,1)S(1)}, u32[]{:S(2)}, u32[]{:S(2)}) collective-permute-start(bf16[24,640]{1,0:T(8,128)(2,1)S(1)} %get-tuple-element.128), channel_id=1, source_target_pairs={{0,16},{1,17},{2,18},{3,19},{4,20},{5,21},{6,22},{7,23},{8,24},{9,... | collective-permute-start | bytes 92168 | tf_op jit(solution)/shard_map/ppermute | solution.py:526
  172.3 5.3 %collective-permute-start.19 = (bf16[24,640]{1,0:T(8,128)(2,1)S(1)}, bf16[24,640]{1,0:T(8,128)(2,1)S(1)}, u32[]{:S(2)}, u32[]{:S(2)}) collective-permute-start(bf16[24,640]{1,0:T(8,128)(2,1)S(1)} %get-tuple-element.129), channel_id=1, source_target_pairs={{0,24},{1,25},{2,26},{3,27},{4,28},{5,29},{6,30},{7,31},{8,16},{9,... | collective-permute-start | bytes 92168 | tf_op jit(solution)/shard_map/ppermute | solution.py:526
  (13 other events, 16.7 us)

commit v2 on v1

--- a/solution.py
+++ b/solution.py
@@ -63,16 +63,54 @@
     return lax.broadcasted_iota(jnp.int32, shape, axis)
 
 
-def kernel_call(body, outs, *args, scalars=0, flops=1_000_000, nbytes=1_000_000):
-    specs = [pl.BlockSpec(memory_space=pltpu.SMEM)] * scalars
-    specs += [pl.BlockSpec(memory_space=pltpu.VMEM)] * (len(args) - scalars)
+class LateRef:
+    def __init__(self, source, target, sem):
+        self.copy = pltpu.make_async_copy(source, target, sem)
+        self.target = target
+        self.shape = target.shape
+        self.pending = True
+        self.copy.start()
+
+    def wait(self):
+        if self.pending:
+            self.copy.wait()
+            self.pending = False
+
+    def __getitem__(self, index):
+        self.wait()
+        return self.target[index]
+
+
+def kernel_call(body, outs, *args, scalars=0, late=(), limit=VMEM_BYTES):
+    count = len(args)
+    late = sorted(late)
+
+    def run(*refs):
+        ins = list(refs[:count])
+        out_refs = refs[count : count + len(outs)]
+        scratch = refs[count + len(outs) :]
+        for n, i in enumerate(late):
+            ins[i] = LateRef(ins[i], scratch[n], scratch[-1].at[n])
+        body(*ins, *out_refs)
+        for i in late:
+            ins[i].wait()
+
+    spaces = [pltpu.SMEM if i < scalars else pltpu.VMEM for i in range(count)]
+    for i in late:
+        spaces[i] = pltpu.HBM
+    scratch = [pltpu.VMEM(args[i].shape, args[i].dtype) for i in late]
+    if late:
+        scratch.append(pltpu.SemaphoreType.DMA((len(late),)))
     return pl.pallas_call(
-        body,
+        run,
         out_shape=[jax.ShapeDtypeStruct(shape, dtype) for shape, dtype in outs],
-        in_specs=specs,
+        in_specs=[pl.BlockSpec(memory_space=space) for space in spaces],
         out_specs=[pl.BlockSpec(memory_space=pltpu.VMEM)] * len(outs),
-        compiler_params=pltpu.CompilerParams(vmem_limit_bytes=VMEM_BYTES),
-        cost_estimate=pl.CostEstimate(flops=flops, bytes_accessed=nbytes, transcendentals=0),
+        scratch_shapes=scratch,
+        compiler_params=pltpu.CompilerParams(vmem_limit_bytes=limit),
+        cost_estimate=pl.CostEstimate(
+            flops=1_000_000, bytes_accessed=1_000_000, transcendentals=0
+        ),
     )(*args)
 
 
@@ -83,27 +121,36 @@
     return picked
 
 
-def pack_weights(group_ref, q_ref, k_ref, v_ref, router_ref, gains_ref, *out_refs):
+def pack_weights(group_ref, q_ref, k_ref, v_ref, router_ref, one_ref, two_ref, wout_ref, docs_ref,
+                 *refs):
+    *out_refs, keep_ref = refs
     rows, width = q_ref.shape
-    experts = router_ref.shape[1]
+    experts = router_ref.shape[0]
     cols = width // 4
     eye = iota((rows, rows), 0) == iota((rows, rows), 1)
+    router = dot(eye.astype(F32).astype(BF16), router_ref[...], ((1,), (1,)))
     columns = [
-        jnp.sum(jnp.where(eye, gains_ref[i : i + 1, :].astype(F32), 0.0), axis=1, keepdims=True)
-        for i in range(2)
+        jnp.sum(jnp.where(eye, ref[...].astype(F32), 0.0), axis=1, keepdims=True)
+        for ref in (one_ref, two_ref)
     ]
-    pad = out_refs[0].shape[1] - 3 * cols - experts - 2
+    docs = docs_ref[...].astype(F32)
+    length = docs.shape[1]
+    doc_cols = -(-length // rows)
+    for t in range(doc_cols):
+        belongs = iota((rows, length), 1) == iota((rows, length), 0) * doc_cols + t
+        columns.append(jnp.sum(jnp.where(belongs, docs, 0.0), axis=1, keepdims=True))
+    pad = out_refs[0].shape[1] - 3 * cols - experts - 2 - doc_cols
     small = jnp.concatenate(
-        [router_ref[...].astype(F32)] + columns + [jnp.zeros((rows, pad), F32)], axis=1
+        [router] + columns + [jnp.zeros((rows, pad), F32)], axis=1
     ).astype(BF16)
+    weights = [ref[...] for ref in (q_ref, k_ref, v_ref)]
     pieces = [
-        jnp.concatenate(
-            [ref[:, j * cols : (j + 1) * cols] for ref in (q_ref, k_ref, v_ref)] + [small], axis=1
-        )
+        jnp.concatenate([w[:, j * cols : (j + 1) * cols] for w in weights] + [small], axis=1)
         for j in range(4)
     ]
     for d, out_ref in enumerate(out_refs):
         out_ref[...] = choose(group_ref[0] ^ d, pieces)
+    keep_ref[...] = wout_ref[...]
 
 
 def spread_weights(group_ref, p0_ref, p1_ref, p2_ref, p3_ref, wout_ref, out_ref):
@@ -121,28 +168,20 @@
         out_ref[dest] = value
 
 
-def prepare(capacity, pad_two, group_ref, table_ref, docs_ref, routes_ref, own_bias_ref,
-            pair_bias_ref, spread_ref, later_ref, gather_ref, send_ref):
+def prepare(capacity, pad_two, group_ref, table_ref, routes_ref, vector_ref, spread_ref, later_ref,
+            gather_ref, send_ref):
     buckets = table_ref.shape[0]
-    own_heads = own_bias_ref.shape[0]
-    length = docs_ref.shape[1]
+    own_heads, length = vector_ref.shape
     toks = length // 2
     group = group_ref[0]
     spot = iota((1, length), 1)
     offset = jnp.where(spot >= toks, spot - length, spot)
     bucket = bucket_of(offset, buckets)
-    vectors = []
     for h in range(own_heads):
         vector = jnp.zeros((1, length), F32)
         for b in range(buckets):
             vector = jnp.where(bucket == b, table_ref[b, group * own_heads + h], vector)
-        full = jnp.broadcast_to(vector, (length, length))
-        vectors.append(pltpu.roll(full, 0, 1, stride=1, stride_axis=0))
-    for r, bias_ref in enumerate((own_bias_ref, pair_bias_ref)):
-        across = jnp.broadcast_to(docs_ref[r : r + 1, :].astype(F32), (length, length))
-        same = across == jnp.transpose(across)
-        for h in range(own_heads):
-            bias_ref[h] = jnp.where(same, vectors[h], MASKED)
+        vector_ref[h : h + 1] = vector
     experts = spread_ref.shape[1] // pad_two
     route = routes_ref[...]
     chosen = route == iota((toks, experts), 1)
@@ -182,11 +221,15 @@
     gains_ref[...] = dot(pick, small, ((1,), (1,)))
 
 
-def attend(scale, head_dim, w_ref, wout_ref, gains_ref, own_ref, across_ref, bias_ref, qkv_ref,
-           probs_ref, att_ref, keep_ref, send_ref):
-    own_heads = bias_ref.shape[0]
+def attend(scale, head_dim, docs, group_ref, w_ref, wout_ref, gains_ref, own_ref, across_ref,
+           vector_ref, qkv_ref, probs_ref, att_ref, keep_ref, send_ref):
+    own_heads, length = vector_ref.shape
     cols = own_heads * head_dim
     toks = own_ref.shape[0]
+    vectors = vector_ref[...]
+    turned = jnp.concatenate([docs[:, toks:], docs[:, :toks]], axis=1)
+    across = jnp.broadcast_to(jnp.where(group_ref[0] < 2, docs, turned), (length, length))
+    same = across == jnp.transpose(across)
     x = jnp.concatenate([own_ref[...], across_ref[...]], axis=0).astype(F32)
     normed = (x * rms_inverse(x) * gains_ref[0:1]).astype(BF16)
     qkv = dot(normed, w_ref[:, : 3 * cols]).astype(BF16)
@@ -197,7 +240,9 @@
         q = qkv[:, at : at + head_dim]
         k = qkv[:, cols + at : cols + at + head_dim]
         v = qkv[:, 2 * cols + at : 2 * cols + at + head_dim]
-        scores = dot(q, k, ((1,), (1,))) * scale + bias_ref[h]
+        full = jnp.broadcast_to(vectors[h : h + 1], (length, length))
+        bias = pltpu.roll(full, 0, 1, stride=1, stride_axis=0)
+        scores = jnp.where(same, dot(q, k, ((1,), (1,))) * scale + bias, MASKED)
         top = jnp.max(scores, axis=1, keepdims=True)
         raised = jnp.exp(scores - top)
         probs = raised * (1.0 / jnp.sum(raised, axis=1, keepdims=True))
@@ -210,17 +255,41 @@
     send_ref[...] = partial[toks:].astype(BF16)
 
 
-def attend_first(scale, head_dim, experts, arrived_ref, own_ref, across_ref, bias_ref, w_ref,
-                 wout_ref, gains_ref, *out_refs):
+def docs_of_pair(at, length, group_ref, place_ref, arrived_ref):
+    sources, total, _ = arrived_ref.shape
+    rows = total // 5
+    doc_cols = -(-length // rows)
+    held = arrived_ref[(place_ref[0] % sources) ^ (sources // 2)]
+    blocks = [held[j * rows : (j + 1) * rows, at : at + doc_cols].astype(F32) for j in range(4)]
+    block = choose(group_ref[0] ^ 1, blocks)
+    docs = jnp.zeros((1, length), F32)
+    for t in range(doc_cols):
+        belongs = iota((rows, length), 1) == iota((rows, length), 0) * doc_cols + t
+        docs = docs + jnp.sum(jnp.where(belongs, block[:, t : t + 1], 0.0), axis=0, keepdims=True)
+    return docs
+
+
+def attend_own(scale, head_dim, group_ref, docs_ref, *refs):
+    attend(scale, head_dim, docs_ref[...].astype(F32), group_ref, *refs)
+
+
+def attend_first(scale, head_dim, experts, group_ref, place_ref, arrived_ref, own_ref, across_ref,
+                 vector_ref, w_ref, wout_ref, gains_ref, *outs):
     place_weights(arrived_ref, w_ref, wout_ref)
-    gain_rows(experts, bias_ref.shape[0] * head_dim, w_ref, gains_ref)
-    attend(scale, head_dim, w_ref, wout_ref, gains_ref, own_ref, across_ref, bias_ref, *out_refs)
-
-
-def attend_first_placed(scale, head_dim, experts, w_ref, wout_ref, own_ref, across_ref, bias_ref,
-                        gains_ref, *out_refs):
-    gain_rows(experts, bias_ref.shape[0] * head_dim, w_ref, gains_ref)
-    attend(scale, head_dim, w_ref, wout_ref, gains_ref, own_ref, across_ref, bias_ref, *out_refs)
+    cols = wout_ref.shape[0]
+    gain_rows(experts, cols, w_ref, gains_ref)
+    docs = docs_of_pair(3 * cols + experts + 2, vector_ref.shape[1], group_ref, place_ref, arrived_ref)
+    attend(scale, head_dim, docs, group_ref, w_ref, wout_ref, gains_ref, own_ref, across_ref,
+           vector_ref, *outs)
+
+
+def attend_first_placed(scale, head_dim, experts, group_ref, place_ref, arrived_ref, w_ref, wout_ref,
+                        own_ref, across_ref, vector_ref, gains_ref, *outs):
+    cols = wout_ref.shape[0]
+    gain_rows(experts, cols, w_ref, gains_ref)
+    docs = docs_of_pair(3 * cols + experts + 2, vector_ref.shape[1], group_ref, place_ref, arrived_ref)
+    attend(scale, head_dim, docs, group_ref, w_ref, wout_ref, gains_ref, own_ref, across_ref,
+           vector_ref, *outs)
 
 
 def route_tokens(x_ref, keep_ref, core_ref, came_ref, gains_ref, w_ref, chosen_ref, send_ref,
@@ -367,11 +436,13 @@
 
 
 def backward_own(scale, head_dim, *refs):
-    gw_ref, gout_ref, keep_ref, gain_ref, offsets_ref = refs[10:]
+    gw_ref, gout_ref, keep_ref, send_ref, gain_ref, offsets_ref = refs[10:]
+    toks = keep_ref.shape[0]
     weights, outs, grad_normed, gain, offsets = attend_backward(scale, head_dim, *refs[:10])
     gw_ref[...] = weights
     gout_ref[...] = outs
-    keep_ref[...] = grad_normed
+    keep_ref[...] = grad_normed[:toks]
+    send_ref[...] = grad_normed[toks:].astype(BF16)
     gain_ref[...] = gain
     for h, value in enumerate(offsets):
         offsets_ref[h : h + 1] = value
@@ -379,13 +450,14 @@
 
 def backward_pair(scale, head_dim, buckets, table_cols, *refs):
     gw_ref, gout_ref, gain_ref, offsets_ref, gain_two_ref, router_ref = refs[10:16]
-    send_ref, full_ref, out_ref = refs[16:]
+    keep_ref, send_ref, full_ref, out_ref = refs[16:]
     weights, outs, grad_normed, gain, offsets = attend_backward(scale, head_dim, *refs[:10])
     own_heads = offsets_ref.shape[0]
     width, experts = router_ref.shape
     length = offsets_ref.shape[1]
     toks = length // 2
-    send_ref[...] = grad_normed.astype(BF16)
+    keep_ref[...] = grad_normed[:toks]
+    send_ref[...] = grad_normed[toks:].astype(BF16)
     rows = own_heads * buckets // table_cols
     spot = iota((1, length), 1)
     offset = jnp.where(spot >= toks, spot - length, spot)
@@ -406,16 +478,13 @@
     weights = weights + gw_ref[...]
     pieces = [weights, router_ref[...].astype(F32), narrow, table]
     spare = full_ref.shape[-1] - sum(p.shape[1] for p in pieces)
-    if len(full_ref.shape) == 2:
-        full_ref[...] = jnp.concatenate(
-            pieces + [jnp.zeros((width, spare), F32)], axis=1
-        ).astype(BF16)
-        out_ref[...] = (outs + gout_ref[...]).astype(BF16)
+    full_ref[...] = jnp.concatenate(pieces + [jnp.zeros((width, spare), F32)], axis=1).astype(BF16)
+    out_ref[...] = (outs + gout_ref[...]).astype(BF16)
 
 
 def backward_pair_message(scale, head_dim, buckets, table_cols, *refs):
-    *rest, send_ref, message_ref, full_ref, out_ref = refs
-    backward_pair(scale, head_dim, buckets, table_cols, *rest, send_ref, full_ref, out_ref)
+    *rest, message_ref, full_ref, out_ref = refs
+    backward_pair(scale, head_dim, buckets, table_cols, *rest, full_ref, out_ref)
     dests, total, wide = message_ref.shape
     rows = total // 5
     used = full_ref.shape[1]
@@ -447,9 +516,9 @@
 
 
 def finish_weights(own_heads, buckets, table_cols, group_ref, p0_ref, p1_ref, p2_ref, p3_ref,
-                   q_ref, k_ref, v_ref, router_ref, gains_ref, table_ref):
+                   q_ref, k_ref, v_ref, router_ref, one_ref, two_ref, table_ref):
     rows, width = q_ref.shape
-    experts = router_ref.shape[1]
+    experts = router_ref.shape[0]
     cols = width // 4
     pieces = [ref[...].astype(F32) for ref in (p0_ref, p1_ref, p2_ref, p3_ref)]
     ordered = [choose(group_ref[0] ^ j, pieces) for j in range(4)]
@@ -457,11 +526,16 @@
         ref[...] = jnp.concatenate([p[:, n * cols : (n + 1) * cols] for p in ordered], axis=1)
     at = 3 * cols
     small = sum(p[:, at : at + experts + 2] for p in pieces)
-    router_ref[...] = small[:, :experts]
+    square = -(-max(rows, experts) // 128) * 128
+    padded = small[:, :experts]
+    if square > experts:
+        padded = jnp.concatenate([padded, jnp.zeros((rows, square - experts), F32)], axis=1)
+    padded = jnp.concatenate([padded, jnp.zeros((square - rows, square), F32)], axis=0)
+    router_ref[...] = jnp.transpose(padded)[:experts, :rows]
     eye = iota((rows, rows), 0) == iota((rows, rows), 1)
-    for i in range(2):
+    for i, ref in enumerate((one_ref, two_ref)):
         column = small[:, experts + i : experts + i + 1]
-        gains_ref[i : i + 1] = jnp.sum(jnp.where(eye, column, 0.0), axis=0, keepdims=True)
+        ref[...] = jnp.sum(jnp.where(eye, column, 0.0), axis=0, keepdims=True)
     at += experts + 2
     lines = []
     lane = iota((rows, 128), 1)
@@ -473,9 +547,7 @@
                 value = jnp.where(belongs & (lane < buckets), p[:, at + t : at + t + 1], 0.0)
                 line = line + jnp.sum(value, axis=0, keepdims=True)
             lines.append(line)
-    heads = len(lines)
-    padded = jnp.concatenate(lines + [jnp.zeros((128 - heads, 128), F32)], axis=0)
-    table_ref[...] = jnp.transpose(padded)[:buckets, :heads]
+    table_ref[...] = jnp.concatenate(lines, axis=0)[:, :buckets]
 
 
 def local(
@@ -517,7 +589,8 @@
     place_at = place.reshape(1).astype(jnp.int32)
     group_at = (2 * core + member).reshape(1).astype(jnp.int32)
     table_cols = max(1, own_heads * buckets // rows)
-    used = -(-(3 * cols + experts + 2 + table_cols) // 128) * 128
+    extra = max(table_cols, -(-length // rows))
+    used = -(-(3 * cols + experts + 2 + extra) // 128) * 128
     wide = max(used, width)
     aligned = rows % 8 == 0
 
@@ -537,37 +610,33 @@
 
     own_tokens = tokens.reshape(toks, width)
     pair_tokens = swap_pair(own_tokens)
-    pair_docs = swap_pair(segment_ids)
-
-    own_piece, *pieces = kernel_call(
-        pack_weights, [((rows, used), BF16)] * 4,
-        group_at, w_query, w_key, w_value, w_router, jnp.stack([gain_one, gain_two]), scalars=1,
+
+    own_piece, *pieces, out_rows = kernel_call(
+        pack_weights, [((rows, used), BF16)] * 4 + [((rows, width), BF16)],
+        group_at, w_query, w_key, w_value, w_router.T, gain_one.reshape(1, rows),
+        gain_two.reshape(1, rows), w_out, segment_ids, scalars=1, late=range(1, 9),
+        limit=60 * 1024 * 1024,
     )
     pieces = across_group(pieces)
-    pair_tokens, pair_docs, own_piece, *pieces = lax.optimization_barrier(
-        (pair_tokens, pair_docs, own_piece, *pieces)
-    )
+    pair_tokens, own_piece, *pieces = lax.optimization_barrier((pair_tokens, own_piece, *pieces))
     (message,) = kernel_call(
         spread_weights, [((half, 5 * rows, wide), BF16)],
-        group_at, own_piece, *pieces, w_out, scalars=1,
+        group_at, own_piece, *pieces, out_rows, scalars=1,
     )
     arrived = exchange_half(message)
 
     own_across = swap_core(own_tokens)
     pair_across = swap_core(pair_tokens)
-    docs_two = jnp.concatenate([segment_ids, pair_docs], axis=0)
-    docs = jnp.where(first_core, docs_two, jnp.roll(docs_two, toks, axis=1))
-    own_bias, pair_bias, spread, later, chosen, send = kernel_call(
+    vectors, spread, later, chosen, send = kernel_call(
         functools.partial(prepare, capacity, pad_two),
         [
-            ((own_heads, length, length), F32),
-            ((own_heads, length, length), F32),
+            ((own_heads, length), F32),
             ((toks, experts * pad_two), BF16),
             ((toks, experts * pad_two), BF16),
             ((toks, experts), F32),
             ((experts * pad_two, 2 * toks), BF16),
         ],
-        group_at, bias_table, docs, routes.reshape(toks, 1), scalars=2,
+        group_at, bias_table, routes.reshape(toks, 1), scalars=2,
     )
     g_low = out_grad.reshape(toks, width)
 
@@ -583,7 +652,7 @@
         weights, out_w, gains, *pair_kept = kernel_call(
             functools.partial(attend_first, scale, head_dim, experts),
             placed + [((8, width), F32)] + row_outs,
-            arrived, pair_tokens, pair_across, pair_bias,
+            group_at, place_at, arrived, pair_tokens, pair_across, vectors, scalars=2,
         )
     else:
         weights = arrived[:, : 4 * rows, :used].reshape(half, 2, 2, rows, used)
@@ -592,14 +661,14 @@
         gains, *pair_kept = kernel_call(
             functools.partial(attend_first_placed, scale, head_dim, experts),
             [((8, width), F32)] + row_outs,
-            weights, out_w, pair_tokens, pair_across, pair_bias,
+            group_at, place_at, arrived, weights, out_w, pair_tokens, pair_across, vectors, scalars=2,
         )
     pair_qkv, pair_probs, pair_att, keep, away = pair_kept
     pair_sum = (keep + swap_core(away).astype(F32)).astype(BF16)
     pair_sum = swap_pair(pair_sum)
     own_qkv, own_probs, own_att, keep, away = kernel_call(
-        functools.partial(attend, scale, head_dim), row_outs,
-        weights, out_w, gains, own_tokens, own_across, own_bias,
+        functools.partial(attend_own, scale, head_dim), row_outs,
+        group_at, segment_ids, weights, out_w, gains, own_tokens, own_across, vectors, scalars=1,
     )
     router_w = weights[:, 3 * cols : 3 * cols + experts]
     middle, gate, outgoing = kernel_call(
@@ -657,31 +726,36 @@
     )
     pair_grad = swap_pair(grad_attn)
     shared = (gains, weights)
-    grad_w, grad_out, grad_normed, gain_part, offsets = kernel_call(
+    grad_w, grad_out, grad_normed, away, gain_part, offsets = kernel_call(
         functools.partial(backward_own, scale, head_dim),
         [
             ((width, 3 * cols), F32),
             ((cols, width), F32),
-            ((length, width), F32),
+            ((toks, width), F32),
+            ((toks, width), BF16),
             ((1, width), F32),
             ((own_heads, length), F32),
         ],
         grad_attn, swap_core(grad_attn), out_w, own_att, own_qkv, own_probs, *shared,
         own_tokens, own_across,
     )
+    grad_normed = grad_normed + swap_core(away).astype(F32)
     last = (
         pair_grad, swap_core(pair_grad), out_w, pair_att, pair_qkv, pair_probs, *shared,
         pair_tokens, pair_across, grad_w, grad_out, gain_part, offsets, grad_gain_two, grad_router,
     )
-    outs = [((length, width), BF16), ((width, used), BF16), ((cols, width), BF16)]
+    outs = [((toks, width), F32), ((toks, width), BF16)]
+    flat = [((width, used), BF16), ((cols, width), BF16)]
     options = (scale, head_dim, buckets, table_cols)
     if aligned:
-        away, message, _, _ = kernel_call(
+        keep, away, message, _, _ = kernel_call(
             functools.partial(backward_pair_message, *options),
-            [outs[0], ((half, 5 * rows, wide), BF16), *outs[1:]], *last,
+            [*outs, ((half, 5 * rows, wide), BF16), *flat], *last,
         )
     else:
-        away, full, grad_out = kernel_call(functools.partial(backward_pair, *options), outs, *last)
+        keep, away, full, grad_out = kernel_call(
+            functools.partial(backward_pair, *options), outs + flat, *last
+        )
         full = full.reshape(2, 2, half, rows, used).transpose(2, 0, 1, 3, 4)
         full = full.reshape(half, 4 * rows, used)
         grad_out = grad_out.reshape(half, rows, width)
@@ -692,40 +766,40 @@
             ],
             axis=1,
         )
-    came = swap_pair(away)
+    message, away, keep = lax.optimization_barrier((message, away, keep))
     arrived = exchange_half(message)
-    (final,) = kernel_call(finish_layer, [((toks, width), BF16)], back, later, middle, gate)
+    came = swap_pair((keep + swap_core(away).astype(F32)).astype(BF16)).astype(F32)
+    (final,) = kernel_call(finish_layer, [((toks, width), BF16)], back, later, middle, gate
+    )
 
     out_grad_w, own_piece, *pieces = kernel_call(
         sum_arrived, [((rows, width), F32), ((rows, used), F32)] + [((rows, used), BF16)] * 3,
         group_at, arrived, scalars=1,
     )
     pieces = across_group(pieces)
-    query_grad, key_grad, value_grad, router_grad, gain_grads, table_grad = kernel_call(
+    query_grad, key_grad, value_grad, router_grad, one_grad, two_grad, table_grad = kernel_call(
         functools.partial(finish_weights, own_heads, buckets, table_cols),
         [((rows, width), F32)] * 3
-        + [((rows, experts), F32), ((2, rows), F32), ((buckets, heads), F32)],
+        + [((experts, rows), F32), ((1, rows), F32), ((1, rows), F32), ((heads, buckets), F32)],
         group_at, own_piece, *pieces, scalars=1,
     )
 
-    grad_normed = grad_normed + came.astype(F32)
-    across = swap_core(grad_normed[toks:].astype(BF16)).astype(F32)
     x = own_tokens.astype(F32)
     inverse_one = rms_inverse(x)
     grad_input = grad_middle + norm_backward(
-        grad_normed[:toks] + across, x * inverse_one, inverse_one, gains[0:1]
+        grad_normed + came, x * inverse_one, inverse_one, gains[0:1]
     )
     return (
         final.reshape(tokens.shape),
         grad_input.astype(BF16).reshape(tokens.shape),
-        gain_grads[0],
+        one_grad.reshape(rows),
         query_grad,
         key_grad,
         value_grad,
         out_grad_w,
-        table_grad,
-        gain_grads[1],
-        router_grad,
+        table_grad.T,
+        two_grad.reshape(rows),
+        router_grad.T,
         grad_inner[None],
         grad_outer[None],
     )

time: 181 us -> 169 us (0.934)
  local copies, waits for them, and re-layouts: 13.3 us -> 7.15 us
  waiting for transfers between devices: 51 us -> 46 us
    ppermute x5 -> x4, waiting for transfers between devices: 34.4 us -> 21.4 us  [swap_pair(): return lax.ppermute(value, 'expert', [(i, i ^ other) for i in range(n)])]
    ppermute x6, waiting for transfers between devices: 0.68 us -> 6.26 us  [across_group(): lax.ppermute(piece, ('dp', 'expert'), [(c * sources + e, (c ^ d >> 1) * s...]
    unnamed x82 -> x75, local copies, waits for them, and re-layouts: 11.7 us -> 6.15 us
    all_to_all x2, waiting for transfers between devices: 12.8 us -> 15.2 us  [exchange_half(): lax.all_to_all(value, 'expert', split_axis=0, concat_axis=0, tiled=True,...]
    pallas_call x13, Pallas kernels: 17 us -> 18.8 us  [kernel_call(): pl.pallas_call(run, out_shape=[jax.ShapeDtypeStruct(shape, dtype) for sha...]
    ppermute x5 -> x4, starting transfers between devices: 11.5 us -> 10.4 us  [swap_pair(): return lax.ppermute(value, 'expert', [(i, i ^ other) for i in range(n)])]
    ppermute x9 -> x10, starting transfers between devices: 10.6 us -> 10.1 us  [swap_core(): return lax.ppermute(value, 'dp', [(0, 1), (1, 0)])]
  transfers between devices with their start and end apart: 22 -> 22, of which waited for: 8 -> 9; matrix products, arithmetic and copies ran while one was open for 7% -> 7% of each run, Pallas kernels for 5% -> 6%
where the time goes in v2:
time: 169 us; the launch traced here: 168 us
  waiting for transfers between devices  46 us (27%)
  blocking collectives  42.2 us (25%)
  starting transfers between devices  36.6 us (22%)
  Pallas kernels  24.3 us (14%)
  matrix products  8.56 us (5%)
  local copies, waits for them, and re-layouts  7.15 us (4%)
  other arithmetic  2.33 us (1%)
    all_to_all x2, blocking collectives, exchange(): lax.all_to_all(value, 'expert', split_axis=0, concat_axis=0, tiled=True)  42.2 us
    ppermute x4, waiting for transfers between devices, swap_pair(): return lax.ppermute(value, 'expert', [(i, i ^ other) for i in range(n)])  21.4 us
    pallas_call x13, Pallas kernels, kernel_call(): pl.pallas_call(run, out_shape=[jax.ShapeDtypeStruct(shape, dtype) for sha...  18.8 us
    all_to_all x2, waiting for transfers between devices, exchange_half(): lax.all_to_all(value, 'expert', split_axis=0, concat_axis=0, tiled=True,...  15.2 us
    ppermute x4, starting transfers between devices, swap_pair(): return lax.ppermute(value, 'expert', [(i, i ^ other) for i in range(n)])  10.4 us
    ppermute x10, starting transfers between devices, swap_core(): return lax.ppermute(value, 'dp', [(0, 1), (1, 0)])  10.1 us
    all_to_all x2, starting transfers between devices, exchange_half(): lax.all_to_all(value, 'expert', split_axis=0, concat_axis=0, tiled=True,...  9.25 us
    dot_general x2, matrix products, dot(): lax.dot_general(left, right, (dims, ((), ())), preferred_element_type=F32)  8.56 us
  transfers between devices with their start and end apart: 22, of which 9 were waited for; matrix products, arithmetic and copies ran while one was open for 7% of the time, Pallas kernels for 6%

profile of v2, /device:TPU:3, one launch (start us, length us, event | category | flops | bytes accessed | tf_op | source)
XLA Modules:
  0.0 168.0 jit_solution(16085508051627120389)
XLA Ops:
  0.6 3.4 %collective-permute-start = (bf16[128,768]{1,0:T(8,128)(2,1)}, bf16[128,768]{1,0:T(8,128)(2,1)S(1)}, u32[]{:S(2)}, u32[]{:S(2)}) collective-permute-start(bf16[128,768]{1,0:T(8,128)(2,1)} %bitcast.32), channel_id=1, source_target_pairs={{0,12},{1,13},{2,14},{3,15},{4,8},{5,9},{6,10},{7,11},{8,4},{9,5},... | collective-permute-start | bytes 589832 | tf_op jit(solution)/shard_map/ppermute | solution.py:39
  4.0 2.0 %shard_map.229 = (bf16[24,640]{1,0:T(8,128)(2,1)}, bf16[24,640]{1,0:T(8,128)(2,1)}, bf16[24,640]{1,0:T(8,128)(2,1)}, bf16[24,640]{1,0:T(8,128)(2,1)}, bf16[24,768]{1,0:T(8,128)(2,1)}) custom-call(s32[1]{0:T(128)} %bitcast.2.refs_0_, bf16[24,768]{1,0:T(8,128)(2,1)} %refs_1_.3, bf16[24,768]{1,0:T(8,128)(2,1)} %refs_2_.1, bf16[24,768]{1,0:T(8,128)(2,1)} %refs_3_.1, ...), custom_call_target="tpu_custom_call" | custom-call | flops 1000000 | bytes 1000000 | tf_op jit(solution)/shard_map/pallas_call | solution.py:104
  6.1 1.0 collective-permute-start.2
  7.2 2.5 %collective-permute-start.3 = (bf16[24,640]{1,0:T(8,128)(2,1)}, bf16[24,640]{1,0:T(8,128)(2,1)S(1)}, u32[]{:S(2)}, u32[]{:S(2)}) collective-permute-start(bf16[24,640]{1,0:T(8,128)(2,1)} %get-tuple-element.84), channel_id=1, source_target_pairs={{0,24},{1,25},{2,26},{3,27},{4,28},{5,29},{6,30},{7,31},{8,16},{9,... | collective-permute-start | bytes 92168 | tf_op jit(solution)/shard_map/ppermute | solution.py:599
  9.6 4.2 %collective-permute-done.1.refs_2_ = bf16[24,640]{1,0:T(8,128)(2,1)S(1)} collective-permute-done((bf16[24,640]{1,0:T(8,128)(2,1)}, bf16[24,640]{1,0:T(8,128)(2,1)S(1)}, u32[]{:S(2)}, u32[]{:S(2)}) %collective-permute-start.1) | collective-permute-done | bytes 30752 | tf_op jit(solution)/shard_map/ppermute | solution.py:599
  13.8 1.6 collective-permute-done.3.refs_4_
  15.4 0.8 copy-done.23
  16.2 0.8 copy-done.24
  16.9 1.2 shard_map.230
  18.2 3.9 %all-to-all-start = ((bf16[8,120,768]{2,1,0:T(8,128)(2,1)}), bf16[8,120,768]{2,1,0:T(8,128)(2,1)S(1)}, u32[]{:S(2)}, u32[]{:S(2)}) async-start(bf16[8,120,768]{2,1,0:T(8,128)(2,1)} %shard_map.230), calls=%async_computation | async-start | bytes 2949120 | tf_op jit(solution)/shard_map/all_to_all | solution.py:49
  22.0 0.9 collective-permute-start.4
  23.2 1.3 shard_map.231
  25.2 0.6 copy-done.19
  25.8 15.2 %all-to-all-done.refs_2_ = bf16[8,120,768]{2,1,0:T(8,128)(2,1)S(1)} async-done(((bf16[8,120,768]{2,1,0:T(8,128)(2,1)}), bf16[8,120,768]{2,1,0:T(8,128)(2,1)S(1)}, u32[]{:S(2)}, u32[]{:S(2)}) %all-to-all-start) | async-done | bytes 1474592 | tf_op jit(solution)/shard_map/all_to_all | solution.py:49
  41.1 1.7 %shard_map.232 = (bf16[768,640]{1,0:T(8,128)(2,1)S(1)}, bf16[192,768]{1,0:T(8,128)(2,1)S(1)}, f32[8,768]{1,0:T(8,128)S(1)}, bf16[256,576]{1,0:T(8,128)(2,1)S(1)}...) custom-call(s32[1]{0:T(128)} %bitcast.2.refs_0_, ...), custom_call_target="tpu_custom_call" | custom-call | flops 1000000 | bytes 1000000 | tf_op jit(solution)/shard_map/pallas_call | solution.py:104
  42.8 1.5 collective-permute-start.7
  44.3 1.5 shard_map.233
  45.9 2.1 %collective-permute-start.8 = (bf16[128,768]{1,0:T(8,128)(2,1)S(1)}, bf16[128,768]{1,0:T(8,128)(2,1)S(1)}, u32[]{:S(2)}, u32[]{:S(2)}) collective-permute-start(bf16[128,768]{1,0:T(8,128)(2,1)S(1)} %add_convert_fusion.1), channel_id=1, source_target_pairs={{0,12},{1,13},{2,14},{3,15},{4,8},{5,9},{6,10},{7,11},{8,4},{9,5},... | collective-permute-start | bytes 589832 | tf_op jit(solution)/shard_map/ppermute | solution.py:39
  48.1 5.7 %collective-permute-done.8.refs_3_ = bf16[128,768]{1,0:T(8,128)(2,1)S(1)} collective-permute-done((bf16[128,768]{1,0:T(8,128)(2,1)S(1)}, bf16[128,768]{1,0:T(8,128)(2,1)S(1)}, u32[]{:S(2)}, u32[]{:S(2)}) %collective-permute-start.8) | collective-permute-done | bytes 196640 | tf_op jit(solution)/shard_map/ppermute | solution.py:39
  53.8 0.8 shard_map.234
  54.6 23.0 %all_to_all.20 = bf16[16,24,768]{2,1,0:T(8,128)(2,1)S(1)} all-to-all(bf16[16,24,768]{2,1,0:T(8,128)(2,1)S(1)} %bitcast.46), channel_id=1, replica_groups=mesh['dp'=2,'expert'=16] {'expert'}, dimensions={0} | all-to-all | bytes 1179648 | tf_op jit(solution)/shard_map/all_to_all | solution.py:43
  77.7 1.9 %collective-permute-start.9 = (bf16[384,768]{1,0:T(8,128)(2,1)S(1)}, bf16[384,768]{1,0:T(8,128)(2,1)S(1)}, u32[]{:S(2)}, u32[]{:S(2)}) collective-permute-start(bf16[384,768]{1,0:T(8,128)(2,1)S(1)} %bitcast.39), channel_id=1, source_target_pairs={{0,16},{16,0},{1,17},{17,1},{2,18},{18,2},{3,19},{19,3},{4,20},{20... | collective-permute-start | bytes 1769480 | tf_op jit(solution)/shard_map/ppermute | solution.py:33
  79.6 1.6 collective-permute-done.9.other_ref
  81.2 5.5 %shard_map.235 = (bf16[320,768]{1,0:T(8,128)(2,1)S(1)}, bf16[320,768]{1,0:T(8,128)(2,1)S(1)}, bf16[160,768]{1,0:T(8,128)(2,1)S(1)}, f32[160,16]{1,0:T(8,128)S(1)...) custom-call(s32[1]{0:T(128)} %bitcast.refs_1_.place_ref.refs_0_, ...), custom_call_target="tpu_custom_call" | custom-call | tf_op jit(solution)/shard_map/pallas_call | solution.py:696
  87.2 1.5 collective-permute-done.10.refs_2_
  88.7 0.9 shard_map.236
  89.7 19.1 %all_to_all.21 = bf16[16,24,768]{2,1,0:T(8,128)(2,1)S(1)} all-to-all(bf16[16,24,768]{2,1,0:T(8,128)(2,1)S(1)} %bitcast.45), channel_id=1, replica_groups=mesh['dp'=2,'expert'=16] {'expert'}, dimensions={0} | all-to-all | bytes 1179648 | tf_op jit(solution)/shard_map/all_to_all | solution.py:43
  109.2 0.7 copy-done.15
  110.0 1.8 %collective-permute-start.13 = (bf16[128,768]{1,0:T(8,128)(2,1)S(1)}, bf16[128,768]{1,0:T(8,128)(2,1)S(1)}, u32[]{:S(2)}, u32[]{:S(2)}) collective-permute-start(bf16[128,768]{1,0:T(8,128)(2,1)S(1)} %get-tuple-element.114.refs_0_), channel_id=1, source_target_pairs={{0,12},{1,13},{2,14},{3,15},{4,8},{5,9},{6,10},{7,11},{8,4},{9,5},... | collective-permute-start | bytes 589832 | tf_op jit(solution)/shard_map/ppermute | solution.py:39
  111.8 1.5 collective-permute-start.11
  113.3 3.1 %collective-permute-done.13.refs_0_ = bf16[128,768]{1,0:T(8,128)(2,1)S(1)} collective-permute-done((bf16[128,768]{1,0:T(8,128)(2,1)S(1)}, bf16[128,768]{1,0:T(8,128)(2,1)S(1)}, u32[]{:S(2)}, u32[]{:S(2)}) %collective-permute-start.13) | collective-permute-done | bytes 196640 | tf_op jit(solution)/shard_map/ppermute | solution.py:39
  116.4 2.9 %collective-permute-start.14 = (bf16[128,768]{1,0:T(8,128)(2,1)S(1)}, bf16[128,768]{1,0:T(8,128)(2,1)S(1)}, u32[]{:S(2)}, u32[]{:S(2)}) collective-permute-start(bf16[128,768]{1,0:T(8,128)(2,1)S(1)} %collective-permute-done.13.refs_0_), channel_id=1, source_target_pairs={{0,16},{16,0},{1,17},{17,1},{2,18},{18,2},{3,19},{19,3},{4,20},{20... | collective-permute-start | bytes 589832 | tf_op jit(solution)/shard_map/ppermute | solution.py:33
  119.3 2.7 %shard_map.239 = (f32[768,576]{1,0:T(8,128)S(1)}, f32[192,768]{1,0:T(8,128)S(1)}, f32[128,768]{1,0:T(8,128)S(1)}, bf16[128,768]{1,0:T(8,128)(2,1)S(1)}, f32[1,768]{1,0:T(1,128)S(1)}, /*index=5*/f32[3,256]{1,0:T(4,128)S(1)}) custom-call(bf16[128,768]{1,0:T(8,128)(2,1)S(1)} %get-tuple-element.114.refs_0_, ...), custom_call_target="tpu_custom_call" | custom-call | flops 1000000 | bytes 1000000 | tf_op jit(solution)/shard_map/pallas_call | solution.py:104
  122.1 3.8 %shard_map.240 = (f32[128,768]{1,0:T(8,128)S(1)}, bf16[128,768]{1,0:T(8,128)(2,1)S(1)}, bf16[8,120,768]{2,1,0:T(8,128)(2,1)S(1)}, bf16[768,640]{1,0:T(8,128)(2,1)}, bf16[192,768]{1,0:T(8,128)(2,1)}) custom-call(bf16[128,768]{1,0:T(8,128)(2,1)S(1)} %collective-permute-done.13.refs_0_, bf16[128,768]{1,0:T(8,128)(2,1)S(1)} %collective-permute-done.14.refs_1_, ...), custom_call_target="tpu_custom_call" | custom-call | flops 1000000 | bytes 1000000 | tf_op jit(solution)/shard_map/pallas_call | solution.py:104
  125.9 0.7 copy-done.13
  126.7 0.7 copy-done.32
  127.9 5.4 %all-to-all-start.3 = ((bf16[8,120,768]{2,1,0:T(8,128)(2,1)}), bf16[8,120,768]{2,1,0:T(8,128)(2,1)S(1)}, u32[]{:S(2)}, u32[]{:S(2)}) async-start(bf16[8,120,768]{2,1,0:T(8,128)(2,1)} %copy-done.3), calls=%async_computation.3 | async-start | bytes 2949120 | tf_op jit(solution)/shard_map/all_to_all | solution.py:49
  133.4 0.8 slice_reduce_fusion
  134.8 4.9 %convolution_bitcast_fusion.1 = f32[1,768,1536]{2,1,0:T(8,128)} fusion(bf16[320,768]{1,0:T(8,128)(2,1)S(1)} %get-tuple-element.104, bf16[320,1536]{1,0:T(8,128)(2,1)} %copy-done.4), kind=kOutput, calls=%fused_computation.1 | convolution fusion | flops 754974720 | bytes 6193152 | tf_op jit(solution)/shard_map/dot_general | solution.py:19
  139.8 3.1 %collective-permute-start.16 = (bf16[128,768]{1,0:T(8,128)(2,1)S(1)}, bf16[128,768]{1,0:T(8,128)(2,1)S(1)}, u32[]{:S(2)}, u32[]{:S(2)}) collective-permute-start(bf16[128,768]{1,0:T(8,128)(2,1)S(1)} %add_convert_fusion), channel_id=1, source_target_pairs={{0,12},{1,13},{2,14},{3,15},{4,8},{5,9},{6,10},{7,11},{8,4},{9,5},... | collective-permute-start | bytes 589832 | tf_op jit(solution)/shard_map/ppermute | solution.py:39
  142.9 3.6 %convolution_bitcast_fusion = f32[1,1536,768]{2,1,0:T(8,128)} fusion(bf16[320,1536]{1,0:T(8,128)(2,1)S(1)} %copy-done.27, bf16[320,768]{1,0:T(8,128)(2,1)S(1)} %copy-done.29), kind=kOutput, calls=%fused_computation | convolution fusion | flops 754974720 | bytes 6193152 | tf_op jit(solution)/shard_map/dot_general | solution.py:19
  146.6 0.9 shard_map.237
  147.5 12.6 %collective-permute-done.16 = bf16[128,768]{1,0:T(8,128)(2,1)S(1)} collective-permute-done((bf16[128,768]{1,0:T(8,128)(2,1)S(1)}, bf16[128,768]{1,0:T(8,128)(2,1)S(1)}, u32[]{:S(2)}, u32[]{:S(2)}) %collective-permute-start.16) | collective-permute-done | bytes 196640 | tf_op jit(solution)/shard_map/ppermute | solution.py:39
  160.8 0.7 shard_map.241
  161.5 0.8 collective-permute-start.18
  162.2 2.5 %collective-permute-start.19 = (bf16[24,640]{1,0:T(8,128)(2,1)S(1)}, bf16[24,640]{1,0:T(8,128)(2,1)S(1)}, u32[]{:S(2)}, u32[]{:S(2)}) collective-permute-start(bf16[24,640]{1,0:T(8,128)(2,1)S(1)} %get-tuple-element.138), channel_id=1, source_target_pairs={{0,24},{1,25},{2,26},{3,27},{4,28},{5,29},{6,30},{7,31},{8,16},{9,... | collective-permute-start | bytes 92168 | tf_op jit(solution)/shard_map/ppermute | solution.py:599
  164.8 1.9 %fusion.8 = bf16[1,128,768]{2,1,0:T(8,128)(2,1)} fusion(f32[128,768]{1,0:T(8,128)S(1)} %copy-done.16, f32[128]{0:T(128)S(1)} %broadcast_multiply_fusion, f32[128]{0:T(128)S(1)} %add_rsqrt_fusion, f32[768]{0:T(1024)S(1)} %slice_reduce_fusion, bf16[128,768]{1,0:T(8,128)(2,1)} %copy-done.34, f32[128,768]{1,0:T(8,128)S(1)} %get-tuple-element.118, ...), kind=kLoop, calls=%fused_computation.15 | loop fusion | flops 1179648 | bytes 1576960 | tf_op jit(solution)/shard_map/reshape | solution.py:794
  167.2 0.9 shard_map.242
  (100 shorter events, 4.8 us)
Async XLA Ops:
  0.6 14.8 %collective-permute-start = (bf16[128,768]{1,0:T(8,128)(2,1)}, bf16[128,768]{1,0:T(8,128)(2,1)S(1)}, u32[]{:S(2)}, u32[]{:S(2)}) collective-permute-start(bf16[128,768]{1,0:T(8,128)(2,1)} %bitcast.32), channel_id=1, source_target_pairs={{0,12},{1,13},{2,14},{3,15},{4,8},{5,9},{6,10},{7,11},{8,4},{9,5},... | collective-permute-start | bytes 589832 | tf_op jit(solution)/shard_map/ppermute | solution.py:39
  4.0 19.0 %copy-start.35 = (f32[32,12]{0,1:T(8,128)S(1)}, f32[32,12]{0,1:T(8,128)}, u32[]{:S(2)}) copy-start(f32[32,12]{0,1:T(8,128)} %param.20) | copy-start | bytes 4612
  4.0 19.1 %copy-start.36 = (s32[1,128,1]{1,2,0:T(1,128)S(1)}, s32[1,128,1]{1,2,0:T(1,128)}, u32[]{:S(2)}) copy-start(s32[1,128,1]{1,2,0:T(1,128)} %param.26) | copy-start | bytes 1540
  4.0 18.9 %copy-start = (bf16[1,128,768]{2,1,0:T(8,128)(2,1)S(1)}, bf16[1,128,768]{2,1,0:T(8,128)(2,1)}, u32[]{:S(2)}) copy-start(bf16[1,128,768]{2,1,0:T(8,128)(2,1)} %param.14) | copy-start | bytes 589828
  6.1 7.7 %collective-permute-start.1 = (bf16[24,640]{1,0:T(8,128)(2,1)}, bf16[24,640]{1,0:T(8,128)(2,1)S(1)}, u32[]{:S(2)}, u32[]{:S(2)}) collective-permute-start(bf16[24,640]{1,0:T(8,128)(2,1)} %get-tuple-element.82), channel_id=1, source_target_pairs={{0,8},{1,9},{2,10},{3,11},{4,12},{5,13},{6,14},{7,15},{8,0},{9,1},... | collective-permute-start | bytes 92168 | tf_op jit(solution)/shard_map/ppermute | solution.py:599
  6.1 7.6 %collective-permute-start.2 = (bf16[24,640]{1,0:T(8,128)(2,1)}, bf16[24,640]{1,0:T(8,128)(2,1)S(1)}, u32[]{:S(2)}, u32[]{:S(2)}) collective-permute-start(bf16[24,640]{1,0:T(8,128)(2,1)} %get-tuple-element.83), channel_id=1, source_target_pairs={{0,16},{1,17},{2,18},{3,19},{4,20},{5,21},{6,22},{7,23},{8,24},{9,... | collective-permute-start | bytes 92168 | tf_op jit(solution)/shard_map/ppermute | solution.py:599
  7.2 8.2 %collective-permute-start.3 = (bf16[24,640]{1,0:T(8,128)(2,1)}, bf16[24,640]{1,0:T(8,128)(2,1)S(1)}, u32[]{:S(2)}, u32[]{:S(2)}) collective-permute-start(bf16[24,640]{1,0:T(8,128)(2,1)} %get-tuple-element.84), channel_id=1, source_target_pairs={{0,24},{1,25},{2,26},{3,27},{4,28},{5,29},{6,30},{7,31},{8,16},{9,... | collective-permute-start | bytes 92168 | tf_op jit(solution)/shard_map/ppermute | solution.py:599
  15.4 25.6 %copy-start.5 = (bf16[128,768]{1,0:T(8,128)(2,1)}, bf16[128,768]{1,0:T(8,128)(2,1)S(1)}, u32[]{:S(2)}) copy-start(bf16[128,768]{1,0:T(8,128)(2,1)S(1)} %collective-permute-done.refs_3_.refs_8_) | copy-start | bytes 589828
  18.1 26.1 %copy-start.25 = (s32[1,256]{1,0:T(1,128)S(1)}, s32[1,256]{1,0:T(1,128)}, u32[]{:S(2)}) copy-start(s32[1,256]{1,0:T(1,128)} %refs_1_.4) | copy-start | bytes 3076
  18.2 22.9 %all-to-all-start = ((bf16[8,120,768]{2,1,0:T(8,128)(2,1)}), bf16[8,120,768]{2,1,0:T(8,128)(2,1)S(1)}, u32[]{:S(2)}, u32[]{:S(2)}) async-start(bf16[8,120,768]{2,1,0:T(8,128)(2,1)} %shard_map.230), calls=%async_computation | async-start | bytes 2949120 | tf_op jit(solution)/shard_map/all_to_all | solution.py:49
  22.0 3.8 %collective-permute-start.4 = (bf16[128,768]{1,0:T(8,128)(2,1)S(1)}, bf16[128,768]{1,0:T(8,128)(2,1)S(1)}, u32[]{:S(2)}, u32[]{:S(2)}) collective-permute-start(bf16[128,768]{1,0:T(8,128)(2,1)S(1)} %collective-permute-done.refs_3_.refs_8_), channel_id=1, source_target_pairs={{0,16},{16,0},{1,17},{17,1},{2,18},{18,2},{3,19},{19,3},{4,20},{20... | collective-permute-start | bytes 589832 | tf_op jit(solution)/shard_map/ppermute | solution.py:33
  22.9 21.3 %collective-permute-start.5 = (bf16[128,768]{1,0:T(8,128)(2,1)S(1)}, bf16[128,768]{1,0:T(8,128)(2,1)S(1)}, u32[]{:S(2)}, u32[]{:S(2)}) collective-permute-start(bf16[128,768]{1,0:T(8,128)(2,1)S(1)} %bitcast.33), channel_id=1, source_target_pairs={{0,16},{16,0},{1,17},{17,1},{2,18},{18,2},{3,19},{19,3},{4,20},{20... | collective-permute-start | bytes 589832 | tf_op jit(solution)/shard_map/ppermute | solution.py:33
  25.8 22.3 %copy-start.7 = (bf16[128,768]{1,0:T(8,128)(2,1)}, bf16[128,768]{1,0:T(8,128)(2,1)S(1)}, u32[]{:S(2)}) copy-start(bf16[128,768]{1,0:T(8,128)(2,1)S(1)} %collective-permute-done.4.refs_4_.refs_9_) | copy-start | bytes 589828
  41.0 12.8 %copy-start.9 = (bf16[1,128,768]{2,1,0:T(8,128)(2,1)S(1)}, bf16[1,128,768]{2,1,0:T(8,128)(2,1)}, u32[]{:S(2)}) copy-start(bf16[1,128,768]{2,1,0:T(8,128)(2,1)} %param.27) | copy-start | bytes 589828
  42.7 79.4 %copy-start.12 = (f32[8,768]{1,0:T(8,128)}, f32[8,768]{1,0:T(8,128)S(1)}, u32[]{:S(2)}) copy-start(f32[8,768]{1,0:T(8,128)S(1)} %get-tuple-element.94.refs_4_.refs_3_.refs_6_) | copy-start | bytes 73732
  42.8 3.1 %collective-permute-start.7 = (bf16[128,768]{1,0:T(8,128)(2,1)S(1)}, bf16[128,768]{1,0:T(8,128)(2,1)S(1)}, u32[]{:S(2)}, u32[]{:S(2)}) collective-permute-start(bf16[128,768]{1,0:T(8,128)(2,1)S(1)} %get-tuple-element.98), channel_id=1, source_target_pairs={{0,16},{16,0},{1,17},{17,1},{2,18},{18,2},{3,19},{19,3},{4,20},{20... | collective-permute-start | bytes 589832 | tf_op jit(solution)/shard_map/ppermute | solution.py:33
  44.3 33.4 %copy-start.10 = (bf16[128,768]{1,0:T(8,128)(2,1)}, bf16[128,768]{1,0:T(8,128)(2,1)S(1)}, u32[]{:S(2)}) copy-start(bf16[128,768]{1,0:T(8,128)(2,1)S(1)} %collective-permute-done.5.refs_6_.refs_9_) | copy-start | bytes 589828
  44.3 36.9 %copy-start.2 = (bf16[1,1536,768]{2,1,0:T(8,128)(2,1)S(1)}, bf16[1,1536,768]{2,1,0:T(8,128)(2,1)}, u32[]{:S(2)}) copy-start(bf16[1,1536,768]{2,1,0:T(8,128)(2,1)} %param.24) | copy-start | bytes 7077892
  45.8 35.4 %copy-start.1 = (bf16[1,768,1536]{2,1,0:T(8,128)(2,1)S(1)}, bf16[1,768,1536]{2,1,0:T(8,128)(2,1)}, u32[]{:S(2)}) copy-start(bf16[1,768,1536]{2,1,0:T(8,128)(2,1)} %param.23) | copy-start | bytes 7077892
  45.8 2.3 %collective-permute-start.6 = (bf16[128,768]{1,0:T(8,128)(2,1)S(1)}, bf16[128,768]{1,0:T(8,128)(2,1)S(1)}, u32[]{:S(2)}, u32[]{:S(2)}) collective-permute-start(bf16[128,768]{1,0:T(8,128)(2,1)S(1)} %get-tuple-element.96), channel_id=1, source_target_pairs={{0,16},{16,0},{1,17},{17,1},{2,18},{18,2},{3,19},{19,3},{4,20},{20... | collective-permute-start | bytes 589832 | tf_op jit(solution)/shard_map/ppermute | solution.py:33
  45.9 7.9 %collective-permute-start.8 = (bf16[128,768]{1,0:T(8,128)(2,1)S(1)}, bf16[128,768]{1,0:T(8,128)(2,1)S(1)}, u32[]{:S(2)}, u32[]{:S(2)}) collective-permute-start(bf16[128,768]{1,0:T(8,128)(2,1)S(1)} %add_convert_fusion.1), channel_id=1, source_target_pairs={{0,12},{1,13},{2,14},{3,15},{4,8},{5,9},{6,10},{7,11},{8,4},{9,5},... | collective-permute-start | bytes 589832 | tf_op jit(solution)/shard_map/ppermute | solution.py:39
  54.6 26.6 %copy-start.21 = (f32[128,1]{1,0:T(8,128)}, f32[128,1]{1,0:T(8,128)S(1)}, u32[]{:S(2)}) copy-start(f32[128,1]{1,0:T(8,128)S(1)} %get-tuple-element.111.refs_3_) | copy-start | bytes 1540
  77.7 3.5 %collective-permute-start.9 = (bf16[384,768]{1,0:T(8,128)(2,1)S(1)}, bf16[384,768]{1,0:T(8,128)(2,1)S(1)}, u32[]{:S(2)}, u32[]{:S(2)}) collective-permute-start(bf16[384,768]{1,0:T(8,128)(2,1)S(1)} %bitcast.39), channel_id=1, source_target_pairs={{0,16},{16,0},{1,17},{17,1},{2,18},{18,2},{3,19},{19,3},{4,20},{20... | collective-permute-start | bytes 1769480 | tf_op jit(solution)/shard_map/ppermute | solution.py:33
  86.7 22.5 %copy-start.26 = (bf16[320,1536]{1,0:T(8,128)(2,1)}, bf16[320,1536]{1,0:T(8,128)(2,1)S(1)}, u32[]{:S(2)}) copy-start(bf16[320,1536]{1,0:T(8,128)(2,1)S(1)} %get-tuple-element.148) | copy-start | bytes 2949124
  86.7 22.5 %copy-start.28 = (bf16[320,768]{1,0:T(8,128)(2,1)}, bf16[320,768]{1,0:T(8,128)(2,1)S(1)}, u32[]{:S(2)}) copy-start(bf16[320,768]{1,0:T(8,128)(2,1)S(1)} %get-tuple-element.149) | copy-start | bytes 1474564
  86.7 35.3 %copy-start.4 = (bf16[320,1536]{1,0:T(8,128)(2,1)}, bf16[320,1536]{1,0:T(8,128)(2,1)S(1)}, u32[]{:S(2)}) copy-start(bf16[320,1536]{1,0:T(8,128)(2,1)S(1)} %get-tuple-element.147) | copy-start | bytes 2949124
  86.7 22.0 %copy-start.18 = (bf16[128,384]{1,0:T(8,128)(2,1)S(1)}, bf16[128,384]{1,0:T(8,128)(2,1)}, u32[]{:S(2)}) copy-start(bf16[128,384]{1,0:T(8,128)(2,1)} %copy-done.17) | copy-start | bytes 294916
  86.8 2.0 %collective-permute-start.10 = (bf16[2,160,768]{2,1,0:T(8,128)(2,1)S(1)}, bf16[2,160,768]{2,1,0:T(8,128)(2,1)S(1)}, u32[]{:S(2)}, u32[]{:S(2)}) collective-permute-start(bf16[2,160,768]{2,1,0:T(8,128)(2,1)S(1)} %get-tuple-element.103), channel_id=1, source_target_pairs={{0,16},{16,0},{1,17},{17,1},{2,18},{18,2},{3,19},{19,3},{4,20},{20... | collective-permute-start | bytes 1474568 | tf_op jit(solution)/shard_map/ppermute | solution.py:33
  88.7 30.6 %copy-start.11 = (bf16[128,768]{1,0:T(8,128)(2,1)S(1)}, bf16[128,768]{1,0:T(8,128)(2,1)}, u32[]{:S(2)}) copy-start(bf16[128,768]{1,0:T(8,128)(2,1)} %copy-done.10) | copy-start | bytes 589828
  108.8 13.3 %copy-start.6 = (bf16[128,768]{1,0:T(8,128)(2,1)S(1)}, bf16[128,768]{1,0:T(8,128)(2,1)}, u32[]{:S(2)}) copy-start(bf16[128,768]{1,0:T(8,128)(2,1)} %copy-done.5) | copy-start | bytes 589828
  108.8 13.3 %copy-start.8 = (bf16[128,768]{1,0:T(8,128)(2,1)S(1)}, bf16[128,768]{1,0:T(8,128)(2,1)}, u32[]{:S(2)}) copy-start(bf16[128,768]{1,0:T(8,128)(2,1)} %copy-done.7) | copy-start | bytes 589828
  110.0 6.4 %collective-permute-start.13 = (bf16[128,768]{1,0:T(8,128)(2,1)S(1)}, bf16[128,768]{1,0:T(8,128)(2,1)S(1)}, u32[]{:S(2)}, u32[]{:S(2)}) collective-permute-start(bf16[128,768]{1,0:T(8,128)(2,1)S(1)} %get-tuple-element.114.refs_0_), channel_id=1, source_target_pairs={{0,12},{1,13},{2,14},{3,15},{4,8},{5,9},{6,10},{7,11},{8,4},{9,5},... | collective-permute-start | bytes 589832 | tf_op jit(solution)/shard_map/ppermute | solution.py:39
  111.8 7.5 %collective-permute-start.11 = (bf16[128,768]{1,0:T(8,128)(2,1)S(1)}, bf16[128,768]{1,0:T(8,128)(2,1)S(1)}, u32[]{:S(2)}, u32[]{:S(2)}) collective-permute-start(bf16[128,768]{1,0:T(8,128)(2,1)S(1)} %get-tuple-element.114.refs_0_), channel_id=1, source_target_pairs={{0,16},{16,0},{1,17},{17,1},{2,18},{18,2},{3,19},{19,3},{4,20},{20... | collective-permute-start | bytes 589832 | tf_op jit(solution)/shard_map/ppermute | solution.py:33
  116.4 5.7 %collective-permute-start.14 = (bf16[128,768]{1,0:T(8,128)(2,1)S(1)}, bf16[128,768]{1,0:T(8,128)(2,1)S(1)}, u32[]{:S(2)}, u32[]{:S(2)}) collective-permute-start(bf16[128,768]{1,0:T(8,128)(2,1)S(1)} %collective-permute-done.13.refs_0_), channel_id=1, source_target_pairs={{0,16},{16,0},{1,17},{17,1},{2,18},{18,2},{3,19},{19,3},{4,20},{20... | collective-permute-start | bytes 589832 | tf_op jit(solution)/shard_map/ppermute | solution.py:33
  122.1 3.9 %copy-start.30 = (bf16[128,768]{1,0:T(8,128)(2,1)}, bf16[128,768]{1,0:T(8,128)(2,1)S(1)}, u32[]{:S(2)}) copy-start(bf16[128,768]{1,0:T(8,128)(2,1)S(1)} %get-tuple-element.119) | copy-start | bytes 589828
  127.9 32.9 %all-to-all-start.3 = ((bf16[8,120,768]{2,1,0:T(8,128)(2,1)}), bf16[8,120,768]{2,1,0:T(8,128)(2,1)S(1)}, u32[]{:S(2)}, u32[]{:S(2)}) async-start(bf16[8,120,768]{2,1,0:T(8,128)(2,1)} %copy-done.3), calls=%async_computation.3 | async-start | bytes 2949120 | tf_op jit(solution)/shard_map/all_to_all | solution.py:49
  134.1 5.6 %collective-permute-start.15 = (bf16[128,768]{1,0:T(8,128)(2,1)}, bf16[128,768]{1,0:T(8,128)(2,1)S(1)}, u32[]{:S(2)}, u32[]{:S(2)}) collective-permute-start(bf16[128,768]{1,0:T(8,128)(2,1)} %copy-done.32), channel_id=1, source_target_pairs={{0,16},{16,0},{1,17},{17,1},{2,18},{18,2},{3,19},{19,3},{4,20},{20... | collective-permute-start | bytes 589832 | tf_op jit(solution)/shard_map/ppermute | solution.py:33
  134.8 5.0 %copy-start.31 = (bf16[128,768]{1,0:T(8,128)(2,1)S(1)}, bf16[128,768]{1,0:T(8,128)(2,1)}, u32[]{:S(2)}) copy-start(bf16[128,768]{1,0:T(8,128)(2,1)} %copy-done.30) | copy-start | bytes 589828
  134.8 5.0 %copy-start.14 = (f32[128,768]{1,0:T(8,128)S(1)}, f32[128,768]{1,0:T(8,128)}, u32[]{:S(2)}) copy-start(f32[128,768]{1,0:T(8,128)} %copy-done.13) | copy-start | bytes 1179652
  134.8 8.1 %copy-start.27 = (bf16[320,1536]{1,0:T(8,128)(2,1)S(1)}, bf16[320,1536]{1,0:T(8,128)(2,1)}, u32[]{:S(2)}) copy-start(bf16[320,1536]{1,0:T(8,128)(2,1)} %copy-done.26) | copy-start | bytes 2949124
  134.8 8.1 %copy-start.29 = (bf16[320,768]{1,0:T(8,128)(2,1)S(1)}, bf16[320,768]{1,0:T(8,128)(2,1)}, u32[]{:S(2)}) copy-start(bf16[320,768]{1,0:T(8,128)(2,1)} %copy-done.28) | copy-start | bytes 1474564
  139.7 7.8 %collective-permute-start.12 = (bf16[128,768]{1,0:T(8,128)(2,1)S(1)}, bf16[128,768]{1,0:T(8,128)(2,1)S(1)}, u32[]{:S(2)}, u32[]{:S(2)}) collective-permute-start(bf16[128,768]{1,0:T(8,128)(2,1)S(1)} %copy-done.31), channel_id=1, source_target_pairs={{0,16},{16,0},{1,17},{17,1},{2,18},{18,2},{3,19},{19,3},{4,20},{20... | collective-permute-start | bytes 589832 | tf_op jit(solution)/shard_map/ppermute | solution.py:33
  139.8 20.3 %collective-permute-start.16 = (bf16[128,768]{1,0:T(8,128)(2,1)S(1)}, bf16[128,768]{1,0:T(8,128)(2,1)S(1)}, u32[]{:S(2)}, u32[]{:S(2)}) collective-permute-start(bf16[128,768]{1,0:T(8,128)(2,1)S(1)} %add_convert_fusion), channel_id=1, source_target_pairs={{0,12},{1,13},{2,14},{3,15},{4,8},{5,9},{6,10},{7,11},{8,4},{9,5},... | collective-permute-start | bytes 589832 | tf_op jit(solution)/shard_map/ppermute | solution.py:39
  146.6 18.2 %copy-start.16 = (f32[128,768]{1,0:T(8,128)S(1)}, f32[128,768]{1,0:T(8,128)}, u32[]{:S(2)}) copy-start(f32[128,768]{1,0:T(8,128)} %copy-done.15) | copy-start | bytes 1179652
  147.5 12.8 %copy-start.33 = (bf16[128,768]{1,0:T(8,128)(2,1)}, bf16[128,768]{1,0:T(8,128)(2,1)S(1)}, u32[]{:S(2)}) copy-start(bf16[128,768]{1,0:T(8,128)(2,1)S(1)} %collective-permute-done.12) | copy-start | bytes 589828
  161.5 5.2 %collective-permute-start.17 = (bf16[24,640]{1,0:T(8,128)(2,1)S(1)}, bf16[24,640]{1,0:T(8,128)(2,1)S(1)}, u32[]{:S(2)}, u32[]{:S(2)}) collective-permute-start(bf16[24,640]{1,0:T(8,128)(2,1)S(1)} %get-tuple-element.136), channel_id=1, source_target_pairs={{0,8},{1,9},{2,10},{3,11},{4,12},{5,13},{6,14},{7,15},{8,0},{9,1},... | collective-permute-start | bytes 92168 | tf_op jit(solution)/shard_map/ppermute | solution.py:599
  161.5 5.2 %collective-permute-start.18 = (bf16[24,640]{1,0:T(8,128)(2,1)S(1)}, bf16[24,640]{1,0:T(8,128)(2,1)S(1)}, u32[]{:S(2)}, u32[]{:S(2)}) collective-permute-start(bf16[24,640]{1,0:T(8,128)(2,1)S(1)} %get-tuple-element.137), channel_id=1, source_target_pairs={{0,16},{1,17},{2,18},{3,19},{4,20},{5,21},{6,22},{7,23},{8,24},{9,... | collective-permute-start | bytes 92168 | tf_op jit(solution)/shard_map/ppermute | solution.py:599
  162.2 4.9 %collective-permute-start.19 = (bf16[24,640]{1,0:T(8,128)(2,1)S(1)}, bf16[24,640]{1,0:T(8,128)(2,1)S(1)}, u32[]{:S(2)}, u32[]{:S(2)}) collective-permute-start(bf16[24,640]{1,0:T(8,128)(2,1)S(1)} %get-tuple-element.138), channel_id=1, source_target_pairs={{0,24},{1,25},{2,26},{3,27},{4,28},{5,29},{6,30},{7,31},{8,16},{9,... | collective-permute-start | bytes 92168 | tf_op jit(solution)/shard_map/ppermute | solution.py:599
  (11 other events, 14.1 us)

commit v3 on v2

--- a/solution.py
+++ b/solution.py
@@ -153,6 +153,31 @@
     keep_ref[...] = wout_ref[...]
 
 
+def put_rows(ref, dest, value):
+    rows, width = value.shape
+    wide = ref.shape[2]
+    if wide >= width:
+        ref[dest, 4 * rows :, :width] = value
+        if wide > width:
+            ref[dest, 4 * rows :, width:] = jnp.zeros((rows, wide - width), BF16)
+        return
+    over = width - wide
+    blocks = rows // 8
+    ref[dest, 4 * rows : 5 * rows] = value[:, :wide]
+    for b in range(blocks):
+        ref[dest, 5 * rows :, b * over : (b + 1) * over] = value[b * 8 : (b + 1) * 8, wide:]
+    ref[dest, 5 * rows :, blocks * over :] = jnp.zeros((8, wide - blocks * over), BF16)
+
+
+def take_rows(held, rows, width):
+    wide = held.shape[1]
+    if wide >= width:
+        return held[4 * rows :, :width]
+    over = width - wide
+    tail = [held[5 * rows :, b * over : (b + 1) * over] for b in range(rows // 8)]
+    return jnp.concatenate([held[4 * rows : 5 * rows], jnp.concatenate(tail, axis=0)], axis=1)
+
+
 def spread_weights(group_ref, p0_ref, p1_ref, p2_ref, p3_ref, wout_ref, out_ref):
     dests, _, wide = out_ref.shape
     rows, used = p0_ref.shape
@@ -161,14 +186,12 @@
     if wide > used:
         value = jnp.concatenate([value, jnp.zeros((4 * rows, wide - used), BF16)], axis=1)
     last = wout_ref[...]
-    if wide > last.shape[1]:
-        last = jnp.concatenate([last, jnp.zeros((rows, wide - last.shape[1]), BF16)], axis=1)
-    value = jnp.concatenate([value, last], axis=0)
     for dest in range(dests):
-        out_ref[dest] = value
-
-
-def prepare(capacity, pad_two, group_ref, table_ref, routes_ref, vector_ref, spread_ref, later_ref,
+        out_ref[dest, : 4 * rows] = value
+        put_rows(out_ref, dest, last)
+
+
+def prepare(capacity, pad, group_ref, table_ref, routes_ref, vector_ref, spread_ref, later_ref,
             gather_ref, send_ref):
     buckets = table_ref.shape[0]
     own_heads, length = vector_ref.shape
@@ -182,28 +205,25 @@
         for b in range(buckets):
             vector = jnp.where(bucket == b, table_ref[b, group * own_heads + h], vector)
         vector_ref[h : h + 1] = vector
-    experts = spread_ref.shape[1] // pad_two
+    experts = gather_ref.shape[1]
     route = routes_ref[...]
     chosen = route == iota((toks, experts), 1)
+    gather_ref[...] = chosen.astype(F32)
     lower = (iota((toks, toks), 0) > iota((toks, toks), 1)).astype(BF16)
     counts = dot(lower, chosen.astype(BF16))
     slot = jnp.sum(jnp.where(chosen, counts, 0.0), axis=1, keepdims=True).astype(jnp.int32)
-    kept = slot < capacity
-    place = jnp.where(kept, route * pad_two + slot, -1)
-    later = jnp.where(kept, route * pad_two + capacity + slot, -1)
-    across = iota((toks, experts * pad_two), 1)
-    first = (place == across).astype(F32)
-    second = (later == across).astype(F32)
-    spread_ref[...] = first.astype(BF16)
-    later_ref[...] = second.astype(BF16)
-    send_ref[:, :toks] = jnp.transpose(first).astype(BF16)
-    send_ref[:, toks:] = jnp.transpose(second).astype(BF16)
-    gather_ref[...] = chosen.astype(F32)
+    across = iota((toks, experts * pad), 1)
+    for i in range(4):
+        place = jnp.where(slot < capacity, route * pad + i * capacity + slot, -1)
+        spread = (place == across).astype(F32)
+        target = (spread_ref, later_ref)[i % 2]
+        target[i // 2] = spread.astype(BF16)
+        send_ref[:, i * toks : (i + 1) * toks] = jnp.transpose(spread).astype(BF16)
 
 
 def place_weights(arrived_ref, w_ref, wout_ref):
-    sources, total, _ = arrived_ref.shape
-    rows = total // 5
+    sources = arrived_ref.shape[0]
+    rows = wout_ref.shape[0] // sources
     used = w_ref.shape[1]
     width = wout_ref.shape[1]
     block = sources * rows
@@ -212,7 +232,7 @@
             w_ref[j * block + s * rows : j * block + (s + 1) * rows] = arrived_ref[
                 s, j * rows : (j + 1) * rows, :used
             ]
-        wout_ref[s * rows : (s + 1) * rows] = arrived_ref[s, 4 * rows :, :width]
+        wout_ref[s * rows : (s + 1) * rows] = take_rows(arrived_ref[s], rows, width)
 
 
 def gain_rows(experts, cols, w_ref, gains_ref):
@@ -255,9 +275,8 @@
     send_ref[...] = partial[toks:].astype(BF16)
 
 
-def docs_of_pair(at, length, group_ref, place_ref, arrived_ref):
-    sources, total, _ = arrived_ref.shape
-    rows = total // 5
+def docs_of_pair(at, length, rows, group_ref, place_ref, arrived_ref):
+    sources = arrived_ref.shape[0]
     doc_cols = -(-length // rows)
     held = arrived_ref[(place_ref[0] % sources) ^ (sources // 2)]
     blocks = [held[j * rows : (j + 1) * rows, at : at + doc_cols].astype(F32) for j in range(4)]
@@ -278,7 +297,10 @@
     place_weights(arrived_ref, w_ref, wout_ref)
     cols = wout_ref.shape[0]
     gain_rows(experts, cols, w_ref, gains_ref)
-    docs = docs_of_pair(3 * cols + experts + 2, vector_ref.shape[1], group_ref, place_ref, arrived_ref)
+    docs = docs_of_pair(
+        3 * cols + experts + 2, vector_ref.shape[1], cols // arrived_ref.shape[0], group_ref, place_ref,
+        arrived_ref,
+    )
     attend(scale, head_dim, docs, group_ref, w_ref, wout_ref, gains_ref, own_ref, across_ref,
            vector_ref, *outs)
 
@@ -287,7 +309,10 @@
                         own_ref, across_ref, vector_ref, gains_ref, *outs):
     cols = wout_ref.shape[0]
     gain_rows(experts, cols, w_ref, gains_ref)
-    docs = docs_of_pair(3 * cols + experts + 2, vector_ref.shape[1], group_ref, place_ref, arrived_ref)
+    docs = docs_of_pair(
+        3 * cols + experts + 2, vector_ref.shape[1], cols // arrived_ref.shape[0], group_ref, place_ref,
+        arrived_ref,
+    )
     attend(scale, head_dim, docs, group_ref, w_ref, wout_ref, gains_ref, own_ref, across_ref,
            vector_ref, *outs)
 
@@ -299,7 +324,9 @@
     )
     middle_ref[...] = middle
     normed = (middle * rms_inverse(middle) * gains_ref[1:2]).astype(BF16)
-    both = jnp.concatenate([normed, g_ref[...]], axis=0)
+    g = g_ref[...]
+    half = g.shape[1] // 2
+    both = jnp.concatenate([normed[:, :half], g[:, :half], normed[:, half:], g[:, half:]], axis=0)
     out_ref[...] = dot(send_ref[...], both).astype(BF16)
     probs = jax.nn.softmax(dot(normed, w_ref[...]), axis=-1)
     gate_ref[...] = jnp.sum(probs * chosen_ref[...], axis=1, keepdims=True)
@@ -319,15 +346,17 @@
         row = iota(shape, 0)
         source = row // capacity
         wanted = source * pad + (row - source * capacity)
-        first = (iota(shape, 1) == wanted).astype(BF16)
-        second = (iota(shape, 1) == wanted + capacity).astype(BF16)
+        select = [(iota(shape, 1) == wanted + i * capacity).astype(BF16) for i in range(4)]
         mine = (iota((1, experts), 1) == place_ref[0]).astype(F32)
         for side, ref in enumerate((own_ref, other_ref)):
             at = side * slots
             rows = ref[...]
-            buffers = dot(first, rows).astype(BF16)
+            buffers, g = [
+                jnp.concatenate([dot(select[i], rows), dot(select[i + 2], rows)], axis=1)
+                for i in range(2)
+            ]
+            buffers = buffers.astype(BF16)
             buf_ref[at : at + slots] = buffers
-            g = dot(second, rows)
             probs = jax.nn.softmax(dot(buffers, router_ref[...]), axis=-1)
             gate = jnp.sum(probs * mine, axis=1, keepdims=True)
             dslot_ref[at : at + slots] = (gate * g).astype(BF16)
@@ -367,17 +396,16 @@
     grad_logits = (grad_gate * gate_ref[...] * (mine - probs_ref[...])).astype(BF16)
     grad_ref[...] = dot(buf_ref[...], grad_logits, ((0,), (0,))).astype(BF16)
     back = total[1].astype(F32) + dot(grad_logits, router_ref[...], ((1,), (1,)))
-    shape = (out_ref.shape[0], 2 * slots)
+    shape = (out_ref.shape[0], 4 * slots)
     row = iota(shape, 0)
     source = row // pad
     inside = row - source * pad
-    wanted = jnp.where(
-        inside < capacity,
-        source * capacity + inside,
-        jnp.where(inside < 2 * capacity, slots + source * capacity + inside - capacity, -1),
-    )
+    part = inside // capacity
+    wanted = jnp.where(part < 4, part * slots + source * capacity + inside - part * capacity, -1)
     expand = (iota(shape, 1) == wanted).astype(BF16)
-    both = jnp.concatenate([back.astype(BF16), result], axis=0)
+    back = back.astype(BF16)
+    half = back.shape[1] // 2
+    both = jnp.concatenate([back[:, :half], result[:, :half], back[:, half:], result[:, half:]], axis=0)
     out_ref[...] = dot(expand, both).astype(BF16)
 
 
@@ -386,7 +414,8 @@
     middle = middle_ref[...]
     inverse = rms_inverse(middle)
     unit = middle * inverse
-    grad_normed = dot(spread_ref[...], back_ref[...])
+    rows = back_ref[...]
+    grad_normed = jnp.concatenate([dot(spread_ref[i], rows) for i in range(2)], axis=1)
     gain_ref[...] = jnp.sum(grad_normed * unit, axis=0, keepdims=True)
     dmiddle = g_ref[...].astype(F32) + norm_backward(grad_normed, unit, inverse, gains_ref[1:2])
     dmiddle_ref[...] = dmiddle
@@ -394,21 +423,23 @@
 
 
 def finish_layer(result_ref, spread_ref, middle_ref, gate_ref, out_ref):
-    combined = dot(spread_ref[...], result_ref[...])
+    rows = result_ref[...]
+    combined = jnp.concatenate([dot(spread_ref[i], rows) for i in range(2)], axis=1)
     out_ref[...] = (middle_ref[...] + gate_ref[...] * combined).astype(BF16)
 
 
-def attend_backward(scale, head_dim, own_ref, across_ref, wout_ref, att_ref, qkv_ref, probs_ref,
-                    gains_ref, w_ref, x_own_ref, x_across_ref):
+def attend_backward(scale, head_dim, own_ref, across_ref, wout_ref, qkv_ref, probs_ref, gains_ref,
+                    w_ref, x_own_ref, x_across_ref, keep_ref, send_ref, grad_ref, gain_ref,
+                    offsets_ref):
     own_heads = probs_ref.shape[0]
     cols = own_heads * head_dim
-    length = 2 * own_ref.shape[0]
+    toks = own_ref.shape[0]
+    length = 2 * toks
     flip = (iota((length, length), 0) + iota((length, length), 1) == length - 1).astype(BF16)
     da = jnp.concatenate([own_ref[...], across_ref[...]], axis=0)
     grad_att = dot(da, wout_ref[...], ((1,), (1,))).astype(BF16)
     qkv = qkv_ref[...]
     parts = [[], [], []]
-    offsets = []
     for h in range(own_heads):
         at = h * head_dim
         q = qkv[:, at : at + head_dim]
@@ -420,44 +451,46 @@
         row_dot = jnp.sum(probs * grad_probs, axis=1, keepdims=True)
         ds = (probs * (grad_probs - row_dot)).astype(BF16)
         turned = pltpu.roll(dot(flip, ds), 1, 1, stride=1, stride_axis=0)
-        offsets.append(jnp.sum(turned, axis=0, keepdims=True))
+        offsets_ref[h : h + 1] = jnp.sum(turned, axis=0, keepdims=True)
         parts[0].append(dot(ds, k) * scale)
         parts[1].append(dot(ds, q, ((0,), (0,))) * scale)
         parts[2].append(dot(probs.astype(BF16), gh, ((0,), (0,))))
     grad_qkv = jnp.concatenate(parts[0] + parts[1] + parts[2], axis=1).astype(BF16)
-    x = jnp.concatenate([x_own_ref[...], x_across_ref[...]], axis=0).astype(F32)
-    unit = x * rms_inverse(x)
-    normed = (unit * gains_ref[0:1]).astype(BF16)
-    weights = dot(normed, grad_qkv, ((0,), (0,)))
-    outs = dot(att_ref[...], da, ((0,), (0,)))
+    grad_ref[...] = grad_qkv
     grad_normed = dot(grad_qkv, w_ref[:, : 3 * cols], ((1,), (1,)))
-    gain = jnp.sum(grad_normed * unit, axis=0, keepdims=True)
-    return weights, outs, grad_normed, gain, offsets
-
-
-def backward_own(scale, head_dim, *refs):
-    gw_ref, gout_ref, keep_ref, send_ref, gain_ref, offsets_ref = refs[10:]
-    toks = keep_ref.shape[0]
-    weights, outs, grad_normed, gain, offsets = attend_backward(scale, head_dim, *refs[:10])
-    gw_ref[...] = weights
-    gout_ref[...] = outs
     keep_ref[...] = grad_normed[:toks]
     send_ref[...] = grad_normed[toks:].astype(BF16)
-    gain_ref[...] = gain
-    for h, value in enumerate(offsets):
-        offsets_ref[h : h + 1] = value
-
-
-def backward_pair(scale, head_dim, buckets, table_cols, *refs):
-    gw_ref, gout_ref, gain_ref, offsets_ref, gain_two_ref, router_ref = refs[10:16]
-    keep_ref, send_ref, full_ref, out_ref = refs[16:]
-    weights, outs, grad_normed, gain, offsets = attend_backward(scale, head_dim, *refs[:10])
-    own_heads = offsets_ref.shape[0]
+    x = jnp.concatenate([x_own_ref[...], x_across_ref[...]], axis=0).astype(F32)
+    gain_ref[...] = jnp.sum(grad_normed * (x * rms_inverse(x)), axis=0, keepdims=True)
+
+
+def row_weights(own_ref, across_ref, att_ref, grad_ref, gains_ref, x_own_ref, x_across_ref):
+    x = jnp.concatenate([x_own_ref[...], x_across_ref[...]], axis=0).astype(F32)
+    normed = (x * rms_inverse(x) * gains_ref[0:1]).astype(BF16)
+    da = jnp.concatenate([own_ref[...], across_ref[...]], axis=0)
+    weights = dot(normed, grad_ref[...], ((0,), (0,)))
+    return weights, dot(att_ref[...], da, ((0,), (0,)))
+
+
+def backward_own(scale, head_dim, own_ref, across_ref, wout_ref, att_ref, qkv_ref, probs_ref,
+                 gains_ref, w_ref, x_own_ref, x_across_ref, gw_ref, gout_ref, keep_ref, send_ref,
+                 grad_ref, gain_ref, offsets_ref):
+    attend_backward(
+        scale, head_dim, own_ref, across_ref, wout_ref, qkv_ref, probs_ref, gains_ref, w_ref,
+        x_own_ref, x_across_ref, keep_ref, send_ref, grad_ref, gain_ref, offsets_ref,
+    )
+    gw_ref[...], gout_ref[...] = row_weights(
+        own_ref, across_ref, att_ref, grad_ref, gains_ref, x_own_ref, x_across_ref
+    )
+
+
+def sum_weights(buckets, table_cols, *refs):
+    gw_ref, gout_ref, own_gain_ref, own_offsets_ref, gain_ref, offsets_ref = refs[7:13]
+    gain_two_ref, router_ref, full_ref, out_ref = refs[13:]
+    weights, outs = row_weights(*refs[:7])
+    own_heads, length = offsets_ref.shape
     width, experts = router_ref.shape
-    length = offsets_ref.shape[1]
     toks = length // 2
-    keep_ref[...] = grad_normed[:toks]
-    send_ref[...] = grad_normed[toks:].astype(BF16)
     rows = own_heads * buckets // table_cols
     spot = iota((1, length), 1)
     offset = jnp.where(spot >= toks, spot - length, spot)
@@ -467,12 +500,12 @@
         column = jnp.zeros((rows, 1), F32)
         for h in range(own_heads):
             belongs = iota((rows, length), 0) * table_cols + t == bucket * own_heads + h
-            value = offsets[h] + offsets_ref[h : h + 1]
+            value = own_offsets_ref[h : h + 1] + offsets_ref[h : h + 1]
             column = column + jnp.sum(jnp.where(belongs, value, 0.0), axis=1, keepdims=True)
         table.append(column)
     table = jnp.concatenate([jnp.concatenate(table, axis=1)] * (width // rows), axis=0)
     narrow = jnp.concatenate(
-        [gain_ref[...] + gain, gain_two_ref[...], jnp.zeros((6, width), F32)], axis=0
+        [own_gain_ref[...] + gain_ref[...], gain_two_ref[...], jnp.zeros((6, width), F32)], axis=0
     )
     narrow = jnp.transpose(narrow)[:, :2]
     weights = weights + gw_ref[...]
@@ -482,11 +515,11 @@
     out_ref[...] = (outs + gout_ref[...]).astype(BF16)
 
 
-def backward_pair_message(scale, head_dim, buckets, table_cols, *refs):
+def sum_weights_message(buckets, table_cols, *refs):
     *rest, message_ref, full_ref, out_ref = refs
-    backward_pair(scale, head_dim, buckets, table_cols, *rest, full_ref, out_ref)
-    dests, total, wide = message_ref.shape
-    rows = total // 5
+    sum_weights(buckets, table_cols, *rest, full_ref, out_ref)
+    dests, _, wide = message_ref.shape
+    rows = out_ref.shape[0] // dests
     used = full_ref.shape[1]
     block = dests * rows
     for s in range(dests):
@@ -497,10 +530,7 @@
                 message_ref[s, j * rows : (j + 1) * rows, used:] = jnp.zeros(
                     (rows, wide - used), BF16
                 )
-        width = out_ref.shape[1]
-        message_ref[s, 4 * rows :, :width] = out_ref[s * rows : (s + 1) * rows]
-        if wide > width:
-            message_ref[s, 4 * rows :, width:] = jnp.zeros((rows, wide - width), BF16)
+        put_rows(message_ref, s, out_ref[s * rows : (s + 1) * rows])
 
 
 def sum_arrived(group_ref, arrived_ref, out_ref, own_ref, *send_refs):
@@ -508,7 +538,7 @@
     total = arrived_ref[0].astype(F32)
     for s in range(1, arrived_ref.shape[0]):
         total = total + arrived_ref[s].astype(F32)
-    out_ref[...] = total[4 * rows :, : out_ref.shape[1]]
+    out_ref[...] = take_rows(total, rows, out_ref.shape[1])
     pieces = [total[j * rows : (j + 1) * rows, :used] for j in range(4)]
     own_ref[...] = choose(group_ref[0], pieces)
     for d, ref in enumerate(send_refs):
@@ -579,7 +609,7 @@
     experts = sources
     capacity = (5 * toks + 4 * experts - 1) // (4 * experts)
     slots = experts * capacity
-    pad_two = -(-2 * capacity // 8) * 8
+    pad = -(-4 * capacity // 8) * 8
     rows = w_query.shape[0]
     core = lax.axis_index("dp")
     place = lax.axis_index("expert")
@@ -591,8 +621,11 @@
     table_cols = max(1, own_heads * buckets // rows)
     extra = max(table_cols, -(-length // rows))
     used = -(-(3 * cols + experts + 2 + extra) // 128) * 128
-    wide = max(used, width)
     aligned = rows % 8 == 0
+    if aligned and used < width and (width - used) * (rows // 8) <= used:
+        wide, total = used, 5 * rows + 8
+    else:
+        wide, total = max(used, width), 5 * rows
 
     def across_group(pieces):
         return [
@@ -620,7 +653,7 @@
     pieces = across_group(pieces)
     pair_tokens, own_piece, *pieces = lax.optimization_barrier((pair_tokens, own_piece, *pieces))
     (message,) = kernel_call(
-        spread_weights, [((half, 5 * rows, wide), BF16)],
+        spread_weights, [((half, total, wide), BF16)],
         group_at, own_piece, *pieces, out_rows, scalars=1,
     )
     arrived = exchange_half(message)
@@ -628,13 +661,13 @@
     own_across = swap_core(own_tokens)
     pair_across = swap_core(pair_tokens)
     vectors, spread, later, chosen, send = kernel_call(
-        functools.partial(prepare, capacity, pad_two),
+        functools.partial(prepare, capacity, pad),
         [
             ((own_heads, length), F32),
-            ((toks, experts * pad_two), BF16),
-            ((toks, experts * pad_two), BF16),
+            ((2, toks, experts * pad), BF16),
+            ((2, toks, experts * pad), BF16),
             ((toks, experts), F32),
-            ((experts * pad_two, 2 * toks), BF16),
+            ((experts * pad, 4 * toks), BF16),
         ],
         group_at, bias_table, routes.reshape(toks, 1), scalars=2,
     )
@@ -665,6 +698,7 @@
         )
     pair_qkv, pair_probs, pair_att, keep, away = pair_kept
     pair_sum = (keep + swap_core(away).astype(F32)).astype(BF16)
+    pair_sum, out_w, gains = lax.optimization_barrier((pair_sum, out_w, gains))
     pair_sum = swap_pair(pair_sum)
     own_qkv, own_probs, own_att, keep, away = kernel_call(
         functools.partial(attend_own, scale, head_dim), row_outs,
@@ -673,10 +707,10 @@
     router_w = weights[:, 3 * cols : 3 * cols + experts]
     middle, gate, outgoing = kernel_call(
         route_tokens,
-        [((toks, width), F32), ((toks, 1), F32), ((experts * pad_two, width), BF16)],
+        [((toks, width), F32), ((toks, 1), F32), ((experts * pad, width // 2), BF16)],
         own_tokens, keep, swap_core(away), pair_sum, gains, router_w, chosen, send, g_low,
     )
-    incoming = exchange(outgoing.reshape(experts, pad_two, width)).reshape(-1, width)
+    incoming = exchange(outgoing.reshape(experts, pad, width // 2)).reshape(-1, width // 2)
 
     inner, outer = w_inner[0], w_outer[0]
     units = inner.shape[1]
@@ -699,8 +733,8 @@
         out_shape=[jax.ShapeDtypeStruct(shape, dtype) for shape, dtype, _ in outs],
         in_specs=[
             pl.BlockSpec(memory_space=pltpu.SMEM),
-            fixed((experts * pad_two, width)),
-            fixed((experts * pad_two, width)),
+            fixed((experts * pad, width // 2)),
+            fixed((experts * pad, width // 2)),
             fixed((width, experts)),
             pl.BlockSpec((width, chunk), lambda i: (0, i)),
             pl.BlockSpec((chunk, width), lambda i: (i, 0)),
@@ -713,11 +747,11 @@
     grad_inner = dot(buffers, dpre, ((0,), (0,)))
     back, grad_router = kernel_call(
         functools.partial(finish_expert, capacity),
-        [((sources * pad_two, width), BF16), ((width, experts), BF16)],
+        [((sources * pad, width // 2), BF16), ((width, experts), BF16)],
         place_at, keep, swap_core(away), buffers[:slots], slot_g, slot_probs, slot_gate, router_w,
         scalars=1,
     )
-    back = exchange(back.reshape(sources, pad_two, width)).reshape(-1, width)
+    back = exchange(back.reshape(sources, pad, width // 2)).reshape(-1, width // 2)
 
     grad_middle, grad_attn, grad_gain_two = kernel_call(
         norm_two_backward,
@@ -726,35 +760,40 @@
     )
     pair_grad = swap_pair(grad_attn)
     shared = (gains, weights)
-    grad_w, grad_out, grad_normed, away, gain_part, offsets = kernel_call(
+    back_outs = [
+        ((toks, width), F32),
+        ((toks, width), BF16),
+        ((length, 3 * cols), BF16),
+        ((1, width), F32),
+        ((own_heads, length), F32),
+    ]
+    grad_w, grad_out, grad_normed, away, _, own_gain, own_offsets = kernel_call(
         functools.partial(backward_own, scale, head_dim),
-        [
-            ((width, 3 * cols), F32),
-            ((cols, width), F32),
-            ((toks, width), F32),
-            ((toks, width), BF16),
-            ((1, width), F32),
-            ((own_heads, length), F32),
-        ],
+        [((width, 3 * cols), F32), ((cols, width), F32)] + back_outs,
         grad_attn, swap_core(grad_attn), out_w, own_att, own_qkv, own_probs, *shared,
         own_tokens, own_across,
     )
-    grad_normed = grad_normed + swap_core(away).astype(F32)
+    pair_grad, grad_w, own_away = lax.optimization_barrier((pair_grad, grad_w, away))
+    grad_normed = grad_normed + swap_core(own_away).astype(F32)
+    pair_grads = (pair_grad, swap_core(pair_grad))
+    keep, away, grad_qkv, pair_gain, pair_offsets = kernel_call(
+        functools.partial(attend_backward, scale, head_dim), back_outs,
+        *pair_grads, out_w, pair_qkv, pair_probs, *shared, pair_tokens, pair_across,
+    )
+    to_pair = (keep + swap_core(away).astype(F32)).astype(BF16)
     last = (
-        pair_grad, swap_core(pair_grad), out_w, pair_att, pair_qkv, pair_probs, *shared,
-        pair_tokens, pair_across, grad_w, grad_out, gain_part, offsets, grad_gain_two, grad_router,
-    )
-    outs = [((toks, width), F32), ((toks, width), BF16)]
+        *pair_grads, pair_att, grad_qkv, gains, pair_tokens, pair_across, grad_w, grad_out,
+        own_gain, own_offsets, pair_gain, pair_offsets, grad_gain_two, grad_router,
+    )
     flat = [((width, used), BF16), ((cols, width), BF16)]
-    options = (scale, head_dim, buckets, table_cols)
     if aligned:
-        keep, away, message, _, _ = kernel_call(
-            functools.partial(backward_pair_message, *options),
-            [*outs, ((half, 5 * rows, wide), BF16), *flat], *last,
+        message, _, _ = kernel_call(
+            functools.partial(sum_weights_message, buckets, table_cols),
+            [((half, total, wide), BF16), *flat], *last,
         )
     else:
-        keep, away, full, grad_out = kernel_call(
-            functools.partial(backward_pair, *options), outs + flat, *last
+        full, grad_out = kernel_call(
+            functools.partial(sum_weights, buckets, table_cols), flat, *last
         )
         full = full.reshape(2, 2, half, rows, used).transpose(2, 0, 1, 3, 4)
         full = full.reshape(half, 4 * rows, used)
@@ -766,16 +805,18 @@
             ],
             axis=1,
         )
-    message, away, keep = lax.optimization_barrier((message, away, keep))
+    message, to_pair = lax.optimization_barrier((message, to_pair))
+    came = swap_pair(to_pair).astype(F32)
     arrived = exchange_half(message)
-    came = swap_pair((keep + swap_core(away).astype(F32)).astype(BF16)).astype(F32)
-    (final,) = kernel_call(finish_layer, [((toks, width), BF16)], back, later, middle, gate
+    (final,) = kernel_call(
+        finish_layer, [((toks, width), BF16)], back, later, middle, gate
     )
 
     out_grad_w, own_piece, *pieces = kernel_call(
         sum_arrived, [((rows, width), F32), ((rows, used), F32)] + [((rows, used), BF16)] * 3,
         group_at, arrived, scalars=1,
     )
+    came, own_piece = lax.optimization_barrier((came, own_piece))
     pieces = across_group(pieces)
     query_grad, key_grad, value_grad, router_grad, one_grad, two_grad, table_grad = kernel_call(
         functools.partial(finish_weights, own_heads, buckets, table_cols),

time: 169 us -> 159 us (0.941)
  blocking collectives: 42.2 us -> 35.2 us
  waiting for transfers between devices: 46 us -> 42.6 us
  Pallas kernels: 24.3 us -> 26.1 us
  local copies, waits for them, and re-layouts: 7.15 us -> 5.38 us
    all_to_all x2, blocking collectives: 42.2 us -> 35.2 us  [exchange(): lax.all_to_all(value, 'expert', split_axis=0, concat_axis=0, tiled=True)]
    ppermute x4, waiting for transfers between devices: 21.4 us -> 18.4 us  [swap_pair(): return lax.ppermute(value, 'expert', [(i, i ^ other) for i in range(n)])]
    all_to_all x2, waiting for transfers between devices: 15.2 us -> 12.7 us  [exchange_half(): lax.all_to_all(value, 'expert', split_axis=0, concat_axis=0, tiled=True,...]
    ppermute x10, waiting for transfers between devices: 3.12 us -> 5.03 us  [swap_core(): return lax.ppermute(value, 'dp', [(0, 1), (1, 0)])]
    pallas_call x13 -> x14, Pallas kernels: 18.8 us -> 20.3 us  [kernel_call(): pl.pallas_call(run, out_shape=[jax.ShapeDtypeStruct(shape, dtype) for sha...]
    unnamed x75 -> x53, local copies, waits for them, and re-layouts: 6.15 us -> 5.12 us
  transfers between devices with their start and end apart: 22 -> 22, of which waited for: 9 -> 11; matrix products, arithmetic and copies ran while one was open for 7% -> 7% of each run, Pallas kernels for 6% -> 7%
where the time goes in v3:
time: 159 us
  waiting for transfers between devices  42.6 us (27%)
  starting transfers between devices  37 us (23%)
  blocking collectives  35.2 us (22%)
  Pallas kernels  26.1 us (16%)
  matrix products  8.54 us (5%)
  local copies, waits for them, and re-layouts  5.38 us (3%)
  other arithmetic  3.02 us (2%)
    all_to_all x2, blocking collectives, exchange(): lax.all_to_all(value, 'expert', split_axis=0, concat_axis=0, tiled=True)  35.2 us
    pallas_call x14, Pallas kernels, kernel_call(): pl.pallas_call(run, out_shape=[jax.ShapeDtypeStruct(shape, dtype) for sha...  20.3 us
    ppermute x4, waiting for transfers between devices, swap_pair(): return lax.ppermute(value, 'expert', [(i, i ^ other) for i in range(n)])  18.4 us
    all_to_all x2, waiting for transfers between devices, exchange_half(): lax.all_to_all(value, 'expert', split_axis=0, concat_axis=0, tiled=True,...  12.7 us
    ppermute x10, starting transfers between devices, swap_core(): return lax.ppermute(value, 'dp', [(0, 1), (1, 0)])  11.2 us
    all_to_all x2, starting transfers between devices, exchange_half(): lax.all_to_all(value, 'expert', split_axis=0, concat_axis=0, tiled=True,...  9.9 us
    ppermute x4, starting transfers between devices, swap_pair(): return lax.ppermute(value, 'expert', [(i, i ^ other) for i in range(n)])  8.96 us
    dot_general x2, matrix products, dot(): lax.dot_general(left, right, (dims, ((), ())), preferred_element_type=F32)  8.54 us
  transfers between devices with their start and end apart: 22, of which 11 were waited for; matrix products, arithmetic and copies ran while one was open for 7% of the time, Pallas kernels for 7%

profile of v3, /device:TPU:3, one launch (start us, length us, event | category | flops | bytes accessed | tf_op | source)
XLA Modules:
  0.0 158.8 jit_solution(5652757653544952417)
XLA Ops:
  0.7 3.4 %collective-permute-start = (bf16[128,768]{1,0:T(8,128)(2,1)}, bf16[128,768]{1,0:T(8,128)(2,1)S(1)}, u32[]{:S(2)}, u32[]{:S(2)}) collective-permute-start(bf16[128,768]{1,0:T(8,128)(2,1)} %bitcast.32), channel_id=1, source_target_pairs={{0,12},{1,13},{2,14},{3,15},{4,8},{5,9},{6,10},{7,11},{8,4},{9,5},... | collective-permute-start | bytes 589832 | tf_op jit(solution)/shard_map/ppermute | solution.py:39
  4.1 2.0 %shard_map.229 = (bf16[24,640]{1,0:T(8,128)(2,1)}, bf16[24,640]{1,0:T(8,128)(2,1)}, bf16[24,640]{1,0:T(8,128)(2,1)}, bf16[24,640]{1,0:T(8,128)(2,1)}, bf16[24,768]{1,0:T(8,128)(2,1)}) custom-call(s32[1]{0:T(128)} %bitcast.2.refs_0_, bf16[24,768]{1,0:T(8,128)(2,1)} %refs_1_.3, bf16[24,768]{1,0:T(8,128)(2,1)} %refs_2_.1, bf16[24,768]{1,0:T(8,128)(2,1)} %refs_3_.1, ...), custom_call_target="tpu_custom_call" | custom-call | flops 1000000 | bytes 1000000 | tf_op jit(solution)/shard_map/pallas_call | solution.py:104
  6.1 1.0 collective-permute-start.2
  7.1 2.5 %collective-permute-start.3 = (bf16[24,640]{1,0:T(8,128)(2,1)}, bf16[24,640]{1,0:T(8,128)(2,1)S(1)}, u32[]{:S(2)}, u32[]{:S(2)}) collective-permute-start(bf16[24,640]{1,0:T(8,128)(2,1)} %get-tuple-element.94), channel_id=1, source_target_pairs={{0,24},{1,25},{2,26},{3,27},{4,28},{5,29},{6,30},{7,31},{8,16},{9,... | collective-permute-start | bytes 92168 | tf_op jit(solution)/shard_map/ppermute | solution.py:632
  9.6 4.2 %collective-permute-done.1.refs_2_ = bf16[24,640]{1,0:T(8,128)(2,1)S(1)} collective-permute-done((bf16[24,640]{1,0:T(8,128)(2,1)}, bf16[24,640]{1,0:T(8,128)(2,1)S(1)}, u32[]{:S(2)}, u32[]{:S(2)}) %collective-permute-start.1) | collective-permute-done | bytes 30752 | tf_op jit(solution)/shard_map/ppermute | solution.py:632
  13.8 1.6 %collective-permute-done.3.refs_4_ = bf16[24,640]{1,0:T(8,128)(2,1)S(1)} collective-permute-done((bf16[24,640]{1,0:T(8,128)(2,1)}, bf16[24,640]{1,0:T(8,128)(2,1)S(1)}, u32[]{:S(2)}, u32[]{:S(2)}) %collective-permute-start.3) | collective-permute-done | bytes 30752 | tf_op jit(solution)/shard_map/ppermute | solution.py:632
  15.4 0.8 copy-done.15
  16.2 0.8 copy-done.16
  17.0 1.2 shard_map.230
  18.1 3.9 %all-to-all-start = ((bf16[8,128,640]{2,1,0:T(8,128)(2,1)}), bf16[8,128,640]{2,1,0:T(8,128)(2,1)S(1)}, u32[]{:S(2)}, u32[]{:S(2)}) async-start(bf16[8,128,640]{2,1,0:T(8,128)(2,1)} %shard_map.230), calls=%async_computation | async-start | bytes 2621440 | tf_op jit(solution)/shard_map/all_to_all | solution.py:49
  22.0 0.9 collective-permute-start.4
  23.1 1.6 shard_map.231
  24.7 0.8 copy-done.8
  26.2 12.7 %all-to-all-done.refs_2_ = bf16[8,128,640]{2,1,0:T(8,128)(2,1)S(1)} async-done(((bf16[8,128,640]{2,1,0:T(8,128)(2,1)}), bf16[8,128,640]{2,1,0:T(8,128)(2,1)S(1)}, u32[]{:S(2)}, u32[]{:S(2)}) %all-to-all-start) | async-done | bytes 1310752 | tf_op jit(solution)/shard_map/all_to_all | solution.py:49
  38.9 1.7 %shard_map.232 = (bf16[768,640]{1,0:T(8,128)(2,1)S(1)}, bf16[192,768]{1,0:T(8,128)(2,1)S(1)}, f32[8,768]{1,0:T(8,128)S(1)}, bf16[256,576]{1,0:T(8,128)(2,1)S(1)}...) custom-call(s32[1]{0:T(128)} %bitcast.2.refs_0_, ...), custom_call_target="tpu_custom_call" | custom-call | flops 1000000 | bytes 1000000 | tf_op jit(solution)/shard_map/pallas_call | solution.py:104
  40.6 1.5 collective-permute-start.5
  42.2 1.0 collective-permute-done.5
  43.2 2.1 %collective-permute-start.8 = (bf16[128,768]{1,0:T(8,128)(2,1)S(1)}, bf16[128,768]{1,0:T(8,128)(2,1)S(1)}, u32[]{:S(2)}, u32[]{:S(2)}) collective-permute-start(bf16[128,768]{1,0:T(8,128)(2,1)S(1)} %add_convert_fusion.1), channel_id=1, source_target_pairs={{0,12},{1,13},{2,14},{3,15},{4,8},{5,9},{6,10},{7,11},{8,4},{9,5},... | collective-permute-start | bytes 589832 | tf_op jit(solution)/shard_map/ppermute | solution.py:39
  45.3 1.5 shard_map.233
  47.6 3.6 %collective-permute-done.8.refs_3_ = bf16[128,768]{1,0:T(8,128)(2,1)S(1)} collective-permute-done((bf16[128,768]{1,0:T(8,128)(2,1)S(1)}, bf16[128,768]{1,0:T(8,128)(2,1)S(1)}, u32[]{:S(2)}, u32[]{:S(2)}) %collective-permute-start.8) | collective-permute-done | bytes 196640 | tf_op jit(solution)/shard_map/ppermute | solution.py:39
  51.2 1.0 shard_map.234
  52.2 18.9 %all_to_all.20 = bf16[16,40,384]{2,1,0:T(8,128)(2,1)S(1)} all-to-all(bf16[16,40,384]{2,1,0:T(8,128)(2,1)S(1)} %bitcast.46), channel_id=1, replica_groups=mesh['dp'=2,'expert'=16] {'expert'}, dimensions={0} | all-to-all | bytes 983040 | tf_op jit(solution)/shard_map/all_to_all | solution.py:43
  71.2 3.0 %collective-permute-start.9 = (bf16[640,384]{1,0:T(8,128)(2,1)S(1)}, bf16[640,384]{1,0:T(8,128)(2,1)S(1)}, u32[]{:S(2)}, u32[]{:S(2)}) collective-permute-start(bf16[640,384]{1,0:T(8,128)(2,1)S(1)} %bitcast.41), channel_id=1, source_target_pairs={{0,16},{16,0},{1,17},{17,1},{2,18},{18,2},{3,19},{19,3},{4,20},{20... | collective-permute-start | bytes 1474568 | tf_op jit(solution)/shard_map/ppermute | solution.py:33
  74.2 1.5 collective-permute-done.9.other_ref
  75.7 5.8 %shard_map.235 = (bf16[320,768]{1,0:T(8,128)(2,1)S(1)}, bf16[320,768]{1,0:T(8,128)(2,1)S(1)}, bf16[160,768]{1,0:T(8,128)(2,1)S(1)}, f32[160,16]{1,0:T(8,128)S(1)...) custom-call(s32[1]{0:T(128)} %bitcast.refs_1_.place_ref.refs_0_, ...), custom_call_target="tpu_custom_call" | custom-call | tf_op jit(solution)/shard_map/pallas_call | solution.py:730
  82.0 1.5 collective-permute-done.10.refs_2_
  83.5 1.3 shard_map.236
  84.8 16.3 %all_to_all.21 = bf16[16,40,384]{2,1,0:T(8,128)(2,1)S(1)} all-to-all(bf16[16,40,384]{2,1,0:T(8,128)(2,1)S(1)} %bitcast.45), channel_id=1, replica_groups=mesh['dp'=2,'expert'=16] {'expert'}, dimensions={0} | all-to-all | bytes 983040 | tf_op jit(solution)/shard_map/all_to_all | solution.py:43
  101.6 0.8 copy-done.10
  102.4 2.5 %collective-permute-start.11 = (bf16[128,768]{1,0:T(8,128)(2,1)S(1)}, bf16[128,768]{1,0:T(8,128)(2,1)S(1)}, u32[]{:S(2)}, u32[]{:S(2)}) collective-permute-start(bf16[128,768]{1,0:T(8,128)(2,1)S(1)} %get-tuple-element.127.refs_0_), channel_id=1, source_target_pairs={{0,16},{16,0},{1,17},{17,1},{2,18},{18,2},{3,19},{19,3},{4,20},{20... | collective-permute-start | bytes 589832 | tf_op jit(solution)/shard_map/ppermute | solution.py:33
  104.8 1.3 collective-permute-start.12
  106.1 3.1 %shard_map.239 = (f32[768,576]{1,0:T(8,128)S(1)}, f32[192,768]{1,0:T(8,128)S(1)}, f32[128,768]{1,0:T(8,128)S(1)}, bf16[128,768]{1,0:T(8,128)(2,1)S(1)}, bf16[256...) custom-call(bf16[128,768]{1,0:T(8,128)(2,1)S(1)} %get-tuple-element.127.refs_0_, ...), custom_call_target="tpu_custom_call" | custom-call | flops 1000000 | bytes 1000000 | tf_op jit(solution)/shard_map/pallas_call | solution.py:104
  109.2 4.0 %collective-permute-done.12.refs_0_ = bf16[128,768]{1,0:T(8,128)(2,1)S(1)} collective-permute-done((bf16[128,768]{1,0:T(8,128)(2,1)S(1)}, bf16[128,768]{1,0:T(8,128)(2,1)S(1)}, u32[]{:S(2)}, u32[]{:S(2)}) %collective-permute-start.12) | collective-permute-done | bytes 196640 | tf_op jit(solution)/shard_map/ppermute | solution.py:39
  113.2 0.8 collective-permute-start.14
  114.1 1.1 collective-permute-done.14.refs_1_
  115.1 2.2 %shard_map.240 = (f32[128,768]{1,0:T(8,128)S(1)}, bf16[128,768]{1,0:T(8,128)(2,1)S(1)}, bf16[256,576]{1,0:T(8,128)(2,1)S(1)}, f32[1,768]{1,0:T(1,128)S(1)}, f32[3,256]{1,0:T(4,128)S(1)}) custom-call(bf16[128,768]{1,0:T(8,128)(2,1)S(1)} %collective-permute-done.12.refs_0_, bf16[128,768]{1,0:T(8,128)(2,1)S(1)} %collective-permute-done.14.refs_1_, ...), custom_call_target="tpu_custom_call" | custom-call | flops 1000000 | bytes 1000000 | tf_op jit(solution)/shard_map/pallas_call | solution.py:104
  117.8 1.8 %shard_map.241 = (bf16[8,128,640]{2,1,0:T(8,128)(2,1)S(1)}, bf16[768,640]{1,0:T(8,128)(2,1)}, bf16[192,768]{1,0:T(8,128)(2,1)}) custom-call(bf16[128,768]{1,0:T(8,128)(2,1)S(1)} %collective-permute-done.12.refs_0_, bf16[128,768]{1,0:T(8,128)(2,1)S(1)} %collective-permute-done.14.refs_1_, bf16[256,192]{1,0:T(8,128)(2,1)S(1)} %get-tuple-element.136.refs_2_, ...), custom_call_target="tpu_custom_call" | custom-call | flops 1000000 | bytes 1000000 | tf_op jit(solution)/shard_map/pallas_call | solution.py:104
  119.6 1.1 copy-done.5
  121.4 6.0 %all-to-all-start.3 = ((bf16[8,128,640]{2,1,0:T(8,128)(2,1)}), bf16[8,128,640]{2,1,0:T(8,128)(2,1)S(1)}, u32[]{:S(2)}, u32[]{:S(2)}) async-start(bf16[8,128,640]{2,1,0:T(8,128)(2,1)} %copy-done.5), calls=%async_computation.3 | async-start | bytes 2621440 | tf_op jit(solution)/shard_map/all_to_all | solution.py:49
  127.6 4.9 %convolution_bitcast_fusion.1 = f32[1,768,1536]{2,1,0:T(8,128)} fusion(bf16[320,768]{1,0:T(8,128)(2,1)S(1)} %get-tuple-element.117, bf16[320,1536]{1,0:T(8,128)(2,1)} %copy-done.6), kind=kOutput, calls=%fused_computation.1 | convolution fusion | flops 754974720 | bytes 6193152 | tf_op jit(solution)/shard_map/dot_general | solution.py:19
  133.3 2.2 %collective-permute-start.16 = (bf16[128,768]{1,0:T(8,128)(2,1)}, bf16[128,768]{1,0:T(8,128)(2,1)S(1)}, u32[]{:S(2)}, u32[]{:S(2)}) collective-permute-start(bf16[128,768]{1,0:T(8,128)(2,1)} %add_convert_fusion), channel_id=1, source_target_pairs={{0,12},{1,13},{2,14},{3,15},{4,8},{5,9},{6,10},{7,11},{8,4},{9,5},... | collective-permute-start | bytes 589832 | tf_op jit(solution)/shard_map/ppermute | solution.py:39
  135.5 3.6 %convolution_bitcast_fusion = f32[1,1536,768]{2,1,0:T(8,128)} fusion(bf16[320,1536]{1,0:T(8,128)(2,1)S(1)} %copy-done.19, bf16[320,768]{1,0:T(8,128)(2,1)S(1)} %copy-done.21), kind=kOutput, calls=%fused_computation | convolution fusion | flops 754974720 | bytes 6193152 | tf_op jit(solution)/shard_map/dot_general | solution.py:19
  139.2 1.0 shard_map.237
  140.2 10.8 %collective-permute-done.16 = bf16[128,768]{1,0:T(8,128)(2,1)S(1)} collective-permute-done((bf16[128,768]{1,0:T(8,128)(2,1)}, bf16[128,768]{1,0:T(8,128)(2,1)S(1)}, u32[]{:S(2)}, u32[]{:S(2)}) %collective-permute-start.16) | collective-permute-done | bytes 196640 | tf_op jit(solution)/shard_map/ppermute | solution.py:39
  151.7 1.0 collective-permute-start.18
  152.7 2.5 %collective-permute-start.19 = (bf16[24,640]{1,0:T(8,128)(2,1)S(1)}, bf16[24,640]{1,0:T(8,128)(2,1)S(1)}, u32[]{:S(2)}, u32[]{:S(2)}) collective-permute-start(bf16[24,640]{1,0:T(8,128)(2,1)S(1)} %get-tuple-element.158), channel_id=1, source_target_pairs={{0,24},{1,25},{2,26},{3,27},{4,28},{5,29},{6,30},{7,31},{8,16},{9,... | collective-permute-start | bytes 92168 | tf_op jit(solution)/shard_map/ppermute | solution.py:632
  155.4 1.9 %fusion.8 = bf16[1,128,768]{2,1,0:T(8,128)(2,1)} fusion(f32[128,768]{1,0:T(8,128)} %copy-done.10, f32[128]{0:T(128)S(1)} %broadcast_multiply_fusion, f32[128]{0:T(128)S(1)} %add_rsqrt_fusion, f32[768]{0:T(1024)S(1)} %slice_reduce_fusion, f32[128,768]{1,0:T(8,128)S(1)} %convert_element_type.30, f32[128,768]{1,0:T(8,128)S(1)} %copy-done.4, ...), kind=kLoop, calls=%fused_computation.15 | loop fusion | flops 1081344 | bytes 1773568 | tf_op jit(solution)/shard_map/reshape | solution.py:835
  157.9 0.9 shard_map.243
  (80 shorter events, 6.6 us)
Async XLA Ops:
  0.6 22.3 %copy-start.24 = (f32[32,12]{0,1:T(8,128)S(1)}, f32[32,12]{0,1:T(8,128)}, u32[]{:S(2)}) copy-start(f32[32,12]{0,1:T(8,128)} %param.20) | copy-start | bytes 4612
  0.7 22.3 %copy-start.25 = (s32[1,128,1]{1,2,0:T(1,128)S(1)}, s32[1,128,1]{1,2,0:T(1,128)}, u32[]{:S(2)}) copy-start(s32[1,128,1]{1,2,0:T(1,128)} %param.26) | copy-start | bytes 1540
  0.7 14.8 %collective-permute-start = (bf16[128,768]{1,0:T(8,128)(2,1)}, bf16[128,768]{1,0:T(8,128)(2,1)S(1)}, u32[]{:S(2)}, u32[]{:S(2)}) collective-permute-start(bf16[128,768]{1,0:T(8,128)(2,1)} %bitcast.32), channel_id=1, source_target_pairs={{0,12},{1,13},{2,14},{3,15},{4,8},{5,9},{6,10},{7,11},{8,4},{9,5},... | collective-permute-start | bytes 589832 | tf_op jit(solution)/shard_map/ppermute | solution.py:39
  6.0 7.8 %collective-permute-start.1 = (bf16[24,640]{1,0:T(8,128)(2,1)}, bf16[24,640]{1,0:T(8,128)(2,1)S(1)}, u32[]{:S(2)}, u32[]{:S(2)}) collective-permute-start(bf16[24,640]{1,0:T(8,128)(2,1)} %get-tuple-element.92), channel_id=1, source_target_pairs={{0,8},{1,9},{2,10},{3,11},{4,12},{5,13},{6,14},{7,15},{8,0},{9,1},... | collective-permute-start | bytes 92168 | tf_op jit(solution)/shard_map/ppermute | solution.py:632
  6.1 7.7 %collective-permute-start.2 = (bf16[24,640]{1,0:T(8,128)(2,1)}, bf16[24,640]{1,0:T(8,128)(2,1)S(1)}, u32[]{:S(2)}, u32[]{:S(2)}) collective-permute-start(bf16[24,640]{1,0:T(8,128)(2,1)} %get-tuple-element.93), channel_id=1, source_target_pairs={{0,16},{1,17},{2,18},{3,19},{4,20},{5,21},{6,22},{7,23},{8,24},{9,... | collective-permute-start | bytes 92168 | tf_op jit(solution)/shard_map/ppermute | solution.py:632
  7.1 8.3 %collective-permute-start.3 = (bf16[24,640]{1,0:T(8,128)(2,1)}, bf16[24,640]{1,0:T(8,128)(2,1)S(1)}, u32[]{:S(2)}, u32[]{:S(2)}) collective-permute-start(bf16[24,640]{1,0:T(8,128)(2,1)} %get-tuple-element.94), channel_id=1, source_target_pairs={{0,24},{1,25},{2,26},{3,27},{4,28},{5,29},{6,30},{7,31},{8,16},{9,... | collective-permute-start | bytes 92168 | tf_op jit(solution)/shard_map/ppermute | solution.py:632
  15.4 0.8 copy-start.15
  16.2 0.8 copy-start.16
  18.1 24.0 %copy-start = (bf16[1,128,768]{2,1,0:T(8,128)(2,1)S(1)}, bf16[1,128,768]{2,1,0:T(8,128)(2,1)}, u32[]{:S(2)}) copy-start(bf16[1,128,768]{2,1,0:T(8,128)(2,1)} %param.14) | copy-start | bytes 589828
  18.1 27.1 %copy-start.17 = (s32[1,256]{1,0:T(1,128)S(1)}, s32[1,256]{1,0:T(1,128)}, u32[]{:S(2)}) copy-start(s32[1,256]{1,0:T(1,128)} %refs_1_.4) | copy-start | bytes 3076
  18.1 20.8 %all-to-all-start = ((bf16[8,128,640]{2,1,0:T(8,128)(2,1)}), bf16[8,128,640]{2,1,0:T(8,128)(2,1)S(1)}, u32[]{:S(2)}, u32[]{:S(2)}) async-start(bf16[8,128,640]{2,1,0:T(8,128)(2,1)} %shard_map.230), calls=%async_computation | async-start | bytes 2621440 | tf_op jit(solution)/shard_map/all_to_all | solution.py:49
  22.0 4.2 %collective-permute-start.4 = (bf16[128,768]{1,0:T(8,128)(2,1)S(1)}, bf16[128,768]{1,0:T(8,128)(2,1)S(1)}, u32[]{:S(2)}, u32[]{:S(2)}) collective-permute-start(bf16[128,768]{1,0:T(8,128)(2,1)S(1)} %collective-permute-done.refs_3_.refs_7_.refs_5_), channel_id=1, source_target_pairs={{0,16},{16,0},{1,17},{17,1},{2,18},{18,2},{3,19},{19,3},{4,20},{20... | collective-permute-start | bytes 589832 | tf_op jit(solution)/shard_map/ppermute | solution.py:33
  23.1 28.1 %copy-start.7 = (bf16[1,128,768]{2,1,0:T(8,128)(2,1)S(1)}, bf16[1,128,768]{2,1,0:T(8,128)(2,1)}, u32[]{:S(2)}) copy-start(bf16[1,128,768]{2,1,0:T(8,128)(2,1)} %param.27) | copy-start | bytes 589828
  24.7 0.8 copy-start.8
  25.5 0.7 copy-start.11
  38.9 12.3 %copy-start.9 = (bf16[640,512]{1,0:T(8,128)(2,1)S(1)}, bf16[640,512]{1,0:T(8,128)(2,1)}, u32[]{:S(2)}) copy-start(bf16[640,512]{1,0:T(8,128)(2,1)} %copy-done.8) | copy-start | bytes 1966084
  40.6 2.6 %collective-permute-start.5 = (bf16[128,768]{1,0:T(8,128)(2,1)S(1)}, bf16[128,768]{1,0:T(8,128)(2,1)S(1)}, u32[]{:S(2)}, u32[]{:S(2)}) collective-permute-start(bf16[128,768]{1,0:T(8,128)(2,1)S(1)} %get-tuple-element.104), channel_id=1, source_target_pairs={{0,16},{16,0},{1,17},{17,1},{2,18},{18,2},{3,19},{19,3},{4,20},{20... | collective-permute-start | bytes 589832 | tf_op jit(solution)/shard_map/ppermute | solution.py:33
  42.1 3.2 %collective-permute-start.6 = (bf16[128,768]{1,0:T(8,128)(2,1)S(1)}, bf16[128,768]{1,0:T(8,128)(2,1)S(1)}, u32[]{:S(2)}, u32[]{:S(2)}) collective-permute-start(bf16[128,768]{1,0:T(8,128)(2,1)S(1)} %bitcast.33), channel_id=1, source_target_pairs={{0,16},{16,0},{1,17},{17,1},{2,18},{18,2},{3,19},{19,3},{4,20},{20... | collective-permute-start | bytes 589832 | tf_op jit(solution)/shard_map/ppermute | solution.py:33
  43.2 8.0 %collective-permute-start.8 = (bf16[128,768]{1,0:T(8,128)(2,1)S(1)}, bf16[128,768]{1,0:T(8,128)(2,1)S(1)}, u32[]{:S(2)}, u32[]{:S(2)}) collective-permute-start(bf16[128,768]{1,0:T(8,128)(2,1)S(1)} %add_convert_fusion.1), channel_id=1, source_target_pairs={{0,12},{1,13},{2,14},{3,15},{4,8},{5,9},{6,10},{7,11},{8,4},{9,5},... | collective-permute-start | bytes 589832 | tf_op jit(solution)/shard_map/ppermute | solution.py:39
  45.3 30.4 %copy-start.1 = (bf16[1,768,1536]{2,1,0:T(8,128)(2,1)S(1)}, bf16[1,768,1536]{2,1,0:T(8,128)(2,1)}, u32[]{:S(2)}) copy-start(bf16[1,768,1536]{2,1,0:T(8,128)(2,1)} %param.23) | copy-start | bytes 7077892
  45.3 30.4 %copy-start.2 = (bf16[1,1536,768]{2,1,0:T(8,128)(2,1)S(1)}, bf16[1,1536,768]{2,1,0:T(8,128)(2,1)}, u32[]{:S(2)}) copy-start(bf16[1,1536,768]{2,1,0:T(8,128)(2,1)} %param.24) | copy-start | bytes 7077892
  46.7 4.5 %collective-permute-start.7 = (bf16[128,768]{1,0:T(8,128)(2,1)S(1)}, bf16[128,768]{1,0:T(8,128)(2,1)S(1)}, u32[]{:S(2)}, u32[]{:S(2)}) collective-permute-start(bf16[128,768]{1,0:T(8,128)(2,1)S(1)} %get-tuple-element.110), channel_id=1, source_target_pairs={{0,16},{16,0},{1,17},{17,1},{2,18},{18,2},{3,19},{19,3},{4,20},{20... | collective-permute-start | bytes 589832 | tf_op jit(solution)/shard_map/ppermute | solution.py:33
  52.2 23.5 %copy-start.13 = (f32[128,1]{1,0:T(8,128)}, f32[128,1]{1,0:T(8,128)S(1)}, u32[]{:S(2)}) copy-start(f32[128,1]{1,0:T(8,128)S(1)} %get-tuple-element.124.refs_3_) | copy-start | bytes 1540
  71.2 4.5 %collective-permute-start.9 = (bf16[640,384]{1,0:T(8,128)(2,1)S(1)}, bf16[640,384]{1,0:T(8,128)(2,1)S(1)}, u32[]{:S(2)}, u32[]{:S(2)}) collective-permute-start(bf16[640,384]{1,0:T(8,128)(2,1)S(1)} %bitcast.41), channel_id=1, source_target_pairs={{0,16},{16,0},{1,17},{17,1},{2,18},{18,2},{3,19},{19,3},{4,20},{20... | collective-permute-start | bytes 1474568 | tf_op jit(solution)/shard_map/ppermute | solution.py:33
  81.5 20.1 %copy-start.6 = (bf16[320,1536]{1,0:T(8,128)(2,1)}, bf16[320,1536]{1,0:T(8,128)(2,1)S(1)}, u32[]{:S(2)}) copy-start(bf16[320,1536]{1,0:T(8,128)(2,1)S(1)} %get-tuple-element.167) | copy-start | bytes 2949124
  81.5 20.1 %copy-start.18 = (bf16[320,1536]{1,0:T(8,128)(2,1)}, bf16[320,1536]{1,0:T(8,128)(2,1)S(1)}, u32[]{:S(2)}) copy-start(bf16[320,1536]{1,0:T(8,128)(2,1)S(1)} %get-tuple-element.168) | copy-start | bytes 2949124
  81.5 20.1 %copy-start.20 = (bf16[320,768]{1,0:T(8,128)(2,1)}, bf16[320,768]{1,0:T(8,128)(2,1)S(1)}, u32[]{:S(2)}) copy-start(bf16[320,768]{1,0:T(8,128)(2,1)S(1)} %get-tuple-element.169) | copy-start | bytes 1474564
  81.5 2.0 %collective-permute-start.10 = (bf16[2,160,768]{2,1,0:T(8,128)(2,1)S(1)}, bf16[2,160,768]{2,1,0:T(8,128)(2,1)S(1)}, u32[]{:S(2)}, u32[]{:S(2)}) collective-permute-start(bf16[2,160,768]{2,1,0:T(8,128)(2,1)S(1)} %get-tuple-element.116), channel_id=1, source_target_pairs={{0,16},{16,0},{1,17},{17,1},{2,18},{18,2},{3,19},{19,3},{4,20},{20... | collective-permute-start | bytes 1474568 | tf_op jit(solution)/shard_map/ppermute | solution.py:33
  101.6 0.8 copy-start.10
  102.4 3.8 %collective-permute-start.11 = (bf16[128,768]{1,0:T(8,128)(2,1)S(1)}, bf16[128,768]{1,0:T(8,128)(2,1)S(1)}, u32[]{:S(2)}, u32[]{:S(2)}) collective-permute-start(bf16[128,768]{1,0:T(8,128)(2,1)S(1)} %get-tuple-element.127.refs_0_), channel_id=1, source_target_pairs={{0,16},{16,0},{1,17},{17,1},{2,18},{18,2},{3,19},{19,3},{4,20},{20... | collective-permute-start | bytes 589832 | tf_op jit(solution)/shard_map/ppermute | solution.py:33
  104.8 8.4 %collective-permute-start.12 = (bf16[128,768]{1,0:T(8,128)(2,1)S(1)}, bf16[128,768]{1,0:T(8,128)(2,1)S(1)}, u32[]{:S(2)}, u32[]{:S(2)}) collective-permute-start(bf16[128,768]{1,0:T(8,128)(2,1)S(1)} %get-tuple-element.127.refs_0_), channel_id=1, source_target_pairs={{0,12},{1,13},{2,14},{3,15},{4,8},{5,9},{6,10},{7,11},{8,4},{9,5},... | collective-permute-start | bytes 589832 | tf_op jit(solution)/shard_map/ppermute | solution.py:39
  109.2 8.2 %copy-start.3 = (f32[128,768]{1,0:T(8,128)}, f32[128,768]{1,0:T(8,128)S(1)}, u32[]{:S(2)}) copy-start(f32[128,768]{1,0:T(8,128)S(1)} %get-tuple-element.131) | copy-start | bytes 1179652
  109.2 10.4 %copy-start.22 = (bf16[128,768]{1,0:T(8,128)(2,1)}, bf16[128,768]{1,0:T(8,128)(2,1)S(1)}, u32[]{:S(2)}) copy-start(bf16[128,768]{1,0:T(8,128)(2,1)S(1)} %get-tuple-element.134) | copy-start | bytes 589828
  113.2 1.9 %collective-permute-start.14 = (bf16[128,768]{1,0:T(8,128)(2,1)S(1)}, bf16[128,768]{1,0:T(8,128)(2,1)S(1)}, u32[]{:S(2)}, u32[]{:S(2)}) collective-permute-start(bf16[128,768]{1,0:T(8,128)(2,1)S(1)} %collective-permute-done.12.refs_0_), channel_id=1, source_target_pairs={{0,16},{16,0},{1,17},{17,1},{2,18},{18,2},{3,19},{19,3},{4,20},{20... | collective-permute-start | bytes 589832 | tf_op jit(solution)/shard_map/ppermute | solution.py:33
  117.4 3.3 %collective-permute-start.15 = (bf16[128,768]{1,0:T(8,128)(2,1)S(1)}, bf16[128,768]{1,0:T(8,128)(2,1)S(1)}, u32[]{:S(2)}, u32[]{:S(2)}) collective-permute-start(bf16[128,768]{1,0:T(8,128)(2,1)S(1)} %get-tuple-element.150), channel_id=1, source_target_pairs={{0,16},{16,0},{1,17},{17,1},{2,18},{18,2},{3,19},{19,3},{4,20},{20... | collective-permute-start | bytes 589832 | tf_op jit(solution)/shard_map/ppermute | solution.py:33
  119.6 1.1 copy-start.5
  121.4 29.6 %all-to-all-start.3 = ((bf16[8,128,640]{2,1,0:T(8,128)(2,1)}), bf16[8,128,640]{2,1,0:T(8,128)(2,1)S(1)}, u32[]{:S(2)}, u32[]{:S(2)}) async-start(bf16[8,128,640]{2,1,0:T(8,128)(2,1)} %copy-done.5), calls=%async_computation.3 | async-start | bytes 2621440 | tf_op jit(solution)/shard_map/all_to_all | solution.py:49
  127.6 5.0 %copy-start.23 = (bf16[128,768]{1,0:T(8,128)(2,1)S(1)}, bf16[128,768]{1,0:T(8,128)(2,1)}, u32[]{:S(2)}) copy-start(bf16[128,768]{1,0:T(8,128)(2,1)} %copy-done.22) | copy-start | bytes 589828
  127.6 7.9 %copy-start.19 = (bf16[320,1536]{1,0:T(8,128)(2,1)S(1)}, bf16[320,1536]{1,0:T(8,128)(2,1)}, u32[]{:S(2)}) copy-start(bf16[320,1536]{1,0:T(8,128)(2,1)} %copy-done.18) | copy-start | bytes 2949124
  127.6 7.9 %copy-start.21 = (bf16[320,768]{1,0:T(8,128)(2,1)S(1)}, bf16[320,768]{1,0:T(8,128)(2,1)}, u32[]{:S(2)}) copy-start(bf16[320,768]{1,0:T(8,128)(2,1)} %copy-done.20) | copy-start | bytes 1474564
  132.6 22.6 %collective-permute-start.13 = (bf16[128,768]{1,0:T(8,128)(2,1)S(1)}, bf16[128,768]{1,0:T(8,128)(2,1)S(1)}, u32[]{:S(2)}, u32[]{:S(2)}) collective-permute-start(bf16[128,768]{1,0:T(8,128)(2,1)S(1)} %copy-done.23), channel_id=1, source_target_pairs={{0,16},{16,0},{1,17},{17,1},{2,18},{18,2},{3,19},{19,3},{4,20},{20... | collective-permute-start | bytes 589832 | tf_op jit(solution)/shard_map/ppermute | solution.py:33
  133.3 17.7 %collective-permute-start.16 = (bf16[128,768]{1,0:T(8,128)(2,1)}, bf16[128,768]{1,0:T(8,128)(2,1)S(1)}, u32[]{:S(2)}, u32[]{:S(2)}) collective-permute-start(bf16[128,768]{1,0:T(8,128)(2,1)} %add_convert_fusion), channel_id=1, source_target_pairs={{0,12},{1,13},{2,14},{3,15},{4,8},{5,9},{6,10},{7,11},{8,4},{9,5},... | collective-permute-start | bytes 589832 | tf_op jit(solution)/shard_map/ppermute | solution.py:39
  135.5 3.6 %copy-start.12 = (bf16[2,128,640]{2,1,0:T(8,128)(2,1)S(1)}, bf16[2,128,640]{2,1,0:T(8,128)(2,1)}, u32[]{:S(2)}) copy-start(bf16[2,128,640]{2,1,0:T(8,128)(2,1)} %copy-done.11) | copy-start | bytes 983044
  135.5 3.6 %copy-start.14 = (f32[128,1]{1,0:T(8,128)S(1)}, f32[128,1]{1,0:T(8,128)}, u32[]{:S(2)}) copy-start(f32[128,1]{1,0:T(8,128)} %copy-done.13) | copy-start | bytes 1540
  139.1 16.1 %copy-start.4 = (f32[128,768]{1,0:T(8,128)S(1)}, f32[128,768]{1,0:T(8,128)}, u32[]{:S(2)}) copy-start(f32[128,768]{1,0:T(8,128)} %copy-done.3) | copy-start | bytes 1179652
  151.7 5.6 %collective-permute-start.17 = (bf16[24,640]{1,0:T(8,128)(2,1)S(1)}, bf16[24,640]{1,0:T(8,128)(2,1)S(1)}, u32[]{:S(2)}, u32[]{:S(2)}) collective-permute-start(bf16[24,640]{1,0:T(8,128)(2,1)S(1)} %get-tuple-element.156), channel_id=1, source_target_pairs={{0,8},{1,9},{2,10},{3,11},{4,12},{5,13},{6,14},{7,15},{8,0},{9,1},... | collective-permute-start | bytes 92168 | tf_op jit(solution)/shard_map/ppermute | solution.py:632
  151.7 5.6 %collective-permute-start.18 = (bf16[24,640]{1,0:T(8,128)(2,1)S(1)}, bf16[24,640]{1,0:T(8,128)(2,1)S(1)}, u32[]{:S(2)}, u32[]{:S(2)}) collective-permute-start(bf16[24,640]{1,0:T(8,128)(2,1)S(1)} %get-tuple-element.157), channel_id=1, source_target_pairs={{0,16},{1,17},{2,18},{3,19},{4,20},{5,21},{6,22},{7,23},{8,24},{9,... | collective-permute-start | bytes 92168 | tf_op jit(solution)/shard_map/ppermute | solution.py:632
  152.7 5.2 %collective-permute-start.19 = (bf16[24,640]{1,0:T(8,128)(2,1)S(1)}, bf16[24,640]{1,0:T(8,128)(2,1)S(1)}, u32[]{:S(2)}, u32[]{:S(2)}) collective-permute-start(bf16[24,640]{1,0:T(8,128)(2,1)S(1)} %get-tuple-element.158), channel_id=1, source_target_pairs={{0,24},{1,25},{2,26},{3,27},{4,28},{5,29},{6,30},{7,31},{8,16},{9,... | collective-permute-start | bytes 92168 | tf_op jit(solution)/shard_map/ppermute | solution.py:632

commit v4 on v3

--- a/solution.py
+++ b/solution.py
@@ -81,7 +81,7 @@
         return self.target[index]
 
 
-def kernel_call(body, outs, *args, scalars=0, late=(), limit=VMEM_BYTES):
+def kernel_call(body, outs, *args, scalars=0, late=(), limit=VMEM_BYTES, held=()):
     count = len(args)
     late = sorted(late)
 
@@ -91,7 +91,7 @@
         scratch = refs[count + len(outs) :]
         for n, i in enumerate(late):
             ins[i] = LateRef(ins[i], scratch[n], scratch[-1].at[n])
-        body(*ins, *out_refs)
+        body(*ins, *out_refs, *scratch[len(late) : len(late) + len(held)])
         for i in late:
             ins[i].wait()
 
@@ -99,6 +99,7 @@
     for i in late:
         spaces[i] = pltpu.HBM
     scratch = [pltpu.VMEM(args[i].shape, args[i].dtype) for i in late]
+    scratch += [pltpu.VMEM(shape, dtype) for shape, dtype in held]
     if late:
         scratch.append(pltpu.SemaphoreType.DMA((len(late),)))
     return pl.pallas_call(
@@ -123,7 +124,7 @@
 
 def pack_weights(group_ref, q_ref, k_ref, v_ref, router_ref, one_ref, two_ref, wout_ref, docs_ref,
                  *refs):
-    *out_refs, keep_ref = refs
+    keep_ref, *out_refs = refs
     rows, width = q_ref.shape
     experts = router_ref.shape[0]
     cols = width // 4
@@ -148,9 +149,11 @@
         jnp.concatenate([w[:, j * cols : (j + 1) * cols] for w in weights] + [small], axis=1)
         for j in range(4)
     ]
-    for d, out_ref in enumerate(out_refs):
+    for d, out_ref in enumerate(out_refs, 1):
         out_ref[...] = choose(group_ref[0] ^ d, pieces)
-    keep_ref[...] = wout_ref[...]
+    used = pieces[0].shape[1]
+    keep_ref[:, :used] = choose(group_ref[0], pieces)
+    keep_ref[:, used:] = wout_ref[...]
 
 
 def put_rows(ref, dest, value):
@@ -178,14 +181,14 @@
     return jnp.concatenate([held[4 * rows : 5 * rows], jnp.concatenate(tail, axis=0)], axis=1)
 
 
-def spread_weights(group_ref, p0_ref, p1_ref, p2_ref, p3_ref, wout_ref, out_ref):
+def spread_weights(group_ref, own_ref, p1_ref, p2_ref, p3_ref, out_ref):
     dests, _, wide = out_ref.shape
-    rows, used = p0_ref.shape
-    pieces = [ref[...] for ref in (p0_ref, p1_ref, p2_ref, p3_ref)]
+    rows, used = p1_ref.shape
+    pieces = [own_ref[:, :used]] + [ref[...] for ref in (p1_ref, p2_ref, p3_ref)]
     value = jnp.concatenate([choose(group_ref[0] ^ j, pieces) for j in range(4)], axis=0)
     if wide > used:
         value = jnp.concatenate([value, jnp.zeros((4 * rows, wide - used), BF16)], axis=1)
-    last = wout_ref[...]
+    last = own_ref[:, used:]
     for dest in range(dests):
         out_ref[dest, : 4 * rows] = value
         put_rows(out_ref, dest, last)
@@ -332,40 +335,34 @@
     gate_ref[...] = jnp.sum(probs * chosen_ref[...], axis=1, keepdims=True)
 
 
-def run_expert(capacity, place_ref, own_ref, other_ref, router_ref, inner_ref, outer_ref,
-               buf_ref, dslot_ref, g_ref, probs_ref, gate_ref, hidden_ref, dpre_ref, keep_ref,
-               send_ref, acc_ref):
-    step = pl.program_id(0)
+def run_expert(capacity, place_ref, own_ref, other_ref, router_ref, inner_ref, outer_ref, buf_ref,
+               dslot_ref, g_ref, probs_ref, gate_ref, hidden_ref, dpre_ref, keep_ref, send_ref):
     slots = buf_ref.shape[0] // 2
+    half = own_ref.shape[1]
     experts = router_ref.shape[1]
     pad = own_ref.shape[0] // (slots // capacity)
-
-    @pl.when(step == 0)
-    def _():
-        shape = (slots, own_ref.shape[0])
-        row = iota(shape, 0)
-        source = row // capacity
-        wanted = source * pad + (row - source * capacity)
-        select = [(iota(shape, 1) == wanted + i * capacity).astype(BF16) for i in range(4)]
-        mine = (iota((1, experts), 1) == place_ref[0]).astype(F32)
-        for side, ref in enumerate((own_ref, other_ref)):
-            at = side * slots
-            rows = ref[...]
-            buffers, g = [
-                jnp.concatenate([dot(select[i], rows), dot(select[i + 2], rows)], axis=1)
-                for i in range(2)
-            ]
-            buffers = buffers.astype(BF16)
-            buf_ref[at : at + slots] = buffers
-            probs = jax.nn.softmax(dot(buffers, router_ref[...]), axis=-1)
-            gate = jnp.sum(probs * mine, axis=1, keepdims=True)
-            dslot_ref[at : at + slots] = (gate * g).astype(BF16)
-            if side == 0:
-                g_ref[...] = g.astype(BF16)
-                probs_ref[...] = probs
-                gate_ref[...] = gate
-        acc_ref[...] = jnp.zeros_like(acc_ref)
-
+    shape = (4 * slots, own_ref.shape[0])
+    row = iota(shape, 0)
+    part = row // slots
+    inside = row - part * slots
+    source = inside // capacity
+    wanted = source * pad + part * capacity + (inside - source * capacity)
+    select = (iota(shape, 1) == wanted).astype(BF16)
+    rows = dot(select, jnp.concatenate([own_ref[...], other_ref[...]], axis=1))
+    mine = (iota((1, experts), 1) == place_ref[0]).astype(F32)
+    for side in range(2):
+        at = side * slots
+        cut = rows[:, side * half : (side + 1) * half]
+        buffers = jnp.concatenate([cut[:slots], cut[2 * slots : 3 * slots]], axis=1).astype(BF16)
+        g = jnp.concatenate([cut[slots : 2 * slots], cut[3 * slots :]], axis=1)
+        buf_ref[at : at + slots] = buffers
+        probs = jax.nn.softmax(dot(buffers, router_ref[...]), axis=-1)
+        gate = jnp.sum(probs * mine, axis=1, keepdims=True)
+        dslot_ref[at : at + slots] = (gate * g).astype(BF16)
+        if side == 0:
+            g_ref[...] = g.astype(BF16)
+            probs_ref[...] = probs
+            gate_ref[...] = gate
     inner = inner_ref[...]
     outer = outer_ref[...]
     pre = dot(buf_ref[...], inner)
@@ -375,13 +372,12 @@
     slope = cdf + pre * jnp.exp(-0.5 * pre * pre) * 0.3989422804014327
     dpre = (dot(dslot_ref[...], outer, ((1,), (1,))) * slope).astype(BF16)
     dpre_ref[...] = dpre
-    acc_ref[0] += dot(hidden, outer)
-    acc_ref[1] += dot(dpre, inner, ((1,), (1,)))
-
-    @pl.when(step == pl.num_programs(0) - 1)
-    def _():
-        keep_ref[...] = acc_ref[:, :slots]
-        send_ref[...] = acc_ref[:, slots:].astype(BF16)
+    result = dot(hidden, outer)
+    keep_ref[0] = result[:slots]
+    send_ref[0] = result[slots:].astype(BF16)
+    back = dot(dpre, inner, ((1,), (1,)))
+    keep_ref[1] = back[:slots]
+    send_ref[1] = back[slots:].astype(BF16)
 
 
 def finish_expert(capacity, place_ref, keep_ref, came_ref, buf_ref, g_ref, probs_ref, gate_ref,
@@ -409,23 +405,28 @@
     out_ref[...] = dot(expand, both).astype(BF16)
 
 
-def norm_two_backward(back_ref, spread_ref, middle_ref, gains_ref, g_ref, dmiddle_ref, da_ref,
-                      gain_ref):
+def middle_backward(back_ref, spread_ref, middle_ref, gains_ref, g_ref):
     middle = middle_ref[...]
     inverse = rms_inverse(middle)
     unit = middle * inverse
     rows = back_ref[...]
     grad_normed = jnp.concatenate([dot(spread_ref[i], rows) for i in range(2)], axis=1)
-    gain_ref[...] = jnp.sum(grad_normed * unit, axis=0, keepdims=True)
     dmiddle = g_ref[...].astype(F32) + norm_backward(grad_normed, unit, inverse, gains_ref[1:2])
-    dmiddle_ref[...] = dmiddle
+    return dmiddle, grad_normed * unit
+
+
+def norm_two_backward(back_ref, spread_ref, middle_ref, gains_ref, g_ref, da_ref, gain_ref):
+    dmiddle, scaled = middle_backward(back_ref, spread_ref, middle_ref, gains_ref, g_ref)
+    gain_ref[...] = jnp.sum(scaled, axis=0, keepdims=True)
     da_ref[...] = dmiddle.astype(BF16)
 
 
-def finish_layer(result_ref, spread_ref, middle_ref, gate_ref, out_ref):
-    rows = result_ref[...]
-    combined = jnp.concatenate([dot(spread_ref[i], rows) for i in range(2)], axis=1)
+def finish_layer(back_ref, spread_ref, later_ref, middle_ref, gains_ref, g_ref, gate_ref, out_ref,
+                 dmiddle_ref):
+    rows = back_ref[...]
+    combined = jnp.concatenate([dot(later_ref[i], rows) for i in range(2)], axis=1)
     out_ref[...] = (middle_ref[...] + gate_ref[...] * combined).astype(BF16)
+    dmiddle_ref[...] = middle_backward(back_ref, spread_ref, middle_ref, gains_ref, g_ref)[0]
 
 
 def attend_backward(scale, head_dim, own_ref, across_ref, wout_ref, qkv_ref, probs_ref, gains_ref,
@@ -546,7 +547,14 @@
 
 
 def finish_weights(own_heads, buckets, table_cols, group_ref, p0_ref, p1_ref, p2_ref, p3_ref,
-                   q_ref, k_ref, v_ref, router_ref, one_ref, two_ref, table_ref):
+                   grad_ref, core_ref, came_ref, dmiddle_ref, x_ref, gains_ref, q_ref, k_ref, v_ref,
+                   router_ref, one_ref, two_ref, table_ref, out_ref):
+    x = x_ref[...].astype(F32)
+    inverse = rms_inverse(x)
+    grad_normed = grad_ref[...] + core_ref[...].astype(F32) + came_ref[...].astype(F32)
+    out_ref[...] = (
+        dmiddle_ref[...] + norm_backward(grad_normed, x * inverse, inverse, gains_ref[0:1])
+    ).astype(BF16)
     rows, width = q_ref.shape
     experts = router_ref.shape[0]
     cols = width // 4
@@ -644,8 +652,8 @@
     own_tokens = tokens.reshape(toks, width)
     pair_tokens = swap_pair(own_tokens)
 
-    own_piece, *pieces, out_rows = kernel_call(
-        pack_weights, [((rows, used), BF16)] * 4 + [((rows, width), BF16)],
+    own_piece, *pieces = kernel_call(
+        pack_weights, [((rows, used + width), BF16)] + [((rows, used), BF16)] * 3,
         group_at, w_query, w_key, w_value, w_router.T, gain_one.reshape(1, rows),
         gain_two.reshape(1, rows), w_out, segment_ids, scalars=1, late=range(1, 9),
         limit=60 * 1024 * 1024,
@@ -654,7 +662,7 @@
     pair_tokens, own_piece, *pieces = lax.optimization_barrier((pair_tokens, own_piece, *pieces))
     (message,) = kernel_call(
         spread_weights, [((half, total, wide), BF16)],
-        group_at, own_piece, *pieces, out_rows, scalars=1,
+        group_at, own_piece, *pieces, scalars=1,
     )
     arrived = exchange_half(message)
 
@@ -714,35 +722,21 @@
 
     inner, outer = w_inner[0], w_outer[0]
     units = inner.shape[1]
-    chunk = units // 3
-    fixed = lambda shape: pl.BlockSpec(shape, lambda i: (0,) * len(shape))
-    outs = [
-        ((2 * slots, width), BF16, None),
-        ((2 * slots, width), BF16, None),
-        ((slots, width), BF16, None),
-        ((slots, experts), F32, None),
-        ((slots, 1), F32, None),
-        ((2 * slots, units), BF16, pl.BlockSpec((2 * slots, chunk), lambda i: (0, i))),
-        ((2 * slots, units), BF16, pl.BlockSpec((2 * slots, chunk), lambda i: (0, i))),
-        ((2, slots, width), F32, None),
-        ((2, slots, width), BF16, None),
-    ]
-    buffers, dslot, slot_g, slot_probs, slot_gate, hidden, dpre, keep, away = pl.pallas_call(
+    buffers, dslot, slot_g, slot_probs, slot_gate, hidden, dpre, keep, away = kernel_call(
         functools.partial(run_expert, capacity),
-        grid=(units // chunk,),
-        out_shape=[jax.ShapeDtypeStruct(shape, dtype) for shape, dtype, _ in outs],
-        in_specs=[
-            pl.BlockSpec(memory_space=pltpu.SMEM),
-            fixed((experts * pad, width // 2)),
-            fixed((experts * pad, width // 2)),
-            fixed((width, experts)),
-            pl.BlockSpec((width, chunk), lambda i: (0, i)),
-            pl.BlockSpec((chunk, width), lambda i: (i, 0)),
+        [
+            ((2 * slots, width), BF16),
+            ((2 * slots, width), BF16),
+            ((slots, width), BF16),
+            ((slots, experts), F32),
+            ((slots, 1), F32),
+            ((2 * slots, units), BF16),
+            ((2 * slots, units), BF16),
+            ((2, slots, width), F32),
+            ((2, slots, width), BF16),
         ],
-        out_specs=[spec or fixed(shape) for shape, _, spec in outs],
-        scratch_shapes=[pltpu.VMEM((2, 2 * slots, width), F32)],
-        compiler_params=pltpu.CompilerParams(vmem_limit_bytes=VMEM_BYTES),
-    )(place_at, incoming, swap_core(incoming), router_w, inner, outer)
+        place_at, incoming, swap_core(incoming), router_w, inner, outer, scalars=1,
+    )
     grad_outer = dot(hidden, dslot, ((0,), (0,)))
     grad_inner = dot(buffers, dpre, ((0,), (0,)))
     back, grad_router = kernel_call(
@@ -753,9 +747,8 @@
     )
     back = exchange(back.reshape(sources, pad, width // 2)).reshape(-1, width // 2)
 
-    grad_middle, grad_attn, grad_gain_two = kernel_call(
-        norm_two_backward,
-        [((toks, width), F32), ((toks, width), BF16), ((1, width), F32)],
+    grad_attn, grad_gain_two = kernel_call(
+        norm_two_backward, [((toks, width), BF16), ((1, width), F32)],
         back, spread, middle, gains, g_low,
     )
     pair_grad = swap_pair(grad_attn)
@@ -774,7 +767,7 @@
         own_tokens, own_across,
     )
     pair_grad, grad_w, own_away = lax.optimization_barrier((pair_grad, grad_w, away))
-    grad_normed = grad_normed + swap_core(own_away).astype(F32)
+    own_came = swap_core(own_away)
     pair_grads = (pair_grad, swap_core(pair_grad))
     keep, away, grad_qkv, pair_gain, pair_offsets = kernel_call(
         functools.partial(attend_backward, scale, head_dim), back_outs,
@@ -787,9 +780,9 @@
     )
     flat = [((width, used), BF16), ((cols, width), BF16)]
     if aligned:
-        message, _, _ = kernel_call(
+        (message,) = kernel_call(
             functools.partial(sum_weights_message, buckets, table_cols),
-            [((half, total, wide), BF16), *flat], *last,
+            [((half, total, wide), BF16)], *last, held=flat,
         )
     else:
         full, grad_out = kernel_call(
@@ -805,34 +798,34 @@
             ],
             axis=1,
         )
-    message, to_pair = lax.optimization_barrier((message, to_pair))
-    came = swap_pair(to_pair).astype(F32)
+    came = swap_pair(to_pair)
     arrived = exchange_half(message)
-    (final,) = kernel_call(
-        finish_layer, [((toks, width), BF16)], back, later, middle, gate
+    final, grad_middle = kernel_call(
+        finish_layer, [((toks, width), BF16), ((toks, width), F32)],
+        back, spread, later, middle, gains, g_low, gate,
+    )
+
+    arrived, grad_inner, grad_outer, final, grad_middle = lax.optimization_barrier(
+        (arrived, grad_inner, grad_outer, final, grad_middle)
     )
 
     out_grad_w, own_piece, *pieces = kernel_call(
         sum_arrived, [((rows, width), F32), ((rows, used), F32)] + [((rows, used), BF16)] * 3,
         group_at, arrived, scalars=1,
     )
-    came, own_piece = lax.optimization_barrier((came, own_piece))
     pieces = across_group(pieces)
-    query_grad, key_grad, value_grad, router_grad, one_grad, two_grad, table_grad = kernel_call(
+    query_grad, key_grad, value_grad, router_grad, one_grad, two_grad, table_grad, grad_input = kernel_call(
         functools.partial(finish_weights, own_heads, buckets, table_cols),
         [((rows, width), F32)] * 3
-        + [((experts, rows), F32), ((1, rows), F32), ((1, rows), F32), ((heads, buckets), F32)],
-        group_at, own_piece, *pieces, scalars=1,
-    )
-
-    x = own_tokens.astype(F32)
-    inverse_one = rms_inverse(x)
-    grad_input = grad_middle + norm_backward(
-        grad_normed + came, x * inverse_one, inverse_one, gains[0:1]
-    )
+        + [((experts, rows), F32), ((1, rows), F32), ((1, rows), F32), ((heads, buckets), F32)]
+        + [((toks, width), BF16)],
+        group_at, own_piece, *pieces, grad_normed, own_came, came, grad_middle, own_tokens, gains,
+        scalars=1,
+    )
+
     return (
         final.reshape(tokens.shape),
-        grad_input.astype(BF16).reshape(tokens.shape),
+        grad_input.reshape(tokens.shape),
         one_grad.reshape(rows),
         query_grad,
         key_grad,

time: 159 us -> 153 us (0.962)
  waiting for transfers between devices: 42.6 us -> 38 us
  other arithmetic: 3.02 us -> 0.77 us
    ppermute x4, waiting for transfers between devices: 18.4 us -> 8.33 us  [swap_pair(): return lax.ppermute(value, 'expert', [(i, i ^ other) for i in range(n)])]
    pallas_call x1 -> x0, Pallas kernels: 5.78 us -> none  [local(): pl.pallas_call(functools.partial(run_expert, capacity), grid=(units // ch...]
    pallas_call x14 -> x15, Pallas kernels: 20.3 us -> 26.1 us  [kernel_call(): pl.pallas_call(run, out_shape=[jax.ShapeDtypeStruct(shape, dtype) for sha...]
    all_to_all x2, waiting for transfers between devices: 12.7 us -> 15.6 us  [exchange_half(): lax.all_to_all(value, 'expert', split_axis=0, concat_axis=0, tiled=True,...]
    ppermute x6, waiting for transfers between devices: 6.41 us -> 9.02 us  [across_group(): lax.ppermute(piece, ('dp', 'expert'), [(c * sources + e, (c ^ d >> 1) * s...]
    reshape x1 -> x0, other arithmetic: 1.89 us -> none  [local(): grad_input.astype(BF16).reshape(tokens.shape)]
    unnamed x53 -> x59, local copies, waits for them, and re-layouts: 5.12 us -> 4.69 us
  transfers between devices with their start and end apart: 22 -> 22, of which waited for: 11 -> 13; matrix products, arithmetic and copies ran while one was open for 7% -> 6% of each run, Pallas kernels for 7% -> 7%
where the time goes in v4:
time: 153 us
  starting transfers between devices  38.2 us (25%)
  waiting for transfers between devices  38 us (25%)
  blocking collectives  35.2 us (23%)
  Pallas kernels  26.1 us (17%)
  matrix products  8.49 us (6%)
  local copies, waits for them, and re-layouts  4.94 us (3%)
    all_to_all x2, blocking collectives, exchange(): lax.all_to_all(value, 'expert', split_axis=0, concat_axis=0, tiled=True)  35.2 us
    pallas_call x15, Pallas kernels, kernel_call(): pl.pallas_call(run, out_shape=[jax.ShapeDtypeStruct(shape, dtype) for sha...  26.1 us
    all_to_all x2, waiting for transfers between devices, exchange_half(): lax.all_to_all(value, 'expert', split_axis=0, concat_axis=0, tiled=True,...  15.6 us
    ppermute x10, starting transfers between devices, swap_core(): return lax.ppermute(value, 'dp', [(0, 1), (1, 0)])  11.1 us
    all_to_all x2, starting transfers between devices, exchange_half(): lax.all_to_all(value, 'expert', split_axis=0, concat_axis=0, tiled=True,...  10 us
    ppermute x6, waiting for transfers between devices, across_group(): lax.ppermute(piece, ('dp', 'expert'), [(c * sources + e, (c ^ d >> 1) * s...  9.02 us
    ppermute x4, starting transfers between devices, swap_pair(): return lax.ppermute(value, 'expert', [(i, i ^ other) for i in range(n)])  8.96 us
    dot_general x2, matrix products, dot(): lax.dot_general(left, right, (dims, ((), ())), preferred_element_type=F32)  8.49 us
  transfers between devices with their start and end apart: 22, of which 13 were waited for; matrix products, arithmetic and copies ran while one was open for 6% of the time, Pallas kernels for 7%

profile of v4, /device:TPU:3, one launch (start us, length us, event | category | flops | bytes accessed | tf_op | source)
XLA Modules:
  0.0 152.6 jit_solution(10098935858260450396)
XLA Ops:
  0.7 3.4 %collective-permute-start = (bf16[128,768]{1,0:T(8,128)(2,1)}, bf16[128,768]{1,0:T(8,128)(2,1)S(1)}, u32[]{:S(2)}, u32[]{:S(2)}) collective-permute-start(bf16[128,768]{1,0:T(8,128)(2,1)} %bitcast.28), channel_id=1, source_target_pairs={{0,12},{1,13},{2,14},{3,15},{4,8},{5,9},{6,10},{7,11},{8,4},{9,5},... | collective-permute-start | bytes 589832 | tf_op jit(solution)/shard_map/ppermute | solution.py:39
  4.1 2.0 %shard_map.229 = (bf16[24,1408]{1,0:T(8,128)(2,1)}, bf16[24,640]{1,0:T(8,128)(2,1)}, bf16[24,640]{1,0:T(8,128)(2,1)}, bf16[24,640]{1,0:T(8,128)(2,1)}) custom-call(s32[1]{0:T(128)} %bitcast.2.refs_0_, bf16[24,768]{1,0:T(8,128)(2,1)} %refs_1_.3, bf16[24,768]{1,0:T(8,128)(2,1)} %refs_2_.1, bf16[24,768]{1,0:T(8,128)(2,1)} %refs_3_.1, bf16[16,24]{1,0:T(8,128)(2,1)} %bitcast.45, ...), custom_call_target="tpu_custom_call" | custom-call | flops 1000000 | bytes 1000000 | tf_op jit(solution)/shard_map/pallas_call | solution.py:105
  6.1 1.0 collective-permute-start.2
  7.2 2.5 %collective-permute-start.3 = (bf16[24,640]{1,0:T(8,128)(2,1)}, bf16[24,640]{1,0:T(8,128)(2,1)S(1)}, u32[]{:S(2)}, u32[]{:S(2)}) collective-permute-start(bf16[24,640]{1,0:T(8,128)(2,1)} %get-tuple-element.95), channel_id=1, source_target_pairs={{0,24},{1,25},{2,26},{3,27},{4,28},{5,29},{6,30},{7,31},{8,16},{9,... | collective-permute-start | bytes 92168 | tf_op jit(solution)/shard_map/ppermute | solution.py:640
  9.6 4.2 %collective-permute-done.1.refs_2_ = bf16[24,640]{1,0:T(8,128)(2,1)S(1)} collective-permute-done((bf16[24,640]{1,0:T(8,128)(2,1)}, bf16[24,640]{1,0:T(8,128)(2,1)S(1)}, u32[]{:S(2)}, u32[]{:S(2)}) %collective-permute-start.1) | collective-permute-done | bytes 30752 | tf_op jit(solution)/shard_map/ppermute | solution.py:640
  13.8 1.6 %collective-permute-done.3.refs_4_ = bf16[24,640]{1,0:T(8,128)(2,1)S(1)} collective-permute-done((bf16[24,640]{1,0:T(8,128)(2,1)}, bf16[24,640]{1,0:T(8,128)(2,1)S(1)}, u32[]{:S(2)}, u32[]{:S(2)}) %collective-permute-start.3) | collective-permute-done | bytes 30752 | tf_op jit(solution)/shard_map/ppermute | solution.py:640
  15.4 0.9 copy-done.22
  16.3 1.2 shard_map.230
  17.5 3.9 %all-to-all-start = ((bf16[8,128,640]{2,1,0:T(8,128)(2,1)}), bf16[8,128,640]{2,1,0:T(8,128)(2,1)S(1)}, u32[]{:S(2)}, u32[]{:S(2)}) async-start(bf16[8,128,640]{2,1,0:T(8,128)(2,1)} %shard_map.230), calls=%async_computation | async-start | bytes 2621440 | tf_op jit(solution)/shard_map/all_to_all | solution.py:49
  21.4 0.9 collective-permute-start.4
  22.5 1.6 %shard_map.231 = (f32[3,256]{1,0:T(4,128)S(1)}, bf16[2,128,640]{2,1,0:T(8,128)(2,1)S(1)}, bf16[2,128,640]{2,1,0:T(8,128)(2,1)S(1)}, f32[128,16]{1,0:T(8,128)S(1)}, bf16[640,512]{1,0:T(8,128)(2,1)S(1)}) custom-call(s32[1]{0:T(128)} %bitcast.2.refs_0_, f32[32,12]{1,0:T(8,128)S(1)} %copy.26.refs_1_, s32[128,1]{1,0:T(8,128)S(1)} %copy.27.refs_2_), custom_call_target="tpu_custom_call" | custom-call | flops 1000000 | bytes 1000000 | tf_op jit(solution)/shard_map/pallas_call | solution.py:105
  25.5 12.8 %all-to-all-done.refs_2_ = bf16[8,128,640]{2,1,0:T(8,128)(2,1)S(1)} async-done(((bf16[8,128,640]{2,1,0:T(8,128)(2,1)}), bf16[8,128,640]{2,1,0:T(8,128)(2,1)S(1)}, u32[]{:S(2)}, u32[]{:S(2)}) %all-to-all-start) | async-done | bytes 1310752 | tf_op jit(solution)/shard_map/all_to_all | solution.py:49
  38.3 1.7 %shard_map.232 = (bf16[768,640]{1,0:T(8,128)(2,1)S(1)}, bf16[192,768]{1,0:T(8,128)(2,1)S(1)}, f32[8,768]{1,0:T(8,128)S(1)}, bf16[256,576]{1,0:T(8,128)(2,1)S(1)}...) custom-call(s32[1]{0:T(128)} %bitcast.2.refs_0_, ...), custom_call_target="tpu_custom_call" | custom-call | flops 1000000 | bytes 1000000 | tf_op jit(solution)/shard_map/pallas_call | solution.py:105
  40.0 1.5 collective-permute-start.5
  41.5 1.0 collective-permute-done.5
  42.6 2.1 %collective-permute-start.8 = (bf16[128,768]{1,0:T(8,128)(2,1)S(1)}, bf16[128,768]{1,0:T(8,128)(2,1)S(1)}, u32[]{:S(2)}, u32[]{:S(2)}) collective-permute-start(bf16[128,768]{1,0:T(8,128)(2,1)S(1)} %add_convert_fusion.1), channel_id=1, source_target_pairs={{0,12},{1,13},{2,14},{3,15},{4,8},{5,9},{6,10},{7,11},{8,4},{9,5},... | collective-permute-start | bytes 589832 | tf_op jit(solution)/shard_map/ppermute | solution.py:39
  44.6 1.5 shard_map.233
  47.0 3.6 %collective-permute-done.8.refs_3_ = bf16[128,768]{1,0:T(8,128)(2,1)S(1)} collective-permute-done((bf16[128,768]{1,0:T(8,128)(2,1)S(1)}, bf16[128,768]{1,0:T(8,128)(2,1)S(1)}, u32[]{:S(2)}, u32[]{:S(2)}) %collective-permute-start.8) | collective-permute-done | bytes 196640 | tf_op jit(solution)/shard_map/ppermute | solution.py:39
  50.6 1.0 shard_map.234
  51.6 18.9 %all_to_all.20 = bf16[16,40,384]{2,1,0:T(8,128)(2,1)S(1)} all-to-all(bf16[16,40,384]{2,1,0:T(8,128)(2,1)S(1)} %bitcast.42), channel_id=1, replica_groups=mesh['dp'=2,'expert'=16] {'expert'}, dimensions={0} | all-to-all | bytes 983040 | tf_op jit(solution)/shard_map/all_to_all | solution.py:43
  70.5 3.0 %collective-permute-start.9 = (bf16[640,384]{1,0:T(8,128)(2,1)S(1)}, bf16[640,384]{1,0:T(8,128)(2,1)S(1)}, u32[]{:S(2)}, u32[]{:S(2)}) collective-permute-start(bf16[640,384]{1,0:T(8,128)(2,1)S(1)} %bitcast.36), channel_id=1, source_target_pairs={{0,16},{16,0},{1,17},{17,1},{2,18},{18,2},{3,19},{19,3},{4,20},{20... | collective-permute-start | bytes 1474568 | tf_op jit(solution)/shard_map/ppermute | solution.py:33
  73.6 1.5 collective-permute-done.9.refs_2_
  75.1 4.8 %shard_map.235 = (bf16[320,768]{1,0:T(8,128)(2,1)S(1)}, bf16[320,768]{1,0:T(8,128)(2,1)S(1)}, bf16[160,768]{1,0:T(8,128)(2,1)S(1)}, f32[160,16]{1,0:T(8,128)S(1)...) custom-call(s32[1]{0:T(128)} %bitcast.refs_1_.refs_0_, ...), custom_call_target="tpu_custom_call" | custom-call | flops 1000000 | bytes 1000000 | tf_op jit(solution)/shard_map/pallas_call | solution.py:105
  79.9 0.8 copy-done.14
  81.2 1.5 collective-permute-done.10.refs_2_
  82.6 1.3 shard_map.236
  83.9 16.3 %all_to_all.21 = bf16[16,40,384]{2,1,0:T(8,128)(2,1)S(1)} all-to-all(bf16[16,40,384]{2,1,0:T(8,128)(2,1)S(1)} %bitcast.41), channel_id=1, replica_groups=mesh['dp'=2,'expert'=16] {'expert'}, dimensions={0} | all-to-all | bytes 983040 | tf_op jit(solution)/shard_map/all_to_all | solution.py:43
  100.8 2.5 %collective-permute-start.12 = (bf16[128,768]{1,0:T(8,128)(2,1)S(1)}, bf16[128,768]{1,0:T(8,128)(2,1)S(1)}, u32[]{:S(2)}, u32[]{:S(2)}) collective-permute-start(bf16[128,768]{1,0:T(8,128)(2,1)S(1)} %get-tuple-element.124.refs_0_), channel_id=1, source_target_pairs={{0,16},{16,0},{1,17},{17,1},{2,18},{18,2},{3,19},{19,3},{4,20},{20... | collective-permute-start | bytes 589832 | tf_op jit(solution)/shard_map/ppermute | solution.py:33
  103.3 1.3 collective-permute-start.11
  104.6 3.3 %shard_map.238 = (f32[768,576]{1,0:T(8,128)S(1)}, f32[192,768]{1,0:T(8,128)S(1)}, f32[128,768]{1,0:T(8,128)S(1)}, bf16[128,768]{1,0:T(8,128)(2,1)}, bf16[256,576...) custom-call(bf16[128,768]{1,0:T(8,128)(2,1)S(1)} %get-tuple-element.124.refs_0_, ...), custom_call_target="tpu_custom_call" | custom-call | flops 1000000 | bytes 1000000 | tf_op jit(solution)/shard_map/pallas_call | solution.py:105
  107.9 3.7 %collective-permute-done.11.refs_0_ = bf16[128,768]{1,0:T(8,128)(2,1)S(1)} collective-permute-done((bf16[128,768]{1,0:T(8,128)(2,1)S(1)}, bf16[128,768]{1,0:T(8,128)(2,1)S(1)}, u32[]{:S(2)}, u32[]{:S(2)}) %collective-permute-start.11) | collective-permute-done | bytes 196640 | tf_op jit(solution)/shard_map/ppermute | solution.py:39
  111.6 0.9 collective-permute-start.13
  112.5 1.1 collective-permute-done.13.refs_1_
  113.6 2.2 %shard_map.239 = (f32[128,768]{1,0:T(8,128)S(1)}, bf16[128,768]{1,0:T(8,128)(2,1)S(1)}, bf16[256,576]{1,0:T(8,128)(2,1)S(1)}, f32[1,768]{1,0:T(1,128)S(1)}, f32[3,256]{1,0:T(4,128)S(1)}) custom-call(bf16[128,768]{1,0:T(8,128)(2,1)S(1)} %collective-permute-done.11.refs_0_, bf16[128,768]{1,0:T(8,128)(2,1)S(1)} %collective-permute-done.13.refs_1_, ...), custom_call_target="tpu_custom_call" | custom-call | flops 1000000 | bytes 1000000 | tf_op jit(solution)/shard_map/pallas_call | solution.py:105
  117.3 1.9 %shard_map.240 = bf16[8,128,640]{2,1,0:T(8,128)(2,1)} custom-call(bf16[128,768]{1,0:T(8,128)(2,1)S(1)} %collective-permute-done.11.refs_0_, bf16[128,768]{1,0:T(8,128)(2,1)S(1)} %collective-permute-done.13.refs_1_, bf16[256,192]{1,0:T(8,128)(2,1)S(1)} %get-tuple-element.131.refs_2_, bf16[256,576]{1,0:T(8,128)(2,1)S(1)} %get-tuple-element.134.refs_3_, ...), custom_call_target="tpu_custom_call" | custom-call | flops 1000000 | bytes 1000000 | tf_op jit(solution)/shard_map/pallas_call | solution.py:105
  119.2 6.2 %all-to-all-start.3 = ((bf16[8,128,640]{2,1,0:T(8,128)(2,1)}), bf16[8,128,640]{2,1,0:T(8,128)(2,1)S(1)}, u32[]{:S(2)}, u32[]{:S(2)}) async-start(bf16[8,128,640]{2,1,0:T(8,128)(2,1)} %shard_map.240), calls=%async_computation.3 | async-start | bytes 2621440 | tf_op jit(solution)/shard_map/all_to_all | solution.py:49
  125.4 0.9 collective-permute-start.18
  126.3 4.9 %fusion = f32[768,1536]{1,0:T(8,128)} fusion(bf16[320,768]{1,0:T(8,128)(2,1)S(1)} %copy-done.7, bf16[320,1536]{1,0:T(8,128)(2,1)} %copy-done.13), kind=kOutput, calls=%fused_computation.2 | convolution fusion | flops 754974720 | bytes 6193152 | tf_op jit(solution)/shard_map/dot_general | solution.py:19
  131.9 2.2 %collective-permute-start.19 = (bf16[128,768]{1,0:T(8,128)(2,1)}, bf16[128,768]{1,0:T(8,128)(2,1)S(1)}, u32[]{:S(2)}, u32[]{:S(2)}) collective-permute-start(bf16[128,768]{1,0:T(8,128)(2,1)} %add_convert_fusion), channel_id=1, source_target_pairs={{0,12},{1,13},{2,14},{3,15},{4,8},{5,9},{6,10},{7,11},{8,4},{9,5},... | collective-permute-start | bytes 589832 | tf_op jit(solution)/shard_map/ppermute | solution.py:39
  134.2 3.6 %fusion.1 = f32[1536,768]{1,0:T(8,128)} fusion(bf16[320,1536]{1,0:T(8,128)(2,1)S(1)} %get-tuple-element.144, bf16[320,768]{1,0:T(8,128)(2,1)S(1)} %copy-done.15), kind=kOutput, calls=%fused_computation.3 | convolution fusion | flops 754974720 | bytes 6193152 | tf_op jit(solution)/shard_map/dot_general | solution.py:19
  137.8 1.4 shard_map.241
  139.2 2.8 %all-to-all-done.3.refs_1_ = bf16[8,128,640]{2,1,0:T(8,128)(2,1)S(1)} async-done(((bf16[8,128,640]{2,1,0:T(8,128)(2,1)}), bf16[8,128,640]{2,1,0:T(8,128)(2,1)S(1)}, u32[]{:S(2)}, u32[]{:S(2)}) %all-to-all-start.3) | async-done | bytes 1310752 | tf_op jit(solution)/shard_map/all_to_all | solution.py:49
  142.7 2.4 %collective-permute-start.14 = (bf16[24,640]{1,0:T(8,128)(2,1)S(1)}, bf16[24,640]{1,0:T(8,128)(2,1)S(1)}, u32[]{:S(2)}, u32[]{:S(2)}) collective-permute-start(bf16[24,640]{1,0:T(8,128)(2,1)S(1)} %get-tuple-element.153), channel_id=1, source_target_pairs={{0,8},{1,9},{2,10},{3,11},{4,12},{5,13},{6,14},{7,15},{8,0},{9,1},... | collective-permute-start | bytes 92168 | tf_op jit(solution)/shard_map/ppermute | solution.py:640
  145.1 2.3 %collective-permute-start.15 = (bf16[24,640]{1,0:T(8,128)(2,1)S(1)}, bf16[24,640]{1,0:T(8,128)(2,1)S(1)}, u32[]{:S(2)}, u32[]{:S(2)}) collective-permute-start(bf16[24,640]{1,0:T(8,128)(2,1)S(1)} %get-tuple-element.154), channel_id=1, source_target_pairs={{0,16},{1,17},{2,18},{3,19},{4,20},{5,21},{6,22},{7,23},{8,24},{9,... | collective-permute-start | bytes 92168 | tf_op jit(solution)/shard_map/ppermute | solution.py:640
  147.4 1.0 collective-permute-done.19.refs_7_
  148.4 2.0 %collective-permute-done.14.refs_2_ = bf16[24,640]{1,0:T(8,128)(2,1)S(1)} collective-permute-done((bf16[24,640]{1,0:T(8,128)(2,1)S(1)}, bf16[24,640]{1,0:T(8,128)(2,1)S(1)}, u32[]{:S(2)}, u32[]{:S(2)}) %collective-permute-start.14) | collective-permute-done | bytes 30752 | tf_op jit(solution)/shard_map/ppermute | solution.py:640
  150.4 1.2 collective-permute-done.16.refs_4_
  151.6 1.0 shard_map.243
  (79 shorter events, 6.6 us)
Async XLA Ops:
  0.6 21.6 %copy-start.27 = (f32[32,12]{0,1:T(8,128)S(1)}, f32[32,12]{0,1:T(8,128)}, u32[]{:S(2)}) copy-start(f32[32,12]{0,1:T(8,128)} %param.20) | copy-start | bytes 4612
  0.7 21.7 %copy-start.28 = (s32[1,128,1]{1,2,0:T(1,128)S(1)}, s32[1,128,1]{1,2,0:T(1,128)}, u32[]{:S(2)}) copy-start(s32[1,128,1]{1,2,0:T(1,128)} %param.26) | copy-start | bytes 1540
  0.7 14.8 %collective-permute-start = (bf16[128,768]{1,0:T(8,128)(2,1)}, bf16[128,768]{1,0:T(8,128)(2,1)S(1)}, u32[]{:S(2)}, u32[]{:S(2)}) collective-permute-start(bf16[128,768]{1,0:T(8,128)(2,1)} %bitcast.28), channel_id=1, source_target_pairs={{0,12},{1,13},{2,14},{3,15},{4,8},{5,9},{6,10},{7,11},{8,4},{9,5},... | collective-permute-start | bytes 589832 | tf_op jit(solution)/shard_map/ppermute | solution.py:39
  6.1 7.7 %collective-permute-start.1 = (bf16[24,640]{1,0:T(8,128)(2,1)}, bf16[24,640]{1,0:T(8,128)(2,1)S(1)}, u32[]{:S(2)}, u32[]{:S(2)}) collective-permute-start(bf16[24,640]{1,0:T(8,128)(2,1)} %get-tuple-element.93), channel_id=1, source_target_pairs={{0,8},{1,9},{2,10},{3,11},{4,12},{5,13},{6,14},{7,15},{8,0},{9,1},... | collective-permute-start | bytes 92168 | tf_op jit(solution)/shard_map/ppermute | solution.py:640
  6.1 7.7 %collective-permute-start.2 = (bf16[24,640]{1,0:T(8,128)(2,1)}, bf16[24,640]{1,0:T(8,128)(2,1)S(1)}, u32[]{:S(2)}, u32[]{:S(2)}) collective-permute-start(bf16[24,640]{1,0:T(8,128)(2,1)} %get-tuple-element.94), channel_id=1, source_target_pairs={{0,16},{1,17},{2,18},{3,19},{4,20},{5,21},{6,22},{7,23},{8,24},{9,... | collective-permute-start | bytes 92168 | tf_op jit(solution)/shard_map/ppermute | solution.py:640
  7.2 8.3 %collective-permute-start.3 = (bf16[24,640]{1,0:T(8,128)(2,1)}, bf16[24,640]{1,0:T(8,128)(2,1)S(1)}, u32[]{:S(2)}, u32[]{:S(2)}) collective-permute-start(bf16[24,640]{1,0:T(8,128)(2,1)} %get-tuple-element.95), channel_id=1, source_target_pairs={{0,24},{1,25},{2,26},{3,27},{4,28},{5,29},{6,30},{7,31},{8,16},{9,... | collective-permute-start | bytes 92168 | tf_op jit(solution)/shard_map/ppermute | solution.py:640
  15.4 0.9 copy-start.22
  17.5 23.9 %copy-start = (bf16[1,128,768]{2,1,0:T(8,128)(2,1)S(1)}, bf16[1,128,768]{2,1,0:T(8,128)(2,1)}, u32[]{:S(2)}) copy-start(bf16[1,128,768]{2,1,0:T(8,128)(2,1)} %param.14) | copy-start | bytes 589828
  17.5 27.1 %copy-start.25 = (s32[1,256]{1,0:T(1,128)S(1)}, s32[1,256]{1,0:T(1,128)}, u32[]{:S(2)}) copy-start(s32[1,256]{1,0:T(1,128)} %refs_1_.4) | copy-start | bytes 3076
  17.5 20.8 %all-to-all-start = ((bf16[8,128,640]{2,1,0:T(8,128)(2,1)}), bf16[8,128,640]{2,1,0:T(8,128)(2,1)S(1)}, u32[]{:S(2)}, u32[]{:S(2)}) async-start(bf16[8,128,640]{2,1,0:T(8,128)(2,1)} %shard_map.230), calls=%async_computation | async-start | bytes 2621440 | tf_op jit(solution)/shard_map/all_to_all | solution.py:49
  21.4 4.1 %collective-permute-start.4 = (bf16[128,768]{1,0:T(8,128)(2,1)S(1)}, bf16[128,768]{1,0:T(8,128)(2,1)S(1)}, u32[]{:S(2)}, u32[]{:S(2)}) collective-permute-start(bf16[128,768]{1,0:T(8,128)(2,1)S(1)} %collective-permute-done.refs_3_.refs_7_.refs_5_), channel_id=1, source_target_pairs={{0,16},{16,0},{1,17},{17,1},{2,18},{18,2},{3,19},{19,3},{4,20},{20... | collective-permute-start | bytes 589832 | tf_op jit(solution)/shard_map/ppermute | solution.py:33
  22.5 28.1 %copy-start.3 = (bf16[1,128,768]{2,1,0:T(8,128)(2,1)S(1)}, bf16[1,128,768]{2,1,0:T(8,128)(2,1)}, u32[]{:S(2)}) copy-start(bf16[1,128,768]{2,1,0:T(8,128)(2,1)} %param.27) | copy-start | bytes 589828
  40.0 2.6 %collective-permute-start.5 = (bf16[128,768]{1,0:T(8,128)(2,1)S(1)}, bf16[128,768]{1,0:T(8,128)(2,1)S(1)}, u32[]{:S(2)}, u32[]{:S(2)}) collective-permute-start(bf16[128,768]{1,0:T(8,128)(2,1)S(1)} %get-tuple-element.104), channel_id=1, source_target_pairs={{0,16},{16,0},{1,17},{17,1},{2,18},{18,2},{3,19},{19,3},{4,20},{20... | collective-permute-start | bytes 589832 | tf_op jit(solution)/shard_map/ppermute | solution.py:33
  41.4 3.2 %collective-permute-start.6 = (bf16[128,768]{1,0:T(8,128)(2,1)S(1)}, bf16[128,768]{1,0:T(8,128)(2,1)S(1)}, u32[]{:S(2)}, u32[]{:S(2)}) collective-permute-start(bf16[128,768]{1,0:T(8,128)(2,1)S(1)} %bitcast.29), channel_id=1, source_target_pairs={{0,16},{16,0},{1,17},{17,1},{2,18},{18,2},{3,19},{19,3},{4,20},{20... | collective-permute-start | bytes 589832 | tf_op jit(solution)/shard_map/ppermute | solution.py:33
  42.6 8.0 %collective-permute-start.8 = (bf16[128,768]{1,0:T(8,128)(2,1)S(1)}, bf16[128,768]{1,0:T(8,128)(2,1)S(1)}, u32[]{:S(2)}, u32[]{:S(2)}) collective-permute-start(bf16[128,768]{1,0:T(8,128)(2,1)S(1)} %add_convert_fusion.1), channel_id=1, source_target_pairs={{0,12},{1,13},{2,14},{3,15},{4,8},{5,9},{6,10},{7,11},{8,4},{9,5},... | collective-permute-start | bytes 589832 | tf_op jit(solution)/shard_map/ppermute | solution.py:39
  44.6 30.4 %copy-start.1 = (bf16[1,768,1536]{2,1,0:T(8,128)(2,1)S(1)}, bf16[1,768,1536]{2,1,0:T(8,128)(2,1)}, u32[]{:S(2)}) copy-start(bf16[1,768,1536]{2,1,0:T(8,128)(2,1)} %param.23) | copy-start | bytes 7077892
  44.6 30.4 %copy-start.2 = (bf16[1,1536,768]{2,1,0:T(8,128)(2,1)S(1)}, bf16[1,1536,768]{2,1,0:T(8,128)(2,1)}, u32[]{:S(2)}) copy-start(bf16[1,1536,768]{2,1,0:T(8,128)(2,1)} %param.24) | copy-start | bytes 7077892
  46.1 4.5 %collective-permute-start.7 = (bf16[128,768]{1,0:T(8,128)(2,1)S(1)}, bf16[128,768]{1,0:T(8,128)(2,1)S(1)}, u32[]{:S(2)}, u32[]{:S(2)}) collective-permute-start(bf16[128,768]{1,0:T(8,128)(2,1)S(1)} %get-tuple-element.110), channel_id=1, source_target_pairs={{0,16},{16,0},{1,17},{17,1},{2,18},{18,2},{3,19},{19,3},{4,20},{20... | collective-permute-start | bytes 589832 | tf_op jit(solution)/shard_map/ppermute | solution.py:33
  51.6 28.3 %copy-start.23 = (f32[128,1]{1,0:T(8,128)}, f32[128,1]{1,0:T(8,128)S(1)}, u32[]{:S(2)}) copy-start(f32[128,1]{1,0:T(8,128)S(1)} %get-tuple-element.147.refs_6_) | copy-start | bytes 1540
  51.6 48.7 %copy-start.8 = (f32[128,768]{1,0:T(8,128)}, f32[128,768]{1,0:T(8,128)S(1)}, u32[]{:S(2)}) copy-start(f32[128,768]{1,0:T(8,128)S(1)} %get-tuple-element.123.refs_2_.refs_3_) | copy-start | bytes 1179652
  70.5 4.5 %collective-permute-start.9 = (bf16[640,384]{1,0:T(8,128)(2,1)S(1)}, bf16[640,384]{1,0:T(8,128)(2,1)S(1)}, u32[]{:S(2)}, u32[]{:S(2)}) collective-permute-start(bf16[640,384]{1,0:T(8,128)(2,1)S(1)} %bitcast.36), channel_id=1, source_target_pairs={{0,16},{16,0},{1,17},{17,1},{2,18},{18,2},{3,19},{19,3},{4,20},{20... | collective-permute-start | bytes 1474568 | tf_op jit(solution)/shard_map/ppermute | solution.py:33
  79.9 0.8 copy-start.14
  80.7 20.1 %copy-start.6 = (bf16[320,768]{1,0:T(8,128)(2,1)}, bf16[320,768]{1,0:T(8,128)(2,1)S(1)}, u32[]{:S(2)}) copy-start(bf16[320,768]{1,0:T(8,128)(2,1)S(1)} %get-tuple-element.117) | copy-start | bytes 1474564
  80.7 23.9 %copy-start.13 = (bf16[320,1536]{1,0:T(8,128)(2,1)}, bf16[320,1536]{1,0:T(8,128)(2,1)S(1)}, u32[]{:S(2)}) copy-start(bf16[320,1536]{1,0:T(8,128)(2,1)S(1)} %get-tuple-element.143) | copy-start | bytes 2949124
  80.7 19.5 %copy-start.4 = (bf16[1,128,768]{2,1,0:T(8,128)(2,1)S(1)}, bf16[1,128,768]{2,1,0:T(8,128)(2,1)}, u32[]{:S(2)}) copy-start(bf16[1,128,768]{2,1,0:T(8,128)(2,1)} %param.27) | copy-start | bytes 589828
  80.7 19.5 %copy-start.11 = (bf16[2,128,640]{2,1,0:T(8,128)(2,1)S(1)}, bf16[2,128,640]{2,1,0:T(8,128)(2,1)}, u32[]{:S(2)}) copy-start(bf16[2,128,640]{2,1,0:T(8,128)(2,1)} %copy-done.10) | copy-start | bytes 983044
  80.7 1.9 %collective-permute-start.10 = (bf16[2,160,768]{2,1,0:T(8,128)(2,1)S(1)}, bf16[2,160,768]{2,1,0:T(8,128)(2,1)S(1)}, u32[]{:S(2)}, u32[]{:S(2)}) collective-permute-start(bf16[2,160,768]{2,1,0:T(8,128)(2,1)S(1)} %get-tuple-element.116), channel_id=1, source_target_pairs={{0,16},{16,0},{1,17},{17,1},{2,18},{18,2},{3,19},{19,3},{4,20},{20... | collective-permute-start | bytes 1474568 | tf_op jit(solution)/shard_map/ppermute | solution.py:33
  100.8 3.8 %collective-permute-start.12 = (bf16[128,768]{1,0:T(8,128)(2,1)S(1)}, bf16[128,768]{1,0:T(8,128)(2,1)S(1)}, u32[]{:S(2)}, u32[]{:S(2)}) collective-permute-start(bf16[128,768]{1,0:T(8,128)(2,1)S(1)} %get-tuple-element.124.refs_0_), channel_id=1, source_target_pairs={{0,16},{16,0},{1,17},{17,1},{2,18},{18,2},{3,19},{19,3},{4,20},{20... | collective-permute-start | bytes 589832 | tf_op jit(solution)/shard_map/ppermute | solution.py:33
  103.3 8.3 %collective-permute-start.11 = (bf16[128,768]{1,0:T(8,128)(2,1)S(1)}, bf16[128,768]{1,0:T(8,128)(2,1)S(1)}, u32[]{:S(2)}, u32[]{:S(2)}) collective-permute-start(bf16[128,768]{1,0:T(8,128)(2,1)S(1)} %get-tuple-element.124.refs_0_), channel_id=1, source_target_pairs={{0,12},{1,13},{2,14},{3,15},{4,8},{5,9},{6,10},{7,11},{8,4},{9,5},... | collective-permute-start | bytes 589832 | tf_op jit(solution)/shard_map/ppermute | solution.py:39
  107.9 8.7 %copy-start.18 = (f32[128,768]{1,0:T(8,128)}, f32[128,768]{1,0:T(8,128)S(1)}, u32[]{:S(2)}) copy-start(f32[128,768]{1,0:T(8,128)S(1)} %get-tuple-element.156.refs_5_) | copy-start | bytes 1179652
  111.6 2.0 %collective-permute-start.13 = (bf16[128,768]{1,0:T(8,128)(2,1)S(1)}, bf16[128,768]{1,0:T(8,128)(2,1)S(1)}, u32[]{:S(2)}, u32[]{:S(2)}) collective-permute-start(bf16[128,768]{1,0:T(8,128)(2,1)S(1)} %collective-permute-done.11.refs_0_), channel_id=1, source_target_pairs={{0,16},{16,0},{1,17},{17,1},{2,18},{18,2},{3,19},{19,3},{4,20},{20... | collective-permute-start | bytes 589832 | tf_op jit(solution)/shard_map/ppermute | solution.py:33
  115.8 0.7 copy-start.16
  119.2 7.1 %copy-start.7 = (bf16[320,768]{1,0:T(8,128)(2,1)S(1)}, bf16[320,768]{1,0:T(8,128)(2,1)}, u32[]{:S(2)}) copy-start(bf16[320,768]{1,0:T(8,128)(2,1)} %copy-done.6) | copy-start | bytes 1474564
  119.2 22.9 %all-to-all-start.3 = ((bf16[8,128,640]{2,1,0:T(8,128)(2,1)}), bf16[8,128,640]{2,1,0:T(8,128)(2,1)S(1)}, u32[]{:S(2)}, u32[]{:S(2)}) async-start(bf16[8,128,640]{2,1,0:T(8,128)(2,1)} %shard_map.240), calls=%async_computation.3 | async-start | bytes 2621440 | tf_op jit(solution)/shard_map/all_to_all | solution.py:49
  125.4 5.8 %collective-permute-start.18 = (bf16[128,768]{1,0:T(8,128)(2,1)}, bf16[128,768]{1,0:T(8,128)(2,1)S(1)}, u32[]{:S(2)}, u32[]{:S(2)}) collective-permute-start(bf16[128,768]{1,0:T(8,128)(2,1)} %copy-done.26), channel_id=1, source_target_pairs={{0,16},{16,0},{1,17},{17,1},{2,18},{18,2},{3,19},{19,3},{4,20},{20... | collective-permute-start | bytes 589832 | tf_op jit(solution)/shard_map/ppermute | solution.py:33
  126.3 4.9 %copy-start.17 = (f32[128,768]{1,0:T(8,128)S(1)}, f32[128,768]{1,0:T(8,128)}, u32[]{:S(2)}) copy-start(f32[128,768]{1,0:T(8,128)} %copy-done.16) | copy-start | bytes 1179652
  126.3 7.9 %copy-start.15 = (bf16[320,768]{1,0:T(8,128)(2,1)S(1)}, bf16[320,768]{1,0:T(8,128)(2,1)}, u32[]{:S(2)}) copy-start(bf16[320,768]{1,0:T(8,128)(2,1)} %copy-done.14) | copy-start | bytes 1474564
  131.2 16.2 %collective-permute-start.17 = (bf16[128,768]{1,0:T(8,128)(2,1)}, bf16[128,768]{1,0:T(8,128)(2,1)S(1)}, u32[]{:S(2)}, u32[]{:S(2)}) collective-permute-start(bf16[128,768]{1,0:T(8,128)(2,1)} %get-tuple-element.157), channel_id=1, source_target_pairs={{0,16},{16,0},{1,17},{17,1},{2,18},{18,2},{3,19},{19,3},{4,20},{20... | collective-permute-start | bytes 589832 | tf_op jit(solution)/shard_map/ppermute | solution.py:33
  131.9 16.5 %collective-permute-start.19 = (bf16[128,768]{1,0:T(8,128)(2,1)}, bf16[128,768]{1,0:T(8,128)(2,1)S(1)}, u32[]{:S(2)}, u32[]{:S(2)}) collective-permute-start(bf16[128,768]{1,0:T(8,128)(2,1)} %add_convert_fusion), channel_id=1, source_target_pairs={{0,12},{1,13},{2,14},{3,15},{4,8},{5,9},{6,10},{7,11},{8,4},{9,5},... | collective-permute-start | bytes 589832 | tf_op jit(solution)/shard_map/ppermute | solution.py:39
  134.2 3.6 %copy-start.5 = (bf16[1,128,768]{2,1,0:T(8,128)(2,1)S(1)}, bf16[1,128,768]{2,1,0:T(8,128)(2,1)}, u32[]{:S(2)}) copy-start(bf16[1,128,768]{2,1,0:T(8,128)(2,1)} %param.27) | copy-start | bytes 589828
  134.2 3.6 %copy-start.9 = (f32[128,768]{1,0:T(8,128)S(1)}, f32[128,768]{1,0:T(8,128)}, u32[]{:S(2)}) copy-start(f32[128,768]{1,0:T(8,128)} %copy-done.8) | copy-start | bytes 1179652
  134.2 3.6 %copy-start.12 = (bf16[2,128,640]{2,1,0:T(8,128)(2,1)S(1)}, bf16[2,128,640]{2,1,0:T(8,128)(2,1)}, u32[]{:S(2)}) copy-start(bf16[2,128,640]{2,1,0:T(8,128)(2,1)} %copy-done.10) | copy-start | bytes 983044
  134.2 3.6 %copy-start.21 = (bf16[2,128,640]{2,1,0:T(8,128)(2,1)S(1)}, bf16[2,128,640]{2,1,0:T(8,128)(2,1)}, u32[]{:S(2)}) copy-start(bf16[2,128,640]{2,1,0:T(8,128)(2,1)} %copy-done.20) | copy-start | bytes 983044
  134.2 3.6 %copy-start.24 = (f32[128,1]{1,0:T(8,128)S(1)}, f32[128,1]{1,0:T(8,128)}, u32[]{:S(2)}) copy-start(f32[128,1]{1,0:T(8,128)} %copy-done.23) | copy-start | bytes 1540
  137.8 13.8 %copy-start.19 = (f32[128,768]{1,0:T(8,128)S(1)}, f32[128,768]{1,0:T(8,128)}, u32[]{:S(2)}) copy-start(f32[128,768]{1,0:T(8,128)} %copy-done.18) | copy-start | bytes 1179652
  142.7 7.6 %collective-permute-start.14 = (bf16[24,640]{1,0:T(8,128)(2,1)S(1)}, bf16[24,640]{1,0:T(8,128)(2,1)S(1)}, u32[]{:S(2)}, u32[]{:S(2)}) collective-permute-start(bf16[24,640]{1,0:T(8,128)(2,1)S(1)} %get-tuple-element.153), channel_id=1, source_target_pairs={{0,8},{1,9},{2,10},{3,11},{4,12},{5,13},{6,14},{7,15},{8,0},{9,1},... | collective-permute-start | bytes 92168 | tf_op jit(solution)/shard_map/ppermute | solution.py:640
  145.1 5.3 %collective-permute-start.15 = (bf16[24,640]{1,0:T(8,128)(2,1)S(1)}, bf16[24,640]{1,0:T(8,128)(2,1)S(1)}, u32[]{:S(2)}, u32[]{:S(2)}) collective-permute-start(bf16[24,640]{1,0:T(8,128)(2,1)S(1)} %get-tuple-element.154), channel_id=1, source_target_pairs={{0,16},{1,17},{2,18},{3,19},{4,20},{5,21},{6,22},{7,23},{8,24},{9,... | collective-permute-start | bytes 92168 | tf_op jit(solution)/shard_map/ppermute | solution.py:640
  147.4 4.2 %collective-permute-start.16 = (bf16[24,640]{1,0:T(8,128)(2,1)S(1)}, bf16[24,640]{1,0:T(8,128)(2,1)S(1)}, u32[]{:S(2)}, u32[]{:S(2)}) collective-permute-start(bf16[24,640]{1,0:T(8,128)(2,1)S(1)} %get-tuple-element.155), channel_id=1, source_target_pairs={{0,24},{1,25},{2,26},{3,27},{4,28},{5,29},{6,30},{7,31},{8,16},{9,... | collective-permute-start | bytes 92168 | tf_op jit(solution)/shard_map/ppermute | solution.py:640
  (3 other events, 2.1 us)

commit v5 on v4

--- a/solution.py
+++ b/solution.py
@@ -12,6 +12,7 @@
 BUCKET_EDGES = (1, 2, 3, 4, 5, 6, 7, 8, 12, 16, 23, 32, 46, 64, 91)
 F32 = jnp.float32
 BF16 = jnp.bfloat16
+ORDER = (3, 1, 2)
 VMEM_BYTES = 24 * 1024 * 1024
 
 
@@ -149,7 +150,7 @@
         jnp.concatenate([w[:, j * cols : (j + 1) * cols] for w in weights] + [small], axis=1)
         for j in range(4)
     ]
-    for d, out_ref in enumerate(out_refs, 1):
+    for d, out_ref in zip(ORDER, out_refs):
         out_ref[...] = choose(group_ref[0] ^ d, pieces)
     used = pieces[0].shape[1]
     keep_ref[:, :used] = choose(group_ref[0], pieces)
@@ -159,29 +160,28 @@
 def put_rows(ref, dest, value):
     rows, width = value.shape
     wide = ref.shape[2]
-    if wide >= width:
-        ref[dest, 4 * rows :, :width] = value
-        if wide > width:
-            ref[dest, 4 * rows :, width:] = jnp.zeros((rows, wide - width), BF16)
-        return
-    over = width - wide
-    blocks = rows // 8
-    ref[dest, 4 * rows : 5 * rows] = value[:, :wide]
-    for b in range(blocks):
-        ref[dest, 5 * rows :, b * over : (b + 1) * over] = value[b * 8 : (b + 1) * 8, wide:]
-    ref[dest, 5 * rows :, blocks * over :] = jnp.zeros((8, wide - blocks * over), BF16)
+    ref[dest, 4 * rows :, : min(wide, width)] = value[:, :wide]
+    if wide > width:
+        ref[dest, 4 * rows :, width:] = jnp.zeros((rows, wide - width), BF16)
+
+
+def spare_lanes(value, wide):
+    over = (value.shape[1] - wide) // 4
+    return jnp.concatenate(
+        [value[:, wide + j * over : wide + (j + 1) * over] for j in range(4)], axis=0
+    )
 
 
 def take_rows(held, rows, width):
     wide = held.shape[1]
     if wide >= width:
         return held[4 * rows :, :width]
-    over = width - wide
-    tail = [held[5 * rows :, b * over : (b + 1) * over] for b in range(rows // 8)]
-    return jnp.concatenate([held[4 * rows : 5 * rows], jnp.concatenate(tail, axis=0)], axis=1)
-
-
-def spread_weights(group_ref, own_ref, p1_ref, p2_ref, p3_ref, out_ref):
+    over = (width - wide) // 4
+    tail = [held[j * rows : (j + 1) * rows, wide - over :] for j in range(4)]
+    return jnp.concatenate([held[4 * rows :]] + tail, axis=1)
+
+
+def spread_weights(group_ref, own_ref, p3_ref, p1_ref, p2_ref, out_ref):
     dests, _, wide = out_ref.shape
     rows, used = p1_ref.shape
     pieces = [own_ref[:, :used]] + [ref[...] for ref in (p1_ref, p2_ref, p3_ref)]
@@ -189,6 +189,9 @@
     if wide > used:
         value = jnp.concatenate([value, jnp.zeros((4 * rows, wide - used), BF16)], axis=1)
     last = own_ref[:, used:]
+    if wide < last.shape[1]:
+        spare = spare_lanes(last, wide)
+        value = jnp.concatenate([value[:, : wide - spare.shape[1]], spare], axis=1)
     for dest in range(dests):
         out_ref[dest, : 4 * rows] = value
         put_rows(out_ref, dest, last)
@@ -485,7 +488,7 @@
     )
 
 
-def sum_weights(buckets, table_cols, *refs):
+def sum_weights(packed, buckets, table_cols, *refs):
     gw_ref, gout_ref, own_gain_ref, own_offsets_ref, gain_ref, offsets_ref = refs[7:13]
     gain_two_ref, router_ref, full_ref, out_ref = refs[13:]
     weights, outs = row_weights(*refs[:7])
@@ -511,14 +514,19 @@
     narrow = jnp.transpose(narrow)[:, :2]
     weights = weights + gw_ref[...]
     pieces = [weights, router_ref[...].astype(F32), narrow, table]
-    spare = full_ref.shape[-1] - sum(p.shape[1] for p in pieces)
-    full_ref[...] = jnp.concatenate(pieces + [jnp.zeros((width, spare), F32)], axis=1).astype(BF16)
-    out_ref[...] = (outs + gout_ref[...]).astype(BF16)
-
-
-def sum_weights_message(buckets, table_cols, *refs):
+    outs = outs + gout_ref[...]
+    out_ref[...] = outs.astype(BF16)
+    used = full_ref.shape[1]
+    tail = [spare_lanes(outs, used)] if packed else []
+    spare = used - sum(p.shape[1] for p in pieces + tail)
+    if spare:
+        tail.insert(0, jnp.zeros((width, spare), F32))
+    full_ref[...] = jnp.concatenate(pieces + tail, axis=1).astype(BF16)
+
+
+def sum_weights_message(packed, buckets, table_cols, *refs):
     *rest, message_ref, full_ref, out_ref = refs
-    sum_weights(buckets, table_cols, *rest, full_ref, out_ref)
+    sum_weights(packed, buckets, table_cols, *rest, full_ref, out_ref)
     dests, _, wide = message_ref.shape
     rows = out_ref.shape[0] // dests
     used = full_ref.shape[1]
@@ -542,19 +550,21 @@
     out_ref[...] = take_rows(total, rows, out_ref.shape[1])
     pieces = [total[j * rows : (j + 1) * rows, :used] for j in range(4)]
     own_ref[...] = choose(group_ref[0], pieces)
-    for d, ref in enumerate(send_refs):
-        ref[...] = choose(group_ref[0] ^ (d + 1), pieces).astype(BF16)
-
-
-def finish_weights(own_heads, buckets, table_cols, group_ref, p0_ref, p1_ref, p2_ref, p3_ref,
-                   grad_ref, core_ref, came_ref, dmiddle_ref, x_ref, gains_ref, q_ref, k_ref, v_ref,
-                   router_ref, one_ref, two_ref, table_ref, out_ref):
+    for d, ref in zip(ORDER, send_refs):
+        ref[...] = choose(group_ref[0] ^ d, pieces).astype(BF16)
+
+
+def finish_input(grad_ref, core_ref, came_ref, dmiddle_ref, x_ref, gains_ref, out_ref):
     x = x_ref[...].astype(F32)
     inverse = rms_inverse(x)
     grad_normed = grad_ref[...] + core_ref[...].astype(F32) + came_ref[...].astype(F32)
     out_ref[...] = (
         dmiddle_ref[...] + norm_backward(grad_normed, x * inverse, inverse, gains_ref[0:1])
     ).astype(BF16)
+
+
+def finish_weights(own_heads, buckets, table_cols, group_ref, p0_ref, p3_ref, p1_ref, p2_ref,
+                   q_ref, k_ref, v_ref, router_ref, one_ref, two_ref, table_ref):
     rows, width = q_ref.shape
     experts = router_ref.shape[0]
     cols = width // 4
@@ -630,10 +640,9 @@
     extra = max(table_cols, -(-length // rows))
     used = -(-(3 * cols + experts + 2 + extra) // 128) * 128
     aligned = rows % 8 == 0
-    if aligned and used < width and (width - used) * (rows // 8) <= used:
-        wide, total = used, 5 * rows + 8
-    else:
-        wide, total = max(used, width), 5 * rows
+    room = used - (3 * cols + experts + 2 + extra)
+    packed = aligned and used < width <= used + 4 * room and (width - used) % 4 == 0
+    wide = used if packed else max(used, width)
 
     def across_group(pieces):
         return [
@@ -646,7 +655,7 @@
                     for e in range(sources)
                 ],
             )
-            for d, piece in enumerate(pieces, 1)
+            for d, piece in zip(ORDER, pieces)
         ]
 
     own_tokens = tokens.reshape(toks, width)
@@ -661,7 +670,7 @@
     pieces = across_group(pieces)
     pair_tokens, own_piece, *pieces = lax.optimization_barrier((pair_tokens, own_piece, *pieces))
     (message,) = kernel_call(
-        spread_weights, [((half, total, wide), BF16)],
+        spread_weights, [((half, 5 * rows, wide), BF16)],
         group_at, own_piece, *pieces, scalars=1,
     )
     arrived = exchange_half(message)
@@ -781,12 +790,12 @@
     flat = [((width, used), BF16), ((cols, width), BF16)]
     if aligned:
         (message,) = kernel_call(
-            functools.partial(sum_weights_message, buckets, table_cols),
-            [((half, total, wide), BF16)], *last, held=flat,
+            functools.partial(sum_weights_message, packed, buckets, table_cols),
+            [((half, 5 * rows, wide), BF16)], *last, held=flat,
         )
     else:
         full, grad_out = kernel_call(
-            functools.partial(sum_weights, buckets, table_cols), flat, *last
+            functools.partial(sum_weights, packed, buckets, table_cols), flat, *last
         )
         full = full.reshape(2, 2, half, rows, used).transpose(2, 0, 1, 3, 4)
         full = full.reshape(half, 4 * rows, used)
@@ -814,15 +823,17 @@
         group_at, arrived, scalars=1,
     )
     pieces = across_group(pieces)
-    query_grad, key_grad, value_grad, router_grad, one_grad, two_grad, table_grad, grad_input = kernel_call(
+    query_grad, key_grad, value_grad, router_grad, one_grad, two_grad, table_grad = kernel_call(
         functools.partial(finish_weights, own_heads, buckets, table_cols),
         [((rows, width), F32)] * 3
-        + [((experts, rows), F32), ((1, rows), F32), ((1, rows), F32), ((heads, buckets), F32)]
-        + [((toks, width), BF16)],
-        group_at, own_piece, *pieces, grad_normed, own_came, came, grad_middle, own_tokens, gains,
-        scalars=1,
-    )
-
+        + [((experts, rows), F32), ((1, rows), F32), ((1, rows), F32), ((heads, buckets), F32)],
+        group_at, own_piece, *pieces, scalars=1,
+    )
+
+    (grad_input,) = kernel_call(
+        finish_input, [((toks, width), BF16)],
+        grad_normed, own_came, came, grad_middle, own_tokens, gains,
+    )
     return (
         final.reshape(tokens.shape),
         grad_input.reshape(tokens.shape),

time: 153 us -> 149 us (0.974)
  waiting for transfers between devices: 38 us -> 32 us
  Pallas kernels: 26.1 us -> 27.7 us
    all_to_all x2, waiting for transfers between devices: 15.6 us -> 12.6 us  [exchange_half(): lax.all_to_all(value, 'expert', split_axis=0, concat_axis=0, tiled=True,...]
    ppermute x6, waiting for transfers between devices: 9.02 us -> 7.1 us  [across_group(): lax.ppermute(piece, ('dp', 'expert'), [(c * sources + e, (c ^ d >> 1) * s...]
    pallas_call x15 -> x16, Pallas kernels: 26.1 us -> 27.7 us  [kernel_call(): pl.pallas_call(run, out_shape=[jax.ShapeDtypeStruct(shape, dtype) for sha...]
  transfers between devices with their start and end apart: 22 -> 22, of which waited for: 13 -> 12; matrix products, arithmetic and copies ran while one was open for 6% -> 7% of each run, Pallas kernels for 7% -> 8%
where the time goes in v5:
time: 149 us; the launch traced here: 148 us
  starting transfers between devices  38.5 us (26%)
  blocking collectives  35.3 us (24%)
  waiting for transfers between devices  32 us (21%)
  Pallas kernels  27.7 us (19%)
  matrix products  8.64 us (6%)
  local copies, waits for them, and re-layouts  4.46 us (3%)
    all_to_all x2, blocking collectives, exchange(): lax.all_to_all(value, 'expert', split_axis=0, concat_axis=0, tiled=True)  35.3 us
    pallas_call x16, Pallas kernels, kernel_call(): pl.pallas_call(run, out_shape=[jax.ShapeDtypeStruct(shape, dtype) for sha...  27.7 us
    all_to_all x2, waiting for transfers between devices, exchange_half(): lax.all_to_all(value, 'expert', split_axis=0, concat_axis=0, tiled=True,...  12.6 us
    ppermute x10, starting transfers between devices, swap_core(): return lax.ppermute(value, 'dp', [(0, 1), (1, 0)])  10.8 us
    ppermute x4, starting transfers between devices, swap_pair(): return lax.ppermute(value, 'expert', [(i, i ^ other) for i in range(n)])  9.95 us
    all_to_all x2, starting transfers between devices, exchange_half(): lax.all_to_all(value, 'expert', split_axis=0, concat_axis=0, tiled=True,...  9.89 us
    dot_general x2, matrix products, dot(): lax.dot_general(left, right, (dims, ((), ())), preferred_element_type=F32)  8.64 us
    ppermute x6, starting transfers between devices, across_group(): lax.ppermute(piece, ('dp', 'expert'), [(c * sources + e, (c ^ d >> 1) * s...  7.84 us
  transfers between devices with their start and end apart: 22, of which 12 were waited for; matrix products, arithmetic and copies ran while one was open for 7% of the time, Pallas kernels for 8%

profile of v5, /device:TPU:3, one launch (start us, length us, event | category | flops | bytes accessed | tf_op | source)
XLA Modules:
  0.0 148.3 jit_solution(10231193266652972776)
XLA Ops:
  0.7 3.4 %collective-permute-start = (bf16[128,768]{1,0:T(8,128)(2,1)}, bf16[128,768]{1,0:T(8,128)(2,1)S(1)}, u32[]{:S(2)}, u32[]{:S(2)}) collective-permute-start(bf16[128,768]{1,0:T(8,128)(2,1)} %bitcast.28), channel_id=1, source_target_pairs={{0,12},{1,13},{2,14},{3,15},{4,8},{5,9},{6,10},{7,11},{8,4},{9,5},... | collective-permute-start | bytes 589832 | tf_op jit(solution)/shard_map/ppermute | solution.py:40
  4.1 2.0 %shard_map.229 = (bf16[24,1408]{1,0:T(8,128)(2,1)}, bf16[24,640]{1,0:T(8,128)(2,1)}, bf16[24,640]{1,0:T(8,128)(2,1)}, bf16[24,640]{1,0:T(8,128)(2,1)}) custom-call(s32[1]{0:T(128)} %bitcast.2.refs_0_, bf16[24,768]{1,0:T(8,128)(2,1)} %refs_1_.3, bf16[24,768]{1,0:T(8,128)(2,1)} %refs_2_.1, bf16[24,768]{1,0:T(8,128)(2,1)} %refs_3_.1, bf16[16,24]{1,0:T(8,128)(2,1)} %bitcast.46, ...), custom_call_target="tpu_custom_call" | custom-call | flops 1000000 | bytes 1000000 | tf_op jit(solution)/shard_map/pallas_call | solution.py:106
  6.1 3.2 %collective-permute-start.2 = (bf16[24,640]{1,0:T(8,128)(2,1)}, bf16[24,640]{1,0:T(8,128)(2,1)S(1)}, u32[]{:S(2)}, u32[]{:S(2)}) collective-permute-start(bf16[24,640]{1,0:T(8,128)(2,1)} %get-tuple-element.93), channel_id=1, source_target_pairs={{0,8},{1,9},{2,10},{3,11},{4,12},{5,13},{6,14},{7,15},{8,0},{9,1},... | collective-permute-start | bytes 92168 | tf_op jit(solution)/shard_map/ppermute | solution.py:649
  9.3 5.8 %collective-permute-done.1.refs_2_ = bf16[24,640]{1,0:T(8,128)(2,1)S(1)} collective-permute-done((bf16[24,640]{1,0:T(8,128)(2,1)}, bf16[24,640]{1,0:T(8,128)(2,1)S(1)}, u32[]{:S(2)}, u32[]{:S(2)}) %collective-permute-start.1) | collective-permute-done | bytes 30752 | tf_op jit(solution)/shard_map/ppermute | solution.py:649
  15.1 0.9 copy-done.20
  16.0 1.2 shard_map.230
  17.2 3.9 %all-to-all-start = ((bf16[8,120,640]{2,1,0:T(8,128)(2,1)}), bf16[8,120,640]{2,1,0:T(8,128)(2,1)S(1)}, u32[]{:S(2)}, u32[]{:S(2)}) async-start(bf16[8,120,640]{2,1,0:T(8,128)(2,1)} %shard_map.230), calls=%async_computation | async-start | bytes 2457600 | tf_op jit(solution)/shard_map/all_to_all | solution.py:50
  21.1 1.5 %collective-permute-start.4 = (bf16[128,768]{1,0:T(8,128)(2,1)S(1)}, bf16[128,768]{1,0:T(8,128)(2,1)S(1)}, u32[]{:S(2)}, u32[]{:S(2)}) collective-permute-start(bf16[128,768]{1,0:T(8,128)(2,1)S(1)} %collective-permute-done.refs_3_.refs_7_.refs_5_), channel_id=1, source_target_pairs={{0,16},{16,0},{1,17},{17,1},{2,18},{18,2},{3,19},{19,3},{4,20},{20... | collective-permute-start | bytes 589832 | tf_op jit(solution)/shard_map/ppermute | solution.py:34
  22.8 1.6 %shard_map.231 = (f32[3,256]{1,0:T(4,128)S(1)}, bf16[2,128,640]{2,1,0:T(8,128)(2,1)S(1)}, bf16[2,128,640]{2,1,0:T(8,128)(2,1)S(1)}, f32[128,16]{1,0:T(8,128)S(1)}, bf16[640,512]{1,0:T(8,128)(2,1)S(1)}) custom-call(s32[1]{0:T(128)} %bitcast.2.refs_0_, f32[32,12]{1,0:T(8,128)S(1)} %copy.26.refs_1_, s32[128,1]{1,0:T(8,128)S(1)} %copy.27.refs_2_), custom_call_target="tpu_custom_call" | custom-call | flops 1000000 | bytes 1000000 | tf_op jit(solution)/shard_map/pallas_call | solution.py:106
  24.4 0.8 copy-done.10
  25.2 0.7 copy-done.18
  26.0 10.8 %all-to-all-done.refs_2_ = bf16[8,120,640]{2,1,0:T(8,128)(2,1)S(1)} async-done(((bf16[8,120,640]{2,1,0:T(8,128)(2,1)}), bf16[8,120,640]{2,1,0:T(8,128)(2,1)S(1)}, u32[]{:S(2)}, u32[]{:S(2)}) %all-to-all-start) | async-done | bytes 1228832 | tf_op jit(solution)/shard_map/all_to_all | solution.py:50
  36.8 1.7 %shard_map.232 = (bf16[768,640]{1,0:T(8,128)(2,1)S(1)}, bf16[192,768]{1,0:T(8,128)(2,1)S(1)}, f32[8,768]{1,0:T(8,128)S(1)}, bf16[256,576]{1,0:T(8,128)(2,1)S(1)}...) custom-call(s32[1]{0:T(128)} %bitcast.2.refs_0_, ...), custom_call_target="tpu_custom_call" | custom-call | flops 1000000 | bytes 1000000 | tf_op jit(solution)/shard_map/pallas_call | solution.py:106
  39.2 1.0 collective-permute-done.5
  40.2 3.1 %collective-permute-start.8 = (bf16[128,768]{1,0:T(8,128)(2,1)S(1)}, bf16[128,768]{1,0:T(8,128)(2,1)S(1)}, u32[]{:S(2)}, u32[]{:S(2)}) collective-permute-start(bf16[128,768]{1,0:T(8,128)(2,1)S(1)} %add_convert_fusion.1), channel_id=1, source_target_pairs={{0,12},{1,13},{2,14},{3,15},{4,8},{5,9},{6,10},{7,11},{8,4},{9,5},... | collective-permute-start | bytes 589832 | tf_op jit(solution)/shard_map/ppermute | solution.py:40
  43.3 1.5 shard_map.233
  45.6 2.6 %collective-permute-done.8.refs_3_ = bf16[128,768]{1,0:T(8,128)(2,1)S(1)} collective-permute-done((bf16[128,768]{1,0:T(8,128)(2,1)S(1)}, bf16[128,768]{1,0:T(8,128)(2,1)S(1)}, u32[]{:S(2)}, u32[]{:S(2)}) %collective-permute-start.8) | collective-permute-done | bytes 196640 | tf_op jit(solution)/shard_map/ppermute | solution.py:40
  48.2 0.8 copy-done.24
  49.1 1.0 shard_map.234
  50.1 19.1 %all_to_all.20 = bf16[16,40,384]{2,1,0:T(8,128)(2,1)S(1)} all-to-all(bf16[16,40,384]{2,1,0:T(8,128)(2,1)S(1)} %bitcast.42), channel_id=1, replica_groups=mesh['dp'=2,'expert'=16] {'expert'}, dimensions={0} | all-to-all | bytes 983040 | tf_op jit(solution)/shard_map/all_to_all | solution.py:44
  69.1 3.0 %collective-permute-start.9 = (bf16[640,384]{1,0:T(8,128)(2,1)S(1)}, bf16[640,384]{1,0:T(8,128)(2,1)S(1)}, u32[]{:S(2)}, u32[]{:S(2)}) collective-permute-start(bf16[640,384]{1,0:T(8,128)(2,1)S(1)} %bitcast.36), channel_id=1, source_target_pairs={{0,16},{16,0},{1,17},{17,1},{2,18},{18,2},{3,19},{19,3},{4,20},{20... | collective-permute-start | bytes 1474568 | tf_op jit(solution)/shard_map/ppermute | solution.py:34
  72.2 1.5 %collective-permute-done.9.refs_2_ = bf16[640,384]{1,0:T(8,128)(2,1)S(1)} collective-permute-done((bf16[640,384]{1,0:T(8,128)(2,1)S(1)}, bf16[640,384]{1,0:T(8,128)(2,1)S(1)}, u32[]{:S(2)}, u32[]{:S(2)}) %collective-permute-start.9) | collective-permute-done | bytes 491552 | tf_op jit(solution)/shard_map/ppermute | solution.py:34
  73.7 4.6 %shard_map.235 = (bf16[320,768]{1,0:T(8,128)(2,1)S(1)}, bf16[320,768]{1,0:T(8,128)(2,1)S(1)}, bf16[160,768]{1,0:T(8,128)(2,1)S(1)}, f32[160,16]{1,0:T(8,128)S(1)...) custom-call(s32[1]{0:T(128)} %bitcast.refs_1_.refs_0_, ...), custom_call_target="tpu_custom_call" | custom-call | flops 1000000 | bytes 1000000 | tf_op jit(solution)/shard_map/pallas_call | solution.py:106
  78.7 1.5 collective-permute-done.10.refs_2_
  80.2 1.3 shard_map.236
  81.5 16.3 %all_to_all.21 = bf16[16,40,384]{2,1,0:T(8,128)(2,1)S(1)} all-to-all(bf16[16,40,384]{2,1,0:T(8,128)(2,1)S(1)} %bitcast.41), channel_id=1, replica_groups=mesh['dp'=2,'expert'=16] {'expert'}, dimensions={0} | all-to-all | bytes 983040 | tf_op jit(solution)/shard_map/all_to_all | solution.py:44
  98.3 2.5 %collective-permute-start.12 = (bf16[128,768]{1,0:T(8,128)(2,1)S(1)}, bf16[128,768]{1,0:T(8,128)(2,1)S(1)}, u32[]{:S(2)}, u32[]{:S(2)}) collective-permute-start(bf16[128,768]{1,0:T(8,128)(2,1)S(1)} %get-tuple-element.123.refs_0_), channel_id=1, source_target_pairs={{0,16},{16,0},{1,17},{17,1},{2,18},{18,2},{3,19},{19,3},{4,20},{20... | collective-permute-start | bytes 589832 | tf_op jit(solution)/shard_map/ppermute | solution.py:34
  100.9 1.3 collective-permute-start.11
  102.2 3.2 %shard_map.238 = (f32[768,576]{1,0:T(8,128)S(1)}, f32[192,768]{1,0:T(8,128)S(1)}, f32[128,768]{1,0:T(8,128)S(1)}, bf16[128,768]{1,0:T(8,128)(2,1)}, bf16[256,576...) custom-call(bf16[128,768]{1,0:T(8,128)(2,1)S(1)} %get-tuple-element.123.refs_0_, ...), custom_call_target="tpu_custom_call" | custom-call | flops 1000000 | bytes 1000000 | tf_op jit(solution)/shard_map/pallas_call | solution.py:106
  105.4 3.8 %collective-permute-done.11.refs_0_ = bf16[128,768]{1,0:T(8,128)(2,1)S(1)} collective-permute-done((bf16[128,768]{1,0:T(8,128)(2,1)S(1)}, bf16[128,768]{1,0:T(8,128)(2,1)S(1)}, u32[]{:S(2)}, u32[]{:S(2)}) %collective-permute-start.11) | collective-permute-done | bytes 196640 | tf_op jit(solution)/shard_map/ppermute | solution.py:40
  109.2 0.9 collective-permute-start.13
  110.1 1.1 collective-permute-done.13.refs_1_
  111.2 2.2 %shard_map.239 = (f32[128,768]{1,0:T(8,128)S(1)}, bf16[128,768]{1,0:T(8,128)(2,1)S(1)}, bf16[256,576]{1,0:T(8,128)(2,1)S(1)}, f32[1,768]{1,0:T(1,128)S(1)}, f32[3,256]{1,0:T(4,128)S(1)}) custom-call(bf16[128,768]{1,0:T(8,128)(2,1)S(1)} %collective-permute-done.11.refs_0_, bf16[128,768]{1,0:T(8,128)(2,1)S(1)} %collective-permute-done.13.refs_1_, ...), custom_call_target="tpu_custom_call" | custom-call | flops 1000000 | bytes 1000000 | tf_op jit(solution)/shard_map/pallas_call | solution.py:106
  113.4 0.7 copy-done.14
  114.1 2.0 %shard_map.240 = bf16[8,120,640]{2,1,0:T(8,128)(2,1)} custom-call(bf16[128,768]{1,0:T(8,128)(2,1)S(1)} %collective-permute-done.11.refs_0_, bf16[128,768]{1,0:T(8,128)(2,1)S(1)} %collective-permute-done.13.refs_1_, bf16[256,192]{1,0:T(8,128)(2,1)S(1)} %get-tuple-element.130.refs_2_, bf16[256,576]{1,0:T(8,128)(2,1)S(1)} %get-tuple-element.133.refs_3_, ...), custom_call_target="tpu_custom_call" | custom-call | flops 1000000 | bytes 1000000 | tf_op jit(solution)/shard_map/pallas_call | solution.py:106
  116.1 6.0 %all-to-all-start.3 = ((bf16[8,120,640]{2,1,0:T(8,128)(2,1)}), bf16[8,120,640]{2,1,0:T(8,128)(2,1)S(1)}, u32[]{:S(2)}, u32[]{:S(2)}) async-start(bf16[8,120,640]{2,1,0:T(8,128)(2,1)} %shard_map.240), calls=%async_computation.3 | async-start | bytes 2457600 | tf_op jit(solution)/shard_map/all_to_all | solution.py:50
  122.2 0.9 collective-permute-start.15
  123.1 5.0 %fusion = f32[768,1536]{1,0:T(8,128)} fusion(bf16[320,768]{1,0:T(8,128)(2,1)} %copy-done.4, bf16[320,1536]{1,0:T(8,128)(2,1)} %copy-done.9), kind=kOutput, calls=%fused_computation.2 | convolution fusion | flops 754974720 | bytes 6193152 | tf_op jit(solution)/shard_map/dot_general | solution.py:20
  128.9 2.2 %collective-permute-start.16 = (bf16[128,768]{1,0:T(8,128)(2,1)}, bf16[128,768]{1,0:T(8,128)(2,1)}, u32[]{:S(2)}, u32[]{:S(2)}) collective-permute-start(bf16[128,768]{1,0:T(8,128)(2,1)} %add_convert_fusion), channel_id=1, source_target_pairs={{0,12},{1,13},{2,14},{3,15},{4,8},{5,9},{6,10},{7,11},{8,4},{9,5},... | collective-permute-start | bytes 589832 | tf_op jit(solution)/shard_map/ppermute | solution.py:40
  131.1 3.6 %fusion.1 = f32[1536,768]{1,0:T(8,128)} fusion(bf16[320,1536]{1,0:T(8,128)(2,1)S(1)} %get-tuple-element.143, bf16[320,768]{1,0:T(8,128)(2,1)S(1)} %copy-done.13), kind=kOutput, calls=%fused_computation.3 | convolution fusion | flops 754974720 | bytes 6193152 | tf_op jit(solution)/shard_map/dot_general | solution.py:20
  134.7 1.4 shard_map.241
  136.1 1.8 %all-to-all-done.3.refs_1_ = bf16[8,120,640]{2,1,0:T(8,128)(2,1)S(1)} async-done(((bf16[8,120,640]{2,1,0:T(8,128)(2,1)}), bf16[8,120,640]{2,1,0:T(8,128)(2,1)S(1)}, u32[]{:S(2)}, u32[]{:S(2)}) %all-to-all-start.3) | async-done | bytes 1228832 | tf_op jit(solution)/shard_map/all_to_all | solution.py:50
  137.9 0.8 shard_map.243
  138.7 4.1 %collective-permute-start.17 = (bf16[24,640]{1,0:T(8,128)(2,1)S(1)}, bf16[24,640]{1,0:T(8,128)(2,1)S(1)}, u32[]{:S(2)}, u32[]{:S(2)}) collective-permute-start(bf16[24,640]{1,0:T(8,128)(2,1)S(1)} %get-tuple-element.157), channel_id=1, source_target_pairs={{0,24},{1,25},{2,26},{3,27},{4,28},{5,29},{6,30},{7,31},{8,16},{9,... | collective-permute-start | bytes 92168 | tf_op jit(solution)/shard_map/ppermute | solution.py:649
  143.3 0.9 collective-permute-done.16.refs_2_
  144.2 1.9 %shard_map.242 = bf16[128,768]{1,0:T(8,128)(2,1)} custom-call(f32[128,768]{1,0:T(8,128)S(1)} %copy-done.17, bf16[128,768]{1,0:T(8,128)(2,1)} %collective-permute-done.14.refs_1_, bf16[128,768]{1,0:T(8,128)(2,1)} %collective-permute-done.16.refs_2_, f32[128,768]{1,0:T(8,128)S(1)} %get-tuple-element.154.refs_3_, bf16[128,768]{1,0:T(8,128)(2,1)S(1)} %bitcast.33, ...), custom_call_target="tpu_custom_call" | custom-call | flops 1000000 | bytes 1000000 | tf_op jit(solution)/shard_map/pallas_call | solution.py:106
  146.4 1.0 collective-permute-done.18.refs_3_
  147.4 0.9 shard_map.244
  (80 shorter events, 4.4 us)
Async XLA Ops:
  0.6 22.0 %copy-start.27 = (f32[32,12]{0,1:T(8,128)S(1)}, f32[32,12]{0,1:T(8,128)}, u32[]{:S(2)}) copy-start(f32[32,12]{0,1:T(8,128)} %param.20) | copy-start | bytes 4612
  0.7 22.0 %copy-start.28 = (s32[1,128,1]{1,2,0:T(1,128)S(1)}, s32[1,128,1]{1,2,0:T(1,128)}, u32[]{:S(2)}) copy-start(s32[1,128,1]{1,2,0:T(1,128)} %param.26) | copy-start | bytes 1540
  0.7 14.4 %collective-permute-start = (bf16[128,768]{1,0:T(8,128)(2,1)}, bf16[128,768]{1,0:T(8,128)(2,1)S(1)}, u32[]{:S(2)}, u32[]{:S(2)}) collective-permute-start(bf16[128,768]{1,0:T(8,128)(2,1)} %bitcast.28), channel_id=1, source_target_pairs={{0,12},{1,13},{2,14},{3,15},{4,8},{5,9},{6,10},{7,11},{8,4},{9,5},... | collective-permute-start | bytes 589832 | tf_op jit(solution)/shard_map/ppermute | solution.py:40
  6.1 9.0 %collective-permute-start.1 = (bf16[24,640]{1,0:T(8,128)(2,1)}, bf16[24,640]{1,0:T(8,128)(2,1)S(1)}, u32[]{:S(2)}, u32[]{:S(2)}) collective-permute-start(bf16[24,640]{1,0:T(8,128)(2,1)} %get-tuple-element.92), channel_id=1, source_target_pairs={{0,24},{1,25},{2,26},{3,27},{4,28},{5,29},{6,30},{7,31},{8,16},{9,... | collective-permute-start | bytes 92168 | tf_op jit(solution)/shard_map/ppermute | solution.py:649
  6.1 9.0 %collective-permute-start.2 = (bf16[24,640]{1,0:T(8,128)(2,1)}, bf16[24,640]{1,0:T(8,128)(2,1)S(1)}, u32[]{:S(2)}, u32[]{:S(2)}) collective-permute-start(bf16[24,640]{1,0:T(8,128)(2,1)} %get-tuple-element.93), channel_id=1, source_target_pairs={{0,8},{1,9},{2,10},{3,11},{4,12},{5,13},{6,14},{7,15},{8,0},{9,1},... | collective-permute-start | bytes 92168 | tf_op jit(solution)/shard_map/ppermute | solution.py:649
  9.3 5.8 %collective-permute-start.3 = (bf16[24,640]{1,0:T(8,128)(2,1)}, bf16[24,640]{1,0:T(8,128)(2,1)S(1)}, u32[]{:S(2)}, u32[]{:S(2)}) collective-permute-start(bf16[24,640]{1,0:T(8,128)(2,1)} %get-tuple-element.94), channel_id=1, source_target_pairs={{0,16},{1,17},{2,18},{3,19},{4,20},{5,21},{6,22},{7,23},{8,24},{9,... | collective-permute-start | bytes 92168 | tf_op jit(solution)/shard_map/ppermute | solution.py:649
  15.1 0.9 copy-start.20
  17.2 21.9 %copy-start = (bf16[1,128,768]{2,1,0:T(8,128)(2,1)S(1)}, bf16[1,128,768]{2,1,0:T(8,128)(2,1)}, u32[]{:S(2)}) copy-start(bf16[1,128,768]{2,1,0:T(8,128)(2,1)} %param.14) | copy-start | bytes 589828
  17.2 26.1 %copy-start.25 = (s32[1,256]{1,0:T(1,128)S(1)}, s32[1,256]{1,0:T(1,128)}, u32[]{:S(2)}) copy-start(s32[1,256]{1,0:T(1,128)} %refs_1_.4) | copy-start | bytes 3076
  17.2 19.6 %all-to-all-start = ((bf16[8,120,640]{2,1,0:T(8,128)(2,1)}), bf16[8,120,640]{2,1,0:T(8,128)(2,1)S(1)}, u32[]{:S(2)}, u32[]{:S(2)}) async-start(bf16[8,120,640]{2,1,0:T(8,128)(2,1)} %shard_map.230), calls=%async_computation | async-start | bytes 2457600 | tf_op jit(solution)/shard_map/all_to_all | solution.py:50
  21.1 27.2 %copy-start.3 = (bf16[1,128,768]{2,1,0:T(8,128)(2,1)S(1)}, bf16[1,128,768]{2,1,0:T(8,128)(2,1)}, u32[]{:S(2)}) copy-start(bf16[1,128,768]{2,1,0:T(8,128)(2,1)} %param.27) | copy-start | bytes 589828
  21.1 4.9 %collective-permute-start.4 = (bf16[128,768]{1,0:T(8,128)(2,1)S(1)}, bf16[128,768]{1,0:T(8,128)(2,1)S(1)}, u32[]{:S(2)}, u32[]{:S(2)}) collective-permute-start(bf16[128,768]{1,0:T(8,128)(2,1)S(1)} %collective-permute-done.refs_3_.refs_7_.refs_5_), channel_id=1, source_target_pairs={{0,16},{16,0},{1,17},{17,1},{2,18},{18,2},{3,19},{19,3},{4,20},{20... | collective-permute-start | bytes 589832 | tf_op jit(solution)/shard_map/ppermute | solution.py:34
  25.9 22.3 %copy-start.23 = (f32[128,16]{1,0:T(8,128)}, f32[128,16]{1,0:T(8,128)S(1)}, u32[]{:S(2)}) copy-start(f32[128,16]{1,0:T(8,128)S(1)} %get-tuple-element.111.refs_6_) | copy-start | bytes 24580
  25.9 71.9 %copy-start.7 = (bf16[2,128,640]{2,1,0:T(8,128)(2,1)}, bf16[2,128,640]{2,1,0:T(8,128)(2,1)S(1)}, u32[]{:S(2)}) copy-start(bf16[2,128,640]{2,1,0:T(8,128)(2,1)S(1)} %get-tuple-element.121.refs_1_) | copy-start | bytes 983044
  36.8 11.5 %copy-start.11 = (bf16[640,512]{1,0:T(8,128)(2,1)S(1)}, bf16[640,512]{1,0:T(8,128)(2,1)}, u32[]{:S(2)}) copy-start(bf16[640,512]{1,0:T(8,128)(2,1)} %copy-done.10) | copy-start | bytes 1966084
  38.4 1.7 %collective-permute-start.5 = (bf16[128,768]{1,0:T(8,128)(2,1)S(1)}, bf16[128,768]{1,0:T(8,128)(2,1)S(1)}, u32[]{:S(2)}, u32[]{:S(2)}) collective-permute-start(bf16[128,768]{1,0:T(8,128)(2,1)S(1)} %get-tuple-element.103), channel_id=1, source_target_pairs={{0,16},{16,0},{1,17},{17,1},{2,18},{18,2},{3,19},{19,3},{4,20},{20... | collective-permute-start | bytes 589832 | tf_op jit(solution)/shard_map/ppermute | solution.py:34
  39.1 4.2 %collective-permute-start.6 = (bf16[128,768]{1,0:T(8,128)(2,1)S(1)}, bf16[128,768]{1,0:T(8,128)(2,1)S(1)}, u32[]{:S(2)}, u32[]{:S(2)}) collective-permute-start(bf16[128,768]{1,0:T(8,128)(2,1)S(1)} %bitcast.29), channel_id=1, source_target_pairs={{0,16},{16,0},{1,17},{17,1},{2,18},{18,2},{3,19},{19,3},{4,20},{20... | collective-permute-start | bytes 589832 | tf_op jit(solution)/shard_map/ppermute | solution.py:34
  40.2 8.0 %collective-permute-start.8 = (bf16[128,768]{1,0:T(8,128)(2,1)S(1)}, bf16[128,768]{1,0:T(8,128)(2,1)S(1)}, u32[]{:S(2)}, u32[]{:S(2)}) collective-permute-start(bf16[128,768]{1,0:T(8,128)(2,1)S(1)} %add_convert_fusion.1), channel_id=1, source_target_pairs={{0,12},{1,13},{2,14},{3,15},{4,8},{5,9},{6,10},{7,11},{8,4},{9,5},... | collective-permute-start | bytes 589832 | tf_op jit(solution)/shard_map/ppermute | solution.py:40
  43.3 30.4 %copy-start.1 = (bf16[1,768,1536]{2,1,0:T(8,128)(2,1)S(1)}, bf16[1,768,1536]{2,1,0:T(8,128)(2,1)}, u32[]{:S(2)}) copy-start(bf16[1,768,1536]{2,1,0:T(8,128)(2,1)} %param.23) | copy-start | bytes 7077892
  43.3 30.4 %copy-start.2 = (bf16[1,1536,768]{2,1,0:T(8,128)(2,1)S(1)}, bf16[1,1536,768]{2,1,0:T(8,128)(2,1)}, u32[]{:S(2)}) copy-start(bf16[1,1536,768]{2,1,0:T(8,128)(2,1)} %param.24) | copy-start | bytes 7077892
  44.7 3.5 %collective-permute-start.7 = (bf16[128,768]{1,0:T(8,128)(2,1)S(1)}, bf16[128,768]{1,0:T(8,128)(2,1)S(1)}, u32[]{:S(2)}, u32[]{:S(2)}) collective-permute-start(bf16[128,768]{1,0:T(8,128)(2,1)S(1)} %get-tuple-element.109), channel_id=1, source_target_pairs={{0,16},{16,0},{1,17},{17,1},{2,18},{18,2},{3,19},{19,3},{4,20},{20... | collective-permute-start | bytes 589832 | tf_op jit(solution)/shard_map/ppermute | solution.py:34
  48.2 0.8 copy-start.24
  50.0 28.2 %copy-start.21 = (f32[128,1]{1,0:T(8,128)}, f32[128,1]{1,0:T(8,128)S(1)}, u32[]{:S(2)}) copy-start(f32[128,1]{1,0:T(8,128)S(1)} %get-tuple-element.146.refs_6_) | copy-start | bytes 1540
  50.1 47.8 %copy-start.5 = (f32[128,768]{1,0:T(8,128)}, f32[128,768]{1,0:T(8,128)S(1)}, u32[]{:S(2)}) copy-start(f32[128,768]{1,0:T(8,128)S(1)} %get-tuple-element.122.refs_2_.refs_3_) | copy-start | bytes 1179652
  69.1 4.5 %collective-permute-start.9 = (bf16[640,384]{1,0:T(8,128)(2,1)S(1)}, bf16[640,384]{1,0:T(8,128)(2,1)S(1)}, u32[]{:S(2)}, u32[]{:S(2)}) collective-permute-start(bf16[640,384]{1,0:T(8,128)(2,1)S(1)} %bitcast.36), channel_id=1, source_target_pairs={{0,16},{16,0},{1,17},{17,1},{2,18},{18,2},{3,19},{19,3},{4,20},{20... | collective-permute-start | bytes 1474568 | tf_op jit(solution)/shard_map/ppermute | solution.py:34
  78.3 20.1 %copy-start.4 = (bf16[320,768]{1,0:T(8,128)(2,1)}, bf16[320,768]{1,0:T(8,128)(2,1)S(1)}, u32[]{:S(2)}) copy-start(bf16[320,768]{1,0:T(8,128)(2,1)S(1)} %get-tuple-element.116) | copy-start | bytes 1474564
  78.3 20.1 %copy-start.12 = (bf16[320,768]{1,0:T(8,128)(2,1)}, bf16[320,768]{1,0:T(8,128)(2,1)S(1)}, u32[]{:S(2)}) copy-start(bf16[320,768]{1,0:T(8,128)(2,1)S(1)} %get-tuple-element.144) | copy-start | bytes 1474564
  78.3 35.1 %copy-start.9 = (bf16[320,1536]{1,0:T(8,128)(2,1)}, bf16[320,1536]{1,0:T(8,128)(2,1)S(1)}, u32[]{:S(2)}) copy-start(bf16[320,1536]{1,0:T(8,128)(2,1)S(1)} %get-tuple-element.142) | copy-start | bytes 2949124
  78.3 1.9 %collective-permute-start.10 = (bf16[2,160,768]{2,1,0:T(8,128)(2,1)S(1)}, bf16[2,160,768]{2,1,0:T(8,128)(2,1)S(1)}, u32[]{:S(2)}, u32[]{:S(2)}) collective-permute-start(bf16[2,160,768]{2,1,0:T(8,128)(2,1)S(1)} %get-tuple-element.115), channel_id=1, source_target_pairs={{0,16},{16,0},{1,17},{17,1},{2,18},{18,2},{3,19},{19,3},{4,20},{20... | collective-permute-start | bytes 1474568 | tf_op jit(solution)/shard_map/ppermute | solution.py:34
  98.3 3.8 %collective-permute-start.12 = (bf16[128,768]{1,0:T(8,128)(2,1)S(1)}, bf16[128,768]{1,0:T(8,128)(2,1)S(1)}, u32[]{:S(2)}, u32[]{:S(2)}) collective-permute-start(bf16[128,768]{1,0:T(8,128)(2,1)S(1)} %get-tuple-element.123.refs_0_), channel_id=1, source_target_pairs={{0,16},{16,0},{1,17},{17,1},{2,18},{18,2},{3,19},{19,3},{4,20},{20... | collective-permute-start | bytes 589832 | tf_op jit(solution)/shard_map/ppermute | solution.py:34
  100.9 8.3 %collective-permute-start.11 = (bf16[128,768]{1,0:T(8,128)(2,1)S(1)}, bf16[128,768]{1,0:T(8,128)(2,1)S(1)}, u32[]{:S(2)}, u32[]{:S(2)}) collective-permute-start(bf16[128,768]{1,0:T(8,128)(2,1)S(1)} %get-tuple-element.123.refs_0_), channel_id=1, source_target_pairs={{0,12},{1,13},{2,14},{3,15},{4,8},{5,9},{6,10},{7,11},{8,4},{9,5},... | collective-permute-start | bytes 589832 | tf_op jit(solution)/shard_map/ppermute | solution.py:40
  105.4 10.7 %copy-start.16 = (f32[128,768]{1,0:T(8,128)}, f32[128,768]{1,0:T(8,128)S(1)}, u32[]{:S(2)}) copy-start(f32[128,768]{1,0:T(8,128)S(1)} %get-tuple-element.150.refs_0_) | copy-start | bytes 1179652
  109.2 2.0 %collective-permute-start.13 = (bf16[128,768]{1,0:T(8,128)(2,1)S(1)}, bf16[128,768]{1,0:T(8,128)(2,1)S(1)}, u32[]{:S(2)}, u32[]{:S(2)}) collective-permute-start(bf16[128,768]{1,0:T(8,128)(2,1)S(1)} %collective-permute-done.11.refs_0_), channel_id=1, source_target_pairs={{0,16},{16,0},{1,17},{17,1},{2,18},{18,2},{3,19},{19,3},{4,20},{20... | collective-permute-start | bytes 589832 | tf_op jit(solution)/shard_map/ppermute | solution.py:34
  114.1 2.0 %copy-start.26 = (bf16[128,768]{1,0:T(8,128)(2,1)}, bf16[128,768]{1,0:T(8,128)(2,1)S(1)}, u32[]{:S(2)}) copy-start(bf16[128,768]{1,0:T(8,128)(2,1)S(1)} %get-tuple-element.153) | copy-start | bytes 589828
  116.1 21.7 %all-to-all-start.3 = ((bf16[8,120,640]{2,1,0:T(8,128)(2,1)}), bf16[8,120,640]{2,1,0:T(8,128)(2,1)S(1)}, u32[]{:S(2)}, u32[]{:S(2)}) async-start(bf16[8,120,640]{2,1,0:T(8,128)(2,1)} %shard_map.240), calls=%async_computation.3 | async-start | bytes 2457600 | tf_op jit(solution)/shard_map/all_to_all | solution.py:50
  122.2 6.0 %collective-permute-start.15 = (bf16[128,768]{1,0:T(8,128)(2,1)}, bf16[128,768]{1,0:T(8,128)(2,1)S(1)}, u32[]{:S(2)}, u32[]{:S(2)}) collective-permute-start(bf16[128,768]{1,0:T(8,128)(2,1)} %copy-done.26), channel_id=1, source_target_pairs={{0,16},{16,0},{1,17},{17,1},{2,18},{18,2},{3,19},{19,3},{4,20},{20... | collective-permute-start | bytes 589832 | tf_op jit(solution)/shard_map/ppermute | solution.py:34
  123.1 5.1 %copy-start.15 = (f32[128,768]{1,0:T(8,128)S(1)}, f32[128,768]{1,0:T(8,128)}, u32[]{:S(2)}) copy-start(f32[128,768]{1,0:T(8,128)} %copy-done.14) | copy-start | bytes 1179652
  123.1 8.0 %copy-start.13 = (bf16[320,768]{1,0:T(8,128)(2,1)S(1)}, bf16[320,768]{1,0:T(8,128)(2,1)}, u32[]{:S(2)}) copy-start(bf16[320,768]{1,0:T(8,128)(2,1)} %copy-done.12) | copy-start | bytes 1474564
  128.2 15.1 %collective-permute-start.14 = (bf16[128,768]{1,0:T(8,128)(2,1)}, bf16[128,768]{1,0:T(8,128)(2,1)}, u32[]{:S(2)}, u32[]{:S(2)}) collective-permute-start(bf16[128,768]{1,0:T(8,128)(2,1)} %get-tuple-element.151), channel_id=1, source_target_pairs={{0,16},{16,0},{1,17},{17,1},{2,18},{18,2},{3,19},{19,3},{4,20},{20... | collective-permute-start | bytes 589832 | tf_op jit(solution)/shard_map/ppermute | solution.py:34
  128.9 15.3 %collective-permute-start.16 = (bf16[128,768]{1,0:T(8,128)(2,1)}, bf16[128,768]{1,0:T(8,128)(2,1)}, u32[]{:S(2)}, u32[]{:S(2)}) collective-permute-start(bf16[128,768]{1,0:T(8,128)(2,1)} %add_convert_fusion), channel_id=1, source_target_pairs={{0,12},{1,13},{2,14},{3,15},{4,8},{5,9},{6,10},{7,11},{8,4},{9,5},... | collective-permute-start | bytes 589832 | tf_op jit(solution)/shard_map/ppermute | solution.py:40
  131.1 3.6 %copy-start.6 = (f32[128,768]{1,0:T(8,128)S(1)}, f32[128,768]{1,0:T(8,128)}, u32[]{:S(2)}) copy-start(f32[128,768]{1,0:T(8,128)} %copy-done.5) | copy-start | bytes 1179652
  131.1 3.6 %copy-start.8 = (bf16[2,128,640]{2,1,0:T(8,128)(2,1)S(1)}, bf16[2,128,640]{2,1,0:T(8,128)(2,1)}, u32[]{:S(2)}) copy-start(bf16[2,128,640]{2,1,0:T(8,128)(2,1)} %copy-done.7) | copy-start | bytes 983044
  131.1 3.6 %copy-start.19 = (bf16[2,128,640]{2,1,0:T(8,128)(2,1)S(1)}, bf16[2,128,640]{2,1,0:T(8,128)(2,1)}, u32[]{:S(2)}) copy-start(bf16[2,128,640]{2,1,0:T(8,128)(2,1)} %copy-done.18) | copy-start | bytes 983044
  131.1 3.6 %copy-start.22 = (f32[128,1]{1,0:T(8,128)S(1)}, f32[128,1]{1,0:T(8,128)}, u32[]{:S(2)}) copy-start(f32[128,1]{1,0:T(8,128)} %copy-done.21) | copy-start | bytes 1540
  134.7 9.5 %copy-start.17 = (f32[128,768]{1,0:T(8,128)S(1)}, f32[128,768]{1,0:T(8,128)}, u32[]{:S(2)}) copy-start(f32[128,768]{1,0:T(8,128)} %copy-done.16) | copy-start | bytes 1179652
  138.7 7.7 %collective-permute-start.17 = (bf16[24,640]{1,0:T(8,128)(2,1)S(1)}, bf16[24,640]{1,0:T(8,128)(2,1)S(1)}, u32[]{:S(2)}, u32[]{:S(2)}) collective-permute-start(bf16[24,640]{1,0:T(8,128)(2,1)S(1)} %get-tuple-element.157), channel_id=1, source_target_pairs={{0,24},{1,25},{2,26},{3,27},{4,28},{5,29},{6,30},{7,31},{8,16},{9,... | collective-permute-start | bytes 92168 | tf_op jit(solution)/shard_map/ppermute | solution.py:649
  142.8 4.6 %collective-permute-start.18 = (bf16[24,640]{1,0:T(8,128)(2,1)S(1)}, bf16[24,640]{1,0:T(8,128)(2,1)S(1)}, u32[]{:S(2)}, u32[]{:S(2)}) collective-permute-start(bf16[24,640]{1,0:T(8,128)(2,1)S(1)} %get-tuple-element.158), channel_id=1, source_target_pairs={{0,8},{1,9},{2,10},{3,11},{4,12},{5,13},{6,14},{7,15},{8,0},{9,1},... | collective-permute-start | bytes 92168 | tf_op jit(solution)/shard_map/ppermute | solution.py:649
  142.9 4.6 %collective-permute-start.19 = (bf16[24,640]{1,0:T(8,128)(2,1)S(1)}, bf16[24,640]{1,0:T(8,128)(2,1)S(1)}, u32[]{:S(2)}, u32[]{:S(2)}) collective-permute-start(bf16[24,640]{1,0:T(8,128)(2,1)S(1)} %get-tuple-element.159), channel_id=1, source_target_pairs={{0,16},{1,17},{2,18},{3,19},{4,20},{5,21},{6,22},{7,23},{8,24},{9,... | collective-permute-start | bytes 92168 | tf_op jit(solution)/shard_map/ppermute | solution.py:649
  (3 other events, 2.3 us)

commit v6 on v5

--- a/solution.py
+++ b/solution.py
@@ -36,8 +36,7 @@
 
 def swap_pair(value):
     n = lax.axis_size("expert")
-    other = 3 * n // 4
-    return lax.ppermute(value, "expert", [(i, i ^ other) for i in range(n)])
+    return lax.ppermute(value, "expert", [(i, i ^ 1) for i in range(n)])
 
 
 def exchange(value):
@@ -126,6 +125,7 @@
 def pack_weights(group_ref, q_ref, k_ref, v_ref, router_ref, one_ref, two_ref, wout_ref, docs_ref,
                  *refs):
     keep_ref, *out_refs = refs
+    first_core = group_ref[0] < 2
     rows, width = q_ref.shape
     experts = router_ref.shape[0]
     cols = width // 4
@@ -141,20 +141,25 @@
     for t in range(doc_cols):
         belongs = iota((rows, length), 1) == iota((rows, length), 0) * doc_cols + t
         columns.append(jnp.sum(jnp.where(belongs, docs, 0.0), axis=1, keepdims=True))
-    pad = out_refs[0].shape[1] - 3 * cols - experts - 2 - doc_cols
+    pad = out_refs[0].shape[1] - 6 * cols - experts - 2 - doc_cols
     small = jnp.concatenate(
         [router] + columns + [jnp.zeros((rows, pad), F32)], axis=1
     ).astype(BF16)
     weights = [ref[...] for ref in (q_ref, k_ref, v_ref)]
     pieces = [
-        jnp.concatenate([w[:, j * cols : (j + 1) * cols] for w in weights] + [small], axis=1)
-        for j in range(4)
+        jnp.concatenate(
+            [w[:, j * cols : (j + 1) * cols] for j in (2 * c, 2 * c + 1) for w in weights] + [small],
+            axis=1,
+        )
+        for c in range(2)
     ]
-    for d, out_ref in zip(ORDER, out_refs):
-        out_ref[...] = choose(group_ref[0] ^ d, pieces)
-    used = pieces[0].shape[1]
-    keep_ref[:, :used] = choose(group_ref[0], pieces)
-    keep_ref[:, used:] = wout_ref[...]
+    here = jnp.where(first_core, pieces[0], pieces[1])
+    there = jnp.where(first_core, pieces[1], pieces[0])
+    held = small.shape[1] + 6 * cols
+    for d, ref in zip((0, *ORDER), (keep_ref, *out_refs)):
+        ref[:, :held] = there if d > 1 else here
+        if d < 2:
+            ref[:, held:] = wout_ref[...]
 
 
 def put_rows(ref, dest, value):
@@ -181,20 +186,26 @@
     return jnp.concatenate([held[4 * rows :]] + tail, axis=1)
 
 
-def spread_weights(group_ref, own_ref, p3_ref, p1_ref, p2_ref, out_ref):
+def spread_weights(cols, used, block_ref, own_ref, p3_ref, p1_ref, p2_ref, out_ref):
     dests, _, wide = out_ref.shape
-    rows, used = p1_ref.shape
-    pieces = [own_ref[:, :used]] + [ref[...] for ref in (p1_ref, p2_ref, p3_ref)]
-    value = jnp.concatenate([choose(group_ref[0] ^ j, pieces) for j in range(4)], axis=0)
-    if wide > used:
-        value = jnp.concatenate([value, jnp.zeros((4 * rows, wide - used), BF16)], axis=1)
-    last = own_ref[:, used:]
-    if wide < last.shape[1]:
-        spare = spare_lanes(last, wide)
-        value = jnp.concatenate([value[:, : wide - spare.shape[1]], spare], axis=1)
-    for dest in range(dests):
-        out_ref[dest, : 4 * rows] = value
-        put_rows(out_ref, dest, last)
+    rows, held = p2_ref.shape
+    block = block_ref[0]
+    pieces = [ref[:, :held] for ref in (own_ref, p1_ref, p2_ref, p3_ref)]
+    both = jnp.concatenate([choose(block ^ j, pieces) for j in range(4)], axis=0)
+    lasts = [own_ref[:, held:], p1_ref[:, held:]]
+    small = both[:, 6 * cols : 3 * cols + used]
+    for variant in range(2):
+        at = variant * 3 * cols
+        value = jnp.concatenate([both[:, at : at + 3 * cols], small], axis=1)
+        if wide > used:
+            value = jnp.concatenate([value, jnp.zeros((4 * rows, wide - used), BF16)], axis=1)
+        last = jnp.where(block % 2 == variant, lasts[0], lasts[1])
+        if wide < last.shape[1]:
+            spare = spare_lanes(last, wide)
+            value = jnp.concatenate([value[:, : wide - spare.shape[1]], spare], axis=1)
+        for dest in range(variant, dests, 2):
+            out_ref[dest, : 4 * rows] = value
+            put_rows(out_ref, dest, last)
 
 
 def prepare(capacity, pad, group_ref, table_ref, routes_ref, vector_ref, spread_ref, later_ref,
@@ -281,12 +292,12 @@
     send_ref[...] = partial[toks:].astype(BF16)
 
 
-def docs_of_pair(at, length, rows, group_ref, place_ref, arrived_ref):
+def docs_of_pair(at, length, rows, block_ref, place_ref, arrived_ref):
     sources = arrived_ref.shape[0]
     doc_cols = -(-length // rows)
-    held = arrived_ref[(place_ref[0] % sources) ^ (sources // 2)]
+    held = arrived_ref[(place_ref[0] % sources) ^ 1]
     blocks = [held[j * rows : (j + 1) * rows, at : at + doc_cols].astype(F32) for j in range(4)]
-    block = choose(group_ref[0] ^ 1, blocks)
+    block = choose(block_ref[0], blocks)
     docs = jnp.zeros((1, length), F32)
     for t in range(doc_cols):
         belongs = iota((rows, length), 1) == iota((rows, length), 0) * doc_cols + t
@@ -298,25 +309,25 @@
     attend(scale, head_dim, docs_ref[...].astype(F32), group_ref, *refs)
 
 
-def attend_first(scale, head_dim, experts, group_ref, place_ref, arrived_ref, own_ref, across_ref,
+def attend_first(scale, head_dim, experts, group_ref, block_ref, place_ref, arrived_ref, own_ref, across_ref,
                  vector_ref, w_ref, wout_ref, gains_ref, *outs):
     place_weights(arrived_ref, w_ref, wout_ref)
     cols = wout_ref.shape[0]
     gain_rows(experts, cols, w_ref, gains_ref)
     docs = docs_of_pair(
-        3 * cols + experts + 2, vector_ref.shape[1], cols // arrived_ref.shape[0], group_ref, place_ref,
+        3 * cols + experts + 2, vector_ref.shape[1], cols // arrived_ref.shape[0], block_ref, place_ref,
         arrived_ref,
     )
     attend(scale, head_dim, docs, group_ref, w_ref, wout_ref, gains_ref, own_ref, across_ref,
            vector_ref, *outs)
 
 
-def attend_first_placed(scale, head_dim, experts, group_ref, place_ref, arrived_ref, w_ref, wout_ref,
+def attend_first_placed(scale, head_dim, experts, group_ref, block_ref, place_ref, arrived_ref, w_ref, wout_ref,
                         own_ref, across_ref, vector_ref, gains_ref, *outs):
     cols = wout_ref.shape[0]
     gain_rows(experts, cols, w_ref, gains_ref)
     docs = docs_of_pair(
-        3 * cols + experts + 2, vector_ref.shape[1], cols // arrived_ref.shape[0], group_ref, place_ref,
+        3 * cols + experts + 2, vector_ref.shape[1], cols // arrived_ref.shape[0], block_ref, place_ref,
         arrived_ref,
     )
     attend(scale, head_dim, docs, group_ref, w_ref, wout_ref, gains_ref, own_ref, across_ref,
@@ -542,16 +553,28 @@
         put_rows(message_ref, s, out_ref[s * rows : (s + 1) * rows])
 
 
-def sum_arrived(group_ref, arrived_ref, out_ref, own_ref, *send_refs):
-    rows, used = own_ref.shape
-    total = arrived_ref[0].astype(F32)
-    for s in range(1, arrived_ref.shape[0]):
-        total = total + arrived_ref[s].astype(F32)
-    out_ref[...] = take_rows(total, rows, out_ref.shape[1])
-    pieces = [total[j * rows : (j + 1) * rows, :used] for j in range(4)]
-    own_ref[...] = choose(group_ref[0], pieces)
+def sum_arrived(used, block_ref, arrived_ref, own_ref, *send_refs):
+    rows, held = own_ref.shape
+    width = held - 2 * used
+    block = block_ref[0]
+    totals = []
+    for variant in range(2):
+        total = arrived_ref[variant].astype(F32)
+        for s in range(variant + 2, arrived_ref.shape[0], 2):
+            total = total + arrived_ref[s].astype(F32)
+        totals.append(total)
+    pieces = [
+        jnp.concatenate([t[j * rows : (j + 1) * rows, :used] for t in totals], axis=1)
+        for j in range(4)
+    ]
+    lasts = [take_rows(t, rows, width) for t in totals]
+    first = block % 2 == 0
+    own_ref[:, : 2 * used] = choose(block, pieces)
+    own_ref[:, 2 * used :] = jnp.where(first, lasts[0], lasts[1])
     for d, ref in zip(ORDER, send_refs):
-        ref[...] = choose(group_ref[0] ^ d, pieces).astype(BF16)
+        ref[:, : 2 * used] = choose(block ^ d, pieces).astype(BF16)
+        if d == 1:
+            ref[:, 2 * used :] = jnp.where(first, lasts[1], lasts[0]).astype(BF16)
 
 
 def finish_input(grad_ref, core_ref, came_ref, dmiddle_ref, x_ref, gains_ref, out_ref):
@@ -563,13 +586,19 @@
     ).astype(BF16)
 
 
-def finish_weights(own_heads, buckets, table_cols, group_ref, p0_ref, p3_ref, p1_ref, p2_ref,
-                   q_ref, k_ref, v_ref, router_ref, one_ref, two_ref, table_ref):
+def finish_weights(own_heads, buckets, table_cols, used, group_ref, p0_ref, p3_ref, p1_ref, p2_ref,
+                   q_ref, k_ref, v_ref, w_ref, router_ref, one_ref, two_ref, table_ref):
     rows, width = q_ref.shape
     experts = router_ref.shape[0]
     cols = width // 4
-    pieces = [ref[...].astype(F32) for ref in (p0_ref, p1_ref, p2_ref, p3_ref)]
-    ordered = [choose(group_ref[0] ^ j, pieces) for j in range(4)]
+    here = p0_ref[...] + p1_ref[...].astype(F32)
+    there = p2_ref[...].astype(F32) + p3_ref[...].astype(F32)
+    w_ref[...] = here[:, 2 * used :]
+    here = here[:, : 2 * used]
+    first_core = group_ref[0] < 2
+    by_core = (jnp.where(first_core, here, there), jnp.where(first_core, there, here))
+    ordered = [c[:, v * used : (v + 1) * used] for c in by_core for v in range(2)]
+    pieces = ordered
     for n, ref in enumerate((q_ref, k_ref, v_ref)):
         ref[...] = jnp.concatenate([p[:, n * cols : (n + 1) * cols] for p in ordered], axis=1)
     at = 3 * cols
@@ -632,7 +661,8 @@
     core = lax.axis_index("dp")
     place = lax.axis_index("expert")
     half = sources // 2
-    member = place // half
+    member = place % 2
+    block_at = (2 * core + place // half).reshape(1).astype(jnp.int32)
     first_core = core == 0
     place_at = place.reshape(1).astype(jnp.int32)
     group_at = (2 * core + member).reshape(1).astype(jnp.int32)
@@ -640,6 +670,7 @@
     extra = max(table_cols, -(-length // rows))
     used = -(-(3 * cols + experts + 2 + extra) // 128) * 128
     aligned = rows % 8 == 0
+    held = -(-(3 * cols + used) // 128) * 128
     room = used - (3 * cols + experts + 2 + extra)
     packed = aligned and used < width <= used + 4 * room and (width - used) % 4 == 0
     wide = used if packed else max(used, width)
@@ -662,7 +693,8 @@
     pair_tokens = swap_pair(own_tokens)
 
     own_piece, *pieces = kernel_call(
-        pack_weights, [((rows, used + width), BF16)] + [((rows, used), BF16)] * 3,
+        pack_weights,
+        [((rows, held + width * (d < 2)), BF16) for d in (0, *ORDER)],
         group_at, w_query, w_key, w_value, w_router.T, gain_one.reshape(1, rows),
         gain_two.reshape(1, rows), w_out, segment_ids, scalars=1, late=range(1, 9),
         limit=60 * 1024 * 1024,
@@ -670,8 +702,8 @@
     pieces = across_group(pieces)
     pair_tokens, own_piece, *pieces = lax.optimization_barrier((pair_tokens, own_piece, *pieces))
     (message,) = kernel_call(
-        spread_weights, [((half, 5 * rows, wide), BF16)],
-        group_at, own_piece, *pieces, scalars=1,
+        functools.partial(spread_weights, cols, used), [((half, 5 * rows, wide), BF16)],
+        block_at, own_piece, *pieces, scalars=1,
     )
     arrived = exchange_half(message)
 
@@ -702,7 +734,7 @@
         weights, out_w, gains, *pair_kept = kernel_call(
             functools.partial(attend_first, scale, head_dim, experts),
             placed + [((8, width), F32)] + row_outs,
-            group_at, place_at, arrived, pair_tokens, pair_across, vectors, scalars=2,
+            group_at, block_at, place_at, arrived, pair_tokens, pair_across, vectors, scalars=3,
         )
     else:
         weights = arrived[:, : 4 * rows, :used].reshape(half, 2, 2, rows, used)
@@ -711,7 +743,8 @@
         gains, *pair_kept = kernel_call(
             functools.partial(attend_first_placed, scale, head_dim, experts),
             [((8, width), F32)] + row_outs,
-            group_at, place_at, arrived, weights, out_w, pair_tokens, pair_across, vectors, scalars=2,
+            group_at, block_at, place_at, arrived, weights, out_w, pair_tokens, pair_across, vectors,
+            scalars=3,
         )
     pair_qkv, pair_probs, pair_att, keep, away = pair_kept
     pair_sum = (keep + swap_core(away).astype(F32)).astype(BF16)
@@ -818,14 +851,16 @@
         (arrived, grad_inner, grad_outer, final, grad_middle)
     )
 
-    out_grad_w, own_piece, *pieces = kernel_call(
-        sum_arrived, [((rows, width), F32), ((rows, used), F32)] + [((rows, used), BF16)] * 3,
-        group_at, arrived, scalars=1,
+    own_piece, *pieces = kernel_call(
+        functools.partial(sum_arrived, used),
+        [((rows, 2 * used + width), F32)]
+        + [((rows, 2 * used + width * (d < 2)), BF16) for d in ORDER],
+        block_at, arrived, scalars=1,
     )
     pieces = across_group(pieces)
-    query_grad, key_grad, value_grad, router_grad, one_grad, two_grad, table_grad = kernel_call(
-        functools.partial(finish_weights, own_heads, buckets, table_cols),
-        [((rows, width), F32)] * 3
+    query_grad, key_grad, value_grad, out_grad_w, router_grad, one_grad, two_grad, table_grad = kernel_call(
+        functools.partial(finish_weights, own_heads, buckets, table_cols, used),
+        [((rows, width), F32)] * 4
         + [((experts, rows), F32), ((1, rows), F32), ((1, rows), F32), ((heads, buckets), F32)],
         group_at, own_piece, *pieces, scalars=1,
     )

time: 149 us -> 144 us (0.966)
  starting transfers between devices: 38.5 us -> 27.9 us
  waiting for transfers between devices: 32 us -> 39.8 us
  blocking collectives: 35.3 us -> 32.5 us
    ppermute x4, starting transfers between devices: 9.95 us -> 1.36 us  [swap_pair(): return lax.ppermute(value, 'expert', [(i, i ^ 1) for i in range(n)])]
    all_to_all x2, waiting for transfers between devices: 12.6 us -> 18.1 us  [exchange_half(): lax.all_to_all(value, 'expert', split_axis=0, concat_axis=0, tiled=True,...]
    ppermute x6, waiting for transfers between devices: 7.1 us -> 10.5 us  [across_group(): lax.ppermute(piece, ('dp', 'expert'), [(c * sources + e, (c ^ d >> 1) * s...]
    all_to_all x2, blocking collectives: 35.3 us -> 32.5 us  [exchange(): lax.all_to_all(value, 'expert', split_axis=0, concat_axis=0, tiled=True)]
  transfers between devices with their start and end apart: 22 -> 22, of which waited for: 12 -> 11; matrix products, arithmetic and copies ran while one was open for 7% -> 7% of each run, Pallas kernels for 8% -> 8%
where the time goes in v6:
time: 144 us; the launch traced here: 143 us
  waiting for transfers between devices  39.8 us (28%)
  blocking collectives  32.5 us (23%)
  starting transfers between devices  27.9 us (19%)
  Pallas kernels  27 us (19%)
  matrix products  8.64 us (6%)
  local copies, waits for them, and re-layouts  5.45 us (4%)
    all_to_all x2, blocking collectives, exchange(): lax.all_to_all(value, 'expert', split_axis=0, concat_axis=0, tiled=True)  32.5 us
    pallas_call x16, Pallas kernels, kernel_call(): pl.pallas_call(run, out_shape=[jax.ShapeDtypeStruct(shape, dtype) for sha...  27 us
    all_to_all x2, waiting for transfers between devices, exchange_half(): lax.all_to_all(value, 'expert', split_axis=0, concat_axis=0, tiled=True,...  18.1 us
    ppermute x6, waiting for transfers between devices, across_group(): lax.ppermute(piece, ('dp', 'expert'), [(c * sources + e, (c ^ d >> 1) * s...  10.5 us
    ppermute x10, starting transfers between devices, swap_core(): return lax.ppermute(value, 'dp', [(0, 1), (1, 0)])  9.53 us
    all_to_all x2, starting transfers between devices, exchange_half(): lax.all_to_all(value, 'expert', split_axis=0, concat_axis=0, tiled=True,...  9.52 us
    dot_general x2, matrix products, dot(): lax.dot_general(left, right, (dims, ((), ())), preferred_element_type=F32)  8.64 us
    ppermute x6, starting transfers between devices, across_group(): lax.ppermute(piece, ('dp', 'expert'), [(c * sources + e, (c ^ d >> 1) * s...  7.52 us
  transfers between devices with their start and end apart: 22, of which 11 were waited for; matrix products, arithmetic and copies ran while one was open for 7% of the time, Pallas kernels for 8%

profile of v6, /device:TPU:3, one launch (start us, length us, event | category | flops | bytes accessed | tf_op | source)
XLA Modules:
  0.0 143.1 jit_solution(14992411774559818567)
XLA Ops:
  0.8 2.0 %shard_map.229 = (bf16[24,2048]{1,0:T(8,128)(2,1)}, bf16[24,1280]{1,0:T(8,128)(2,1)}, bf16[24,2048]{1,0:T(8,128)(2,1)}, bf16[24,1280]{1,0:T(8,128)(2,1)}) custom-call(s32[1]{0:T(128)} %bitcast.2.refs_0_, bf16[24,768]{1,0:T(8,128)(2,1)} %refs_1_.3, bf16[24,768]{1,0:T(8,128)(2,1)} %refs_2_.1, bf16[24,768]{1,0:T(8,128)(2,1)} %refs_3_.1, ...), custom_call_target="tpu_custom_call" | custom-call | flops 1000000 | bytes 1000000 | tf_op jit(solution)/shard_map/pallas_call | solution.py:105
  2.8 2.6 %collective-permute-start.2 = (bf16[24,2048]{1,0:T(8,128)(2,1)}, bf16[24,2048]{1,0:T(8,128)(2,1)S(1)}, u32[]{:S(2)}, u32[]{:S(2)}) collective-permute-start(bf16[24,2048]{1,0:T(8,128)(2,1)} %get-tuple-element.93), channel_id=1, source_target_pairs={{0,8},{1,9},{2,10},{3,11},{4,12},{5,13},{6,14},{7,15},{8,0},{9,1},... | collective-permute-start | bytes 294920 | tf_op jit(solution)/shard_map/ppermute | solution.py:680
  5.4 0.9 collective-permute-start.1
  6.6 6.8 %collective-permute-done.1.refs_2_ = bf16[24,1280]{1,0:T(8,128)(2,1)S(1)} collective-permute-done((bf16[24,1280]{1,0:T(8,128)(2,1)}, bf16[24,1280]{1,0:T(8,128)(2,1)S(1)}, u32[]{:S(2)}, u32[]{:S(2)}) %collective-permute-start.1) | collective-permute-done | bytes 61472 | tf_op jit(solution)/shard_map/ppermute | solution.py:680
  13.4 0.9 copy-done.20
  14.3 1.2 shard_map.230
  15.6 4.9 %all-to-all-start = ((bf16[8,120,640]{2,1,0:T(8,128)(2,1)}), bf16[8,120,640]{2,1,0:T(8,128)(2,1)S(1)}, u32[]{:S(2)}, u32[]{:S(2)}) async-start(bf16[8,120,640]{2,1,0:T(8,128)(2,1)} %shard_map.230), calls=%async_computation | async-start | bytes 2457600 | tf_op jit(solution)/shard_map/all_to_all | solution.py:49
  20.4 0.5 collective-permute-start.4
  21.1 1.6 %shard_map.231 = (f32[3,256]{1,0:T(4,128)S(1)}, bf16[2,128,640]{2,1,0:T(8,128)(2,1)S(1)}, bf16[2,128,640]{2,1,0:T(8,128)(2,1)S(1)}, f32[128,16]{1,0:T(8,128)S(1)}, bf16[640,512]{1,0:T(8,128)(2,1)S(1)}) custom-call(s32[1]{0:T(128)} %bitcast.2.refs_0_, f32[32,12]{1,0:T(8,128)S(1)} %copy.26.refs_1_, s32[128,1]{1,0:T(8,128)S(1)} %copy.27.refs_2_), custom_call_target="tpu_custom_call" | custom-call | flops 1000000 | bytes 1000000 | tf_op jit(solution)/shard_map/pallas_call | solution.py:105
  22.7 0.8 copy-done.10
  23.5 0.7 copy-done.18
  24.3 13.0 %all-to-all-done.refs_3_ = bf16[8,120,640]{2,1,0:T(8,128)(2,1)S(1)} async-done(((bf16[8,120,640]{2,1,0:T(8,128)(2,1)}), bf16[8,120,640]{2,1,0:T(8,128)(2,1)S(1)}, u32[]{:S(2)}, u32[]{:S(2)}) %all-to-all-start) | async-done | bytes 1228832 | tf_op jit(solution)/shard_map/all_to_all | solution.py:49
  37.3 1.7 %shard_map.232 = (bf16[768,640]{1,0:T(8,128)(2,1)S(1)}, bf16[192,768]{1,0:T(8,128)(2,1)S(1)}, f32[8,768]{1,0:T(8,128)S(1)}, bf16[256,576]{1,0:T(8,128)(2,1)S(1)}...) custom-call(s32[1]{0:T(128)} %bitcast.2.refs_0_, ...), custom_call_target="tpu_custom_call" | custom-call | flops 1000000 | bytes 1000000 | tf_op jit(solution)/shard_map/pallas_call | solution.py:105
  39.0 1.1 collective-permute-start.5
  40.1 1.0 collective-permute-done.5
  41.5 1.5 %shard_map.233 = (bf16[256,576]{1,0:T(8,128)(2,1)S(1)}, f32[3,256,256]{2,1,0:T(8,128)S(1)}, bf16[256,192]{1,0:T(8,128)(2,1)S(1)}, f32[128,768]{1,0:T(8,128)S(1)}, bf16[128,768]{1,0:T(8,128)(2,1)S(1)}) custom-call(s32[1]{0:T(128)} %bitcast.2.refs_0_, s32[1,256]{1,0:T(1,128)S(1)} %copy-done.25, ...), custom_call_target="tpu_custom_call" | custom-call | flops 1000000 | bytes 1000000 | tf_op jit(solution)/shard_map/pallas_call | solution.py:105
  43.4 3.9 %collective-permute-done.8.refs_3_ = bf16[128,768]{1,0:T(8,128)(2,1)S(1)} collective-permute-done((bf16[128,768]{1,0:T(8,128)(2,1)S(1)}, bf16[128,768]{1,0:T(8,128)(2,1)S(1)}, u32[]{:S(2)}, u32[]{:S(2)}) %collective-permute-start.8) | collective-permute-done | bytes 196640 | tf_op jit(solution)/shard_map/ppermute | solution.py:39
  47.4 0.8 copy-done.24
  48.2 1.0 shard_map.234
  49.2 16.2 %all_to_all.20 = bf16[16,40,384]{2,1,0:T(8,128)(2,1)S(1)} all-to-all(bf16[16,40,384]{2,1,0:T(8,128)(2,1)S(1)} %bitcast.43), channel_id=1, replica_groups=mesh['dp'=2,'expert'=16] {'expert'}, dimensions={0} | all-to-all | bytes 983040 | tf_op jit(solution)/shard_map/all_to_all | solution.py:43
  65.4 3.0 %collective-permute-start.9 = (bf16[640,384]{1,0:T(8,128)(2,1)S(1)}, bf16[640,384]{1,0:T(8,128)(2,1)S(1)}, u32[]{:S(2)}, u32[]{:S(2)}) collective-permute-start(bf16[640,384]{1,0:T(8,128)(2,1)S(1)} %bitcast.37), channel_id=1, source_target_pairs={{0,16},{16,0},{1,17},{17,1},{2,18},{18,2},{3,19},{19,3},{4,20},{20... | collective-permute-start | bytes 1474568 | tf_op jit(solution)/shard_map/ppermute | solution.py:34
  68.5 1.5 %collective-permute-done.9.refs_2_ = bf16[640,384]{1,0:T(8,128)(2,1)S(1)} collective-permute-done((bf16[640,384]{1,0:T(8,128)(2,1)S(1)}, bf16[640,384]{1,0:T(8,128)(2,1)S(1)}, u32[]{:S(2)}, u32[]{:S(2)}) %collective-permute-start.9) | collective-permute-done | bytes 491552 | tf_op jit(solution)/shard_map/ppermute | solution.py:34
  70.0 4.6 %shard_map.235 = (bf16[320,768]{1,0:T(8,128)(2,1)S(1)}, bf16[320,768]{1,0:T(8,128)(2,1)S(1)}, bf16[160,768]{1,0:T(8,128)(2,1)S(1)}, f32[160,16]{1,0:T(8,128)S(1)...) custom-call(s32[1]{0:T(128)} %bitcast.refs_2_.refs_0_, ...), custom_call_target="tpu_custom_call" | custom-call | flops 1000000 | bytes 1000000 | tf_op jit(solution)/shard_map/pallas_call | solution.py:105
  75.0 1.5 %collective-permute-done.10.refs_2_ = bf16[2,160,768]{2,1,0:T(8,128)(2,1)S(1)} collective-permute-done((bf16[2,160,768]{2,1,0:T(8,128)(2,1)S(1)}, bf16[2,160,768]{2,1,0:T(8,128)(2,1)S(1)}, u32[]{:S(2)}, u32[]{:S(2)}) %collective-permute-start.10) | collective-permute-done | bytes 491552 | tf_op jit(solution)/shard_map/ppermute | solution.py:34
  76.5 1.3 shard_map.236
  77.8 16.3 %all_to_all.21 = bf16[16,40,384]{2,1,0:T(8,128)(2,1)S(1)} all-to-all(bf16[16,40,384]{2,1,0:T(8,128)(2,1)S(1)} %bitcast.42), channel_id=1, replica_groups=mesh['dp'=2,'expert'=16] {'expert'}, dimensions={0} | all-to-all | bytes 983040 | tf_op jit(solution)/shard_map/all_to_all | solution.py:43
  94.1 0.5 shard_map.237
  94.6 2.5 %collective-permute-start.12 = (bf16[128,768]{1,0:T(8,128)(2,1)S(1)}, bf16[128,768]{1,0:T(8,128)(2,1)S(1)}, u32[]{:S(2)}, u32[]{:S(2)}) collective-permute-start(bf16[128,768]{1,0:T(8,128)(2,1)S(1)} %get-tuple-element.123.refs_0_), channel_id=1, source_target_pairs={{0,16},{16,0},{1,17},{17,1},{2,18},{18,2},{3,19},{19,3},{4,20},{20... | collective-permute-start | bytes 589832 | tf_op jit(solution)/shard_map/ppermute | solution.py:34
  97.2 1.2 collective-permute-start.11
  98.4 3.2 %shard_map.238 = (f32[768,576]{1,0:T(8,128)S(1)}, f32[192,768]{1,0:T(8,128)S(1)}, f32[128,768]{1,0:T(8,128)S(1)}, bf16[128,768]{1,0:T(8,128)(2,1)}, bf16[256,576...) custom-call(bf16[128,768]{1,0:T(8,128)(2,1)S(1)} %get-tuple-element.123.refs_0_, ...), custom_call_target="tpu_custom_call" | custom-call | flops 1000000 | bytes 1000000 | tf_op jit(solution)/shard_map/pallas_call | solution.py:105
  101.6 2.0 %collective-permute-done.11.refs_0_ = bf16[128,768]{1,0:T(8,128)(2,1)S(1)} collective-permute-done((bf16[128,768]{1,0:T(8,128)(2,1)S(1)}, bf16[128,768]{1,0:T(8,128)(2,1)S(1)}, u32[]{:S(2)}, u32[]{:S(2)}) %collective-permute-start.11) | collective-permute-done | bytes 196640 | tf_op jit(solution)/shard_map/ppermute | solution.py:39
  103.7 0.8 collective-permute-start.13
  104.5 1.1 collective-permute-done.13.refs_1_
  105.6 2.2 %shard_map.239 = (f32[128,768]{1,0:T(8,128)S(1)}, bf16[128,768]{1,0:T(8,128)(2,1)S(1)}, bf16[256,576]{1,0:T(8,128)(2,1)S(1)}, f32[1,768]{1,0:T(1,128)S(1)}, f32[3,256]{1,0:T(4,128)S(1)}) custom-call(bf16[128,768]{1,0:T(8,128)(2,1)S(1)} %collective-permute-done.11.refs_0_, bf16[128,768]{1,0:T(8,128)(2,1)S(1)} %collective-permute-done.13.refs_1_, ...), custom_call_target="tpu_custom_call" | custom-call | flops 1000000 | bytes 1000000 | tf_op jit(solution)/shard_map/pallas_call | solution.py:105
  107.8 0.7 copy-done.14
  108.5 2.0 %shard_map.240 = bf16[8,120,640]{2,1,0:T(8,128)(2,1)} custom-call(bf16[128,768]{1,0:T(8,128)(2,1)S(1)} %collective-permute-done.11.refs_0_, bf16[128,768]{1,0:T(8,128)(2,1)S(1)} %collective-permute-done.13.refs_1_, bf16[256,192]{1,0:T(8,128)(2,1)S(1)} %get-tuple-element.130.refs_2_, bf16[256,576]{1,0:T(8,128)(2,1)S(1)} %get-tuple-element.133.refs_3_, ...), custom_call_target="tpu_custom_call" | custom-call | flops 1000000 | bytes 1000000 | tf_op jit(solution)/shard_map/pallas_call | solution.py:105
  110.5 4.7 %all-to-all-start.3 = ((bf16[8,120,640]{2,1,0:T(8,128)(2,1)}), bf16[8,120,640]{2,1,0:T(8,128)(2,1)S(1)}, u32[]{:S(2)}, u32[]{:S(2)}) async-start(bf16[8,120,640]{2,1,0:T(8,128)(2,1)} %shard_map.240), calls=%async_computation.3 | async-start | bytes 2457600 | tf_op jit(solution)/shard_map/all_to_all | solution.py:49
  115.2 0.7 collective-permute-start.15
  115.8 5.0 %fusion = f32[768,1536]{1,0:T(8,128)} fusion(bf16[320,768]{1,0:T(8,128)(2,1)} %copy-done.4, bf16[320,1536]{1,0:T(8,128)(2,1)} %copy-done.9), kind=kOutput, calls=%fused_computation.2 | convolution fusion | flops 754974720 | bytes 6193152 | tf_op jit(solution)/shard_map/dot_general | solution.py:20
  120.9 0.7 add_convert_fusion
  121.6 3.6 %fusion.1 = f32[1536,768]{1,0:T(8,128)} fusion(bf16[320,1536]{1,0:T(8,128)(2,1)S(1)} %get-tuple-element.143, bf16[320,768]{1,0:T(8,128)(2,1)S(1)} %copy-done.13), kind=kOutput, calls=%fused_computation.3 | convolution fusion | flops 754974720 | bytes 6193152 | tf_op jit(solution)/shard_map/dot_general | solution.py:20
  125.3 1.4 shard_map.241
  126.6 5.0 %all-to-all-done.3.refs_1_ = bf16[8,120,640]{2,1,0:T(8,128)(2,1)S(1)} async-done(((bf16[8,120,640]{2,1,0:T(8,128)(2,1)}), bf16[8,120,640]{2,1,0:T(8,128)(2,1)S(1)}, u32[]{:S(2)}, u32[]{:S(2)}) %all-to-all-start.3) | async-done | bytes 1228832 | tf_op jit(solution)/shard_map/all_to_all | solution.py:49
  132.0 3.6 %collective-permute-start.17 = (bf16[24,1280]{1,0:T(8,128)(2,1)S(1)}, bf16[24,1280]{1,0:T(8,128)(2,1)S(1)}, u32[]{:S(2)}, u32[]{:S(2)}) collective-permute-start(bf16[24,1280]{1,0:T(8,128)(2,1)S(1)} %get-tuple-element.157), channel_id=1, source_target_pairs={{0,24},{1,25},{2,26},{3,27},{4,28},{5,29},{6,30},{7,31},{8,16},{9,... | collective-permute-start | bytes 184328 | tf_op jit(solution)/shard_map/ppermute | solution.py:680
  135.6 1.0 copy-done.17
  136.6 1.9 %shard_map.242 = bf16[128,768]{1,0:T(8,128)(2,1)} custom-call(f32[128,768]{1,0:T(8,128)S(1)} %copy-done.17, bf16[128,768]{1,0:T(8,128)(2,1)S(1)} %collective-permute-done.14.refs_1_, bf16[128,768]{1,0:T(8,128)(2,1)} %collective-permute-done.16.refs_2_, f32[128,768]{1,0:T(8,128)S(1)} %get-tuple-element.154.refs_3_, bf16[128,768]{1,0:T(8,128)(2,1)S(1)} %bitcast.34, ...), custom_call_target="tpu_custom_call" | custom-call | flops 1000000 | bytes 1000000 | tf_op jit(solution)/shard_map/pallas_call | solution.py:105
  138.5 3.7 %collective-permute-done.17.refs_2_ = bf16[24,1280]{1,0:T(8,128)(2,1)S(1)} collective-permute-done((bf16[24,1280]{1,0:T(8,128)(2,1)S(1)}, bf16[24,1280]{1,0:T(8,128)(2,1)S(1)}, u32[]{:S(2)}, u32[]{:S(2)}) %collective-permute-start.17) | collective-permute-done | bytes 61472 | tf_op jit(solution)/shard_map/ppermute | solution.py:680
  142.2 0.9 shard_map.244
  (80 shorter events, 2.4 us)
Async XLA Ops:
  0.6 20.3 %copy-start.27 = (f32[32,12]{0,1:T(8,128)S(1)}, f32[32,12]{0,1:T(8,128)}, u32[]{:S(2)}) copy-start(f32[32,12]{0,1:T(8,128)} %param.20) | copy-start | bytes 4612
  0.7 20.3 %copy-start.28 = (s32[1,128,1]{1,2,0:T(1,128)S(1)}, s32[1,128,1]{1,2,0:T(1,128)}, u32[]{:S(2)}) copy-start(s32[1,128,1]{1,2,0:T(1,128)} %param.26) | copy-start | bytes 1540
  0.7 12.8 %collective-permute-start = (bf16[128,768]{1,0:T(8,128)(2,1)}, bf16[128,768]{1,0:T(8,128)(2,1)S(1)}, u32[]{:S(2)}, u32[]{:S(2)}) collective-permute-start(bf16[128,768]{1,0:T(8,128)(2,1)} %bitcast.29), channel_id=1, source_target_pairs={{0,1},{1,0},{2,3},{3,2},{4,5},{5,4},{6,7},{7,6},{8,9},{9,8},{10,11... | collective-permute-start | bytes 589832 | tf_op jit(solution)/shard_map/ppermute | solution.py:39
  2.8 10.6 %collective-permute-start.2 = (bf16[24,2048]{1,0:T(8,128)(2,1)}, bf16[24,2048]{1,0:T(8,128)(2,1)S(1)}, u32[]{:S(2)}, u32[]{:S(2)}) collective-permute-start(bf16[24,2048]{1,0:T(8,128)(2,1)} %get-tuple-element.93), channel_id=1, source_target_pairs={{0,8},{1,9},{2,10},{3,11},{4,12},{5,13},{6,14},{7,15},{8,0},{9,1},... | collective-permute-start | bytes 294920 | tf_op jit(solution)/shard_map/ppermute | solution.py:680
  5.4 8.0 %collective-permute-start.1 = (bf16[24,1280]{1,0:T(8,128)(2,1)}, bf16[24,1280]{1,0:T(8,128)(2,1)S(1)}, u32[]{:S(2)}, u32[]{:S(2)}) collective-permute-start(bf16[24,1280]{1,0:T(8,128)(2,1)} %get-tuple-element.92), channel_id=1, source_target_pairs={{0,24},{1,25},{2,26},{3,27},{4,28},{5,29},{6,30},{7,31},{8,16},{9,... | collective-permute-start | bytes 184328 | tf_op jit(solution)/shard_map/ppermute | solution.py:680
  6.3 7.1 %collective-permute-start.3 = (bf16[24,1280]{1,0:T(8,128)(2,1)}, bf16[24,1280]{1,0:T(8,128)(2,1)S(1)}, u32[]{:S(2)}, u32[]{:S(2)}) collective-permute-start(bf16[24,1280]{1,0:T(8,128)(2,1)} %get-tuple-element.94), channel_id=1, source_target_pairs={{0,16},{1,17},{2,18},{3,19},{4,20},{5,21},{6,22},{7,23},{8,24},{9,... | collective-permute-start | bytes 184328 | tf_op jit(solution)/shard_map/ppermute | solution.py:680
  13.4 0.9 copy-start.20
  15.6 24.5 %copy-start = (bf16[1,128,768]{2,1,0:T(8,128)(2,1)S(1)}, bf16[1,128,768]{2,1,0:T(8,128)(2,1)}, u32[]{:S(2)}) copy-start(bf16[1,128,768]{2,1,0:T(8,128)(2,1)} %param.14) | copy-start | bytes 589828
  15.6 25.9 %copy-start.25 = (s32[1,256]{1,0:T(1,128)S(1)}, s32[1,256]{1,0:T(1,128)}, u32[]{:S(2)}) copy-start(s32[1,256]{1,0:T(1,128)} %refs_1_.4) | copy-start | bytes 3076
  15.6 21.7 %all-to-all-start = ((bf16[8,120,640]{2,1,0:T(8,128)(2,1)}), bf16[8,120,640]{2,1,0:T(8,128)(2,1)S(1)}, u32[]{:S(2)}, u32[]{:S(2)}) async-start(bf16[8,120,640]{2,1,0:T(8,128)(2,1)} %shard_map.230), calls=%async_computation | async-start | bytes 2457600 | tf_op jit(solution)/shard_map/all_to_all | solution.py:49
  20.4 26.9 %copy-start.3 = (bf16[1,128,768]{2,1,0:T(8,128)(2,1)S(1)}, bf16[1,128,768]{2,1,0:T(8,128)(2,1)}, u32[]{:S(2)}) copy-start(bf16[1,128,768]{2,1,0:T(8,128)(2,1)} %param.27) | copy-start | bytes 589828
  20.4 3.9 %collective-permute-start.4 = (bf16[128,768]{1,0:T(8,128)(2,1)S(1)}, bf16[128,768]{1,0:T(8,128)(2,1)S(1)}, u32[]{:S(2)}, u32[]{:S(2)}) collective-permute-start(bf16[128,768]{1,0:T(8,128)(2,1)S(1)} %collective-permute-done.refs_4_.refs_7_.refs_5_), channel_id=1, source_target_pairs={{0,16},{16,0},{1,17},{17,1},{2,18},{18,2},{3,19},{19,3},{4,20},{20... | collective-permute-start | bytes 589832 | tf_op jit(solution)/shard_map/ppermute | solution.py:34
  24.3 23.1 %copy-start.23 = (f32[128,16]{1,0:T(8,128)}, f32[128,16]{1,0:T(8,128)S(1)}, u32[]{:S(2)}) copy-start(f32[128,16]{1,0:T(8,128)S(1)} %get-tuple-element.111.refs_6_) | copy-start | bytes 24580
  24.3 69.8 %copy-start.7 = (bf16[2,128,640]{2,1,0:T(8,128)(2,1)}, bf16[2,128,640]{2,1,0:T(8,128)(2,1)S(1)}, u32[]{:S(2)}) copy-start(bf16[2,128,640]{2,1,0:T(8,128)(2,1)S(1)} %get-tuple-element.121.refs_1_) | copy-start | bytes 983044
  37.3 10.1 %copy-start.11 = (bf16[640,512]{1,0:T(8,128)(2,1)S(1)}, bf16[640,512]{1,0:T(8,128)(2,1)}, u32[]{:S(2)}) copy-start(bf16[640,512]{1,0:T(8,128)(2,1)} %copy-done.10) | copy-start | bytes 1966084
  39.0 2.1 %collective-permute-start.5 = (bf16[128,768]{1,0:T(8,128)(2,1)S(1)}, bf16[128,768]{1,0:T(8,128)(2,1)S(1)}, u32[]{:S(2)}, u32[]{:S(2)}) collective-permute-start(bf16[128,768]{1,0:T(8,128)(2,1)S(1)} %get-tuple-element.103), channel_id=1, source_target_pairs={{0,16},{16,0},{1,17},{17,1},{2,18},{18,2},{3,19},{19,3},{4,20},{20... | collective-permute-start | bytes 589832 | tf_op jit(solution)/shard_map/ppermute | solution.py:34
  40.0 1.4 %collective-permute-start.6 = (bf16[128,768]{1,0:T(8,128)(2,1)S(1)}, bf16[128,768]{1,0:T(8,128)(2,1)S(1)}, u32[]{:S(2)}, u32[]{:S(2)}) collective-permute-start(bf16[128,768]{1,0:T(8,128)(2,1)S(1)} %bitcast.30), channel_id=1, source_target_pairs={{0,16},{16,0},{1,17},{17,1},{2,18},{18,2},{3,19},{19,3},{4,20},{20... | collective-permute-start | bytes 589832 | tf_op jit(solution)/shard_map/ppermute | solution.py:34
  41.2 6.2 %collective-permute-start.8 = (bf16[128,768]{1,0:T(8,128)(2,1)S(1)}, bf16[128,768]{1,0:T(8,128)(2,1)S(1)}, u32[]{:S(2)}, u32[]{:S(2)}) collective-permute-start(bf16[128,768]{1,0:T(8,128)(2,1)S(1)} %add_convert_fusion.1), channel_id=1, source_target_pairs={{0,1},{1,0},{2,3},{3,2},{4,5},{5,4},{6,7},{7,6},{8,9},{9,8},{10,11... | collective-permute-start | bytes 589832 | tf_op jit(solution)/shard_map/ppermute | solution.py:39
  41.5 28.5 %copy-start.1 = (bf16[1,768,1536]{2,1,0:T(8,128)(2,1)S(1)}, bf16[1,768,1536]{2,1,0:T(8,128)(2,1)}, u32[]{:S(2)}) copy-start(bf16[1,768,1536]{2,1,0:T(8,128)(2,1)} %param.23) | copy-start | bytes 7077892
  41.5 28.5 %copy-start.2 = (bf16[1,1536,768]{2,1,0:T(8,128)(2,1)S(1)}, bf16[1,1536,768]{2,1,0:T(8,128)(2,1)}, u32[]{:S(2)}) copy-start(bf16[1,1536,768]{2,1,0:T(8,128)(2,1)} %param.24) | copy-start | bytes 7077892
  43.0 4.4 %collective-permute-start.7 = (bf16[128,768]{1,0:T(8,128)(2,1)S(1)}, bf16[128,768]{1,0:T(8,128)(2,1)S(1)}, u32[]{:S(2)}, u32[]{:S(2)}) collective-permute-start(bf16[128,768]{1,0:T(8,128)(2,1)S(1)} %get-tuple-element.109), channel_id=1, source_target_pairs={{0,16},{16,0},{1,17},{17,1},{2,18},{18,2},{3,19},{19,3},{4,20},{20... | collective-permute-start | bytes 589832 | tf_op jit(solution)/shard_map/ppermute | solution.py:34
  47.4 0.8 copy-start.24
  49.2 25.4 %copy-start.21 = (f32[128,1]{1,0:T(8,128)}, f32[128,1]{1,0:T(8,128)S(1)}, u32[]{:S(2)}) copy-start(f32[128,1]{1,0:T(8,128)S(1)} %get-tuple-element.146.refs_6_) | copy-start | bytes 1540
  49.2 44.9 %copy-start.5 = (f32[128,768]{1,0:T(8,128)}, f32[128,768]{1,0:T(8,128)S(1)}, u32[]{:S(2)}) copy-start(f32[128,768]{1,0:T(8,128)S(1)} %get-tuple-element.122.refs_2_.refs_3_) | copy-start | bytes 1179652
  65.4 4.5 %collective-permute-start.9 = (bf16[640,384]{1,0:T(8,128)(2,1)S(1)}, bf16[640,384]{1,0:T(8,128)(2,1)S(1)}, u32[]{:S(2)}, u32[]{:S(2)}) collective-permute-start(bf16[640,384]{1,0:T(8,128)(2,1)S(1)} %bitcast.37), channel_id=1, source_target_pairs={{0,16},{16,0},{1,17},{17,1},{2,18},{18,2},{3,19},{19,3},{4,20},{20... | collective-permute-start | bytes 1474568 | tf_op jit(solution)/shard_map/ppermute | solution.py:34
  74.5 20.1 %copy-start.4 = (bf16[320,768]{1,0:T(8,128)(2,1)}, bf16[320,768]{1,0:T(8,128)(2,1)S(1)}, u32[]{:S(2)}) copy-start(bf16[320,768]{1,0:T(8,128)(2,1)S(1)} %get-tuple-element.116) | copy-start | bytes 1474564
  74.6 20.1 %copy-start.12 = (bf16[320,768]{1,0:T(8,128)(2,1)}, bf16[320,768]{1,0:T(8,128)(2,1)S(1)}, u32[]{:S(2)}) copy-start(bf16[320,768]{1,0:T(8,128)(2,1)S(1)} %get-tuple-element.144) | copy-start | bytes 1474564
  74.6 33.2 %copy-start.9 = (bf16[320,1536]{1,0:T(8,128)(2,1)}, bf16[320,1536]{1,0:T(8,128)(2,1)S(1)}, u32[]{:S(2)}) copy-start(bf16[320,1536]{1,0:T(8,128)(2,1)S(1)} %get-tuple-element.142) | copy-start | bytes 2949124
  74.6 1.9 %collective-permute-start.10 = (bf16[2,160,768]{2,1,0:T(8,128)(2,1)S(1)}, bf16[2,160,768]{2,1,0:T(8,128)(2,1)S(1)}, u32[]{:S(2)}, u32[]{:S(2)}) collective-permute-start(bf16[2,160,768]{2,1,0:T(8,128)(2,1)S(1)} %get-tuple-element.115), channel_id=1, source_target_pairs={{0,16},{16,0},{1,17},{17,1},{2,18},{18,2},{3,19},{19,3},{4,20},{20... | collective-permute-start | bytes 1474568 | tf_op jit(solution)/shard_map/ppermute | solution.py:34
  94.6 3.7 %collective-permute-start.12 = (bf16[128,768]{1,0:T(8,128)(2,1)S(1)}, bf16[128,768]{1,0:T(8,128)(2,1)S(1)}, u32[]{:S(2)}, u32[]{:S(2)}) collective-permute-start(bf16[128,768]{1,0:T(8,128)(2,1)S(1)} %get-tuple-element.123.refs_0_), channel_id=1, source_target_pairs={{0,16},{16,0},{1,17},{17,1},{2,18},{18,2},{3,19},{19,3},{4,20},{20... | collective-permute-start | bytes 589832 | tf_op jit(solution)/shard_map/ppermute | solution.py:34
  97.2 6.5 %collective-permute-start.11 = (bf16[128,768]{1,0:T(8,128)(2,1)S(1)}, bf16[128,768]{1,0:T(8,128)(2,1)S(1)}, u32[]{:S(2)}, u32[]{:S(2)}) collective-permute-start(bf16[128,768]{1,0:T(8,128)(2,1)S(1)} %get-tuple-element.123.refs_0_), channel_id=1, source_target_pairs={{0,1},{1,0},{2,3},{3,2},{4,5},{5,4},{6,7},{7,6},{8,9},{9,8},{10,11... | collective-permute-start | bytes 589832 | tf_op jit(solution)/shard_map/ppermute | solution.py:39
  101.6 8.9 %copy-start.16 = (f32[128,768]{1,0:T(8,128)}, f32[128,768]{1,0:T(8,128)S(1)}, u32[]{:S(2)}) copy-start(f32[128,768]{1,0:T(8,128)S(1)} %get-tuple-element.150.refs_0_) | copy-start | bytes 1179652
  103.7 1.9 %collective-permute-start.13 = (bf16[128,768]{1,0:T(8,128)(2,1)S(1)}, bf16[128,768]{1,0:T(8,128)(2,1)S(1)}, u32[]{:S(2)}, u32[]{:S(2)}) collective-permute-start(bf16[128,768]{1,0:T(8,128)(2,1)S(1)} %collective-permute-done.11.refs_0_), channel_id=1, source_target_pairs={{0,16},{16,0},{1,17},{17,1},{2,18},{18,2},{3,19},{19,3},{4,20},{20... | collective-permute-start | bytes 589832 | tf_op jit(solution)/shard_map/ppermute | solution.py:34
  108.5 2.0 %copy-start.26 = (bf16[128,768]{1,0:T(8,128)(2,1)}, bf16[128,768]{1,0:T(8,128)(2,1)S(1)}, u32[]{:S(2)}) copy-start(bf16[128,768]{1,0:T(8,128)(2,1)S(1)} %get-tuple-element.153) | copy-start | bytes 589828
  110.5 21.1 %all-to-all-start.3 = ((bf16[8,120,640]{2,1,0:T(8,128)(2,1)}), bf16[8,120,640]{2,1,0:T(8,128)(2,1)S(1)}, u32[]{:S(2)}, u32[]{:S(2)}) async-start(bf16[8,120,640]{2,1,0:T(8,128)(2,1)} %shard_map.240), calls=%async_computation.3 | async-start | bytes 2457600 | tf_op jit(solution)/shard_map/all_to_all | solution.py:49
  115.2 5.7 %collective-permute-start.15 = (bf16[128,768]{1,0:T(8,128)(2,1)}, bf16[128,768]{1,0:T(8,128)(2,1)S(1)}, u32[]{:S(2)}, u32[]{:S(2)}) collective-permute-start(bf16[128,768]{1,0:T(8,128)(2,1)} %copy-done.26), channel_id=1, source_target_pairs={{0,16},{16,0},{1,17},{17,1},{2,18},{18,2},{3,19},{19,3},{4,20},{20... | collective-permute-start | bytes 589832 | tf_op jit(solution)/shard_map/ppermute | solution.py:34
  115.8 5.1 %copy-start.15 = (f32[128,768]{1,0:T(8,128)S(1)}, f32[128,768]{1,0:T(8,128)}, u32[]{:S(2)}) copy-start(f32[128,768]{1,0:T(8,128)} %copy-done.14) | copy-start | bytes 1179652
  115.8 5.8 %copy-start.13 = (bf16[320,768]{1,0:T(8,128)(2,1)S(1)}, bf16[320,768]{1,0:T(8,128)(2,1)}, u32[]{:S(2)}) copy-start(bf16[320,768]{1,0:T(8,128)(2,1)} %copy-done.12) | copy-start | bytes 1474564
  120.9 14.7 %collective-permute-start.14 = (bf16[128,768]{1,0:T(8,128)(2,1)}, bf16[128,768]{1,0:T(8,128)(2,1)S(1)}, u32[]{:S(2)}, u32[]{:S(2)}) collective-permute-start(bf16[128,768]{1,0:T(8,128)(2,1)} %get-tuple-element.151), channel_id=1, source_target_pairs={{0,16},{16,0},{1,17},{17,1},{2,18},{18,2},{3,19},{19,3},{4,20},{20... | collective-permute-start | bytes 589832 | tf_op jit(solution)/shard_map/ppermute | solution.py:34
  121.6 14.0 %collective-permute-start.16 = (bf16[128,768]{1,0:T(8,128)(2,1)}, bf16[128,768]{1,0:T(8,128)(2,1)}, u32[]{:S(2)}, u32[]{:S(2)}) collective-permute-start(bf16[128,768]{1,0:T(8,128)(2,1)} %add_convert_fusion), channel_id=1, source_target_pairs={{0,1},{1,0},{2,3},{3,2},{4,5},{5,4},{6,7},{7,6},{8,9},{9,8},{10,11... | collective-permute-start | bytes 589832 | tf_op jit(solution)/shard_map/ppermute | solution.py:39
  121.6 3.6 %copy-start.6 = (f32[128,768]{1,0:T(8,128)S(1)}, f32[128,768]{1,0:T(8,128)}, u32[]{:S(2)}) copy-start(f32[128,768]{1,0:T(8,128)} %copy-done.5) | copy-start | bytes 1179652
  121.6 3.6 %copy-start.8 = (bf16[2,128,640]{2,1,0:T(8,128)(2,1)S(1)}, bf16[2,128,640]{2,1,0:T(8,128)(2,1)}, u32[]{:S(2)}) copy-start(bf16[2,128,640]{2,1,0:T(8,128)(2,1)} %copy-done.7) | copy-start | bytes 983044
  121.6 3.6 %copy-start.19 = (bf16[2,128,640]{2,1,0:T(8,128)(2,1)S(1)}, bf16[2,128,640]{2,1,0:T(8,128)(2,1)}, u32[]{:S(2)}) copy-start(bf16[2,128,640]{2,1,0:T(8,128)(2,1)} %copy-done.18) | copy-start | bytes 983044
  121.6 3.6 %copy-start.22 = (f32[128,1]{1,0:T(8,128)S(1)}, f32[128,1]{1,0:T(8,128)}, u32[]{:S(2)}) copy-start(f32[128,1]{1,0:T(8,128)} %copy-done.21) | copy-start | bytes 1540
  131.9 10.3 %collective-permute-start.18 = (bf16[24,2048]{1,0:T(8,128)(2,1)S(1)}, bf16[24,2048]{1,0:T(8,128)(2,1)S(1)}, u32[]{:S(2)}, u32[]{:S(2)}) collective-permute-start(bf16[24,2048]{1,0:T(8,128)(2,1)S(1)} %get-tuple-element.158), channel_id=1, source_target_pairs={{0,8},{1,9},{2,10},{3,11},{4,12},{5,13},{6,14},{7,15},{8,0},{9,1},... | collective-permute-start | bytes 294920 | tf_op jit(solution)/shard_map/ppermute | solution.py:680
  132.0 10.2 %collective-permute-start.17 = (bf16[24,1280]{1,0:T(8,128)(2,1)S(1)}, bf16[24,1280]{1,0:T(8,128)(2,1)S(1)}, u32[]{:S(2)}, u32[]{:S(2)}) collective-permute-start(bf16[24,1280]{1,0:T(8,128)(2,1)S(1)} %get-tuple-element.157), channel_id=1, source_target_pairs={{0,24},{1,25},{2,26},{3,27},{4,28},{5,29},{6,30},{7,31},{8,16},{9,... | collective-permute-start | bytes 184328 | tf_op jit(solution)/shard_map/ppermute | solution.py:680
  135.6 6.6 %collective-permute-start.19 = (bf16[24,1280]{1,0:T(8,128)(2,1)S(1)}, bf16[24,1280]{1,0:T(8,128)(2,1)S(1)}, u32[]{:S(2)}, u32[]{:S(2)}) collective-permute-start(bf16[24,1280]{1,0:T(8,128)(2,1)S(1)} %get-tuple-element.159), channel_id=1, source_target_pairs={{0,16},{1,17},{2,18},{3,19},{4,20},{5,21},{6,22},{7,23},{8,24},{9,... | collective-permute-start | bytes 184328 | tf_op jit(solution)/shard_map/ppermute | solution.py:680
  135.6 1.0 copy-start.17
  (3 other events, 2.3 us)

commit v7 on v6

--- a/solution.py
+++ b/solution.py
@@ -209,7 +209,7 @@
 
 
 def prepare(capacity, pad, group_ref, table_ref, routes_ref, vector_ref, spread_ref, later_ref,
-            gather_ref, send_ref):
+            gather_ref):
     buckets = table_ref.shape[0]
     own_heads, length = vector_ref.shape
     toks = length // 2
@@ -235,7 +235,6 @@
         spread = (place == across).astype(F32)
         target = (spread_ref, later_ref)[i % 2]
         target[i // 2] = spread.astype(BF16)
-        send_ref[:, i * toks : (i + 1) * toks] = jnp.transpose(spread).astype(BF16)
 
 
 def place_weights(arrived_ref, w_ref, wout_ref):
@@ -334,8 +333,8 @@
            vector_ref, *outs)
 
 
-def route_tokens(x_ref, keep_ref, core_ref, came_ref, gains_ref, w_ref, chosen_ref, send_ref,
-                 g_ref, middle_ref, gate_ref, out_ref):
+def route_tokens(capacity, pad, x_ref, keep_ref, core_ref, came_ref, gains_ref, w_ref, chosen_ref,
+                 routes_ref, g_ref, middle_ref, gate_ref, out_ref):
     middle = x_ref[...].astype(F32) + (
         (keep_ref[...] + core_ref[...].astype(F32)) + came_ref[...].astype(F32)
     )
@@ -344,7 +343,20 @@
     g = g_ref[...]
     half = g.shape[1] // 2
     both = jnp.concatenate([normed[:, :half], g[:, :half], normed[:, half:], g[:, half:]], axis=0)
-    out_ref[...] = dot(send_ref[...], both).astype(BF16)
+    toks = g.shape[0]
+    experts = w_ref.shape[1]
+    route = routes_ref[...]
+    chosen = iota((experts, toks), 0) == route
+    upper = (iota((toks, toks), 0) < iota((toks, toks), 1)).astype(BF16)
+    counts = dot(chosen.astype(BF16), upper)
+    slot = jnp.sum(jnp.where(chosen, counts, 0.0), axis=0, keepdims=True).astype(jnp.int32)
+    rows = out_ref.shape[0]
+    place = jnp.where(slot < capacity, route * pad + slot, -4 * rows)
+    down = iota((rows, toks), 0)
+    send = jnp.concatenate(
+        [(down == place + i * capacity).astype(BF16) for i in range(4)], axis=1
+    )
+    out_ref[...] = dot(send, both).astype(BF16)
     probs = jax.nn.softmax(dot(normed, w_ref[...]), axis=-1)
     gate_ref[...] = jnp.sum(probs * chosen_ref[...], axis=1, keepdims=True)
 
@@ -709,14 +721,13 @@
 
     own_across = swap_core(own_tokens)
     pair_across = swap_core(pair_tokens)
-    vectors, spread, later, chosen, send = kernel_call(
+    vectors, spread, later, chosen = kernel_call(
         functools.partial(prepare, capacity, pad),
         [
             ((own_heads, length), F32),
             ((2, toks, experts * pad), BF16),
             ((2, toks, experts * pad), BF16),
             ((toks, experts), F32),
-            ((experts * pad, 4 * toks), BF16),
         ],
         group_at, bias_table, routes.reshape(toks, 1), scalars=2,
     )
@@ -756,9 +767,10 @@
     )
     router_w = weights[:, 3 * cols : 3 * cols + experts]
     middle, gate, outgoing = kernel_call(
-        route_tokens,
+        functools.partial(route_tokens, capacity, pad),
         [((toks, width), F32), ((toks, 1), F32), ((experts * pad, width // 2), BF16)],
-        own_tokens, keep, swap_core(away), pair_sum, gains, router_w, chosen, send, g_low,
+        own_tokens, keep, swap_core(away), pair_sum, gains, router_w, chosen,
+        routes.reshape(1, toks), g_low,
     )
     incoming = exchange(outgoing.reshape(experts, pad, width // 2)).reshape(-1, width // 2)
 

time: 144 us -> 144 us (level)
  local copies, waits for them, and re-layouts: 5.45 us -> 3.75 us
    unnamed x59 -> x51, local copies, waits for them, and re-layouts: 5.21 us -> 3.51 us
where the time goes in v7:
time: 144 us; the launch traced here: 142 us
  waiting for transfers between devices  40.9 us (28%)
  blocking collectives  32.5 us (23%)
  starting transfers between devices  27.9 us (19%)
  Pallas kernels  26.8 us (19%)
  matrix products  8.64 us (6%)
  local copies, waits for them, and re-layouts  3.75 us (3%)
    all_to_all x2, blocking collectives, exchange(): lax.all_to_all(value, 'expert', split_axis=0, concat_axis=0, tiled=True)  32.5 us
    pallas_call x16, Pallas kernels, kernel_call(): pl.pallas_call(run, out_shape=[jax.ShapeDtypeStruct(shape, dtype) for sha...  26.8 us
    all_to_all x2, waiting for transfers between devices, exchange_half(): lax.all_to_all(value, 'expert', split_axis=0, concat_axis=0, tiled=True,...  19.2 us
    ppermute x6, waiting for transfers between devices, across_group(): lax.ppermute(piece, ('dp', 'expert'), [(c * sources + e, (c ^ d >> 1) * s...  10.5 us
    ppermute x10, starting transfers between devices, swap_core(): return lax.ppermute(value, 'dp', [(0, 1), (1, 0)])  9.55 us
    all_to_all x2, starting transfers between devices, exchange_half(): lax.all_to_all(value, 'expert', split_axis=0, concat_axis=0, tiled=True,...  9.5 us
    dot_general x2, matrix products, dot(): lax.dot_general(left, right, (dims, ((), ())), preferred_element_type=F32)  8.64 us
    ppermute x6, starting transfers between devices, across_group(): lax.ppermute(piece, ('dp', 'expert'), [(c * sources + e, (c ^ d >> 1) * s...  7.52 us
  transfers between devices with their start and end apart: 22, of which 11 were waited for; matrix products, arithmetic and copies ran while one was open for 7% of the time, Pallas kernels for 8%

profile of v7, /device:TPU:3, one launch (start us, length us, event | category | flops | bytes accessed | tf_op | source)
XLA Modules:
  0.0 142.2 jit_solution(2089815515483303076)
XLA Ops:
  0.8 2.0 %shard_map.229 = (bf16[24,2048]{1,0:T(8,128)(2,1)}, bf16[24,1280]{1,0:T(8,128)(2,1)}, bf16[24,2048]{1,0:T(8,128)(2,1)}, bf16[24,1280]{1,0:T(8,128)(2,1)}) custom-call(s32[1]{0:T(128)} %bitcast.2.refs_0_, bf16[24,768]{1,0:T(8,128)(2,1)} %refs_1_.3, bf16[24,768]{1,0:T(8,128)(2,1)} %refs_2_.1, bf16[24,768]{1,0:T(8,128)(2,1)} %refs_3_.1, ...), custom_call_target="tpu_custom_call" | custom-call | flops 1000000 | bytes 1000000 | tf_op jit(solution)/shard_map/pallas_call | solution.py:105
  2.8 2.6 %collective-permute-start.2 = (bf16[24,2048]{1,0:T(8,128)(2,1)}, bf16[24,2048]{1,0:T(8,128)(2,1)S(1)}, u32[]{:S(2)}, u32[]{:S(2)}) collective-permute-start(bf16[24,2048]{1,0:T(8,128)(2,1)} %get-tuple-element.92), channel_id=1, source_target_pairs={{0,8},{1,9},{2,10},{3,11},{4,12},{5,13},{6,14},{7,15},{8,0},{9,1},... | collective-permute-start | bytes 294920 | tf_op jit(solution)/shard_map/ppermute | solution.py:692
  5.4 0.9 collective-permute-start.1
  6.6 6.8 %collective-permute-done.1.refs_2_ = bf16[24,1280]{1,0:T(8,128)(2,1)S(1)} collective-permute-done((bf16[24,1280]{1,0:T(8,128)(2,1)}, bf16[24,1280]{1,0:T(8,128)(2,1)S(1)}, u32[]{:S(2)}, u32[]{:S(2)}) %collective-permute-start.1) | collective-permute-done | bytes 61472 | tf_op jit(solution)/shard_map/ppermute | solution.py:692
  13.4 0.9 copy-done.18
  14.3 1.2 shard_map.230
  15.6 4.9 %all-to-all-start = ((bf16[8,120,640]{2,1,0:T(8,128)(2,1)}), bf16[8,120,640]{2,1,0:T(8,128)(2,1)S(1)}, u32[]{:S(2)}, u32[]{:S(2)}) async-start(bf16[8,120,640]{2,1,0:T(8,128)(2,1)} %shard_map.230), calls=%async_computation | async-start | bytes 2457600 | tf_op jit(solution)/shard_map/all_to_all | solution.py:49
  20.4 0.5 collective-permute-start.4
  21.1 1.3 shard_map.231
  22.4 0.7 copy-done.16
  23.1 14.2 %all-to-all-done.refs_3_ = bf16[8,120,640]{2,1,0:T(8,128)(2,1)S(1)} async-done(((bf16[8,120,640]{2,1,0:T(8,128)(2,1)}), bf16[8,120,640]{2,1,0:T(8,128)(2,1)S(1)}, u32[]{:S(2)}, u32[]{:S(2)}) %all-to-all-start) | async-done | bytes 1228832 | tf_op jit(solution)/shard_map/all_to_all | solution.py:49
  37.3 1.7 %shard_map.232 = (bf16[768,640]{1,0:T(8,128)(2,1)S(1)}, bf16[192,768]{1,0:T(8,128)(2,1)S(1)}, f32[8,768]{1,0:T(8,128)S(1)}, bf16[256,576]{1,0:T(8,128)(2,1)S(1)}...) custom-call(s32[1]{0:T(128)} %bitcast.2.refs_0_, ...), custom_call_target="tpu_custom_call" | custom-call | flops 1000000 | bytes 1000000 | tf_op jit(solution)/shard_map/pallas_call | solution.py:105
  39.0 1.1 collective-permute-start.5
  40.1 1.0 collective-permute-done.5
  41.5 1.5 %shard_map.233 = (bf16[256,576]{1,0:T(8,128)(2,1)S(1)}, f32[3,256,256]{2,1,0:T(8,128)S(1)}, bf16[256,192]{1,0:T(8,128)(2,1)S(1)}, f32[128,768]{1,0:T(8,128)S(1)}, bf16[128,768]{1,0:T(8,128)(2,1)S(1)}) custom-call(s32[1]{0:T(128)} %bitcast.2.refs_0_, s32[1,256]{1,0:T(1,128)S(1)} %copy-done.21, ...), custom_call_target="tpu_custom_call" | custom-call | flops 1000000 | bytes 1000000 | tf_op jit(solution)/shard_map/pallas_call | solution.py:105
  43.0 0.3 collective-permute-start.7
  43.4 3.9 %collective-permute-done.8.refs_3_ = bf16[128,768]{1,0:T(8,128)(2,1)S(1)} collective-permute-done((bf16[128,768]{1,0:T(8,128)(2,1)S(1)}, bf16[128,768]{1,0:T(8,128)(2,1)S(1)}, u32[]{:S(2)}, u32[]{:S(2)}) %collective-permute-start.8) | collective-permute-done | bytes 196640 | tf_op jit(solution)/shard_map/ppermute | solution.py:39
  47.4 1.0 shard_map.234
  48.4 16.2 %all_to_all.20 = bf16[16,40,384]{2,1,0:T(8,128)(2,1)S(1)} all-to-all(bf16[16,40,384]{2,1,0:T(8,128)(2,1)S(1)} %bitcast.44), channel_id=1, replica_groups=mesh['dp'=2,'expert'=16] {'expert'}, dimensions={0} | all-to-all | bytes 983040 | tf_op jit(solution)/shard_map/all_to_all | solution.py:43
  64.6 3.0 %collective-permute-start.9 = (bf16[640,384]{1,0:T(8,128)(2,1)S(1)}, bf16[640,384]{1,0:T(8,128)(2,1)S(1)}, u32[]{:S(2)}, u32[]{:S(2)}) collective-permute-start(bf16[640,384]{1,0:T(8,128)(2,1)S(1)} %bitcast.38), channel_id=1, source_target_pairs={{0,16},{16,0},{1,17},{17,1},{2,18},{18,2},{3,19},{19,3},{4,20},{20... | collective-permute-start | bytes 1474568 | tf_op jit(solution)/shard_map/ppermute | solution.py:34
  67.7 1.5 %collective-permute-done.9.refs_2_ = bf16[640,384]{1,0:T(8,128)(2,1)S(1)} collective-permute-done((bf16[640,384]{1,0:T(8,128)(2,1)S(1)}, bf16[640,384]{1,0:T(8,128)(2,1)S(1)}, u32[]{:S(2)}, u32[]{:S(2)}) %collective-permute-start.9) | collective-permute-done | bytes 491552 | tf_op jit(solution)/shard_map/ppermute | solution.py:34
  69.2 4.6 %shard_map.235 = (bf16[320,768]{1,0:T(8,128)(2,1)S(1)}, bf16[320,768]{1,0:T(8,128)(2,1)S(1)}, bf16[160,768]{1,0:T(8,128)(2,1)S(1)}, f32[160,16]{1,0:T(8,128)S(1)...) custom-call(s32[1]{0:T(128)} %bitcast.refs_2_.refs_0_, ...), custom_call_target="tpu_custom_call" | custom-call | flops 1000000 | bytes 1000000 | tf_op jit(solution)/shard_map/pallas_call | solution.py:105
  73.8 0.4 collective-permute-start.10
  74.2 1.5 %collective-permute-done.10.refs_2_ = bf16[2,160,768]{2,1,0:T(8,128)(2,1)S(1)} collective-permute-done((bf16[2,160,768]{2,1,0:T(8,128)(2,1)S(1)}, bf16[2,160,768]{2,1,0:T(8,128)(2,1)S(1)}, u32[]{:S(2)}, u32[]{:S(2)}) %collective-permute-start.10) | collective-permute-done | bytes 491552 | tf_op jit(solution)/shard_map/ppermute | solution.py:34
  75.7 1.3 shard_map.236
  77.0 16.3 %all_to_all.21 = bf16[16,40,384]{2,1,0:T(8,128)(2,1)S(1)} all-to-all(bf16[16,40,384]{2,1,0:T(8,128)(2,1)S(1)} %bitcast.43), channel_id=1, replica_groups=mesh['dp'=2,'expert'=16] {'expert'}, dimensions={0} | all-to-all | bytes 983040 | tf_op jit(solution)/shard_map/all_to_all | solution.py:43
  93.3 0.5 shard_map.237
  93.8 2.5 %collective-permute-start.12 = (bf16[128,768]{1,0:T(8,128)(2,1)S(1)}, bf16[128,768]{1,0:T(8,128)(2,1)S(1)}, u32[]{:S(2)}, u32[]{:S(2)}) collective-permute-start(bf16[128,768]{1,0:T(8,128)(2,1)S(1)} %get-tuple-element.121.refs_0_), channel_id=1, source_target_pairs={{0,16},{16,0},{1,17},{17,1},{2,18},{18,2},{3,19},{19,3},{4,20},{20... | collective-permute-start | bytes 589832 | tf_op jit(solution)/shard_map/ppermute | solution.py:34
  96.4 1.2 collective-permute-start.11
  97.6 3.2 %shard_map.238 = (f32[768,576]{1,0:T(8,128)S(1)}, f32[192,768]{1,0:T(8,128)S(1)}, f32[128,768]{1,0:T(8,128)S(1)}, bf16[128,768]{1,0:T(8,128)(2,1)}, bf16[256,576...) custom-call(bf16[128,768]{1,0:T(8,128)(2,1)S(1)} %get-tuple-element.121.refs_0_, ...), custom_call_target="tpu_custom_call" | custom-call | flops 1000000 | bytes 1000000 | tf_op jit(solution)/shard_map/pallas_call | solution.py:105
  100.8 2.1 %collective-permute-done.11.refs_0_ = bf16[128,768]{1,0:T(8,128)(2,1)S(1)} collective-permute-done((bf16[128,768]{1,0:T(8,128)(2,1)S(1)}, bf16[128,768]{1,0:T(8,128)(2,1)S(1)}, u32[]{:S(2)}, u32[]{:S(2)}) %collective-permute-start.11) | collective-permute-done | bytes 196640 | tf_op jit(solution)/shard_map/ppermute | solution.py:39
  102.8 0.8 collective-permute-start.13
  103.7 1.1 collective-permute-done.13.refs_1_
  104.8 2.2 %shard_map.239 = (f32[128,768]{1,0:T(8,128)S(1)}, bf16[128,768]{1,0:T(8,128)(2,1)S(1)}, bf16[256,576]{1,0:T(8,128)(2,1)S(1)}, f32[1,768]{1,0:T(1,128)S(1)}, f32[3,256]{1,0:T(4,128)S(1)}) custom-call(bf16[128,768]{1,0:T(8,128)(2,1)S(1)} %collective-permute-done.11.refs_0_, bf16[128,768]{1,0:T(8,128)(2,1)S(1)} %collective-permute-done.13.refs_1_, ...), custom_call_target="tpu_custom_call" | custom-call | flops 1000000 | bytes 1000000 | tf_op jit(solution)/shard_map/pallas_call | solution.py:105
  107.0 0.7 copy-done.12
  107.7 2.0 %shard_map.240 = bf16[8,120,640]{2,1,0:T(8,128)(2,1)} custom-call(bf16[128,768]{1,0:T(8,128)(2,1)S(1)} %collective-permute-done.11.refs_0_, bf16[128,768]{1,0:T(8,128)(2,1)S(1)} %collective-permute-done.13.refs_1_, bf16[256,192]{1,0:T(8,128)(2,1)S(1)} %get-tuple-element.128.refs_2_, bf16[256,576]{1,0:T(8,128)(2,1)S(1)} %get-tuple-element.131.refs_3_, ...), custom_call_target="tpu_custom_call" | custom-call | flops 1000000 | bytes 1000000 | tf_op jit(solution)/shard_map/pallas_call | solution.py:105
  109.7 4.7 %all-to-all-start.3 = ((bf16[8,120,640]{2,1,0:T(8,128)(2,1)}), bf16[8,120,640]{2,1,0:T(8,128)(2,1)S(1)}, u32[]{:S(2)}, u32[]{:S(2)}) async-start(bf16[8,120,640]{2,1,0:T(8,128)(2,1)} %shard_map.240), calls=%async_computation.3 | async-start | bytes 2457600 | tf_op jit(solution)/shard_map/all_to_all | solution.py:49
  114.4 0.7 collective-permute-start.15
  115.0 5.0 %fusion = f32[768,1536]{1,0:T(8,128)} fusion(bf16[320,768]{1,0:T(8,128)(2,1)} %copy-done.4, bf16[320,1536]{1,0:T(8,128)(2,1)} %copy-done.9), kind=kOutput, calls=%fused_computation.2 | convolution fusion | flops 754974720 | bytes 6193152 | tf_op jit(solution)/shard_map/dot_general | solution.py:20
  120.1 0.7 add_convert_fusion
  120.8 3.6 %fusion.1 = f32[1536,768]{1,0:T(8,128)} fusion(bf16[320,1536]{1,0:T(8,128)(2,1)S(1)} %get-tuple-element.141, bf16[320,768]{1,0:T(8,128)(2,1)S(1)} %copy-done.11), kind=kOutput, calls=%fused_computation.3 | convolution fusion | flops 754974720 | bytes 6193152 | tf_op jit(solution)/shard_map/dot_general | solution.py:20
  124.5 1.4 shard_map.241
  125.8 5.0 %all-to-all-done.3.refs_1_ = bf16[8,120,640]{2,1,0:T(8,128)(2,1)S(1)} async-done(((bf16[8,120,640]{2,1,0:T(8,128)(2,1)}), bf16[8,120,640]{2,1,0:T(8,128)(2,1)S(1)}, u32[]{:S(2)}, u32[]{:S(2)}) %all-to-all-start.3) | async-done | bytes 1228832 | tf_op jit(solution)/shard_map/all_to_all | solution.py:49
  131.2 3.6 %collective-permute-start.17 = (bf16[24,1280]{1,0:T(8,128)(2,1)S(1)}, bf16[24,1280]{1,0:T(8,128)(2,1)S(1)}, u32[]{:S(2)}, u32[]{:S(2)}) collective-permute-start(bf16[24,1280]{1,0:T(8,128)(2,1)S(1)} %get-tuple-element.155), channel_id=1, source_target_pairs={{0,24},{1,25},{2,26},{3,27},{4,28},{5,29},{6,30},{7,31},{8,16},{9,... | collective-permute-start | bytes 184328 | tf_op jit(solution)/shard_map/ppermute | solution.py:692
  134.8 1.0 copy-done.15
  135.8 1.9 %shard_map.242 = bf16[128,768]{1,0:T(8,128)(2,1)} custom-call(f32[128,768]{1,0:T(8,128)S(1)} %copy-done.15, bf16[128,768]{1,0:T(8,128)(2,1)S(1)} %collective-permute-done.14.refs_1_, bf16[128,768]{1,0:T(8,128)(2,1)} %collective-permute-done.16.refs_2_, f32[128,768]{1,0:T(8,128)S(1)} %get-tuple-element.152.refs_3_, bf16[128,768]{1,0:T(8,128)(2,1)S(1)} %bitcast.35, ...), custom_call_target="tpu_custom_call" | custom-call | flops 1000000 | bytes 1000000 | tf_op jit(solution)/shard_map/pallas_call | solution.py:105
  137.7 3.7 %collective-permute-done.17.refs_2_ = bf16[24,1280]{1,0:T(8,128)(2,1)S(1)} collective-permute-done((bf16[24,1280]{1,0:T(8,128)(2,1)S(1)}, bf16[24,1280]{1,0:T(8,128)(2,1)S(1)}, u32[]{:S(2)}, u32[]{:S(2)}) %collective-permute-start.17) | collective-permute-done | bytes 61472 | tf_op jit(solution)/shard_map/ppermute | solution.py:692
  141.3 0.9 shard_map.244
  (72 shorter events, 1.6 us)
Async XLA Ops:
  0.6 20.3 %copy-start.24 = (f32[32,12]{0,1:T(8,128)S(1)}, f32[32,12]{0,1:T(8,128)}, u32[]{:S(2)}) copy-start(f32[32,12]{0,1:T(8,128)} %param.20) | copy-start | bytes 4612
  0.7 20.3 %copy-start.22 = (s32[1,128,1]{1,2,0:T(1,128)S(1)}, s32[1,128,1]{1,2,0:T(1,128)}, u32[]{:S(2)}) copy-start(s32[1,128,1]{1,2,0:T(1,128)} %param.26) | copy-start | bytes 1540
  0.7 12.8 %collective-permute-start = (bf16[128,768]{1,0:T(8,128)(2,1)}, bf16[128,768]{1,0:T(8,128)(2,1)S(1)}, u32[]{:S(2)}, u32[]{:S(2)}) collective-permute-start(bf16[128,768]{1,0:T(8,128)(2,1)} %bitcast.30), channel_id=1, source_target_pairs={{0,1},{1,0},{2,3},{3,2},{4,5},{5,4},{6,7},{7,6},{8,9},{9,8},{10,11... | collective-permute-start | bytes 589832 | tf_op jit(solution)/shard_map/ppermute | solution.py:39
  2.8 10.6 %collective-permute-start.2 = (bf16[24,2048]{1,0:T(8,128)(2,1)}, bf16[24,2048]{1,0:T(8,128)(2,1)S(1)}, u32[]{:S(2)}, u32[]{:S(2)}) collective-permute-start(bf16[24,2048]{1,0:T(8,128)(2,1)} %get-tuple-element.92), channel_id=1, source_target_pairs={{0,8},{1,9},{2,10},{3,11},{4,12},{5,13},{6,14},{7,15},{8,0},{9,1},... | collective-permute-start | bytes 294920 | tf_op jit(solution)/shard_map/ppermute | solution.py:692
  5.4 8.0 %collective-permute-start.1 = (bf16[24,1280]{1,0:T(8,128)(2,1)}, bf16[24,1280]{1,0:T(8,128)(2,1)S(1)}, u32[]{:S(2)}, u32[]{:S(2)}) collective-permute-start(bf16[24,1280]{1,0:T(8,128)(2,1)} %get-tuple-element.91), channel_id=1, source_target_pairs={{0,24},{1,25},{2,26},{3,27},{4,28},{5,29},{6,30},{7,31},{8,16},{9,... | collective-permute-start | bytes 184328 | tf_op jit(solution)/shard_map/ppermute | solution.py:692
  6.3 7.1 %collective-permute-start.3 = (bf16[24,1280]{1,0:T(8,128)(2,1)}, bf16[24,1280]{1,0:T(8,128)(2,1)S(1)}, u32[]{:S(2)}, u32[]{:S(2)}) collective-permute-start(bf16[24,1280]{1,0:T(8,128)(2,1)} %get-tuple-element.93), channel_id=1, source_target_pairs={{0,16},{1,17},{2,18},{3,19},{4,20},{5,21},{6,22},{7,23},{8,24},{9,... | collective-permute-start | bytes 184328 | tf_op jit(solution)/shard_map/ppermute | solution.py:692
  13.4 0.9 copy-start.18
  15.6 24.5 %copy-start = (bf16[1,128,768]{2,1,0:T(8,128)(2,1)S(1)}, bf16[1,128,768]{2,1,0:T(8,128)(2,1)}, u32[]{:S(2)}) copy-start(bf16[1,128,768]{2,1,0:T(8,128)(2,1)} %param.14) | copy-start | bytes 589828
  15.6 25.9 %copy-start.21 = (s32[1,256]{1,0:T(1,128)S(1)}, s32[1,256]{1,0:T(1,128)}, u32[]{:S(2)}) copy-start(s32[1,256]{1,0:T(1,128)} %refs_1_.4) | copy-start | bytes 3076
  15.6 21.7 %all-to-all-start = ((bf16[8,120,640]{2,1,0:T(8,128)(2,1)}), bf16[8,120,640]{2,1,0:T(8,128)(2,1)S(1)}, u32[]{:S(2)}, u32[]{:S(2)}) async-start(bf16[8,120,640]{2,1,0:T(8,128)(2,1)} %shard_map.230), calls=%async_computation | async-start | bytes 2457600 | tf_op jit(solution)/shard_map/all_to_all | solution.py:49
  20.4 26.9 %copy-start.3 = (bf16[1,128,768]{2,1,0:T(8,128)(2,1)S(1)}, bf16[1,128,768]{2,1,0:T(8,128)(2,1)}, u32[]{:S(2)}) copy-start(bf16[1,128,768]{2,1,0:T(8,128)(2,1)} %param.27) | copy-start | bytes 589828
  20.4 2.7 %collective-permute-start.4 = (bf16[128,768]{1,0:T(8,128)(2,1)S(1)}, bf16[128,768]{1,0:T(8,128)(2,1)S(1)}, u32[]{:S(2)}, u32[]{:S(2)}) collective-permute-start(bf16[128,768]{1,0:T(8,128)(2,1)S(1)} %collective-permute-done.refs_4_.refs_7_.refs_5_), channel_id=1, source_target_pairs={{0,16},{16,0},{1,17},{17,1},{2,18},{18,2},{3,19},{19,3},{4,20},{20... | collective-permute-start | bytes 589832 | tf_op jit(solution)/shard_map/ppermute | solution.py:34
  22.4 0.7 copy-start.16
  23.1 70.2 %copy-start.7 = (bf16[2,128,640]{2,1,0:T(8,128)(2,1)}, bf16[2,128,640]{2,1,0:T(8,128)(2,1)S(1)}, u32[]{:S(2)}) copy-start(bf16[2,128,640]{2,1,0:T(8,128)(2,1)S(1)} %get-tuple-element.119.refs_1_) | copy-start | bytes 983044
  39.0 2.1 %collective-permute-start.5 = (bf16[128,768]{1,0:T(8,128)(2,1)S(1)}, bf16[128,768]{1,0:T(8,128)(2,1)S(1)}, u32[]{:S(2)}, u32[]{:S(2)}) collective-permute-start(bf16[128,768]{1,0:T(8,128)(2,1)S(1)} %get-tuple-element.102), channel_id=1, source_target_pairs={{0,16},{16,0},{1,17},{17,1},{2,18},{18,2},{3,19},{19,3},{4,20},{20... | collective-permute-start | bytes 589832 | tf_op jit(solution)/shard_map/ppermute | solution.py:34
  40.0 1.4 %collective-permute-start.6 = (bf16[128,768]{1,0:T(8,128)(2,1)S(1)}, bf16[128,768]{1,0:T(8,128)(2,1)S(1)}, u32[]{:S(2)}, u32[]{:S(2)}) collective-permute-start(bf16[128,768]{1,0:T(8,128)(2,1)S(1)} %bitcast.31), channel_id=1, source_target_pairs={{0,16},{16,0},{1,17},{17,1},{2,18},{18,2},{3,19},{19,3},{4,20},{20... | collective-permute-start | bytes 589832 | tf_op jit(solution)/shard_map/ppermute | solution.py:34
  41.1 28.0 %copy-start.2 = (bf16[1,1536,768]{2,1,0:T(8,128)(2,1)S(1)}, bf16[1,1536,768]{2,1,0:T(8,128)(2,1)}, u32[]{:S(2)}) copy-start(bf16[1,1536,768]{2,1,0:T(8,128)(2,1)} %param.24) | copy-start | bytes 7077892
  41.2 28.0 %copy-start.1 = (bf16[1,768,1536]{2,1,0:T(8,128)(2,1)S(1)}, bf16[1,768,1536]{2,1,0:T(8,128)(2,1)}, u32[]{:S(2)}) copy-start(bf16[1,768,1536]{2,1,0:T(8,128)(2,1)} %param.23) | copy-start | bytes 7077892
  41.2 6.2 %collective-permute-start.8 = (bf16[128,768]{1,0:T(8,128)(2,1)S(1)}, bf16[128,768]{1,0:T(8,128)(2,1)S(1)}, u32[]{:S(2)}, u32[]{:S(2)}) collective-permute-start(bf16[128,768]{1,0:T(8,128)(2,1)S(1)} %add_convert_fusion.1), channel_id=1, source_target_pairs={{0,1},{1,0},{2,3},{3,2},{4,5},{5,4},{6,7},{7,6},{8,9},{9,8},{10,11... | collective-permute-start | bytes 589832 | tf_op jit(solution)/shard_map/ppermute | solution.py:39
  43.0 4.4 %collective-permute-start.7 = (bf16[128,768]{1,0:T(8,128)(2,1)S(1)}, bf16[128,768]{1,0:T(8,128)(2,1)S(1)}, u32[]{:S(2)}, u32[]{:S(2)}) collective-permute-start(bf16[128,768]{1,0:T(8,128)(2,1)S(1)} %get-tuple-element.108), channel_id=1, source_target_pairs={{0,16},{16,0},{1,17},{17,1},{2,18},{18,2},{3,19},{19,3},{4,20},{20... | collective-permute-start | bytes 589832 | tf_op jit(solution)/shard_map/ppermute | solution.py:34
  48.4 20.8 %copy-start.19 = (f32[128,1]{1,0:T(8,128)}, f32[128,1]{1,0:T(8,128)S(1)}, u32[]{:S(2)}) copy-start(f32[128,1]{1,0:T(8,128)S(1)} %get-tuple-element.144.refs_6_) | copy-start | bytes 1540
  48.4 44.9 %copy-start.5 = (f32[128,768]{1,0:T(8,128)}, f32[128,768]{1,0:T(8,128)S(1)}, u32[]{:S(2)}) copy-start(f32[128,768]{1,0:T(8,128)S(1)} %get-tuple-element.120.refs_2_.refs_3_) | copy-start | bytes 1179652
  64.6 4.5 %collective-permute-start.9 = (bf16[640,384]{1,0:T(8,128)(2,1)S(1)}, bf16[640,384]{1,0:T(8,128)(2,1)S(1)}, u32[]{:S(2)}, u32[]{:S(2)}) collective-permute-start(bf16[640,384]{1,0:T(8,128)(2,1)S(1)} %bitcast.38), channel_id=1, source_target_pairs={{0,16},{16,0},{1,17},{17,1},{2,18},{18,2},{3,19},{19,3},{4,20},{20... | collective-permute-start | bytes 1474568 | tf_op jit(solution)/shard_map/ppermute | solution.py:34
  73.7 20.1 %copy-start.4 = (bf16[320,768]{1,0:T(8,128)(2,1)}, bf16[320,768]{1,0:T(8,128)(2,1)S(1)}, u32[]{:S(2)}) copy-start(bf16[320,768]{1,0:T(8,128)(2,1)S(1)} %get-tuple-element.114) | copy-start | bytes 1474564
  73.7 20.1 %copy-start.10 = (bf16[320,768]{1,0:T(8,128)(2,1)}, bf16[320,768]{1,0:T(8,128)(2,1)S(1)}, u32[]{:S(2)}) copy-start(bf16[320,768]{1,0:T(8,128)(2,1)S(1)} %get-tuple-element.142) | copy-start | bytes 1474564
  73.8 33.2 %copy-start.9 = (bf16[320,1536]{1,0:T(8,128)(2,1)}, bf16[320,1536]{1,0:T(8,128)(2,1)S(1)}, u32[]{:S(2)}) copy-start(bf16[320,1536]{1,0:T(8,128)(2,1)S(1)} %get-tuple-element.140) | copy-start | bytes 2949124
  73.8 1.9 %collective-permute-start.10 = (bf16[2,160,768]{2,1,0:T(8,128)(2,1)S(1)}, bf16[2,160,768]{2,1,0:T(8,128)(2,1)S(1)}, u32[]{:S(2)}, u32[]{:S(2)}) collective-permute-start(bf16[2,160,768]{2,1,0:T(8,128)(2,1)S(1)} %get-tuple-element.113), channel_id=1, source_target_pairs={{0,16},{16,0},{1,17},{17,1},{2,18},{18,2},{3,19},{19,3},{4,20},{20... | collective-permute-start | bytes 1474568 | tf_op jit(solution)/shard_map/ppermute | solution.py:34
  93.8 3.7 %collective-permute-start.12 = (bf16[128,768]{1,0:T(8,128)(2,1)S(1)}, bf16[128,768]{1,0:T(8,128)(2,1)S(1)}, u32[]{:S(2)}, u32[]{:S(2)}) collective-permute-start(bf16[128,768]{1,0:T(8,128)(2,1)S(1)} %get-tuple-element.121.refs_0_), channel_id=1, source_target_pairs={{0,16},{16,0},{1,17},{17,1},{2,18},{18,2},{3,19},{19,3},{4,20},{20... | collective-permute-start | bytes 589832 | tf_op jit(solution)/shard_map/ppermute | solution.py:34
  96.4 6.5 %collective-permute-start.11 = (bf16[128,768]{1,0:T(8,128)(2,1)S(1)}, bf16[128,768]{1,0:T(8,128)(2,1)S(1)}, u32[]{:S(2)}, u32[]{:S(2)}) collective-permute-start(bf16[128,768]{1,0:T(8,128)(2,1)S(1)} %get-tuple-element.121.refs_0_), channel_id=1, source_target_pairs={{0,1},{1,0},{2,3},{3,2},{4,5},{5,4},{6,7},{7,6},{8,9},{9,8},{10,11... | collective-permute-start | bytes 589832 | tf_op jit(solution)/shard_map/ppermute | solution.py:39
  100.8 8.9 %copy-start.14 = (f32[128,768]{1,0:T(8,128)}, f32[128,768]{1,0:T(8,128)S(1)}, u32[]{:S(2)}) copy-start(f32[128,768]{1,0:T(8,128)S(1)} %get-tuple-element.148.refs_0_) | copy-start | bytes 1179652
  102.8 1.9 %collective-permute-start.13 = (bf16[128,768]{1,0:T(8,128)(2,1)S(1)}, bf16[128,768]{1,0:T(8,128)(2,1)S(1)}, u32[]{:S(2)}, u32[]{:S(2)}) collective-permute-start(bf16[128,768]{1,0:T(8,128)(2,1)S(1)} %collective-permute-done.11.refs_0_), channel_id=1, source_target_pairs={{0,16},{16,0},{1,17},{17,1},{2,18},{18,2},{3,19},{19,3},{4,20},{20... | collective-permute-start | bytes 589832 | tf_op jit(solution)/shard_map/ppermute | solution.py:34
  107.0 0.7 copy-start.12
  107.7 2.0 %copy-start.23 = (bf16[128,768]{1,0:T(8,128)(2,1)}, bf16[128,768]{1,0:T(8,128)(2,1)S(1)}, u32[]{:S(2)}) copy-start(bf16[128,768]{1,0:T(8,128)(2,1)S(1)} %get-tuple-element.151) | copy-start | bytes 589828
  109.7 21.1 %all-to-all-start.3 = ((bf16[8,120,640]{2,1,0:T(8,128)(2,1)}), bf16[8,120,640]{2,1,0:T(8,128)(2,1)S(1)}, u32[]{:S(2)}, u32[]{:S(2)}) async-start(bf16[8,120,640]{2,1,0:T(8,128)(2,1)} %shard_map.240), calls=%async_computation.3 | async-start | bytes 2457600 | tf_op jit(solution)/shard_map/all_to_all | solution.py:49
  114.4 5.7 %collective-permute-start.15 = (bf16[128,768]{1,0:T(8,128)(2,1)}, bf16[128,768]{1,0:T(8,128)(2,1)S(1)}, u32[]{:S(2)}, u32[]{:S(2)}) collective-permute-start(bf16[128,768]{1,0:T(8,128)(2,1)} %copy-done.23), channel_id=1, source_target_pairs={{0,16},{16,0},{1,17},{17,1},{2,18},{18,2},{3,19},{19,3},{4,20},{20... | collective-permute-start | bytes 589832 | tf_op jit(solution)/shard_map/ppermute | solution.py:34
  115.0 5.1 %copy-start.13 = (f32[128,768]{1,0:T(8,128)S(1)}, f32[128,768]{1,0:T(8,128)}, u32[]{:S(2)}) copy-start(f32[128,768]{1,0:T(8,128)} %copy-done.12) | copy-start | bytes 1179652
  115.0 5.8 %copy-start.11 = (bf16[320,768]{1,0:T(8,128)(2,1)S(1)}, bf16[320,768]{1,0:T(8,128)(2,1)}, u32[]{:S(2)}) copy-start(bf16[320,768]{1,0:T(8,128)(2,1)} %copy-done.10) | copy-start | bytes 1474564
  120.1 14.7 %collective-permute-start.14 = (bf16[128,768]{1,0:T(8,128)(2,1)}, bf16[128,768]{1,0:T(8,128)(2,1)S(1)}, u32[]{:S(2)}, u32[]{:S(2)}) collective-permute-start(bf16[128,768]{1,0:T(8,128)(2,1)} %get-tuple-element.149), channel_id=1, source_target_pairs={{0,16},{16,0},{1,17},{17,1},{2,18},{18,2},{3,19},{19,3},{4,20},{20... | collective-permute-start | bytes 589832 | tf_op jit(solution)/shard_map/ppermute | solution.py:34
  120.8 14.0 %collective-permute-start.16 = (bf16[128,768]{1,0:T(8,128)(2,1)}, bf16[128,768]{1,0:T(8,128)(2,1)}, u32[]{:S(2)}, u32[]{:S(2)}) collective-permute-start(bf16[128,768]{1,0:T(8,128)(2,1)} %add_convert_fusion), channel_id=1, source_target_pairs={{0,1},{1,0},{2,3},{3,2},{4,5},{5,4},{6,7},{7,6},{8,9},{9,8},{10,11... | collective-permute-start | bytes 589832 | tf_op jit(solution)/shard_map/ppermute | solution.py:39
  120.8 3.6 %copy-start.6 = (f32[128,768]{1,0:T(8,128)S(1)}, f32[128,768]{1,0:T(8,128)}, u32[]{:S(2)}) copy-start(f32[128,768]{1,0:T(8,128)} %copy-done.5) | copy-start | bytes 1179652
  120.8 3.6 %copy-start.8 = (bf16[2,128,640]{2,1,0:T(8,128)(2,1)S(1)}, bf16[2,128,640]{2,1,0:T(8,128)(2,1)}, u32[]{:S(2)}) copy-start(bf16[2,128,640]{2,1,0:T(8,128)(2,1)} %copy-done.7) | copy-start | bytes 983044
  120.8 3.6 %copy-start.17 = (bf16[2,128,640]{2,1,0:T(8,128)(2,1)S(1)}, bf16[2,128,640]{2,1,0:T(8,128)(2,1)}, u32[]{:S(2)}) copy-start(bf16[2,128,640]{2,1,0:T(8,128)(2,1)} %copy-done.16) | copy-start | bytes 983044
  120.8 3.6 %copy-start.20 = (f32[128,1]{1,0:T(8,128)S(1)}, f32[128,1]{1,0:T(8,128)}, u32[]{:S(2)}) copy-start(f32[128,1]{1,0:T(8,128)} %copy-done.19) | copy-start | bytes 1540
  131.1 10.2 %collective-permute-start.18 = (bf16[24,2048]{1,0:T(8,128)(2,1)S(1)}, bf16[24,2048]{1,0:T(8,128)(2,1)S(1)}, u32[]{:S(2)}, u32[]{:S(2)}) collective-permute-start(bf16[24,2048]{1,0:T(8,128)(2,1)S(1)} %get-tuple-element.156), channel_id=1, source_target_pairs={{0,8},{1,9},{2,10},{3,11},{4,12},{5,13},{6,14},{7,15},{8,0},{9,1},... | collective-permute-start | bytes 294920 | tf_op jit(solution)/shard_map/ppermute | solution.py:692
  131.2 10.1 %collective-permute-start.17 = (bf16[24,1280]{1,0:T(8,128)(2,1)S(1)}, bf16[24,1280]{1,0:T(8,128)(2,1)S(1)}, u32[]{:S(2)}, u32[]{:S(2)}) collective-permute-start(bf16[24,1280]{1,0:T(8,128)(2,1)S(1)} %get-tuple-element.155), channel_id=1, source_target_pairs={{0,24},{1,25},{2,26},{3,27},{4,28},{5,29},{6,30},{7,31},{8,16},{9,... | collective-permute-start | bytes 184328 | tf_op jit(solution)/shard_map/ppermute | solution.py:692
  134.8 6.5 %collective-permute-start.19 = (bf16[24,1280]{1,0:T(8,128)(2,1)S(1)}, bf16[24,1280]{1,0:T(8,128)(2,1)S(1)}, u32[]{:S(2)}, u32[]{:S(2)}) collective-permute-start(bf16[24,1280]{1,0:T(8,128)(2,1)S(1)} %get-tuple-element.157), channel_id=1, source_target_pairs={{0,16},{1,17},{2,18},{3,19},{4,20},{5,21},{6,22},{7,23},{8,24},{9,... | collective-permute-start | bytes 184328 | tf_op jit(solution)/shard_map/ppermute | solution.py:692
  134.8 1.0 copy-start.15

commit v8 on v7

--- a/solution.py
+++ b/solution.py
@@ -184,6 +184,10 @@
     over = (width - wide) // 4
     tail = [held[j * rows : (j + 1) * rows, wide - over :] for j in range(4)]
     return jnp.concatenate([held[4 * rows :]] + tail, axis=1)
+
+
+def hand_on(in_ref, out_ref):
+    out_ref[...] = in_ref[...]
 
 
 def spread_weights(cols, used, block_ref, own_ref, p3_ref, p1_ref, p2_ref, out_ref):
@@ -712,6 +716,7 @@
         limit=60 * 1024 * 1024,
     )
     pieces = across_group(pieces)
+    (own_piece,) = kernel_call(hand_on, [(own_piece.shape, BF16)], own_piece)
     pair_tokens, own_piece, *pieces = lax.optimization_barrier((pair_tokens, own_piece, *pieces))
     (message,) = kernel_call(
         functools.partial(spread_weights, cols, used), [((half, 5 * rows, wide), BF16)],

time: 144 us -> 143 us (level)
    pallas_call x16 -> x17, Pallas kernels: 26.8 us -> 26.8 us  [kernel_call(): pl.pallas_call(run, out_shape=[jax.ShapeDtypeStruct(shape, dtype) for sha...]
where the time goes in v8:
time: 143 us; the launch traced here: 141 us
  waiting for transfers between devices  40 us (28%)
  blocking collectives  32.5 us (23%)
  starting transfers between devices  27.9 us (20%)
  Pallas kernels  26.8 us (19%)
  matrix products  8.64 us (6%)
  local copies, waits for them, and re-layouts  3.76 us (3%)
    all_to_all x2, blocking collectives, exchange(): lax.all_to_all(value, 'expert', split_axis=0, concat_axis=0, tiled=True)  32.5 us
    pallas_call x17, Pallas kernels, kernel_call(): pl.pallas_call(run, out_shape=[jax.ShapeDtypeStruct(shape, dtype) for sha...  26.8 us
    all_to_all x2, waiting for transfers between devices, exchange_half(): lax.all_to_all(value, 'expert', split_axis=0, concat_axis=0, tiled=True,...  19.2 us
    ppermute x6, waiting for transfers between devices, across_group(): lax.ppermute(piece, ('dp', 'expert'), [(c * sources + e, (c ^ d >> 1) * s...  9.56 us
    ppermute x10, starting transfers between devices, swap_core(): return lax.ppermute(value, 'dp', [(0, 1), (1, 0)])  9.55 us
    all_to_all x2, starting transfers between devices, exchange_half(): lax.all_to_all(value, 'expert', split_axis=0, concat_axis=0, tiled=True,...  9.5 us
    dot_general x2, matrix products, dot(): lax.dot_general(left, right, (dims, ((), ())), preferred_element_type=F32)  8.64 us
    ppermute x6, starting transfers between devices, across_group(): lax.ppermute(piece, ('dp', 'expert'), [(c * sources + e, (c ^ d >> 1) * s...  7.52 us
  transfers between devices with their start and end apart: 22, of which 11 were waited for; matrix products, arithmetic and copies ran while one was open for 7% of the time, Pallas kernels for 8%

profile of v8, /device:TPU:3, one launch (start us, length us, event | category | flops | bytes accessed | tf_op | source)
XLA Modules:
  0.0 141.3 jit_solution(7293999224295335121)
XLA Ops:
  0.8 2.0 %shard_map.229 = (bf16[24,2048]{1,0:T(8,128)(2,1)}, bf16[24,1280]{1,0:T(8,128)(2,1)}, bf16[24,2048]{1,0:T(8,128)(2,1)}, bf16[24,1280]{1,0:T(8,128)(2,1)}) custom-call(s32[1]{0:T(128)} %bitcast.2.refs_0_, bf16[24,768]{1,0:T(8,128)(2,1)} %refs_1_.3, bf16[24,768]{1,0:T(8,128)(2,1)} %refs_2_.1, bf16[24,768]{1,0:T(8,128)(2,1)} %refs_3_.1, ...), custom_call_target="tpu_custom_call" | custom-call | flops 1000000 | bytes 1000000 | tf_op jit(solution)/shard_map/pallas_call | solution.py:105
  2.8 2.6 %collective-permute-start.2 = (bf16[24,2048]{1,0:T(8,128)(2,1)}, bf16[24,2048]{1,0:T(8,128)(2,1)S(1)}, u32[]{:S(2)}, u32[]{:S(2)}) collective-permute-start(bf16[24,2048]{1,0:T(8,128)(2,1)} %get-tuple-element.92), channel_id=1, source_target_pairs={{0,8},{1,9},{2,10},{3,11},{4,12},{5,13},{6,14},{7,15},{8,0},{9,1},... | collective-permute-start | bytes 294920 | tf_op jit(solution)/shard_map/ppermute | solution.py:696
  5.4 0.9 collective-permute-start.1
  6.6 0.9 copy-done.18
  7.5 5.9 %collective-permute-done.1.refs_2_ = bf16[24,1280]{1,0:T(8,128)(2,1)S(1)} collective-permute-done((bf16[24,1280]{1,0:T(8,128)(2,1)}, bf16[24,1280]{1,0:T(8,128)(2,1)S(1)}, u32[]{:S(2)}, u32[]{:S(2)}) %collective-permute-start.1) | collective-permute-done | bytes 61472 | tf_op jit(solution)/shard_map/ppermute | solution.py:696
  13.4 1.2 shard_map.231
  14.7 4.9 %all-to-all-start = ((bf16[8,120,640]{2,1,0:T(8,128)(2,1)}), bf16[8,120,640]{2,1,0:T(8,128)(2,1)S(1)}, u32[]{:S(2)}, u32[]{:S(2)}) async-start(bf16[8,120,640]{2,1,0:T(8,128)(2,1)} %shard_map.231), calls=%async_computation | async-start | bytes 2457600 | tf_op jit(solution)/shard_map/all_to_all | solution.py:49
  19.5 0.5 collective-permute-start.4
  20.2 1.3 shard_map.232
  21.5 0.7 copy-done.16
  22.2 14.2 %all-to-all-done.refs_3_ = bf16[8,120,640]{2,1,0:T(8,128)(2,1)S(1)} async-done(((bf16[8,120,640]{2,1,0:T(8,128)(2,1)}), bf16[8,120,640]{2,1,0:T(8,128)(2,1)S(1)}, u32[]{:S(2)}, u32[]{:S(2)}) %all-to-all-start) | async-done | bytes 1228832 | tf_op jit(solution)/shard_map/all_to_all | solution.py:49
  36.4 1.7 %shard_map.233 = (bf16[768,640]{1,0:T(8,128)(2,1)S(1)}, bf16[192,768]{1,0:T(8,128)(2,1)S(1)}, f32[8,768]{1,0:T(8,128)S(1)}, bf16[256,576]{1,0:T(8,128)(2,1)S(1)}...) custom-call(s32[1]{0:T(128)} %bitcast.2.refs_0_, ...), custom_call_target="tpu_custom_call" | custom-call | flops 1000000 | bytes 1000000 | tf_op jit(solution)/shard_map/pallas_call | solution.py:105
  38.1 1.1 collective-permute-start.5
  39.2 1.0 collective-permute-done.5
  40.6 1.5 %shard_map.234 = (bf16[256,576]{1,0:T(8,128)(2,1)S(1)}, f32[3,256,256]{2,1,0:T(8,128)S(1)}, bf16[256,192]{1,0:T(8,128)(2,1)S(1)}, f32[128,768]{1,0:T(8,128)S(1)}, bf16[128,768]{1,0:T(8,128)(2,1)S(1)}) custom-call(s32[1]{0:T(128)} %bitcast.2.refs_0_, s32[1,256]{1,0:T(1,128)S(1)} %copy-done.21, ...), custom_call_target="tpu_custom_call" | custom-call | flops 1000000 | bytes 1000000 | tf_op jit(solution)/shard_map/pallas_call | solution.py:105
  42.1 0.3 collective-permute-start.7
  42.5 3.9 %collective-permute-done.8.refs_3_ = bf16[128,768]{1,0:T(8,128)(2,1)S(1)} collective-permute-done((bf16[128,768]{1,0:T(8,128)(2,1)S(1)}, bf16[128,768]{1,0:T(8,128)(2,1)S(1)}, u32[]{:S(2)}, u32[]{:S(2)}) %collective-permute-start.8) | collective-permute-done | bytes 196640 | tf_op jit(solution)/shard_map/ppermute | solution.py:39
  46.5 1.0 shard_map.235
  47.5 16.2 %all_to_all.20 = bf16[16,40,384]{2,1,0:T(8,128)(2,1)S(1)} all-to-all(bf16[16,40,384]{2,1,0:T(8,128)(2,1)S(1)} %bitcast.44), channel_id=1, replica_groups=mesh['dp'=2,'expert'=16] {'expert'}, dimensions={0} | all-to-all | bytes 983040 | tf_op jit(solution)/shard_map/all_to_all | solution.py:43
  63.7 3.0 %collective-permute-start.9 = (bf16[640,384]{1,0:T(8,128)(2,1)S(1)}, bf16[640,384]{1,0:T(8,128)(2,1)S(1)}, u32[]{:S(2)}, u32[]{:S(2)}) collective-permute-start(bf16[640,384]{1,0:T(8,128)(2,1)S(1)} %bitcast.38), channel_id=1, source_target_pairs={{0,16},{16,0},{1,17},{17,1},{2,18},{18,2},{3,19},{19,3},{4,20},{20... | collective-permute-start | bytes 1474568 | tf_op jit(solution)/shard_map/ppermute | solution.py:34
  66.8 1.5 %collective-permute-done.9.refs_2_ = bf16[640,384]{1,0:T(8,128)(2,1)S(1)} collective-permute-done((bf16[640,384]{1,0:T(8,128)(2,1)S(1)}, bf16[640,384]{1,0:T(8,128)(2,1)S(1)}, u32[]{:S(2)}, u32[]{:S(2)}) %collective-permute-start.9) | collective-permute-done | bytes 491552 | tf_op jit(solution)/shard_map/ppermute | solution.py:34
  68.3 4.6 %shard_map.236 = (bf16[320,768]{1,0:T(8,128)(2,1)S(1)}, bf16[320,768]{1,0:T(8,128)(2,1)S(1)}, bf16[160,768]{1,0:T(8,128)(2,1)S(1)}, f32[160,16]{1,0:T(8,128)S(1)...) custom-call(s32[1]{0:T(128)} %bitcast.refs_2_.refs_0_, ...), custom_call_target="tpu_custom_call" | custom-call | flops 1000000 | bytes 1000000 | tf_op jit(solution)/shard_map/pallas_call | solution.py:105
  72.9 0.4 collective-permute-start.10
  73.3 1.5 %collective-permute-done.10.refs_2_ = bf16[2,160,768]{2,1,0:T(8,128)(2,1)S(1)} collective-permute-done((bf16[2,160,768]{2,1,0:T(8,128)(2,1)S(1)}, bf16[2,160,768]{2,1,0:T(8,128)(2,1)S(1)}, u32[]{:S(2)}, u32[]{:S(2)}) %collective-permute-start.10) | collective-permute-done | bytes 491552 | tf_op jit(solution)/shard_map/ppermute | solution.py:34
  74.8 1.3 shard_map.237
  76.1 16.3 %all_to_all.21 = bf16[16,40,384]{2,1,0:T(8,128)(2,1)S(1)} all-to-all(bf16[16,40,384]{2,1,0:T(8,128)(2,1)S(1)} %bitcast.43), channel_id=1, replica_groups=mesh['dp'=2,'expert'=16] {'expert'}, dimensions={0} | all-to-all | bytes 983040 | tf_op jit(solution)/shard_map/all_to_all | solution.py:43
  92.4 0.5 shard_map.238
  93.0 2.5 %collective-permute-start.12 = (bf16[128,768]{1,0:T(8,128)(2,1)S(1)}, bf16[128,768]{1,0:T(8,128)(2,1)S(1)}, u32[]{:S(2)}, u32[]{:S(2)}) collective-permute-start(bf16[128,768]{1,0:T(8,128)(2,1)S(1)} %get-tuple-element.121.refs_0_), channel_id=1, source_target_pairs={{0,16},{16,0},{1,17},{17,1},{2,18},{18,2},{3,19},{19,3},{4,20},{20... | collective-permute-start | bytes 589832 | tf_op jit(solution)/shard_map/ppermute | solution.py:34
  95.5 1.2 collective-permute-start.11
  96.7 3.2 %shard_map.239 = (f32[768,576]{1,0:T(8,128)S(1)}, f32[192,768]{1,0:T(8,128)S(1)}, f32[128,768]{1,0:T(8,128)S(1)}, bf16[128,768]{1,0:T(8,128)(2,1)}, bf16[256,576...) custom-call(bf16[128,768]{1,0:T(8,128)(2,1)S(1)} %get-tuple-element.121.refs_0_, ...), custom_call_target="tpu_custom_call" | custom-call | flops 1000000 | bytes 1000000 | tf_op jit(solution)/shard_map/pallas_call | solution.py:105
  99.9 2.1 %collective-permute-done.11.refs_0_ = bf16[128,768]{1,0:T(8,128)(2,1)S(1)} collective-permute-done((bf16[128,768]{1,0:T(8,128)(2,1)S(1)}, bf16[128,768]{1,0:T(8,128)(2,1)S(1)}, u32[]{:S(2)}, u32[]{:S(2)}) %collective-permute-start.11) | collective-permute-done | bytes 196640 | tf_op jit(solution)/shard_map/ppermute | solution.py:39
  102.0 0.8 collective-permute-start.13
  102.8 1.1 collective-permute-done.13.refs_1_
  103.9 2.2 %shard_map.240 = (f32[128,768]{1,0:T(8,128)S(1)}, bf16[128,768]{1,0:T(8,128)(2,1)S(1)}, bf16[256,576]{1,0:T(8,128)(2,1)S(1)}, f32[1,768]{1,0:T(1,128)S(1)}, f32[3,256]{1,0:T(4,128)S(1)}) custom-call(bf16[128,768]{1,0:T(8,128)(2,1)S(1)} %collective-permute-done.11.refs_0_, bf16[128,768]{1,0:T(8,128)(2,1)S(1)} %collective-permute-done.13.refs_1_, ...), custom_call_target="tpu_custom_call" | custom-call | flops 1000000 | bytes 1000000 | tf_op jit(solution)/shard_map/pallas_call | solution.py:105
  106.1 0.7 copy-done.12
  106.8 2.0 %shard_map.241 = bf16[8,120,640]{2,1,0:T(8,128)(2,1)} custom-call(bf16[128,768]{1,0:T(8,128)(2,1)S(1)} %collective-permute-done.11.refs_0_, bf16[128,768]{1,0:T(8,128)(2,1)S(1)} %collective-permute-done.13.refs_1_, bf16[256,192]{1,0:T(8,128)(2,1)S(1)} %get-tuple-element.128.refs_2_, bf16[256,576]{1,0:T(8,128)(2,1)S(1)} %get-tuple-element.131.refs_3_, ...), custom_call_target="tpu_custom_call" | custom-call | flops 1000000 | bytes 1000000 | tf_op jit(solution)/shard_map/pallas_call | solution.py:105
  108.9 4.7 %all-to-all-start.3 = ((bf16[8,120,640]{2,1,0:T(8,128)(2,1)}), bf16[8,120,640]{2,1,0:T(8,128)(2,1)S(1)}, u32[]{:S(2)}, u32[]{:S(2)}) async-start(bf16[8,120,640]{2,1,0:T(8,128)(2,1)} %shard_map.241), calls=%async_computation.3 | async-start | bytes 2457600 | tf_op jit(solution)/shard_map/all_to_all | solution.py:49
  113.5 0.7 collective-permute-start.15
  114.2 5.0 %fusion = f32[768,1536]{1,0:T(8,128)} fusion(bf16[320,768]{1,0:T(8,128)(2,1)} %copy-done.4, bf16[320,1536]{1,0:T(8,128)(2,1)} %copy-done.9), kind=kOutput, calls=%fused_computation.2 | convolution fusion | flops 754974720 | bytes 6193152 | tf_op jit(solution)/shard_map/dot_general | solution.py:20
  119.2 0.7 add_convert_fusion
  120.0 3.6 %fusion.1 = f32[1536,768]{1,0:T(8,128)} fusion(bf16[320,1536]{1,0:T(8,128)(2,1)S(1)} %get-tuple-element.141, bf16[320,768]{1,0:T(8,128)(2,1)S(1)} %copy-done.11), kind=kOutput, calls=%fused_computation.3 | convolution fusion | flops 754974720 | bytes 6193152 | tf_op jit(solution)/shard_map/dot_general | solution.py:20
  123.6 1.4 shard_map.242
  125.0 5.0 %all-to-all-done.3.refs_1_ = bf16[8,120,640]{2,1,0:T(8,128)(2,1)S(1)} async-done(((bf16[8,120,640]{2,1,0:T(8,128)(2,1)}), bf16[8,120,640]{2,1,0:T(8,128)(2,1)S(1)}, u32[]{:S(2)}, u32[]{:S(2)}) %all-to-all-start.3) | async-done | bytes 1228832 | tf_op jit(solution)/shard_map/all_to_all | solution.py:49
  130.3 3.6 %collective-permute-start.17 = (bf16[24,1280]{1,0:T(8,128)(2,1)S(1)}, bf16[24,1280]{1,0:T(8,128)(2,1)S(1)}, u32[]{:S(2)}, u32[]{:S(2)}) collective-permute-start(bf16[24,1280]{1,0:T(8,128)(2,1)S(1)} %get-tuple-element.155), channel_id=1, source_target_pairs={{0,24},{1,25},{2,26},{3,27},{4,28},{5,29},{6,30},{7,31},{8,16},{9,... | collective-permute-start | bytes 184328 | tf_op jit(solution)/shard_map/ppermute | solution.py:696
  133.9 1.0 copy-done.15
  134.9 1.9 %shard_map.243 = bf16[128,768]{1,0:T(8,128)(2,1)} custom-call(f32[128,768]{1,0:T(8,128)S(1)} %copy-done.15, bf16[128,768]{1,0:T(8,128)(2,1)S(1)} %collective-permute-done.14.refs_1_, bf16[128,768]{1,0:T(8,128)(2,1)} %collective-permute-done.16.refs_2_, f32[128,768]{1,0:T(8,128)S(1)} %get-tuple-element.152.refs_3_, bf16[128,768]{1,0:T(8,128)(2,1)S(1)} %bitcast.35, ...), custom_call_target="tpu_custom_call" | custom-call | flops 1000000 | bytes 1000000 | tf_op jit(solution)/shard_map/pallas_call | solution.py:105
  136.8 3.7 %collective-permute-done.17.refs_2_ = bf16[24,1280]{1,0:T(8,128)(2,1)S(1)} collective-permute-done((bf16[24,1280]{1,0:T(8,128)(2,1)S(1)}, bf16[24,1280]{1,0:T(8,128)(2,1)S(1)}, u32[]{:S(2)}, u32[]{:S(2)}) %collective-permute-start.17) | collective-permute-done | bytes 61472 | tf_op jit(solution)/shard_map/ppermute | solution.py:696
  140.4 0.9 shard_map.245
  (73 shorter events, 1.6 us)
Async XLA Ops:
  0.6 19.4 %copy-start.24 = (f32[32,12]{0,1:T(8,128)S(1)}, f32[32,12]{0,1:T(8,128)}, u32[]{:S(2)}) copy-start(f32[32,12]{0,1:T(8,128)} %param.20) | copy-start | bytes 4612
  0.7 19.5 %copy-start.22 = (s32[1,128,1]{1,2,0:T(1,128)S(1)}, s32[1,128,1]{1,2,0:T(1,128)}, u32[]{:S(2)}) copy-start(s32[1,128,1]{1,2,0:T(1,128)} %param.26) | copy-start | bytes 1540
  0.7 12.8 %collective-permute-start = (bf16[128,768]{1,0:T(8,128)(2,1)}, bf16[128,768]{1,0:T(8,128)(2,1)S(1)}, u32[]{:S(2)}, u32[]{:S(2)}) collective-permute-start(bf16[128,768]{1,0:T(8,128)(2,1)} %bitcast.30), channel_id=1, source_target_pairs={{0,1},{1,0},{2,3},{3,2},{4,5},{5,4},{6,7},{7,6},{8,9},{9,8},{10,11... | collective-permute-start | bytes 589832 | tf_op jit(solution)/shard_map/ppermute | solution.py:39
  2.8 10.6 %collective-permute-start.2 = (bf16[24,2048]{1,0:T(8,128)(2,1)}, bf16[24,2048]{1,0:T(8,128)(2,1)S(1)}, u32[]{:S(2)}, u32[]{:S(2)}) collective-permute-start(bf16[24,2048]{1,0:T(8,128)(2,1)} %get-tuple-element.92), channel_id=1, source_target_pairs={{0,8},{1,9},{2,10},{3,11},{4,12},{5,13},{6,14},{7,15},{8,0},{9,1},... | collective-permute-start | bytes 294920 | tf_op jit(solution)/shard_map/ppermute | solution.py:696
  5.4 8.0 %collective-permute-start.1 = (bf16[24,1280]{1,0:T(8,128)(2,1)}, bf16[24,1280]{1,0:T(8,128)(2,1)S(1)}, u32[]{:S(2)}, u32[]{:S(2)}) collective-permute-start(bf16[24,1280]{1,0:T(8,128)(2,1)} %get-tuple-element.91), channel_id=1, source_target_pairs={{0,24},{1,25},{2,26},{3,27},{4,28},{5,29},{6,30},{7,31},{8,16},{9,... | collective-permute-start | bytes 184328 | tf_op jit(solution)/shard_map/ppermute | solution.py:696
  6.3 7.1 %collective-permute-start.3 = (bf16[24,1280]{1,0:T(8,128)(2,1)}, bf16[24,1280]{1,0:T(8,128)(2,1)S(1)}, u32[]{:S(2)}, u32[]{:S(2)}) collective-permute-start(bf16[24,1280]{1,0:T(8,128)(2,1)} %get-tuple-element.93), channel_id=1, source_target_pairs={{0,16},{1,17},{2,18},{3,19},{4,20},{5,21},{6,22},{7,23},{8,24},{9,... | collective-permute-start | bytes 184328 | tf_op jit(solution)/shard_map/ppermute | solution.py:696
  6.6 0.9 copy-start.18
  14.7 24.5 %copy-start = (bf16[1,128,768]{2,1,0:T(8,128)(2,1)S(1)}, bf16[1,128,768]{2,1,0:T(8,128)(2,1)}, u32[]{:S(2)}) copy-start(bf16[1,128,768]{2,1,0:T(8,128)(2,1)} %param.14) | copy-start | bytes 589828
  14.7 25.9 %copy-start.21 = (s32[1,256]{1,0:T(1,128)S(1)}, s32[1,256]{1,0:T(1,128)}, u32[]{:S(2)}) copy-start(s32[1,256]{1,0:T(1,128)} %refs_1_.4) | copy-start | bytes 3076
  14.7 21.7 %all-to-all-start = ((bf16[8,120,640]{2,1,0:T(8,128)(2,1)}), bf16[8,120,640]{2,1,0:T(8,128)(2,1)S(1)}, u32[]{:S(2)}, u32[]{:S(2)}) async-start(bf16[8,120,640]{2,1,0:T(8,128)(2,1)} %shard_map.231), calls=%async_computation | async-start | bytes 2457600 | tf_op jit(solution)/shard_map/all_to_all | solution.py:49
  19.5 26.9 %copy-start.3 = (bf16[1,128,768]{2,1,0:T(8,128)(2,1)S(1)}, bf16[1,128,768]{2,1,0:T(8,128)(2,1)}, u32[]{:S(2)}) copy-start(bf16[1,128,768]{2,1,0:T(8,128)(2,1)} %param.27) | copy-start | bytes 589828
  19.5 2.7 %collective-permute-start.4 = (bf16[128,768]{1,0:T(8,128)(2,1)S(1)}, bf16[128,768]{1,0:T(8,128)(2,1)S(1)}, u32[]{:S(2)}, u32[]{:S(2)}) collective-permute-start(bf16[128,768]{1,0:T(8,128)(2,1)S(1)} %collective-permute-done.refs_4_.refs_7_.refs_5_), channel_id=1, source_target_pairs={{0,16},{16,0},{1,17},{17,1},{2,18},{18,2},{3,19},{19,3},{4,20},{20... | collective-permute-start | bytes 589832 | tf_op jit(solution)/shard_map/ppermute | solution.py:34
  21.5 0.7 copy-start.16
  22.2 70.2 %copy-start.7 = (bf16[2,128,640]{2,1,0:T(8,128)(2,1)}, bf16[2,128,640]{2,1,0:T(8,128)(2,1)S(1)}, u32[]{:S(2)}) copy-start(bf16[2,128,640]{2,1,0:T(8,128)(2,1)S(1)} %get-tuple-element.119.refs_1_) | copy-start | bytes 983044
  38.1 2.1 %collective-permute-start.5 = (bf16[128,768]{1,0:T(8,128)(2,1)S(1)}, bf16[128,768]{1,0:T(8,128)(2,1)S(1)}, u32[]{:S(2)}, u32[]{:S(2)}) collective-permute-start(bf16[128,768]{1,0:T(8,128)(2,1)S(1)} %get-tuple-element.102), channel_id=1, source_target_pairs={{0,16},{16,0},{1,17},{17,1},{2,18},{18,2},{3,19},{19,3},{4,20},{20... | collective-permute-start | bytes 589832 | tf_op jit(solution)/shard_map/ppermute | solution.py:34
  39.2 1.4 %collective-permute-start.6 = (bf16[128,768]{1,0:T(8,128)(2,1)S(1)}, bf16[128,768]{1,0:T(8,128)(2,1)S(1)}, u32[]{:S(2)}, u32[]{:S(2)}) collective-permute-start(bf16[128,768]{1,0:T(8,128)(2,1)S(1)} %bitcast.31), channel_id=1, source_target_pairs={{0,16},{16,0},{1,17},{17,1},{2,18},{18,2},{3,19},{19,3},{4,20},{20... | collective-permute-start | bytes 589832 | tf_op jit(solution)/shard_map/ppermute | solution.py:34
  40.2 28.0 %copy-start.2 = (bf16[1,1536,768]{2,1,0:T(8,128)(2,1)S(1)}, bf16[1,1536,768]{2,1,0:T(8,128)(2,1)}, u32[]{:S(2)}) copy-start(bf16[1,1536,768]{2,1,0:T(8,128)(2,1)} %param.24) | copy-start | bytes 7077892
  40.3 28.0 %copy-start.1 = (bf16[1,768,1536]{2,1,0:T(8,128)(2,1)S(1)}, bf16[1,768,1536]{2,1,0:T(8,128)(2,1)}, u32[]{:S(2)}) copy-start(bf16[1,768,1536]{2,1,0:T(8,128)(2,1)} %param.23) | copy-start | bytes 7077892
  40.3 6.2 %collective-permute-start.8 = (bf16[128,768]{1,0:T(8,128)(2,1)S(1)}, bf16[128,768]{1,0:T(8,128)(2,1)S(1)}, u32[]{:S(2)}, u32[]{:S(2)}) collective-permute-start(bf16[128,768]{1,0:T(8,128)(2,1)S(1)} %add_convert_fusion.1), channel_id=1, source_target_pairs={{0,1},{1,0},{2,3},{3,2},{4,5},{5,4},{6,7},{7,6},{8,9},{9,8},{10,11... | collective-permute-start | bytes 589832 | tf_op jit(solution)/shard_map/ppermute | solution.py:39
  42.1 4.4 %collective-permute-start.7 = (bf16[128,768]{1,0:T(8,128)(2,1)S(1)}, bf16[128,768]{1,0:T(8,128)(2,1)S(1)}, u32[]{:S(2)}, u32[]{:S(2)}) collective-permute-start(bf16[128,768]{1,0:T(8,128)(2,1)S(1)} %get-tuple-element.108), channel_id=1, source_target_pairs={{0,16},{16,0},{1,17},{17,1},{2,18},{18,2},{3,19},{19,3},{4,20},{20... | collective-permute-start | bytes 589832 | tf_op jit(solution)/shard_map/ppermute | solution.py:34
  47.5 20.8 %copy-start.19 = (f32[128,1]{1,0:T(8,128)}, f32[128,1]{1,0:T(8,128)S(1)}, u32[]{:S(2)}) copy-start(f32[128,1]{1,0:T(8,128)S(1)} %get-tuple-element.144.refs_6_) | copy-start | bytes 1540
  47.5 44.9 %copy-start.5 = (f32[128,768]{1,0:T(8,128)}, f32[128,768]{1,0:T(8,128)S(1)}, u32[]{:S(2)}) copy-start(f32[128,768]{1,0:T(8,128)S(1)} %get-tuple-element.120.refs_2_.refs_3_) | copy-start | bytes 1179652
  63.7 4.5 %collective-permute-start.9 = (bf16[640,384]{1,0:T(8,128)(2,1)S(1)}, bf16[640,384]{1,0:T(8,128)(2,1)S(1)}, u32[]{:S(2)}, u32[]{:S(2)}) collective-permute-start(bf16[640,384]{1,0:T(8,128)(2,1)S(1)} %bitcast.38), channel_id=1, source_target_pairs={{0,16},{16,0},{1,17},{17,1},{2,18},{18,2},{3,19},{19,3},{4,20},{20... | collective-permute-start | bytes 1474568 | tf_op jit(solution)/shard_map/ppermute | solution.py:34
  72.8 20.1 %copy-start.4 = (bf16[320,768]{1,0:T(8,128)(2,1)}, bf16[320,768]{1,0:T(8,128)(2,1)S(1)}, u32[]{:S(2)}) copy-start(bf16[320,768]{1,0:T(8,128)(2,1)S(1)} %get-tuple-element.114) | copy-start | bytes 1474564
  72.9 20.1 %copy-start.10 = (bf16[320,768]{1,0:T(8,128)(2,1)}, bf16[320,768]{1,0:T(8,128)(2,1)S(1)}, u32[]{:S(2)}) copy-start(bf16[320,768]{1,0:T(8,128)(2,1)S(1)} %get-tuple-element.142) | copy-start | bytes 1474564
  72.9 33.2 %copy-start.9 = (bf16[320,1536]{1,0:T(8,128)(2,1)}, bf16[320,1536]{1,0:T(8,128)(2,1)S(1)}, u32[]{:S(2)}) copy-start(bf16[320,1536]{1,0:T(8,128)(2,1)S(1)} %get-tuple-element.140) | copy-start | bytes 2949124
  72.9 1.9 %collective-permute-start.10 = (bf16[2,160,768]{2,1,0:T(8,128)(2,1)S(1)}, bf16[2,160,768]{2,1,0:T(8,128)(2,1)S(1)}, u32[]{:S(2)}, u32[]{:S(2)}) collective-permute-start(bf16[2,160,768]{2,1,0:T(8,128)(2,1)S(1)} %get-tuple-element.113), channel_id=1, source_target_pairs={{0,16},{16,0},{1,17},{17,1},{2,18},{18,2},{3,19},{19,3},{4,20},{20... | collective-permute-start | bytes 1474568 | tf_op jit(solution)/shard_map/ppermute | solution.py:34
  93.0 3.7 %collective-permute-start.12 = (bf16[128,768]{1,0:T(8,128)(2,1)S(1)}, bf16[128,768]{1,0:T(8,128)(2,1)S(1)}, u32[]{:S(2)}, u32[]{:S(2)}) collective-permute-start(bf16[128,768]{1,0:T(8,128)(2,1)S(1)} %get-tuple-element.121.refs_0_), channel_id=1, source_target_pairs={{0,16},{16,0},{1,17},{17,1},{2,18},{18,2},{3,19},{19,3},{4,20},{20... | collective-permute-start | bytes 589832 | tf_op jit(solution)/shard_map/ppermute | solution.py:34
  95.5 6.5 %collective-permute-start.11 = (bf16[128,768]{1,0:T(8,128)(2,1)S(1)}, bf16[128,768]{1,0:T(8,128)(2,1)S(1)}, u32[]{:S(2)}, u32[]{:S(2)}) collective-permute-start(bf16[128,768]{1,0:T(8,128)(2,1)S(1)} %get-tuple-element.121.refs_0_), channel_id=1, source_target_pairs={{0,1},{1,0},{2,3},{3,2},{4,5},{5,4},{6,7},{7,6},{8,9},{9,8},{10,11... | collective-permute-start | bytes 589832 | tf_op jit(solution)/shard_map/ppermute | solution.py:39
  99.9 8.9 %copy-start.14 = (f32[128,768]{1,0:T(8,128)}, f32[128,768]{1,0:T(8,128)S(1)}, u32[]{:S(2)}) copy-start(f32[128,768]{1,0:T(8,128)S(1)} %get-tuple-element.148.refs_0_) | copy-start | bytes 1179652
  102.0 1.9 %collective-permute-start.13 = (bf16[128,768]{1,0:T(8,128)(2,1)S(1)}, bf16[128,768]{1,0:T(8,128)(2,1)S(1)}, u32[]{:S(2)}, u32[]{:S(2)}) collective-permute-start(bf16[128,768]{1,0:T(8,128)(2,1)S(1)} %collective-permute-done.11.refs_0_), channel_id=1, source_target_pairs={{0,16},{16,0},{1,17},{17,1},{2,18},{18,2},{3,19},{19,3},{4,20},{20... | collective-permute-start | bytes 589832 | tf_op jit(solution)/shard_map/ppermute | solution.py:34
  106.1 0.7 copy-start.12
  106.8 2.0 %copy-start.23 = (bf16[128,768]{1,0:T(8,128)(2,1)}, bf16[128,768]{1,0:T(8,128)(2,1)S(1)}, u32[]{:S(2)}) copy-start(bf16[128,768]{1,0:T(8,128)(2,1)S(1)} %get-tuple-element.151) | copy-start | bytes 589828
  108.9 21.1 %all-to-all-start.3 = ((bf16[8,120,640]{2,1,0:T(8,128)(2,1)}), bf16[8,120,640]{2,1,0:T(8,128)(2,1)S(1)}, u32[]{:S(2)}, u32[]{:S(2)}) async-start(bf16[8,120,640]{2,1,0:T(8,128)(2,1)} %shard_map.241), calls=%async_computation.3 | async-start | bytes 2457600 | tf_op jit(solution)/shard_map/all_to_all | solution.py:49
  113.5 5.7 %collective-permute-start.15 = (bf16[128,768]{1,0:T(8,128)(2,1)}, bf16[128,768]{1,0:T(8,128)(2,1)S(1)}, u32[]{:S(2)}, u32[]{:S(2)}) collective-permute-start(bf16[128,768]{1,0:T(8,128)(2,1)} %copy-done.23), channel_id=1, source_target_pairs={{0,16},{16,0},{1,17},{17,1},{2,18},{18,2},{3,19},{19,3},{4,20},{20... | collective-permute-start | bytes 589832 | tf_op jit(solution)/shard_map/ppermute | solution.py:34
  114.2 5.1 %copy-start.13 = (f32[128,768]{1,0:T(8,128)S(1)}, f32[128,768]{1,0:T(8,128)}, u32[]{:S(2)}) copy-start(f32[128,768]{1,0:T(8,128)} %copy-done.12) | copy-start | bytes 1179652
  114.2 5.8 %copy-start.11 = (bf16[320,768]{1,0:T(8,128)(2,1)S(1)}, bf16[320,768]{1,0:T(8,128)(2,1)}, u32[]{:S(2)}) copy-start(bf16[320,768]{1,0:T(8,128)(2,1)} %copy-done.10) | copy-start | bytes 1474564
  119.2 14.7 %collective-permute-start.14 = (bf16[128,768]{1,0:T(8,128)(2,1)}, bf16[128,768]{1,0:T(8,128)(2,1)S(1)}, u32[]{:S(2)}, u32[]{:S(2)}) collective-permute-start(bf16[128,768]{1,0:T(8,128)(2,1)} %get-tuple-element.149), channel_id=1, source_target_pairs={{0,16},{16,0},{1,17},{17,1},{2,18},{18,2},{3,19},{19,3},{4,20},{20... | collective-permute-start | bytes 589832 | tf_op jit(solution)/shard_map/ppermute | solution.py:34
  119.9 14.0 %collective-permute-start.16 = (bf16[128,768]{1,0:T(8,128)(2,1)}, bf16[128,768]{1,0:T(8,128)(2,1)}, u32[]{:S(2)}, u32[]{:S(2)}) collective-permute-start(bf16[128,768]{1,0:T(8,128)(2,1)} %add_convert_fusion), channel_id=1, source_target_pairs={{0,1},{1,0},{2,3},{3,2},{4,5},{5,4},{6,7},{7,6},{8,9},{9,8},{10,11... | collective-permute-start | bytes 589832 | tf_op jit(solution)/shard_map/ppermute | solution.py:39
  119.9 3.6 %copy-start.6 = (f32[128,768]{1,0:T(8,128)S(1)}, f32[128,768]{1,0:T(8,128)}, u32[]{:S(2)}) copy-start(f32[128,768]{1,0:T(8,128)} %copy-done.5) | copy-start | bytes 1179652
  119.9 3.6 %copy-start.8 = (bf16[2,128,640]{2,1,0:T(8,128)(2,1)S(1)}, bf16[2,128,640]{2,1,0:T(8,128)(2,1)}, u32[]{:S(2)}) copy-start(bf16[2,128,640]{2,1,0:T(8,128)(2,1)} %copy-done.7) | copy-start | bytes 983044
  119.9 3.6 %copy-start.17 = (bf16[2,128,640]{2,1,0:T(8,128)(2,1)S(1)}, bf16[2,128,640]{2,1,0:T(8,128)(2,1)}, u32[]{:S(2)}) copy-start(bf16[2,128,640]{2,1,0:T(8,128)(2,1)} %copy-done.16) | copy-start | bytes 983044
  119.9 3.6 %copy-start.20 = (f32[128,1]{1,0:T(8,128)S(1)}, f32[128,1]{1,0:T(8,128)}, u32[]{:S(2)}) copy-start(f32[128,1]{1,0:T(8,128)} %copy-done.19) | copy-start | bytes 1540
  130.2 10.2 %collective-permute-start.18 = (bf16[24,2048]{1,0:T(8,128)(2,1)S(1)}, bf16[24,2048]{1,0:T(8,128)(2,1)S(1)}, u32[]{:S(2)}, u32[]{:S(2)}) collective-permute-start(bf16[24,2048]{1,0:T(8,128)(2,1)S(1)} %get-tuple-element.156), channel_id=1, source_target_pairs={{0,8},{1,9},{2,10},{3,11},{4,12},{5,13},{6,14},{7,15},{8,0},{9,1},... | collective-permute-start | bytes 294920 | tf_op jit(solution)/shard_map/ppermute | solution.py:696
  130.3 10.1 %collective-permute-start.17 = (bf16[24,1280]{1,0:T(8,128)(2,1)S(1)}, bf16[24,1280]{1,0:T(8,128)(2,1)S(1)}, u32[]{:S(2)}, u32[]{:S(2)}) collective-permute-start(bf16[24,1280]{1,0:T(8,128)(2,1)S(1)} %get-tuple-element.155), channel_id=1, source_target_pairs={{0,24},{1,25},{2,26},{3,27},{4,28},{5,29},{6,30},{7,31},{8,16},{9,... | collective-permute-start | bytes 184328 | tf_op jit(solution)/shard_map/ppermute | solution.py:696
  133.9 6.5 %collective-permute-start.19 = (bf16[24,1280]{1,0:T(8,128)(2,1)S(1)}, bf16[24,1280]{1,0:T(8,128)(2,1)S(1)}, u32[]{:S(2)}, u32[]{:S(2)}) collective-permute-start(bf16[24,1280]{1,0:T(8,128)(2,1)S(1)} %get-tuple-element.157), channel_id=1, source_target_pairs={{0,16},{1,17},{2,18},{3,19},{4,20},{5,21},{6,22},{7,23},{8,24},{9,... | collective-permute-start | bytes 184328 | tf_op jit(solution)/shard_map/ppermute | solution.py:696
  133.9 1.0 copy-start.15
